TPU v7x, 32 devices: a whole 2x2x4 slice. The times are simulated.
32 devices in a mesh: section: 2 (over core), seq: 4 (over y, x), mp: 4 (over z).
Axes of the slice: x: 2, y: 2, z: 4, core: 2. Of those that a mesh axis runs over, the one named last changes fastest.
Arguments:
- patches: bfloat16 [4, 256, 1280], P('seq'), may hold values from -50 to 50
- image_place: int32 [4, 4, 16], replicated, may hold values from -1 to 31, as said below
- slot_map: int32 [4, 4], replicated, may hold values from 0 to 15, as said below
- text: bfloat16 [4, 128, 8192], P('seq', ('section', 'mp')), may hold values from -50 to 50
- vision_gain: float32 [1280], replicated, may hold values from 0.25 to 1.75
- qkv_weight: bfloat16 [1280, 3, 1280], P(None, None, ('section', 'mp')), may hold values from -0.15625 to 0.15625
- qkv_bias: float32 [3, 1280], P(None, ('section', 'mp')), may hold values from -4 to 4
- out_weight: bfloat16 [1280, 1280], P(('section', 'mp')), may hold values from -0.625 to 0.625
- out_bias: float32 [1280], replicated, may hold values from -4 to 4
- merge_gain: float32 [1280], replicated, may hold values from 0.25 to 1.75
- merge_up: bfloat16 [5120, 2560], P(None, ('section', 'mp')), may hold values from -0.078125 to 0.078125
- merge_up_bias: float32 [2560], P(('section', 'mp')), may hold values from -4 to 4
- merge_down: bfloat16 [2560, 8192], P(('section', 'mp')), may hold values from -0.125 to 0.125
- merge_down_bias: float32 [8192], replicated, may hold values from -4 to 4
- input_gain: float32 [8192], replicated, may hold values from 0.25 to 1.75
- kv_weight: bfloat16 [8192, 2048], P(None, ('section', 'mp')), may hold values from -0.0625 to 0.0625
- kv_bias: float32 [2048], P(('section', 'mp')), may hold values from -4 to 4
Outputs:
- kv_cache: bfloat16 [2, 16, 32, 1024], P('section', 'seq', None, 'mp')
Inputs may be any that keep to these rules, and one draw needn't show every extreme that they name: In every window the units w with image_place >= 0 come first and are at least one; their values are distinct and form a run of consecutive positions; some window has all 16 units placed. slot_map maps the requests one to one onto the slots; the owners slot_map[j, i] // 4 of the 4 requests of any shard j are all different.
All inputs are finite; a program needn't handle non-finite values.
Results may differ from a plain program's by a relative error of at most 0.01.
Values may be sent and summed in bfloat16 or wider, within the bound.
No kernel may reach another device: no remote copies, remote signals or barrier semaphores. Data moves between devices by JAX's collectives and lax.ppermute only.
A program may use at most 128 MiB of HBM per device.

v0:
```python
import math

import jax
import jax.numpy as jnp
from jax import lax
from jax.sharding import PartitionSpec as P

VHEAD = 80
CTX = 32


NORM_EPS = 1e-06


def rms_scaled(values, gain):
    float_values = values.astype(jnp.float32)
    return (
        float_values
        * lax.rsqrt(jnp.mean(float_values * float_values, axis=-1, keepdims=True) + NORM_EPS)
        * gain
    )


def shards(
    patches,
    image_place,
    slot_map,
    text,
    vision_gain,
    qkv_weight,
    qkv_bias,
    out_weight,
    out_bias,
    merge_gain,
    merge_up,
    merge_up_bias,
    merge_down,
    merge_down_bias,
    input_gain,
    kv_weight,
    kv_bias,
):
    group_count = lax.axis_size(("section", "mp"))
    shard_count = lax.axis_size("seq")
    own_shard = lax.axis_index("seq")
    patch_rows = patches[0]
    row_total, vision_width = patch_rows.shape
    unit_count = image_place.shape[2]
    window_rows = 4 * unit_count
    own_units = lax.dynamic_index_in_dim(image_place, own_shard, 0, keepdims=False)
    normed_patches = rms_scaled(patch_rows, vision_gain).astype(jnp.bfloat16)
    projected = jnp.einsum(
        "rd,dtc->trc", normed_patches, qkv_weight, preferred_element_type=jnp.float32
    )
    projected = (projected + qkv_bias[:, None, :]).astype(jnp.bfloat16)
    head_here = projected.shape[2] // VHEAD
    split_shape = (shard_count, window_rows, head_here, VHEAD)
    queries = projected[0].reshape(split_shape)
    key_rows = projected[1].reshape(split_shape)
    value_rows = projected[2].reshape(split_shape)
    scores = jnp.einsum(
        "bqhe,bkhe->bhqk", queries, key_rows, preferred_element_type=jnp.float32
    ) / math.sqrt(VHEAD)
    key_mask = jnp.repeat((own_units >= 0).astype(jnp.float32), 4, axis=1)
    raised = jnp.exp(scores) * key_mask[:, None, None, :]
    probs = (raised / jnp.sum(raised, axis=-1, keepdims=True)).astype(jnp.bfloat16)
    head_out = jnp.einsum("bhqk,bkhe->bqhe", probs, value_rows, preferred_element_type=jnp.float32)
    head_out = head_out.astype(jnp.bfloat16).reshape(row_total, head_here * VHEAD)
    partial_out = jnp.dot(head_out, out_weight, preferred_element_type=jnp.float32)
    attended = lax.psum(partial_out.astype(jnp.bfloat16), ("section", "mp")).astype(jnp.float32)
    residual_rows = patch_rows.astype(jnp.float32) + attended + out_bias
    merge_rows = (
        rms_scaled(residual_rows, merge_gain)
        .astype(jnp.bfloat16)
        .reshape(row_total // 4, 4 * vision_width)
    )
    hidden_rows = jax.nn.gelu(
        jnp.dot(merge_rows, merge_up, preferred_element_type=jnp.float32) + merge_up_bias,
        approximate=False,
    ).astype(jnp.bfloat16)
    share = unit_count // group_count
    hidden_width = hidden_rows.shape[1]
    ordered = hidden_rows.reshape(shard_count, group_count, share, hidden_width).transpose(
        1, 0, 2, 3
    )
    ordered = ordered.reshape(group_count * shard_count * share, hidden_width)
    merged = lax.psum_scatter(
        jnp.dot(ordered, merge_down, preferred_element_type=jnp.float32).astype(jnp.bfloat16),
        ("section", "mp"),
        scatter_dimension=0,
        tiled=True,
    ).astype(jnp.float32)
    image_own = (
        (merged + merge_down_bias).astype(jnp.bfloat16).reshape(shard_count, share, merged.shape[1])
    )
    model_width = image_own.shape[2]
    text_rows = text[0]
    text_all, image_all = (
        lax.all_gather(text_rows, ("section", "mp"), axis=0, tiled=True),
        lax.all_gather(image_own, ("section", "mp"), axis=1, tiled=True),
    )
    image_mine = lax.all_to_all(image_all, "seq", split_axis=0, concat_axis=0, tiled=True)
    prompt_text = rms_scaled(text_all, input_gain).astype(jnp.bfloat16)
    prompt_image = rms_scaled(image_mine, input_gain).astype(jnp.bfloat16)
    prompt_total = prompt_text.shape[0]
    place_here = lax.dynamic_index_in_dim(image_place, own_shard, 1, keepdims=False)
    starts = (jnp.arange(shard_count, dtype=jnp.int32) * CTX)[:, None]
    target = jnp.where(place_here >= 0, starts + place_here, prompt_total).reshape(-1)
    prompt = prompt_text.at[target].set(prompt_image.reshape(-1, model_width), mode="drop")
    keyval = (jnp.dot(prompt, kv_weight, preferred_element_type=jnp.float32) + kv_bias).astype(
        jnp.bfloat16
    )
    kv_width = keyval.shape[1]
    requests = keyval.reshape(shard_count, CTX, kv_width)
    owner_ids = jnp.arange(shard_count, dtype=jnp.int32)
    slot_row = lax.dynamic_index_in_dim(slot_map, own_shard, 0, keepdims=False)
    chosen = slot_row[None, :] // shard_count == owner_ids[:, None]
    send_order = jnp.sum(jnp.where(chosen, owner_ids[None, :], 0), axis=1)
    outgoing = jnp.take(requests, send_order, axis=0)
    incoming = lax.all_to_all(outgoing, "seq", split_axis=0, concat_axis=0, tiled=True)
    mine = slot_map // shard_count == own_shard
    seat = jnp.sum(jnp.where(mine, slot_map % shard_count, 0), axis=1)
    source_of_seat = jnp.sum(
        jnp.where(seat[None, :] == owner_ids[:, None], owner_ids[None, :], 0), axis=1
    )
    cache = jnp.take(incoming, source_of_seat, axis=0)
    return cache[None]


def solution(mesh):
    placed = (
        P("seq", None, None),
        P(),
        P(),
        P("seq", ("section", "mp"), None),
        P(),
        P(None, None, ("section", "mp")),
        P(None, ("section", "mp")),
        P(("section", "mp"), None),
        P(),
        P(),
        P(None, ("section", "mp")),
        P(("section", "mp")),
        P(("section", "mp"), None),
        P(),
        P(),
        P(None, ("section", "mp")),
        P(("section", "mp")),
    )
    return jax.shard_map(
        shards,
        mesh=mesh,
        in_specs=placed,
        out_specs=P("section", "seq", None, "mp"),
        check_vma=False,
    )
```

profile of v0, /device:TPU:10, one launch (start us, length us, event | category | flops | bytes accessed | tf_op | source)
XLA Modules:
  0.0 232.0 jit_solution(17792721740241612997)
XLA Ops:
  6.5 1.5 fusion.6
  8.0 2.1 fusion.14
  10.9 0.8 reshape_squeeze.9
  11.7 1.0 reshape_squeeze.11
  12.7 0.8 reshape_squeeze.10
  13.7 1.9 fusion.11
  15.6 2.0 fusion.12
  17.6 1.1 copy.39
  18.8 2.2 convolution_convert_fusion.1
  21.1 57.2 %all-reduce.2.cloned.1.call-done = bf16[256,1280]{1,0:T(8,128)(2,1)} async-done(((bf16[256,1280]{1,0:T(8,128)(2,1)}), bf16[256,1280]{1,0:T(8,128)(2,1)}) %all-reduce.2.cloned.1.call-update) | async-done | bytes 655376 | tf_op jit(solution)/shard_map/psum | solution.py:70
  78.4 1.6 multiply_reduce_fusion
  80.0 2.4 %multiply_convert_fusion = bf16[256,1280]{1,0:T(8,128)(2,1)} fusion(bf16[256,1280]{1,0:T(8,128)(2,1)} %all-reduce.2.cloned.1.call-done, bf16[1,256,1280]{2,1,0:T(8,128)(2,1)} %param.19, f32[1280]{0:T(1024)S(1)} %copy-done.4, f32[256]{0:T(256)S(1)} %add_rsqrt_fusion.1, f32[1280]{0:T(1024)S(1)} %copy-done.2), kind=kLoop, calls=%fused_computation.22 | loop fusion | flops 2293760 | bytes 1977344 | tf_op jit(solution)/shard_map/convert_element_type | solution.py:74
  82.5 2.2 reshape.122
  84.7 2.3 %fusion.27 = bf16[64,320]{1,0:T(8,128)(2,1)S(1)} fusion(bf16[64,5120]{1,0:T(8,128)(2,1)} %reshape.122, bf16[5120,320]{0,1:T(8,128)(2,1)S(1)} %copy-done, f32[320]{0:T(512)S(1)} %copy-done.9), kind=kOutput, calls=%fused_computation.47 | convolution fusion | flops 211066880 | bytes 3974400 | tf_op jit(solution)/shard_map/dot_general | solution.py:78
  87.2 4.6 %convolution_convert_fusion = bf16[64,8192]{1,0:T(8,128)(2,1)} fusion(bf16[64,320]{1,0:T(8,128)(2,1)S(1)} %reshape.124, bf16[320,8192]{1,0:T(8,128)(2,1)} %param.31), kind=kOutput, calls=%fused_computation.3 | convolution fusion | flops 336068608 | bytes 6332416 | tf_op jit(solution)/shard_map/dot_general | solution.py:88
  93.5 31.8 %reduce-scatter.2.cloned.1.call-done = bf16[8,8192]{1,0:T(8,128)(2,1)} async-done(((bf16[64,8192]{1,0:T(8,128)(2,1)}), bf16[8,8192]{1,0:T(8,128)(2,1)}) %reduce-scatter.2.cloned.1.call-update) | async-done | bytes 131088 | tf_op jit(solution)/shard_map/reduce_scatter | solution.py:87
  125.4 0.9 add_convert_fusion.1
  126.4 0.8 copy.41
  128.8 28.5 %all-gather.6.cloned.1.call-done = bf16[1,128,8192]{2,1,0:T(8,128)(2,1)} async-done(((bf16[1,16,8192]{2,1,0:T(8,128)(2,1)}), bf16[1,128,8192]{2,1,0:T(8,128)(2,1)}) %all-gather.6.cloned.1.call-update) | async-done | bytes 2097168 | tf_op jit(solution)/shard_map/all_gather | solution.py:99
  157.3 2.1 fusion
  159.4 21.2 %all-gather.4.cloned.1.call-done = bf16[4,16,8192]{2,0,1:T(4,128)(2,1)} async-done(((bf16[4,2,8192]{2,0,1:T(4,128)(2,1)}), bf16[4,16,8192]{2,0,1:T(4,128)(2,1)}) %all-gather.4.cloned.1.call-update) | async-done | bytes 1048592 | tf_op jit(solution)/shard_map/all_gather | solution.py:100
  180.6 2.8 %copy.42 = bf16[4,16,8192]{2,1,0:T(8,128)(2,1)} copy(bf16[4,16,8192]{2,0,1:T(4,128)(2,1)} %all-gather.4.cloned.1.call-done) | data formatting | bytes 2097152 | tf_op jit(solution)/shard_map/all_gather | solution.py:100
  183.4 4.8 %all-to-all-start = ((bf16[4,16,8192]{2,1,0:T(8,128)(2,1)}), bf16[4,16,8192]{2,1,0:T(8,128)(2,1)}, u32[]{:S(2)}, u32[]{:S(2)}) async-start(bf16[4,16,8192]{2,1,0:T(8,128)(2,1)} %copy.42), calls=%async_computation.1 | async-start | bytes 2097152 | tf_op jit(solution)/shard_map/all_to_all | solution.py:102
  188.3 3.5 %fusion.2 = bf16[128,8192]{1,0:T(8,128)(2,1)} fusion(bf16[1,128,8192]{2,1,0:T(8,128)(2,1)} %all-gather.6.cloned.1.call-done, f32[8192]{0:T(1024)S(1)} %copy-done.1, f32[128]{0:T(128)S(1)} %add_rsqrt_fusion.3), kind=kLoop, calls=%fused_computation.8 | loop fusion | flops 4194304 | bytes 4227584 | tf_op jit(solution)/shard_map/convert_element_type | solution.py:103
  191.7 10.4 %all-to-all-done = bf16[4,16,8192]{2,1,0:T(8,128)(2,1)} async-done(((bf16[4,16,8192]{2,1,0:T(8,128)(2,1)}), bf16[4,16,8192]{2,1,0:T(8,128)(2,1)}, u32[]{:S(2)}, u32[]{:S(2)}) %all-to-all-start) | async-done | bytes 1048608 | tf_op jit(solution)/shard_map/all_to_all | solution.py:102
  202.1 1.5 fusion.3
  203.6 2.5 %fusion.5 = bf16[4,16,8192]{2,1,0:T(8,128)(2,1)} fusion(bf16[4,16,8192]{2,1,0:T(8,128)(2,1)} %all-to-all-done, f32[8192]{0:T(1024)S(1)} %copy-done.1, f32[4,16]{1,0:T(4,128)S(1)} %add_rsqrt_fusion), kind=kLoop, calls=%fused_computation.14 | loop fusion | flops 2097152 | bytes 2130176 | tf_op jit(solution)/shard_map/convert_element_type | solution.py:104
  206.2 5.9 %scatter_fusion = bf16[128,8192]{1,0:T(8,128)(2,1)} fusion(bf16[128,8192]{1,0:T(8,128)(2,1)} %fusion.2, s32[64]{0:T(128)S(1)} %fusion.40, bf16[64,8192]{1,0:T(8,128)(2,1)} %bitcast.50), kind=kCustom, calls=%fused_computation.2 | custom fusion | bytes 3145984 | tf_op jit(solution)/shard_map/scatter | solution.py:109
  212.0 3.5 %fusion.13 = bf16[128,256]{1,0:T(8,128)(2,1)S(1)} fusion(bf16[128,8192]{1,0:T(8,128)(2,1)} %scatter_fusion, bf16[8192,256]{1,0:T(8,128)(2,1)} %param.34, f32[256]{0:T(256)S(1)} %copy-done.8), kind=kOutput, calls=%fused_computation.30 | convolution fusion | flops 536936448 | bytes 6358016 | tf_op jit(solution)/shard_map/dot_general | solution.py:110
  216.1 0.7 broadcast_select_fusion
  216.8 3.9 %all-to-all-start.1 = ((bf16[4,32,256]{2,1,0:T(8,128)(2,1)}), bf16[4,32,256]{2,1,0:T(8,128)(2,1)S(1)}, u32[]{:S(2)}, u32[]{:S(2)}) async-start(bf16[4,32,256]{2,1,0:T(8,128)(2,1)} %broadcast_select_fusion), calls=%async_computation.2 | async-start | bytes 131072 | tf_op jit(solution)/shard_map/all_to_all | solution.py:120
  220.7 3.6 %all-to-all-done.1 = bf16[4,32,256]{2,1,0:T(8,128)(2,1)S(1)} async-done(((bf16[4,32,256]{2,1,0:T(8,128)(2,1)}), bf16[4,32,256]{2,1,0:T(8,128)(2,1)S(1)}, u32[]{:S(2)}, u32[]{:S(2)}) %all-to-all-start.1) | async-done | bytes 65568 | tf_op jit(solution)/shard_map/all_to_all | solution.py:120
  (61 shorter events, 6.6 us)
Async XLA Ops:
  6.5 78.2 %copy-start = (bf16[5120,320]{0,1:T(8,128)(2,1)S(1)}, bf16[5120,320]{0,1:T(8,128)(2,1)}, u32[]{:S(2)}) copy-start(bf16[5120,320]{0,1:T(8,128)(2,1)} %param.29) | copy-start | bytes 9830404
  6.5 3.6 %copy-start.5 = (f32[3,160]{1,0:T(4,128)S(1)}, f32[3,160]{1,0:T(4,128)}, u32[]{:S(2)}) copy-start(f32[3,160]{1,0:T(4,128)} %param.25) | copy-start | bytes 5764
  6.5 71.8 %all-reduce.2.cloned.1.call-start = ((), (), s32[]{:S(2)}) async-start(), calls=%async_computation.3 | async-start | bytes 1310720 | tf_op jit(solution)/shard_map/psum | solution.py:70
  8.0 5.5 %copy-start.7 = (s32[4,4,16]{2,1,0:T(4,128)S(1)}, s32[4,4,16]{2,1,0:T(4,128)}, u32[]{:S(2)}) copy-start(s32[4,4,16]{2,1,0:T(4,128)} %param.20) | copy-start | bytes 3076
  13.6 64.8 %copy-start.2 = (f32[1280]{0:T(1024)S(1)}, f32[1280]{0:T(1024)}, u32[]{:S(2)}) copy-start(f32[1280]{0:T(1024)} %param.27) | copy-start | bytes 15364
  17.6 62.4 %copy-start.4 = (f32[1280]{0:T(1024)S(1)}, f32[1280]{0:T(1024)}, u32[]{:S(2)}) copy-start(f32[1280]{0:T(1024)} %param.28) | copy-start | bytes 15364
  21.1 63.6 %copy-start.9 = (f32[320]{0:T(512)S(1)}, f32[320]{0:T(512)}, u32[]{:S(2)}) copy-start(f32[320]{0:T(512)} %param.30) | copy-start | bytes 3844
  21.1 104.3 %reduce-scatter.2.cloned.1.call-start = ((), (), s32[]{:S(2)}) async-start(), calls=%async_computation.4 | async-start | bytes 1179648 | tf_op jit(solution)/shard_map/reduce_scatter | solution.py:87
  87.2 5.7 %copy-start.6 = (s32[4,4]{1,0:T(4,128)S(1)}, s32[4,4]{1,0:T(4,128)}, u32[]{:S(2)}) copy-start(s32[4,4]{1,0:T(4,128)} %param.21) | copy-start | bytes 196
  87.2 38.2 %copy-start.3 = (f32[8192]{0:T(1024)S(1)}, f32[8192]{0:T(1024)}, u32[]{:S(2)}) copy-start(f32[8192]{0:T(1024)} %param.32) | copy-start | bytes 98308
  91.8 65.4 %all-gather.6.cloned.1.call-start = ((), (), s32[]{:S(2)}) async-start(), calls=%async_computation.6 | async-start | bytes 2359296 | tf_op jit(solution)/shard_map/all_gather | solution.py:99
  92.6 88.0 %all-gather.4.cloned.1.call-start = ((), (), s32[]{:S(2)}) async-start(), calls=%async_computation.5 | async-start | bytes 1179648 | tf_op jit(solution)/shard_map/all_gather | solution.py:100
  159.4 28.9 %copy-start.1 = (f32[8192]{0:T(1024)S(1)}, f32[8192]{0:T(1024)}, u32[]{:S(2)}) copy-start(f32[8192]{0:T(1024)} %param.33) | copy-start | bytes 98308
  183.4 18.7 %all-to-all-start = ((bf16[4,16,8192]{2,1,0:T(8,128)(2,1)}), bf16[4,16,8192]{2,1,0:T(8,128)(2,1)}, u32[]{:S(2)}, u32[]{:S(2)}) async-start(bf16[4,16,8192]{2,1,0:T(8,128)(2,1)} %copy.42), calls=%async_computation.1 | async-start | bytes 2097152 | tf_op jit(solution)/shard_map/all_to_all | solution.py:102
  206.2 5.9 %copy-start.8 = (f32[256]{0:T(256)S(1)}, f32[256]{0:T(256)}, u32[]{:S(2)}) copy-start(f32[256]{0:T(256)} %param.35) | copy-start | bytes 3076
  216.8 7.4 %all-to-all-start.1 = ((bf16[4,32,256]{2,1,0:T(8,128)(2,1)}), bf16[4,32,256]{2,1,0:T(8,128)(2,1)S(1)}, u32[]{:S(2)}, u32[]{:S(2)}) async-start(bf16[4,32,256]{2,1,0:T(8,128)(2,1)} %broadcast_select_fusion), calls=%async_computation.2 | async-start | bytes 131072 | tf_op jit(solution)/shard_map/all_to_all | solution.py:120
Sparse Core Ops, SparseCore 0:
  21.2 57.1 all-reduce.1
  92.0 33.3 reduce-scatter.1
  127.0 30.2 all-gather.5
  158.7 21.8 all-gather.3
where the time goes:
time: 235 us; the launch traced here: 232 us
  waiting for transfers between devices  153 us (65%)
  other arithmetic  19.9 us (8%)
  matrix products  18.7 us (8%)
  local copies, waits for them, and re-layouts  17.9 us (8%)
  between operations  13.3 us (6%)
  starting transfers between devices  8.81 us (4%)
    psum x1, waiting for transfers between devices, shards(): lax.psum(partial_out.astype(jnp.bfloat16), ('section', 'mp'))  57.2 us
    reduce_scatter x1, waiting for transfers between devices, shards(): lax.psum_scatter(jnp.dot(ordered, merge_down, preferred_element_type=jnp....  31.8 us
    all_gather x1, waiting for transfers between devices, shards(): lax.all_gather(text_rows, ('section', 'mp'), axis=0, tiled=True)  28.5 us
    all_gather x1, waiting for transfers between devices, shards(): lax.all_gather(image_own, ('section', 'mp'), axis=1, tiled=True)  21.2 us
    all_to_all x1, waiting for transfers between devices, shards(): lax.all_to_all(image_all, 'seq', split_axis=0, concat_axis=0, tiled=True)  10.4 us
    reduce_sum x4, other arithmetic, rms_scaled(): jnp.mean(float_values * float_values, axis=-1, keepdims=True) + NORM_EPS  6.67 us
    scatter x1, local copies, waits for them, and re-layouts, shards(): prompt_text.at[target]  5.86 us
    all_to_all x1, starting transfers between devices, shards(): lax.all_to_all(image_all, 'seq', split_axis=0, concat_axis=0, tiled=True)  4.83 us
  transfers between devices with their start and end apart: 6, of which 6 were waited for; matrix products, arithmetic and copies ran while one was open for 4% of the time, Pallas kernels for 0%

commit v1 on v0

v1 whole, which is shorter than its diff:
```python
import functools
import math

import jax
import jax.numpy as jnp
from jax import lax
from jax.experimental import pallas as pl
from jax.experimental.pallas import tpu as pltpu
from jax.sharding import PartitionSpec as P

VHEAD = 80
CTX = 32
WIN = 64
JOIN = 4
NORM_EPS = 1e-06
F32 = jnp.float32
BF16 = jnp.bfloat16
VMEM_LIMIT = 48 * 1024 * 1024
NT = (((1,), (1,)), ((), ()))


def call(kernel, outs, args, scratch=(), smem=0, flops=0):
    vmem = pl.BlockSpec(memory_space=pltpu.VMEM)
    scalar = pl.BlockSpec(memory_space=pltpu.SMEM)
    moved = sum(math.prod(a.shape) * a.dtype.itemsize for a in list(args) + list(outs))
    return pl.pallas_call(
        kernel,
        out_shape=outs,
        in_specs=[scalar] * smem + [vmem] * (len(args) - smem),
        out_specs=[vmem] * len(outs),
        scratch_shapes=list(scratch),
        compiler_params=pltpu.CompilerParams(vmem_limit_bytes=VMEM_LIMIT),
        cost_estimate=pl.CostEstimate(flops=flops, bytes_accessed=moved, transcendentals=0),
    )(*args)


def struct(shape, dtype):
    return jax.ShapeDtypeStruct(shape, dtype)


def shifted(x, axis, count, k):
    return lax.ppermute(x, axis, [(i, (i + k) % count) for i in range(count)])


def chunk_of(section, z, n_z):
    return section * (n_z // JOIN) + z // JOIN


def front_kernel(n_z, block, place, x_ref, gain_ref, w_ref, b_ref, wo_ref, ob_ref,
                 keep_ref, send_ref, base_ref, hf):
    c, z, s = lax.axis_index("section"), lax.axis_index("mp"), lax.axis_index("seq")
    rows, width = x_ref.shape
    head_width = hf.shape[1]
    units = place.shape[2]
    tile = 256
    per_tile = tile // WIN

    def one(t, carry):
        at = pl.ds(pl.multiple_of(t * tile, tile), tile)
        x = x_ref[at, :].astype(F32)
        scale = lax.rsqrt(jnp.mean(x * x, axis=-1, keepdims=True) + NORM_EPS)
        y = (x * scale * gain_ref[...]).astype(BF16)
        parts = []
        for i in range(3):
            w = w_ref[i * head_width:(i + 1) * head_width, :]
            part = lax.dot_general(y, w, NT, preferred_element_type=F32)
            parts.append((part + b_ref[i:i + 1, :]).astype(BF16))
        q, k, v = parts
        key = lax.broadcasted_iota(jnp.int32, (tile, tile), 1)
        row = lax.broadcasted_iota(jnp.int32, (tile, tile), 0)
        same = key // WIN == row // WIN
        end = jnp.zeros((tile, tile), jnp.int32)
        for j in range(per_tile):
            count = jnp.int32(0)
            for u in range(units):
                count += (place[s, t * per_tile + j, u] >= 0).astype(jnp.int32)
            end = jnp.where(key // WIN == j, j * WIN + count * JOIN, end)
        live = same & (key < end)
        lane = lax.broadcasted_iota(jnp.int32, (1, head_width), 1)
        total = jnp.zeros((tile, head_width), F32)
        for h in range(head_width // VHEAD):
            mine = lane // VHEAD == h
            qh = jnp.where(mine, q, jnp.zeros_like(q))
            scores = lax.dot_general(qh, k, NT, preferred_element_type=F32) * (1.0 / math.sqrt(VHEAD))
            raised = jnp.where(live, jnp.exp(scores), 0.0)
            probs = (raised / jnp.sum(raised, axis=-1, keepdims=True)).astype(BF16)
            out = jnp.dot(probs, v, preferred_element_type=F32)
            total = jnp.where(mine, out, total)
        hf[at, :] = total.astype(BF16)
        return carry

    if rows == tile:
        one(0, 0)
    else:
        lax.fori_loop(0, rows // tile, one, 0)

    def picked(section, zz, count):
        i = lax.broadcasted_iota(jnp.int32, (count, rows), 0)
        device = zz + i // block
        first = JOIN * block * chunk_of(section, device, n_z) + device % JOIN
        source = first + JOIN * (i % block)
        return (lax.broadcasted_iota(jnp.int32, (count, rows), 1) == source).astype(BF16)

    wo = wo_ref[...]
    heads = hf[...]
    for section, out in ((1 - c, send_ref), (c, keep_ref)):
        order = picked(section, 0, rows // 2)
        chosen = jnp.dot(order, heads, preferred_element_type=F32).astype(BF16)
        out[...] = jnp.dot(chosen, wo, preferred_element_type=F32).astype(BF16)
    own = jnp.dot(picked(c, z, block), x_ref[...], preferred_element_type=F32)
    base_ref[...] = own + ob_ref[...]


def pair_rows_kernel(n_z, block, keep_ref, got_ref, *outs):
    z = lax.axis_index("mp")
    for k in range(n_z):
        at = pl.ds(pl.multiple_of(lax.rem(z + k, n_z) * block, block), block)
        total = keep_ref[at, :].astype(F32) + got_ref[at, :].astype(F32)
        outs[k][...] = total.astype(outs[k].dtype)


def resid_kernel(base_ref, gain_ref, own_ref, *refs):
    out_ref = refs[-1]
    total = own_ref[...]
    for r in refs[:-1]:
        total += r[...].astype(F32)
    x = base_ref[...] + total
    scale = lax.rsqrt(jnp.mean(x * x, axis=-1, keepdims=True) + NORM_EPS)
    out_ref[...] = (x * scale * gain_ref[...]).astype(BF16)


def merge_kernel(n_z, block, up_ref, ub_ref, down_ref, *refs):
    c, z = lax.axis_index("section"), lax.axis_index("mp")
    pieces, (keep_ref, send_ref, xs) = refs[:2 * n_z], refs[2 * n_z:]
    width = xs.shape[2]
    for side in range(2):
        section = c if side == 0 else 1 - c
        for k in range(n_z):
            zz = lax.rem(z - k + n_z, n_z)
            chunk = chunk_of(section, zz, n_z)
            at = pl.ds(pl.multiple_of(chunk * block, block), block)
            xs[lax.rem(zz, JOIN), at, :] = pieces[side * n_z + k][...]
    acc = ub_ref[...]
    for q in range(JOIN):
        acc = acc + lax.dot_general(
            xs[q], up_ref[:, q * width:(q + 1) * width], NT, preferred_element_type=F32)
    hidden = (0.5 * acc * (1.0 + lax.erf(acc * (1.0 / math.sqrt(2.0))))).astype(BF16)
    half = keep_ref.shape[1]
    for section, out in ((1 - c, send_ref), (c, keep_ref)):
        at = pl.ds(pl.multiple_of(section * half, half), half)
        out[...] = jnp.dot(hidden, down_ref[:, at], preferred_element_type=F32).astype(BF16)


def pair_columns_kernel(n_z, block, keep_ref, got_ref, *outs):
    z = lax.axis_index("mp")
    for k in range(n_z):
        at = pl.ds(pl.multiple_of(lax.rem(z + k, n_z) * block, block), block)
        total = keep_ref[:, at].astype(F32) + got_ref[:, at].astype(F32)
        outs[k][...] = total.astype(outs[k].dtype)


def image_kernel(n_z, bias_ref, own_ref, *refs):
    out_ref = refs[-1]
    block = out_ref.shape[1]
    d = lax.axis_index("section") * n_z + lax.axis_index("mp")
    total = own_ref[...]
    for r in refs[:-1]:
        total += r[...].astype(F32)
    at = pl.ds(pl.multiple_of(d * block, block), block)
    out_ref[...] = (total + bias_ref[:, at]).astype(BF16)


def image_keyval_kernel(n_z, gain_ref, w_ref, b_ref, *refs):
    c, z = lax.axis_index("section"), lax.axis_index("mp")
    pieces, out_ref = refs[:-1], refs[-1]
    rows, block = pieces[0].shape
    acc = jnp.zeros(out_ref.shape, F32)
    squares = jnp.zeros((rows, 1), F32)
    for side in range(2):
        section = c if side == 0 else 1 - c
        for k in range(n_z):
            d = section * n_z + lax.rem(z - k + n_z, n_z)
            at = pl.ds(pl.multiple_of(d * block, block), block)
            x = pieces[side * n_z + k][...].astype(F32)
            squares += jnp.sum(x * x, axis=-1, keepdims=True)
            acc += jnp.dot((x * gain_ref[:, at]).astype(BF16), w_ref[at, :], preferred_element_type=F32)
    scale = lax.rsqrt(squares * (1.0 / w_ref.shape[0]) + NORM_EPS)
    out_ref[...] = (acc * scale + b_ref[...]).astype(BF16)


def text_norm_kernel(x_ref, gain_ref, out_ref):
    x = x_ref[...].astype(F32)
    scale = lax.rsqrt(jnp.mean(x * x, axis=-1, keepdims=True) + NORM_EPS)
    out_ref[...] = (x * scale * gain_ref[...]).astype(BF16)


def text_keyval_kernel(n_z, w_ref, b_ref, *refs):
    c, z = lax.axis_index("section"), lax.axis_index("mp")
    pieces, out_ref = refs[:-1], refs[-1]
    block = pieces[0].shape[0]
    x = jnp.concatenate([p[...] for p in pieces], axis=0)
    acc = jnp.dot(x, w_ref[...], preferred_element_type=F32) + b_ref[...]
    for side in range(2):
        section = c if side == 0 else 1 - c
        for k in range(n_z):
            d = section * n_z + lax.rem(z - k + n_z, n_z)
            at = pl.ds(pl.multiple_of(d * block, block), block)
            i = side * n_z + k
            out_ref[at, :] = acc[i * block:(i + 1) * block].astype(BF16)


def place_kernel(n_s, slot_map, place_ref, *refs):
    s = lax.axis_index("seq")
    texts, images, (out_ref, held) = refs[:n_s], refs[n_s:2 * n_s], refs[2 * n_s:]
    units = place_ref.shape[2]
    for k in range(n_s):
        held[lax.rem(s - k + n_s, n_s)] = images[k][...]
    position = lax.broadcasted_iota(jnp.int32, (CTX, units), 0)
    for k in range(n_s):
        j = lax.rem(s - k + n_s, n_s)

        def one(i, carry):
            slot = slot_map[j, i] - s * n_s

            @pl.when((slot >= 0) & (slot < n_s))
            def _():
                chosen = position == place_ref[i, pl.ds(j, 1), :]
                covered = jnp.sum(chosen.astype(F32), axis=1, keepdims=True) > 0.5
                rows = held[i, pl.ds(pl.multiple_of(j * units, units), units), :]
                image = jnp.dot(chosen.astype(BF16), rows, preferred_element_type=F32)
                text = texts[k][pl.ds(pl.multiple_of(i * CTX, CTX), CTX), :]
                out_ref[slot] = jnp.where(covered, image, text.astype(F32)).astype(BF16)

            return carry

        lax.fori_loop(0, n_s, one, 0)


def shards(
    patches,
    image_place,
    slot_map,
    text,
    vision_gain,
    qkv_weight,
    qkv_bias,
    out_weight,
    out_bias,
    merge_gain,
    merge_up,
    merge_up_bias,
    merge_down,
    merge_down_bias,
    input_gain,
    kv_weight,
    kv_bias,
):
    n_z, n_s = lax.axis_size("mp"), lax.axis_size("seq")
    n_d = lax.axis_size("section") * n_z
    x = patches[0]
    rows, width = x.shape
    units = rows // JOIN
    block = rows // n_d
    head_width = out_weight.shape[0]
    hidden = merge_up.shape[1]
    model = merge_down.shape[1]
    columns = model // n_d
    kv_width = kv_weight.shape[1]

    def flat(v):
        return v.reshape(1, -1)

    def swap(v):
        return lax.ppermute(v, "section", [(0, 1), (1, 0)])

    def spread(own):
        here = [own] + [shifted(own, "mp", n_z, k) for k in range(1, n_z)]
        return here + [swap(v) for v in here]

    text_own, = call(text_norm_kernel, [struct(text.shape[1:], BF16)], [text[0], flat(input_gain)])
    text_pieces = spread(text_own)
    prompt = n_d * text.shape[1]
    text_keyval, = call(
        functools.partial(text_keyval_kernel, n_z),
        [struct((prompt, kv_width), BF16)],
        [kv_weight, flat(kv_bias)] + text_pieces,
        flops=2 * prompt * model * kv_width,
    )
    texts = [text_keyval] + [shifted(text_keyval, "seq", n_s, k) for k in range(1, n_s)]

    w = qkv_weight.transpose(1, 2, 0).reshape(3 * head_width, width)
    keep, send, base = call(
        functools.partial(front_kernel, n_z, block),
        [struct((rows // 2, width), BF16)] * 2 + [struct((block, width), F32)],
        [image_place, x, flat(vision_gain), w, qkv_bias, out_weight, flat(out_bias)],
        [pltpu.VMEM((rows, head_width), BF16)],
        smem=1,
        flops=2 * rows * width * 4 * head_width,
    )
    got = swap(send)
    parts = call(
        functools.partial(pair_rows_kernel, n_z, block),
        [struct((block, width), F32)] + [struct((block, width), BF16)] * (n_z - 1),
        [keep, got],
    )
    sums = [parts[0]] + [shifted(parts[k], "mp", n_z, k) for k in range(1, n_z)]
    merged, = call(resid_kernel, [struct((block, width), BF16)], [base, flat(merge_gain)] + sums)
    pieces = spread(merged)

    keep, send = call(
        functools.partial(merge_kernel, n_z, block),
        [struct((units, model // 2), BF16)] * 2,
        [merge_up.T, flat(merge_up_bias), merge_down] + pieces,
        [pltpu.VMEM((JOIN, units, width), BF16)],
        flops=2 * units * hidden * (JOIN * width + model),
    )
    got = swap(send)
    parts = call(
        functools.partial(pair_columns_kernel, n_z, columns),
        [struct((units, columns), F32)] + [struct((units, columns), BF16)] * (n_z - 1),
        [keep, got],
    )
    sums = [parts[0]] + [shifted(parts[k], "mp", n_z, k) for k in range(1, n_z)]
    image, = call(
        functools.partial(image_kernel, n_z), [struct((units, columns), BF16)], [flat(merge_down_bias)] + sums)
    image_pieces = spread(image)

    image_keyval, = call(
        functools.partial(image_keyval_kernel, n_z),
        [struct((units, kv_width), BF16)],
        [flat(input_gain), kv_weight, flat(kv_bias)] + image_pieces,
        flops=2 * units * model * kv_width,
    )
    images = [image_keyval] + [shifted(image_keyval, "seq", n_s, k) for k in range(1, n_s)]
    cache, = call(
        functools.partial(place_kernel, n_s),
        [struct((n_s, CTX, kv_width), BF16)],
        [slot_map, image_place] + texts + images,
        [pltpu.VMEM((n_s, units, kv_width), BF16)],
        smem=1,
    )
    return cache[None]


def solution(mesh):
    placed = (
        P("seq", None, None),
        P(),
        P(),
        P("seq", ("section", "mp"), None),
        P(),
        P(None, None, ("section", "mp")),
        P(None, ("section", "mp")),
        P(("section", "mp"), None),
        P(),
        P(),
        P(None, ("section", "mp")),
        P(("section", "mp")),
        P(("section", "mp"), None),
        P(),
        P(),
        P(None, ("section", "mp")),
        P(("section", "mp")),
    )
    return jax.shard_map(
        shards,
        mesh=mesh,
        in_specs=placed,
        out_specs=P("section", "seq", None, "mp"),
        check_vma=False,
    )
```

time: 235 us -> 108 us (0.46)
  waiting for transfers between devices: 153 us -> 57.7 us
  other arithmetic: 19.9 us -> 0 us
  matrix products: 18.7 us -> 0 us
  starting transfers between devices: 8.81 us -> 26.7 us
  Pallas kernels: 0 us -> 14.6 us
  between operations: 13.3 us -> 0.19 us
  local copies, waits for them, and re-layouts: 17.9 us -> 7.88 us
    ppermute x0 -> x35, waiting for transfers between devices: none -> 57.7 us  [the longest x21 55.5 us: shifted(): return lax.ppermute(x, axis, [(i, (i + k) % count) for i in range(count)])]
    psum x1 -> x0, waiting for transfers between devices: 57.2 us -> none  [shards(): lax.psum(partial_out.astype(jnp.bfloat16), ('section', 'mp'))]
    all_gather x2 -> x0, waiting for transfers between devices: 49.7 us -> none  [the longest x1 28.5 us: shards(): lax.all_gather(text_rows, ('section', 'mp'), axis=0, tiled=True)]
    reduce_scatter x1 -> x0, waiting for transfers between devices: 31.8 us -> none  [shards(): lax.psum_scatter(jnp.dot(ordered, merge_down, preferred_element_type=jnp....]
    ppermute x0 -> x35, starting transfers between devices: none -> 26.7 us  [the longest x21 26.3 us: shifted(): return lax.ppermute(x, axis, [(i, (i + k) % count) for i in range(count)])]
    dot_general x6 -> x0, matrix products: 16.6 us -> none  [the longest x1 4.62 us: shards(): jnp.dot(ordered, merge_down, preferred_element_type=jnp.float32)]
    pallas_call x0 -> x10, Pallas kernels: none -> 14.6 us  [call(): pl.pallas_call(kernel, out_shape=outs, in_specs=[scalar] * smem + [vmem]...]
    all_to_all x2 -> x0, waiting for transfers between devices: 13.9 us -> none  [the longest x1 10.4 us: shards(): lax.all_to_all(image_all, 'seq', split_axis=0, concat_axis=0, tiled=True)]
  transfers between devices with their start and end apart: 6 -> 35, of which waited for: 6 -> 17; matrix products, arithmetic and copies ran while one was open for 4% -> 1% of each run, Pallas kernels for 0% -> 4%
where the time goes in v1:
time: 108 us; the launch traced here: 107 us
  waiting for transfers between devices  57.7 us (53%)
  starting transfers between devices  26.7 us (25%)
  Pallas kernels  14.6 us (14%)
  local copies, waits for them, and re-layouts  7.88 us (7%)
    ppermute x21, waiting for transfers between devices, shifted(): return lax.ppermute(x, axis, [(i, (i + k) % count) for i in range(count)])  55.5 us
    ppermute x21, starting transfers between devices, shifted(): return lax.ppermute(x, axis, [(i, (i + k) % count) for i in range(count)])  26.3 us
    pallas_call x10, Pallas kernels, call(): pl.pallas_call(kernel, out_shape=outs, in_specs=[scalar] * smem + [vmem]...  14.6 us
    unnamed x26, local copies, waits for them, and re-layouts  4.8 us
    reshape x4, local copies, waits for them, and re-layouts, flat(): return v.reshape(1, -1)  3.08 us
    ppermute x14, waiting for transfers between devices, swap(): return lax.ppermute(v, 'section', [(0, 1), (1, 0)])  2.21 us
  transfers between devices with their start and end apart: 35, of which 17 were waited for; matrix products, arithmetic and copies ran while one was open for 1% of the time, Pallas kernels for 4%

profile of v1, /device:TPU:10, one launch (start us, length us, event | category | flops | bytes accessed | tf_op | source)
XLA Modules:
  0.0 107.1 jit_solution(14926451248620383892)
XLA Ops:
  1.7 1.3 %copy-done.2 = bf16[1280,3,160]{0,2,1:T(8,128)(2,1)S(1)} copy-done((bf16[1280,3,160]{0,2,1:T(8,128)(2,1)S(1)}, bf16[1280,3,160]{0,2,1:T(8,128)(2,1)}, u32[]{:S(2)}) %copy-start.2) | copy-done | bytes 1228824
  6.5 2.7 %shard_map.165 = (bf16[128,1280]{1,0:T(8,128)(2,1)S(1)}, bf16[128,1280]{1,0:T(8,128)(2,1)S(1)}, f32[32,1280]{1,0:T(8,128)S(1)}) custom-call(s32[4,4,16]{2,1,0:T(4,128)S(1)} %copy-done.7, bf16[256,1280]{1,0:T(8,128)(2,1)S(1)} %bitcast.12, f32[1,1280]{1,0:T(1,128)S(1)} %reshape.30.gain_ref, bf16[480,1280]{1,0:T(8,128)(2,1)S(1)} %bitcast.11, ...), custom_call_target="tpu_custom_call" | custom-call | flops 419430400 | bytes 3126144 | tf_op jit(solution)/shard_map/pallas_call | solution.py:26
  9.3 1.6 %collective-permute-done.10.got_ref = bf16[128,1280]{1,0:T(8,128)(2,1)S(1)} collective-permute-done((bf16[128,1280]{1,0:T(8,128)(2,1)S(1)}, bf16[128,1280]{1,0:T(8,128)(2,1)S(1)}, u32[]{:S(2)}, u32[]{:S(2)}) %collective-permute-start.10) | collective-permute-done | bytes 327712 | tf_op jit(solution)/shard_map/ppermute | solution.py:274
  11.0 1.6 %collective-permute-start.11 = (bf16[32,1280]{1,0:T(8,128)(2,1)S(1)}, bf16[32,1280]{1,0:T(8,128)(2,1)S(1)}, u32[]{:S(2)}, u32[]{:S(2)}) collective-permute-start(bf16[32,1280]{1,0:T(8,128)(2,1)S(1)} %get-tuple-element.22), channel_id=1, source_target_pairs={{0,1},{1,2},{2,3},{3,0},{4,5},{5,6},{6,7},{7,4},{8,9},{9,10},{10,1... | collective-permute-start | bytes 245768 | tf_op jit(solution)/shard_map/ppermute | solution.py:42
  13.8 1.8 %collective-permute-start.13 = (bf16[32,1280]{1,0:T(8,128)(2,1)S(1)}, bf16[32,1280]{1,0:T(8,128)(2,1)S(1)}, u32[]{:S(2)}, u32[]{:S(2)}) collective-permute-start(bf16[32,1280]{1,0:T(8,128)(2,1)S(1)} %get-tuple-element.24), channel_id=1, source_target_pairs={{0,3},{1,0},{2,1},{3,2},{4,7},{5,4},{6,5},{7,6},{8,11},{9,8},{10,9... | collective-permute-start | bytes 245768 | tf_op jit(solution)/shard_map/ppermute | solution.py:42
  16.4 3.5 %collective-permute-done.12.refs_1_ = bf16[32,1280]{1,0:T(8,128)(2,1)S(1)} collective-permute-done((bf16[32,1280]{1,0:T(8,128)(2,1)S(1)}, bf16[32,1280]{1,0:T(8,128)(2,1)S(1)}, u32[]{:S(2)}, u32[]{:S(2)}) %collective-permute-start.12) | collective-permute-done | bytes 81952 | tf_op jit(solution)/shard_map/ppermute | solution.py:42
  19.9 1.8 %collective-permute-done.13.refs_2_ = bf16[32,1280]{1,0:T(8,128)(2,1)S(1)} collective-permute-done((bf16[32,1280]{1,0:T(8,128)(2,1)S(1)}, bf16[32,1280]{1,0:T(8,128)(2,1)S(1)}, u32[]{:S(2)}, u32[]{:S(2)}) %collective-permute-start.13) | collective-permute-done | bytes 81952 | tf_op jit(solution)/shard_map/ppermute | solution.py:42
  21.9 2.4 %collective-permute-start.15 = (bf16[32,1280]{1,0:T(8,128)(2,1)S(1)}, bf16[32,1280]{1,0:T(8,128)(2,1)S(1)}, u32[]{:S(2)}, u32[]{:S(2)}) collective-permute-start(bf16[32,1280]{1,0:T(8,128)(2,1)S(1)} %shard_map.167.refs_0_), channel_id=1, source_target_pairs={{0,2},{1,3},{2,0},{3,1},{4,6},{5,7},{6,4},{7,5},{8,10},{9,11},{10,... | collective-permute-start | bytes 245768 | tf_op jit(solution)/shard_map/ppermute | solution.py:42
  24.2 1.3 %collective-permute-start.16 = (bf16[32,1280]{1,0:T(8,128)(2,1)S(1)}, bf16[32,1280]{1,0:T(8,128)(2,1)S(1)}, u32[]{:S(2)}, u32[]{:S(2)}) collective-permute-start(bf16[32,1280]{1,0:T(8,128)(2,1)S(1)} %shard_map.167.refs_0_), channel_id=1, source_target_pairs={{0,3},{1,0},{2,1},{3,2},{4,7},{5,4},{6,5},{7,6},{8,11},{9,8},{10,9... | collective-permute-start | bytes 245768 | tf_op jit(solution)/shard_map/ppermute | solution.py:42
  25.5 1.7 %collective-permute-done.14.refs_1_ = bf16[32,1280]{1,0:T(8,128)(2,1)S(1)} collective-permute-done((bf16[32,1280]{1,0:T(8,128)(2,1)S(1)}, bf16[32,1280]{1,0:T(8,128)(2,1)S(1)}, u32[]{:S(2)}, u32[]{:S(2)}) %collective-permute-start.14) | collective-permute-done | bytes 81952 | tf_op jit(solution)/shard_map/ppermute | solution.py:42
  27.2 2.2 %collective-permute-done.15.refs_2_ = bf16[32,1280]{1,0:T(8,128)(2,1)S(1)} collective-permute-done((bf16[32,1280]{1,0:T(8,128)(2,1)S(1)}, bf16[32,1280]{1,0:T(8,128)(2,1)S(1)}, u32[]{:S(2)}, u32[]{:S(2)}) %collective-permute-start.15) | collective-permute-done | bytes 81952 | tf_op jit(solution)/shard_map/ppermute | solution.py:42
  29.3 2.3 %collective-permute-done.16.refs_3_ = bf16[32,1280]{1,0:T(8,128)(2,1)S(1)} collective-permute-done((bf16[32,1280]{1,0:T(8,128)(2,1)S(1)}, bf16[32,1280]{1,0:T(8,128)(2,1)S(1)}, u32[]{:S(2)}, u32[]{:S(2)}) %collective-permute-start.16) | collective-permute-done | bytes 81952 | tf_op jit(solution)/shard_map/ppermute | solution.py:42
  32.9 5.6 %shard_map.168 = (bf16[64,4096]{1,0:T(8,128)(2,1)S(1)}, bf16[64,4096]{1,0:T(8,128)(2,1)S(1)}) custom-call(bf16[320,5120]{1,0:T(8,128)(2,1)S(1)} %bitcast.10, f32[1,320]{1,0:T(1,128)S(1)} %reshape.29.ub_ref, bf16[320,8192]{1,0:T(8,128)(2,1)} %down_ref.1, bf16[32,1280]{1,0:T(8,128)(2,1)S(1)} %shard_map.167.refs_0_, ...), custom_call_target="tpu_custom_call" | custom-call | flops 545259520 | bytes 10224896 | tf_op jit(solution)/shard_map/pallas_call | solution.py:26
  39.1 2.5 %collective-permute-start.1 = (bf16[16,8192]{1,0:T(8,128)(2,1)S(1)}, bf16[16,8192]{1,0:T(8,128)(2,1)S(1)}, u32[]{:S(2)}, u32[]{:S(2)}) collective-permute-start(bf16[16,8192]{1,0:T(8,128)(2,1)S(1)} %shard_map.163.refs_0_), channel_id=1, source_target_pairs={{0,2},{1,3},{2,0},{3,1},{4,6},{5,7},{6,4},{7,5},{8,10},{9,11},{10,... | collective-permute-start | bytes 786440 | tf_op jit(solution)/shard_map/ppermute | solution.py:42
  43.8 4.4 %collective-permute-done.refs_1_ = bf16[16,8192]{1,0:T(8,128)(2,1)S(1)} collective-permute-done((bf16[16,8192]{1,0:T(8,128)(2,1)S(1)}, bf16[16,8192]{1,0:T(8,128)(2,1)S(1)}, u32[]{:S(2)}, u32[]{:S(2)}) %collective-permute-start) | collective-permute-done | bytes 262176 | tf_op jit(solution)/shard_map/ppermute | solution.py:42
  48.2 17.2 %collective-permute-done.1.refs_2_ = bf16[16,8192]{1,0:T(8,128)(2,1)S(1)} collective-permute-done((bf16[16,8192]{1,0:T(8,128)(2,1)S(1)}, bf16[16,8192]{1,0:T(8,128)(2,1)S(1)}, u32[]{:S(2)}, u32[]{:S(2)}) %collective-permute-start.1) | collective-permute-done | bytes 262176 | tf_op jit(solution)/shard_map/ppermute | solution.py:42
  65.4 3.4 %collective-permute-start.23 = (bf16[64,1024]{1,0:T(8,128)(2,1)S(1)}, bf16[64,1024]{1,0:T(8,128)(2,1)S(1)}, u32[]{:S(2)}, u32[]{:S(2)}) collective-permute-start(bf16[64,1024]{1,0:T(8,128)(2,1)S(1)} %get-tuple-element.29), channel_id=1, source_target_pairs={{0,2},{1,3},{2,0},{3,1},{4,6},{5,7},{6,4},{7,5},{8,10},{9,11},{10,... | collective-permute-start | bytes 393224 | tf_op jit(solution)/shard_map/ppermute | solution.py:42
  68.9 5.1 %collective-permute-done.23.refs_1_ = bf16[64,1024]{1,0:T(8,128)(2,1)S(1)} collective-permute-done((bf16[64,1024]{1,0:T(8,128)(2,1)S(1)}, bf16[64,1024]{1,0:T(8,128)(2,1)S(1)}, u32[]{:S(2)}, u32[]{:S(2)}) %collective-permute-start.23) | collective-permute-done | bytes 131104 | tf_op jit(solution)/shard_map/ppermute | solution.py:42
  74.0 2.1 %collective-permute-done.24.refs_2_ = bf16[64,1024]{1,0:T(8,128)(2,1)S(1)} collective-permute-done((bf16[64,1024]{1,0:T(8,128)(2,1)S(1)}, bf16[64,1024]{1,0:T(8,128)(2,1)S(1)}, u32[]{:S(2)}, u32[]{:S(2)}) %collective-permute-start.24) | collective-permute-done | bytes 131104 | tf_op jit(solution)/shard_map/ppermute | solution.py:42
  76.2 1.4 %collective-permute-start.26 = (bf16[64,1024]{1,0:T(8,128)(2,1)S(1)}, bf16[64,1024]{1,0:T(8,128)(2,1)S(1)}, u32[]{:S(2)}, u32[]{:S(2)}) collective-permute-start(bf16[64,1024]{1,0:T(8,128)(2,1)S(1)} %shard_map.170.refs_0_), channel_id=1, source_target_pairs={{0,2},{1,3},{2,0},{3,1},{4,6},{5,7},{6,4},{7,5},{8,10},{9,11},{10,... | collective-permute-start | bytes 393224 | tf_op jit(solution)/shard_map/ppermute | solution.py:42
  77.6 1.9 %collective-permute-start.27 = (bf16[64,1024]{1,0:T(8,128)(2,1)S(1)}, bf16[64,1024]{1,0:T(8,128)(2,1)S(1)}, u32[]{:S(2)}, u32[]{:S(2)}) collective-permute-start(bf16[64,1024]{1,0:T(8,128)(2,1)S(1)} %shard_map.170.refs_0_), channel_id=1, source_target_pairs={{0,3},{1,0},{2,1},{3,2},{4,7},{5,4},{6,5},{7,6},{8,11},{9,8},{10,9... | collective-permute-start | bytes 393224 | tf_op jit(solution)/shard_map/ppermute | solution.py:42
  79.5 3.0 %collective-permute-done.25.refs_1_ = bf16[64,1024]{1,0:T(8,128)(2,1)S(1)} collective-permute-done((bf16[64,1024]{1,0:T(8,128)(2,1)S(1)}, bf16[64,1024]{1,0:T(8,128)(2,1)S(1)}, u32[]{:S(2)}, u32[]{:S(2)}) %collective-permute-start.25) | collective-permute-done | bytes 131104 | tf_op jit(solution)/shard_map/ppermute | solution.py:42
  82.5 5.3 %collective-permute-done.26.refs_2_ = bf16[64,1024]{1,0:T(8,128)(2,1)S(1)} collective-permute-done((bf16[64,1024]{1,0:T(8,128)(2,1)S(1)}, bf16[64,1024]{1,0:T(8,128)(2,1)S(1)}, u32[]{:S(2)}, u32[]{:S(2)}) %collective-permute-start.26) | collective-permute-done | bytes 131104 | tf_op jit(solution)/shard_map/ppermute | solution.py:42
  87.8 2.2 %collective-permute-done.27.refs_3_ = bf16[64,1024]{1,0:T(8,128)(2,1)S(1)} collective-permute-done((bf16[64,1024]{1,0:T(8,128)(2,1)S(1)}, bf16[64,1024]{1,0:T(8,128)(2,1)S(1)}, u32[]{:S(2)}, u32[]{:S(2)}) %collective-permute-start.27) | collective-permute-done | bytes 131104 | tf_op jit(solution)/shard_map/ppermute | solution.py:42
  90.1 2.9 %shard_map.164.refs_0_ = bf16[128,256]{1,0:T(8,128)(2,1)S(1)} custom-call(bf16[8192,256]{1,0:T(8,128)(2,1)} %w_ref.3, f32[1,256]{1,0:T(1,128)S(1)} %bitcast.17, bf16[16,8192]{1,0:T(8,128)(2,1)S(1)} %shard_map.163.refs_0_, bf16[16,8192]{1,0:T(8,128)(2,1)S(1)} %collective-permute-done.refs_1_, bf16[16,8192]{1,0:T(8,128)(2,1)S(1)} %collective-permute-done.1.refs_2_, ...), custom_call_target="tpu_custom_call" | custom-call | flops 536870912 | bytes 6358016 | tf_op jit(solution)/shard_map/pallas_call | solution.py:26
  93.0 1.6 %collective-permute-start.7 = (bf16[128,256]{1,0:T(8,128)(2,1)S(1)}, bf16[128,256]{1,0:T(8,128)(2,1)S(1)}, u32[]{:S(2)}, u32[]{:S(2)}) collective-permute-start(bf16[128,256]{1,0:T(8,128)(2,1)S(1)} %shard_map.164.refs_0_), channel_id=1, source_target_pairs={{0,4},{4,8},{8,12},{12,0},{1,5},{5,9},{9,13},{13,1},{2,6},{6,10},{... | collective-permute-start | bytes 196616 | tf_op jit(solution)/shard_map/ppermute | solution.py:42
  95.1 1.6 %collective-permute-start.9 = (bf16[128,256]{1,0:T(8,128)(2,1)S(1)}, bf16[128,256]{1,0:T(8,128)(2,1)S(1)}, u32[]{:S(2)}, u32[]{:S(2)}) collective-permute-start(bf16[128,256]{1,0:T(8,128)(2,1)S(1)} %shard_map.164.refs_0_), channel_id=1, source_target_pairs={{0,12},{4,0},{8,4},{12,8},{1,13},{5,1},{9,5},{13,9},{2,14},{6,2},{... | collective-permute-start | bytes 196616 | tf_op jit(solution)/shard_map/ppermute | solution.py:42
  97.6 1.4 %collective-permute-start.32 = (bf16[64,256]{1,0:T(8,128)(2,1)S(1)}, bf16[64,256]{1,0:T(8,128)(2,1)S(1)}, u32[]{:S(2)}, u32[]{:S(2)}) collective-permute-start(bf16[64,256]{1,0:T(8,128)(2,1)S(1)} %shard_map.171.refs_4_), channel_id=1, source_target_pairs={{0,4},{4,8},{8,12},{12,0},{1,5},{5,9},{9,13},{13,1},{2,6},{6,10},{... | collective-permute-start | bytes 98312 | tf_op jit(solution)/shard_map/ppermute | solution.py:42
  99.0 1.5 %collective-permute-start.33 = (bf16[64,256]{1,0:T(8,128)(2,1)S(1)}, bf16[64,256]{1,0:T(8,128)(2,1)S(1)}, u32[]{:S(2)}, u32[]{:S(2)}) collective-permute-start(bf16[64,256]{1,0:T(8,128)(2,1)S(1)} %shard_map.171.refs_4_), channel_id=1, source_target_pairs={{0,8},{4,12},{8,0},{12,4},{1,9},{5,13},{9,1},{13,5},{2,10},{6,14},... | collective-permute-start | bytes 98312 | tf_op jit(solution)/shard_map/ppermute | solution.py:42
  101.6 1.4 %collective-permute-done.33.refs_6_ = bf16[64,256]{1,0:T(8,128)(2,1)S(1)} collective-permute-done((bf16[64,256]{1,0:T(8,128)(2,1)S(1)}, bf16[64,256]{1,0:T(8,128)(2,1)S(1)}, u32[]{:S(2)}, u32[]{:S(2)}) %collective-permute-start.33) | collective-permute-done | bytes 32800 | tf_op jit(solution)/shard_map/ppermute | solution.py:42
  103.0 2.4 %collective-permute-done.34.refs_7_ = bf16[64,256]{1,0:T(8,128)(2,1)S(1)} collective-permute-done((bf16[64,256]{1,0:T(8,128)(2,1)S(1)}, bf16[64,256]{1,0:T(8,128)(2,1)S(1)}, u32[]{:S(2)}, u32[]{:S(2)}) %collective-permute-start.34) | collective-permute-done | bytes 32800 | tf_op jit(solution)/shard_map/ppermute | solution.py:42
  105.4 1.7 %shard_map.172 = bf16[4,32,256]{2,1,0:T(8,128)(2,1)} custom-call(s32[4,4]{1,0:T(4,128)S(1)} %copy-done.12, s32[4,4,16]{2,1,0:T(4,128)S(1)} %copy-done.8, bf16[128,256]{1,0:T(8,128)(2,1)S(1)} %shard_map.164.refs_0_, bf16[128,256]{1,0:T(8,128)(2,1)S(1)} %collective-permute-done.7.refs_1_, bf16[128,256]{1,0:T(8,128)(2,1)S(1)} %collective-permute-done.8.refs_2_, ...), custom_call_target="tpu_custom_call" | custom-call | bytes 459840 | tf_op jit(solution)/shard_map/pallas_call | solution.py:26
  (78 shorter events, 14.2 us)
Async XLA Ops:
  11.0 5.4 %collective-permute-start.11 = (bf16[32,1280]{1,0:T(8,128)(2,1)S(1)}, bf16[32,1280]{1,0:T(8,128)(2,1)S(1)}, u32[]{:S(2)}, u32[]{:S(2)}) collective-permute-start(bf16[32,1280]{1,0:T(8,128)(2,1)S(1)} %get-tuple-element.22), channel_id=1, source_target_pairs={{0,1},{1,2},{2,3},{3,0},{4,5},{5,6},{6,7},{7,4},{8,9},{9,10},{10,1... | collective-permute-start | bytes 245768 | tf_op jit(solution)/shard_map/ppermute | solution.py:42
  12.6 7.3 %collective-permute-start.12 = (bf16[32,1280]{1,0:T(8,128)(2,1)S(1)}, bf16[32,1280]{1,0:T(8,128)(2,1)S(1)}, u32[]{:S(2)}, u32[]{:S(2)}) collective-permute-start(bf16[32,1280]{1,0:T(8,128)(2,1)S(1)} %get-tuple-element.23), channel_id=1, source_target_pairs={{0,2},{1,3},{2,0},{3,1},{4,6},{5,7},{6,4},{7,5},{8,10},{9,11},{10,... | collective-permute-start | bytes 245768 | tf_op jit(solution)/shard_map/ppermute | solution.py:42
  13.8 7.8 %collective-permute-start.13 = (bf16[32,1280]{1,0:T(8,128)(2,1)S(1)}, bf16[32,1280]{1,0:T(8,128)(2,1)S(1)}, u32[]{:S(2)}, u32[]{:S(2)}) collective-permute-start(bf16[32,1280]{1,0:T(8,128)(2,1)S(1)} %get-tuple-element.24), channel_id=1, source_target_pairs={{0,3},{1,0},{2,1},{3,2},{4,7},{5,4},{6,5},{7,6},{8,11},{9,8},{10,9... | collective-permute-start | bytes 245768 | tf_op jit(solution)/shard_map/ppermute | solution.py:42
  21.8 5.4 %collective-permute-start.14 = (bf16[32,1280]{1,0:T(8,128)(2,1)S(1)}, bf16[32,1280]{1,0:T(8,128)(2,1)S(1)}, u32[]{:S(2)}, u32[]{:S(2)}) collective-permute-start(bf16[32,1280]{1,0:T(8,128)(2,1)S(1)} %shard_map.167.refs_0_), channel_id=1, source_target_pairs={{0,1},{1,2},{2,3},{3,0},{4,5},{5,6},{6,7},{7,4},{8,9},{9,10},{10,1... | collective-permute-start | bytes 245768 | tf_op jit(solution)/shard_map/ppermute | solution.py:42
  21.9 7.5 %collective-permute-start.15 = (bf16[32,1280]{1,0:T(8,128)(2,1)S(1)}, bf16[32,1280]{1,0:T(8,128)(2,1)S(1)}, u32[]{:S(2)}, u32[]{:S(2)}) collective-permute-start(bf16[32,1280]{1,0:T(8,128)(2,1)S(1)} %shard_map.167.refs_0_), channel_id=1, source_target_pairs={{0,2},{1,3},{2,0},{3,1},{4,6},{5,7},{6,4},{7,5},{8,10},{9,11},{10,... | collective-permute-start | bytes 245768 | tf_op jit(solution)/shard_map/ppermute | solution.py:42
  24.2 7.3 %collective-permute-start.16 = (bf16[32,1280]{1,0:T(8,128)(2,1)S(1)}, bf16[32,1280]{1,0:T(8,128)(2,1)S(1)}, u32[]{:S(2)}, u32[]{:S(2)}) collective-permute-start(bf16[32,1280]{1,0:T(8,128)(2,1)S(1)} %shard_map.167.refs_0_), channel_id=1, source_target_pairs={{0,3},{1,0},{2,1},{3,2},{4,7},{5,4},{6,5},{7,6},{8,11},{9,8},{10,9... | collective-permute-start | bytes 245768 | tf_op jit(solution)/shard_map/ppermute | solution.py:42
  25.5 6.8 %collective-permute-start.17 = (bf16[32,1280]{1,0:T(8,128)(2,1)S(1)}, bf16[32,1280]{1,0:T(8,128)(2,1)S(1)}, u32[]{:S(2)}, u32[]{:S(2)}) collective-permute-start(bf16[32,1280]{1,0:T(8,128)(2,1)S(1)} %shard_map.167.refs_0_), channel_id=1, source_target_pairs={{0,16},{16,0},{1,17},{17,1},{2,18},{18,2},{3,19},{19,3},{4,20},{20... | collective-permute-start | bytes 245768 | tf_op jit(solution)/shard_map/ppermute | solution.py:274
  27.2 5.1 %collective-permute-start.18 = (bf16[32,1280]{1,0:T(8,128)(2,1)S(1)}, bf16[32,1280]{1,0:T(8,128)(2,1)S(1)}, u32[]{:S(2)}, u32[]{:S(2)}) collective-permute-start(bf16[32,1280]{1,0:T(8,128)(2,1)S(1)} %collective-permute-done.14.refs_1_), channel_id=1, source_target_pairs={{0,16},{16,0},{1,17},{17,1},{2,18},{18,2},{3,19},{19,3},{4,20},{20... | collective-permute-start | bytes 245768 | tf_op jit(solution)/shard_map/ppermute | solution.py:274
  38.5 4.0 %collective-permute-start.21 = (bf16[64,4096]{1,0:T(8,128)(2,1)S(1)}, bf16[64,4096]{1,0:T(8,128)(2,1)S(1)}, u32[]{:S(2)}, u32[]{:S(2)}) collective-permute-start(bf16[64,4096]{1,0:T(8,128)(2,1)S(1)} %get-tuple-element.26), channel_id=1, source_target_pairs={{0,16},{16,0},{1,17},{17,1},{2,18},{18,2},{3,19},{19,3},{4,20},{20... | collective-permute-start | bytes 1572872 | tf_op jit(solution)/shard_map/ppermute | solution.py:274
  39.0 9.2 %collective-permute-start = (bf16[16,8192]{1,0:T(8,128)(2,1)S(1)}, bf16[16,8192]{1,0:T(8,128)(2,1)S(1)}, u32[]{:S(2)}, u32[]{:S(2)}) collective-permute-start(bf16[16,8192]{1,0:T(8,128)(2,1)S(1)} %shard_map.163.refs_0_), channel_id=1, source_target_pairs={{0,1},{1,2},{2,3},{3,0},{4,5},{5,6},{6,7},{7,4},{8,9},{9,10},{10,1... | collective-permute-start | bytes 786440 | tf_op jit(solution)/shard_map/ppermute | solution.py:42
  39.1 26.4 %collective-permute-start.1 = (bf16[16,8192]{1,0:T(8,128)(2,1)S(1)}, bf16[16,8192]{1,0:T(8,128)(2,1)S(1)}, u32[]{:S(2)}, u32[]{:S(2)}) collective-permute-start(bf16[16,8192]{1,0:T(8,128)(2,1)S(1)} %shard_map.163.refs_0_), channel_id=1, source_target_pairs={{0,2},{1,3},{2,0},{3,1},{4,6},{5,7},{6,4},{7,5},{8,10},{9,11},{10,... | collective-permute-start | bytes 786440 | tf_op jit(solution)/shard_map/ppermute | solution.py:42
  41.6 27.2 %collective-permute-start.2 = (bf16[16,8192]{1,0:T(8,128)(2,1)S(1)}, bf16[16,8192]{1,0:T(8,128)(2,1)S(1)}, u32[]{:S(2)}, u32[]{:S(2)}) collective-permute-start(bf16[16,8192]{1,0:T(8,128)(2,1)S(1)} %shard_map.163.refs_0_), channel_id=1, source_target_pairs={{0,3},{1,0},{2,1},{3,2},{4,7},{5,4},{6,5},{7,6},{8,11},{9,8},{10,9... | collective-permute-start | bytes 786440 | tf_op jit(solution)/shard_map/ppermute | solution.py:42
  42.6 26.2 %collective-permute-start.22 = (bf16[64,1024]{1,0:T(8,128)(2,1)S(1)}, bf16[64,1024]{1,0:T(8,128)(2,1)S(1)}, u32[]{:S(2)}, u32[]{:S(2)}) collective-permute-start(bf16[64,1024]{1,0:T(8,128)(2,1)S(1)} %get-tuple-element.28), channel_id=1, source_target_pairs={{0,1},{1,2},{2,3},{3,0},{4,5},{5,6},{6,7},{7,4},{8,9},{9,10},{10,1... | collective-permute-start | bytes 393224 | tf_op jit(solution)/shard_map/ppermute | solution.py:42
  43.8 32.4 %collective-permute-start.3 = (bf16[16,8192]{1,0:T(8,128)(2,1)S(1)}, bf16[16,8192]{1,0:T(8,128)(2,1)S(1)}, u32[]{:S(2)}, u32[]{:S(2)}) collective-permute-start(bf16[16,8192]{1,0:T(8,128)(2,1)S(1)} %shard_map.163.refs_0_), channel_id=1, source_target_pairs={{0,16},{16,0},{1,17},{17,1},{2,18},{18,2},{3,19},{19,3},{4,20},{20... | collective-permute-start | bytes 786440 | tf_op jit(solution)/shard_map/ppermute | solution.py:274
  48.2 29.4 %collective-permute-start.4 = (bf16[16,8192]{1,0:T(8,128)(2,1)S(1)}, bf16[16,8192]{1,0:T(8,128)(2,1)S(1)}, u32[]{:S(2)}, u32[]{:S(2)}) collective-permute-start(bf16[16,8192]{1,0:T(8,128)(2,1)S(1)} %collective-permute-done.refs_1_), channel_id=1, source_target_pairs={{0,16},{16,0},{1,17},{17,1},{2,18},{18,2},{3,19},{19,3},{4,20},{20... | collective-permute-start | bytes 786440 | tf_op jit(solution)/shard_map/ppermute | solution.py:274
  65.4 8.6 %collective-permute-start.23 = (bf16[64,1024]{1,0:T(8,128)(2,1)S(1)}, bf16[64,1024]{1,0:T(8,128)(2,1)S(1)}, u32[]{:S(2)}, u32[]{:S(2)}) collective-permute-start(bf16[64,1024]{1,0:T(8,128)(2,1)S(1)} %get-tuple-element.29), channel_id=1, source_target_pairs={{0,2},{1,3},{2,0},{3,1},{4,6},{5,7},{6,4},{7,5},{8,10},{9,11},{10,... | collective-permute-start | bytes 393224 | tf_op jit(solution)/shard_map/ppermute | solution.py:42
  68.8 7.2 %collective-permute-start.24 = (bf16[64,1024]{1,0:T(8,128)(2,1)S(1)}, bf16[64,1024]{1,0:T(8,128)(2,1)S(1)}, u32[]{:S(2)}, u32[]{:S(2)}) collective-permute-start(bf16[64,1024]{1,0:T(8,128)(2,1)S(1)} %get-tuple-element.30), channel_id=1, source_target_pairs={{0,3},{1,0},{2,1},{3,2},{4,7},{5,4},{6,5},{7,6},{8,11},{9,8},{10,9... | collective-permute-start | bytes 393224 | tf_op jit(solution)/shard_map/ppermute | solution.py:42
  68.8 10.7 %collective-permute-start.5 = (bf16[16,8192]{1,0:T(8,128)(2,1)S(1)}, bf16[16,8192]{1,0:T(8,128)(2,1)S(1)}, u32[]{:S(2)}, u32[]{:S(2)}) collective-permute-start(bf16[16,8192]{1,0:T(8,128)(2,1)S(1)} %collective-permute-done.1.refs_2_), channel_id=1, source_target_pairs={{0,16},{16,0},{1,17},{17,1},{2,18},{18,2},{3,19},{19,3},{4,20},{20... | collective-permute-start | bytes 786440 | tf_op jit(solution)/shard_map/ppermute | solution.py:274
  74.0 16.1 %collective-permute-start.6 = (bf16[16,8192]{1,0:T(8,128)(2,1)S(1)}, bf16[16,8192]{1,0:T(8,128)(2,1)S(1)}, u32[]{:S(2)}, u32[]{:S(2)}) collective-permute-start(bf16[16,8192]{1,0:T(8,128)(2,1)S(1)} %collective-permute-done.2.refs_3_), channel_id=1, source_target_pairs={{0,16},{16,0},{1,17},{17,1},{2,18},{18,2},{3,19},{19,3},{4,20},{20... | collective-permute-start | bytes 786440 | tf_op jit(solution)/shard_map/ppermute | solution.py:274
  76.1 6.4 %collective-permute-start.25 = (bf16[64,1024]{1,0:T(8,128)(2,1)S(1)}, bf16[64,1024]{1,0:T(8,128)(2,1)S(1)}, u32[]{:S(2)}, u32[]{:S(2)}) collective-permute-start(bf16[64,1024]{1,0:T(8,128)(2,1)S(1)} %shard_map.170.refs_0_), channel_id=1, source_target_pairs={{0,1},{1,2},{2,3},{3,0},{4,5},{5,6},{6,7},{7,4},{8,9},{9,10},{10,1... | collective-permute-start | bytes 393224 | tf_op jit(solution)/shard_map/ppermute | solution.py:42
  76.2 11.6 %collective-permute-start.26 = (bf16[64,1024]{1,0:T(8,128)(2,1)S(1)}, bf16[64,1024]{1,0:T(8,128)(2,1)S(1)}, u32[]{:S(2)}, u32[]{:S(2)}) collective-permute-start(bf16[64,1024]{1,0:T(8,128)(2,1)S(1)} %shard_map.170.refs_0_), channel_id=1, source_target_pairs={{0,2},{1,3},{2,0},{3,1},{4,6},{5,7},{6,4},{7,5},{8,10},{9,11},{10,... | collective-permute-start | bytes 393224 | tf_op jit(solution)/shard_map/ppermute | solution.py:42
  77.6 12.5 %collective-permute-start.27 = (bf16[64,1024]{1,0:T(8,128)(2,1)S(1)}, bf16[64,1024]{1,0:T(8,128)(2,1)S(1)}, u32[]{:S(2)}, u32[]{:S(2)}) collective-permute-start(bf16[64,1024]{1,0:T(8,128)(2,1)S(1)} %shard_map.170.refs_0_), channel_id=1, source_target_pairs={{0,3},{1,0},{2,1},{3,2},{4,7},{5,4},{6,5},{7,6},{8,11},{9,8},{10,9... | collective-permute-start | bytes 393224 | tf_op jit(solution)/shard_map/ppermute | solution.py:42
  79.5 15.1 %collective-permute-start.28 = (bf16[64,1024]{1,0:T(8,128)(2,1)S(1)}, bf16[64,1024]{1,0:T(8,128)(2,1)S(1)}, u32[]{:S(2)}, u32[]{:S(2)}) collective-permute-start(bf16[64,1024]{1,0:T(8,128)(2,1)S(1)} %shard_map.170.refs_0_), channel_id=1, source_target_pairs={{0,16},{16,0},{1,17},{17,1},{2,18},{18,2},{3,19},{19,3},{4,20},{20... | collective-permute-start | bytes 393224 | tf_op jit(solution)/shard_map/ppermute | solution.py:274
  82.5 12.6 %collective-permute-start.29 = (bf16[64,1024]{1,0:T(8,128)(2,1)S(1)}, bf16[64,1024]{1,0:T(8,128)(2,1)S(1)}, u32[]{:S(2)}, u32[]{:S(2)}) collective-permute-start(bf16[64,1024]{1,0:T(8,128)(2,1)S(1)} %collective-permute-done.25.refs_1_), channel_id=1, source_target_pairs={{0,16},{16,0},{1,17},{17,1},{2,18},{18,2},{3,19},{19,3},{4,20},{20... | collective-permute-start | bytes 393224 | tf_op jit(solution)/shard_map/ppermute | solution.py:274
  87.8 8.9 %collective-permute-start.30 = (bf16[64,1024]{1,0:T(8,128)(2,1)S(1)}, bf16[64,1024]{1,0:T(8,128)(2,1)S(1)}, u32[]{:S(2)}, u32[]{:S(2)}) collective-permute-start(bf16[64,1024]{1,0:T(8,128)(2,1)S(1)} %collective-permute-done.26.refs_2_), channel_id=1, source_target_pairs={{0,16},{16,0},{1,17},{17,1},{2,18},{18,2},{3,19},{19,3},{4,20},{20... | collective-permute-start | bytes 393224 | tf_op jit(solution)/shard_map/ppermute | solution.py:274
  90.1 6.6 %collective-permute-start.31 = (bf16[64,1024]{1,0:T(8,128)(2,1)S(1)}, bf16[64,1024]{1,0:T(8,128)(2,1)S(1)}, u32[]{:S(2)}, u32[]{:S(2)}) collective-permute-start(bf16[64,1024]{1,0:T(8,128)(2,1)S(1)} %collective-permute-done.27.refs_3_), channel_id=1, source_target_pairs={{0,16},{16,0},{1,17},{17,1},{2,18},{18,2},{3,19},{19,3},{4,20},{20... | collective-permute-start | bytes 393224 | tf_op jit(solution)/shard_map/ppermute | solution.py:274
  93.0 7.5 %collective-permute-start.7 = (bf16[128,256]{1,0:T(8,128)(2,1)S(1)}, bf16[128,256]{1,0:T(8,128)(2,1)S(1)}, u32[]{:S(2)}, u32[]{:S(2)}) collective-permute-start(bf16[128,256]{1,0:T(8,128)(2,1)S(1)} %shard_map.164.refs_0_), channel_id=1, source_target_pairs={{0,4},{4,8},{8,12},{12,0},{1,5},{5,9},{9,13},{13,1},{2,6},{6,10},{... | collective-permute-start | bytes 196616 | tf_op jit(solution)/shard_map/ppermute | solution.py:42
  94.6 6.0 %collective-permute-start.8 = (bf16[128,256]{1,0:T(8,128)(2,1)S(1)}, bf16[128,256]{1,0:T(8,128)(2,1)S(1)}, u32[]{:S(2)}, u32[]{:S(2)}) collective-permute-start(bf16[128,256]{1,0:T(8,128)(2,1)S(1)} %shard_map.164.refs_0_), channel_id=1, source_target_pairs={{0,8},{4,12},{8,0},{12,4},{1,9},{5,13},{9,1},{13,5},{2,10},{6,14},... | collective-permute-start | bytes 196616 | tf_op jit(solution)/shard_map/ppermute | solution.py:42
  95.1 5.5 %collective-permute-start.9 = (bf16[128,256]{1,0:T(8,128)(2,1)S(1)}, bf16[128,256]{1,0:T(8,128)(2,1)S(1)}, u32[]{:S(2)}, u32[]{:S(2)}) collective-permute-start(bf16[128,256]{1,0:T(8,128)(2,1)S(1)} %shard_map.164.refs_0_), channel_id=1, source_target_pairs={{0,12},{4,0},{8,4},{12,8},{1,13},{5,1},{9,5},{13,9},{2,14},{6,2},{... | collective-permute-start | bytes 196616 | tf_op jit(solution)/shard_map/ppermute | solution.py:42
  97.6 4.0 %collective-permute-start.32 = (bf16[64,256]{1,0:T(8,128)(2,1)S(1)}, bf16[64,256]{1,0:T(8,128)(2,1)S(1)}, u32[]{:S(2)}, u32[]{:S(2)}) collective-permute-start(bf16[64,256]{1,0:T(8,128)(2,1)S(1)} %shard_map.171.refs_4_), channel_id=1, source_target_pairs={{0,4},{4,8},{8,12},{12,0},{1,5},{5,9},{9,13},{13,1},{2,6},{6,10},{... | collective-permute-start | bytes 98312 | tf_op jit(solution)/shard_map/ppermute | solution.py:42
  99.0 3.9 %collective-permute-start.33 = (bf16[64,256]{1,0:T(8,128)(2,1)S(1)}, bf16[64,256]{1,0:T(8,128)(2,1)S(1)}, u32[]{:S(2)}, u32[]{:S(2)}) collective-permute-start(bf16[64,256]{1,0:T(8,128)(2,1)S(1)} %shard_map.171.refs_4_), channel_id=1, source_target_pairs={{0,8},{4,12},{8,0},{12,4},{1,9},{5,13},{9,1},{13,5},{2,10},{6,14},... | collective-permute-start | bytes 98312 | tf_op jit(solution)/shard_map/ppermute | solution.py:42
  100.6 4.8 %collective-permute-start.34 = (bf16[64,256]{1,0:T(8,128)(2,1)S(1)}, bf16[64,256]{1,0:T(8,128)(2,1)S(1)}, u32[]{:S(2)}, u32[]{:S(2)}) collective-permute-start(bf16[64,256]{1,0:T(8,128)(2,1)S(1)} %shard_map.171.refs_4_), channel_id=1, source_target_pairs={{0,12},{4,0},{8,4},{12,8},{1,13},{5,1},{9,5},{13,9},{2,14},{6,2},{... | collective-permute-start | bytes 98312 | tf_op jit(solution)/shard_map/ppermute | solution.py:42
  (16 other events, 238.1 us)

commit v2 on v1

--- a/solution.py
+++ b/solution.py
@@ -15,23 +15,31 @@
 NORM_EPS = 1e-06
 F32 = jnp.float32
 BF16 = jnp.bfloat16
-VMEM_LIMIT = 48 * 1024 * 1024
+MIB = 1024 * 1024
 NT = (((1,), (1,)), ((), ()))
 
 
-def call(kernel, outs, args, scratch=(), smem=0, flops=0):
-    vmem = pl.BlockSpec(memory_space=pltpu.VMEM)
+def call(kernel, outs, args, after=(), scratch=(), smem=0, raw=False, flops=0, grant=8):
+    space = pl.BlockSpec(memory_space=pltpu.HBM if raw else pltpu.VMEM)
     scalar = pl.BlockSpec(memory_space=pltpu.SMEM)
+    unread = pl.BlockSpec(memory_space=pl.ANY)
     moved = sum(math.prod(a.shape) * a.dtype.itemsize for a in list(args) + list(outs))
+    count = len(after)
+    if raw:
+        args = [pltpu.with_memory_space_constraint(a, pltpu.HBM) for a in args]
+
+    def body(*refs):
+        kernel(*refs[count:])
+
     return pl.pallas_call(
-        kernel,
+        body,
         out_shape=outs,
-        in_specs=[scalar] * smem + [vmem] * (len(args) - smem),
-        out_specs=[vmem] * len(outs),
+        in_specs=[unread] * count + [scalar] * smem + [space] * (len(args) - smem),
+        out_specs=[pl.BlockSpec(memory_space=pltpu.VMEM)] * len(outs),
         scratch_shapes=list(scratch),
-        compiler_params=pltpu.CompilerParams(vmem_limit_bytes=VMEM_LIMIT),
+        compiler_params=pltpu.CompilerParams(vmem_limit_bytes=grant * MIB),
         cost_estimate=pl.CostEstimate(flops=flops, bytes_accessed=moved, transcendentals=0),
-    )(*args)
+    )(*after, *args)
 
 
 def struct(shape, dtype):
@@ -46,20 +54,31 @@
     return section * (n_z // JOIN) + z // JOIN
 
 
-def front_kernel(n_z, block, place, x_ref, gain_ref, w_ref, b_ref, wo_ref, ob_ref,
-                 keep_ref, send_ref, base_ref, hf):
+def front_kernel(n_z, block, kept, place_hbm, x_hbm, gain_hbm, w_hbm, b_hbm, wo_hbm, ob_hbm, *refs):
+    later, refs = refs[:kept], refs[kept:]
+    (keep_ref, send_ref, base_ref), held, refs = refs[:3], refs[3:3 + kept], refs[3 + kept:]
+    hf, place, x_ref, gain_ref, w_ref, b_ref, wo_ref, ob_ref, sems = refs
+    brought = (
+        (x_hbm, x_ref), (gain_hbm, gain_ref), (w_hbm, w_ref), (b_hbm, b_ref),
+        (place_hbm, place), (wo_hbm, wo_ref), (ob_hbm, ob_ref), *zip(later, held),
+    )
+    copies = [pltpu.make_async_copy(a, b, sems.at[i]) for i, (a, b) in enumerate(brought)]
+    for copy in copies:
+        copy.start()
     c, z, s = lax.axis_index("section"), lax.axis_index("mp"), lax.axis_index("seq")
     rows, width = x_ref.shape
     head_width = hf.shape[1]
     units = place.shape[2]
     tile = 256
     per_tile = tile // WIN
+    for copy in copies[:5]:
+        copy.wait()
 
     def one(t, carry):
         at = pl.ds(pl.multiple_of(t * tile, tile), tile)
         x = x_ref[at, :].astype(F32)
         scale = lax.rsqrt(jnp.mean(x * x, axis=-1, keepdims=True) + NORM_EPS)
-        y = (x * scale * gain_ref[...]).astype(BF16)
+        y = (x * scale * gain_ref[...][None, :]).astype(BF16)
         parts = []
         for i in range(3):
             w = w_ref[i * head_width:(i + 1) * head_width, :]
@@ -101,6 +120,8 @@
         source = first + JOIN * (i % block)
         return (lax.broadcasted_iota(jnp.int32, (count, rows), 1) == source).astype(BF16)
 
+    copies[5].wait()
+    copies[6].wait()
     wo = wo_ref[...]
     heads = hf[...]
     for section, out in ((1 - c, send_ref), (c, keep_ref)):
@@ -108,7 +129,9 @@
         chosen = jnp.dot(order, heads, preferred_element_type=F32).astype(BF16)
         out[...] = jnp.dot(chosen, wo, preferred_element_type=F32).astype(BF16)
     own = jnp.dot(picked(c, z, block), x_ref[...], preferred_element_type=F32)
-    base_ref[...] = own + ob_ref[...]
+    base_ref[...] = own + ob_ref[...][None, :]
+    for copy in copies[7:]:
+        copy.wait()
 
 
 def pair_rows_kernel(n_z, block, keep_ref, got_ref, *outs):
@@ -126,12 +149,12 @@
         total += r[...].astype(F32)
     x = base_ref[...] + total
     scale = lax.rsqrt(jnp.mean(x * x, axis=-1, keepdims=True) + NORM_EPS)
-    out_ref[...] = (x * scale * gain_ref[...]).astype(BF16)
-
-
-def merge_kernel(n_z, block, up_ref, ub_ref, down_ref, *refs):
+    out_ref[...] = (x * scale * gain_ref[...][None, :]).astype(BF16)
+
+
+def hidden_kernel(n_z, block, up_ref, ub_ref, *refs):
     c, z = lax.axis_index("section"), lax.axis_index("mp")
-    pieces, (keep_ref, send_ref, xs) = refs[:2 * n_z], refs[2 * n_z:]
+    pieces, (out_ref, xs) = refs[:2 * n_z], refs[2 * n_z:]
     width = xs.shape[2]
     for side in range(2):
         section = c if side == 0 else 1 - c
@@ -140,15 +163,18 @@
             chunk = chunk_of(section, zz, n_z)
             at = pl.ds(pl.multiple_of(chunk * block, block), block)
             xs[lax.rem(zz, JOIN), at, :] = pieces[side * n_z + k][...]
-    acc = ub_ref[...]
+    acc = ub_ref[...][None, :]
     for q in range(JOIN):
         acc = acc + lax.dot_general(
             xs[q], up_ref[:, q * width:(q + 1) * width], NT, preferred_element_type=F32)
-    hidden = (0.5 * acc * (1.0 + lax.erf(acc * (1.0 / math.sqrt(2.0))))).astype(BF16)
-    half = keep_ref.shape[1]
-    for section, out in ((1 - c, send_ref), (c, keep_ref)):
-        at = pl.ds(pl.multiple_of(section * half, half), half)
-        out[...] = jnp.dot(hidden, down_ref[:, at], preferred_element_type=F32).astype(BF16)
+    out_ref[...] = (0.5 * acc * (1.0 + lax.erf(acc * (1.0 / math.sqrt(2.0))))).astype(BF16)
+
+
+def down_kernel(other, hidden_ref, down_ref, out_ref):
+    c = lax.axis_index("section")
+    half = out_ref.shape[1]
+    at = pl.ds(pl.multiple_of((1 - c if other else c) * half, half), half)
+    out_ref[...] = jnp.dot(hidden_ref[...], down_ref[:, at], preferred_element_type=F32).astype(BF16)
 
 
 def pair_columns_kernel(n_z, block, keep_ref, got_ref, *outs):
@@ -167,14 +193,16 @@
     for r in refs[:-1]:
         total += r[...].astype(F32)
     at = pl.ds(pl.multiple_of(d * block, block), block)
-    out_ref[...] = (total + bias_ref[:, at]).astype(BF16)
-
-
-def image_keyval_kernel(n_z, gain_ref, w_ref, b_ref, *refs):
+    out_ref[...] = (total + bias_ref[at][None, :]).astype(BF16)
+
+
+def image_keyval_kernel(n_z, text_ref, gain_ref, w_ref, b_ref, *refs):
     c, z = lax.axis_index("section"), lax.axis_index("mp")
     pieces, out_ref = refs[:-1], refs[-1]
     rows, block = pieces[0].shape
-    acc = jnp.zeros(out_ref.shape, F32)
+    prompt = text_ref.shape[0]
+    out_ref[:prompt, :] = text_ref[...]
+    acc = jnp.zeros((rows, out_ref.shape[1]), F32)
     squares = jnp.zeros((rows, 1), F32)
     for side in range(2):
         section = c if side == 0 else 1 - c
@@ -183,23 +211,29 @@
             at = pl.ds(pl.multiple_of(d * block, block), block)
             x = pieces[side * n_z + k][...].astype(F32)
             squares += jnp.sum(x * x, axis=-1, keepdims=True)
-            acc += jnp.dot((x * gain_ref[:, at]).astype(BF16), w_ref[at, :], preferred_element_type=F32)
+            acc += jnp.dot((x * gain_ref[at][None, :]).astype(BF16), w_ref[at, :], preferred_element_type=F32)
     scale = lax.rsqrt(squares * (1.0 / w_ref.shape[0]) + NORM_EPS)
-    out_ref[...] = (acc * scale + b_ref[...]).astype(BF16)
-
-
-def text_norm_kernel(x_ref, gain_ref, out_ref):
-    x = x_ref[...].astype(F32)
-    scale = lax.rsqrt(jnp.mean(x * x, axis=-1, keepdims=True) + NORM_EPS)
-    out_ref[...] = (x * scale * gain_ref[...]).astype(BF16)
-
-
-def text_keyval_kernel(n_z, w_ref, b_ref, *refs):
+    out_ref[prompt:, :] = (acc * scale + b_ref[...][None, :]).astype(BF16)
+
+
+def relay_kernel(in_ref, out_ref):
+    out_ref[...] = in_ref[...]
+
+
+def text_keyval_kernel(n_z, gain_ref, w_ref, b_ref, *refs):
     c, z = lax.axis_index("section"), lax.axis_index("mp")
     pieces, out_ref = refs[:-1], refs[-1]
-    block = pieces[0].shape[0]
-    x = jnp.concatenate([p[...] for p in pieces], axis=0)
-    acc = jnp.dot(x, w_ref[...], preferred_element_type=F32) + b_ref[...]
+    block, model = pieces[0].shape
+    acc = jnp.zeros(out_ref.shape, F32)
+    squares = jnp.zeros((out_ref.shape[0], 1), F32)
+    step = 1024
+    for first in range(0, model, step):
+        x = jnp.concatenate([p[:, first:first + step] for p in pieces], axis=0).astype(F32)
+        squares += jnp.sum(x * x, axis=-1, keepdims=True)
+        y = (x * gain_ref[first:first + step][None, :]).astype(BF16)
+        acc += jnp.dot(y, w_ref[first:first + step, :], preferred_element_type=F32)
+    scale = lax.rsqrt(squares * (1.0 / model) + NORM_EPS)
+    acc = acc * scale + b_ref[...][None, :]
     for side in range(2):
         section = c if side == 0 else 1 - c
         for k in range(n_z):
@@ -211,10 +245,11 @@
 
 def place_kernel(n_s, slot_map, place_ref, *refs):
     s = lax.axis_index("seq")
-    texts, images, (out_ref, held) = refs[:n_s], refs[n_s:2 * n_s], refs[2 * n_s:]
+    keyvals, (out_ref, held) = refs[:n_s], refs[n_s:]
     units = place_ref.shape[2]
+    prompt = n_s * CTX
     for k in range(n_s):
-        held[lax.rem(s - k + n_s, n_s)] = images[k][...]
+        held[lax.rem(s - k + n_s, n_s)] = keyvals[k][prompt:, :]
     position = lax.broadcasted_iota(jnp.int32, (CTX, units), 0)
     for k in range(n_s):
         j = lax.rem(s - k + n_s, n_s)
@@ -228,7 +263,7 @@
                 covered = jnp.sum(chosen.astype(F32), axis=1, keepdims=True) > 0.5
                 rows = held[i, pl.ds(pl.multiple_of(j * units, units), units), :]
                 image = jnp.dot(chosen.astype(BF16), rows, preferred_element_type=F32)
-                text = texts[k][pl.ds(pl.multiple_of(i * CTX, CTX), CTX), :]
+                text = keyvals[k][pl.ds(pl.multiple_of(i * CTX, CTX), CTX), :]
                 out_ref[slot] = jnp.where(covered, image, text.astype(F32)).astype(BF16)
 
             return carry
@@ -262,14 +297,10 @@
     units = rows // JOIN
     block = rows // n_d
     head_width = out_weight.shape[0]
-    hidden = merge_up.shape[1]
     model = merge_down.shape[1]
     columns = model // n_d
     kv_width = kv_weight.shape[1]
 
-    def flat(v):
-        return v.reshape(1, -1)
-
     def swap(v):
         return lax.ppermute(v, "section", [(0, 1), (1, 0)])
 
@@ -277,24 +308,24 @@
         here = [own] + [shifted(own, "mp", n_z, k) for k in range(1, n_z)]
         return here + [swap(v) for v in here]
 
-    text_own, = call(text_norm_kernel, [struct(text.shape[1:], BF16)], [text[0], flat(input_gain)])
-    text_pieces = spread(text_own)
-    prompt = n_d * text.shape[1]
-    text_keyval, = call(
-        functools.partial(text_keyval_kernel, n_z),
-        [struct((prompt, kv_width), BF16)],
-        [kv_weight, flat(kv_bias)] + text_pieces,
-        flops=2 * prompt * model * kv_width,
-    )
-    texts = [text_keyval] + [shifted(text_keyval, "seq", n_s, k) for k in range(1, n_s)]
+    text_own = text[0]
+    text_at = {k: shifted(text_own, "mp", n_z, k) for k in range(1, n_z)}
 
     w = qkv_weight.transpose(1, 2, 0).reshape(3 * head_width, width)
-    keep, send, base = call(
-        functools.partial(front_kernel, n_z, block),
-        [struct((rows // 2, width), BF16)] * 2 + [struct((block, width), F32)],
-        [image_place, x, flat(vision_gain), w, qkv_bias, out_weight, flat(out_bias)],
-        [pltpu.VMEM((rows, head_width), BF16)],
-        smem=1,
+    later = [merge_gain, merge_up.T, merge_up_bias, merge_down_bias, input_gain, kv_bias]
+    keep, send, base, gain, up, up_bias, down_bias, text_gain, bias = call(
+        functools.partial(front_kernel, n_z, block, len(later)),
+        [struct((rows // 2, width), BF16)] * 2 + [struct((block, width), F32)]
+        + [struct(v.shape, v.dtype) for v in later],
+        [image_place, x, vision_gain, w, qkv_bias, out_weight, out_bias] + later,
+        scratch=[
+            pltpu.VMEM((rows, head_width), BF16), pltpu.SMEM(image_place.shape, jnp.int32),
+            pltpu.VMEM(x.shape, BF16), pltpu.VMEM(vision_gain.shape, F32), pltpu.VMEM(w.shape, BF16),
+            pltpu.VMEM(qkv_bias.shape, F32), pltpu.VMEM(out_weight.shape, BF16), pltpu.VMEM(out_bias.shape, F32),
+            pltpu.SemaphoreType.DMA((7 + len(later),)),
+        ],
+        raw=True,
+        grant=24,
         flops=2 * rows * width * 4 * head_width,
     )
     got = swap(send)
@@ -304,40 +335,66 @@
         [keep, got],
     )
     sums = [parts[0]] + [shifted(parts[k], "mp", n_z, k) for k in range(1, n_z)]
-    merged, = call(resid_kernel, [struct((block, width), BF16)], [base, flat(merge_gain)] + sums)
+    merged, = call(
+        resid_kernel, [struct((block, width), BF16)], [base, gain] + sums, after=[text_at[1]])
     pieces = spread(merged)
 
-    keep, send = call(
-        functools.partial(merge_kernel, n_z, block),
-        [struct((units, model // 2), BF16)] * 2,
-        [merge_up.T, flat(merge_up_bias), merge_down] + pieces,
-        [pltpu.VMEM((JOIN, units, width), BF16)],
-        flops=2 * units * hidden * (JOIN * width + model),
+    hidden, = call(
+        functools.partial(hidden_kernel, n_z, block),
+        [struct((units, merge_up.shape[1]), BF16)],
+        [up, up_bias] + pieces,
+        scratch=[pltpu.VMEM((JOIN, units, width), BF16)],
+        flops=2 * units * merge_up.size,
+    )
+    send, keep = (
+        call(
+            functools.partial(down_kernel, other),
+            [struct((units, model // 2), BF16)],
+            [hidden, merge_down],
+            flops=units * merge_down.size,
+            grant=16,
+        )[0]
+        for other in (True, False)
     )
     got = swap(send)
     parts = call(
         functools.partial(pair_columns_kernel, n_z, columns),
         [struct((units, columns), F32)] + [struct((units, columns), BF16)] * (n_z - 1),
         [keep, got],
+        after=[text_at[n_z - 1]],
     )
     sums = [parts[0]] + [shifted(parts[k], "mp", n_z, k) for k in range(1, n_z)]
     image, = call(
-        functools.partial(image_kernel, n_z), [struct((units, columns), BF16)], [flat(merge_down_bias)] + sums)
+        functools.partial(image_kernel, n_z), [struct((units, columns), BF16)], [down_bias] + sums)
     image_pieces = spread(image)
 
-    image_keyval, = call(
+    for k in range(2, n_z - 1):
+        text_at[k] = call(relay_kernel, [struct(text_own.shape, BF16)], [text_at[k]], after=[image])[0]
+    text_here = [text_own] + [text_at[k] for k in range(1, n_z)]
+    prompt = n_d * text.shape[1]
+    text_keyval, = call(
+        functools.partial(text_keyval_kernel, n_z),
+        [struct((prompt, kv_width), BF16)],
+        [text_gain, kv_weight, bias] + text_here + [swap(v) for v in text_here],
+        flops=2 * prompt * model * kv_width,
+        grant=16,
+    )
+
+    keyval, = call(
         functools.partial(image_keyval_kernel, n_z),
-        [struct((units, kv_width), BF16)],
-        [flat(input_gain), kv_weight, flat(kv_bias)] + image_pieces,
+        [struct((prompt + units, kv_width), BF16)],
+        [text_keyval, text_gain, kv_weight, bias] + image_pieces,
         flops=2 * units * model * kv_width,
-    )
-    images = [image_keyval] + [shifted(image_keyval, "seq", n_s, k) for k in range(1, n_s)]
+        grant=16,
+    )
+    keyvals = [keyval] + [shifted(keyval, "seq", n_s, k) for k in range(1, n_s)]
     cache, = call(
         functools.partial(place_kernel, n_s),
         [struct((n_s, CTX, kv_width), BF16)],
-        [slot_map, image_place] + texts + images,
-        [pltpu.VMEM((n_s, units, kv_width), BF16)],
+        [slot_map, image_place] + keyvals,
+        scratch=[pltpu.VMEM((n_s, units, kv_width), BF16)],
         smem=1,
+        grant=16,
     )
     return cache[None]
 

time: 108 us -> 94.4 us (0.87)
  local copies, waits for them, and re-layouts: 7.88 us -> 0.03 us
  Pallas kernels: 14.6 us -> 10.3 us
  starting transfers between devices: 26.7 us -> 24.3 us
  waiting for transfers between devices: 57.7 us -> 59.5 us
    unnamed x26 -> x12, local copies, waits for them, and re-layouts: 4.8 us -> 0.03 us
    pallas_call x10 -> x12, Pallas kernels: 14.6 us -> 10.3 us  [call(): pl.pallas_call(body, out_shape=outs, in_specs=[unread] * count + [scalar]...]
    reshape x4 -> x0, local copies, waits for them, and re-layouts: 3.08 us -> none  [flat(): return v.reshape(1, -1)]
    ppermute x21 -> x18, starting transfers between devices: 26.3 us -> 23.3 us  [shifted(): return lax.ppermute(x, axis, [(i, (i + k) % count) for i in range(count)])]
    ppermute x21 -> x18, waiting for transfers between devices: 55.5 us -> 57.9 us  [shifted(): return lax.ppermute(x, axis, [(i, (i + k) % count) for i in range(count)])]
  transfers between devices with their start and end apart: 35 -> 32, of which waited for: 17 -> 18; matrix products, arithmetic and copies ran while one was open for 1% -> 0% of each run, Pallas kernels for 4% -> 2%
where the time goes in v2:
time: 94.4 us; the launch traced here: 94.2 us
  waiting for transfers between devices  59.5 us (63%)
  starting transfers between devices  24.3 us (26%)
  Pallas kernels  10.3 us (11%)
    ppermute x18, waiting for transfers between devices, shifted(): return lax.ppermute(x, axis, [(i, (i + k) % count) for i in range(count)])  57.9 us
    ppermute x18, starting transfers between devices, shifted(): return lax.ppermute(x, axis, [(i, (i + k) % count) for i in range(count)])  23.3 us
    pallas_call x12, Pallas kernels, call(): pl.pallas_call(body, out_shape=outs, in_specs=[unread] * count + [scalar]...  10.3 us
  transfers between devices with their start and end apart: 32, of which 18 were waited for; matrix products, arithmetic and copies ran while one was open for 0% of the time, Pallas kernels for 2%

profile of v2, /device:TPU:10, one launch (start us, length us, event | category | flops | bytes accessed | tf_op | source)
XLA Modules:
  0.0 94.2 jit_solution(12279681344425774574)
XLA Ops:
  0.0 3.9 %shard_map.163 = (bf16[128,1280]{1,0:T(8,128)(2,1)S(1)}, bf16[128,1280]{1,0:T(8,128)(2,1)S(1)}, f32[32,1280]{1,0:T(8,128)S(1)}, f32[1280]{0:T(1024)S(1)}, bf16[3...) custom-call(s32[4,4,16]{2,1,0:T(4,128)} %refs_1_.7, ...), custom_call_target="tpu_custom_call" | custom-call | flops 419430400 | bytes 9825664 | tf_op jit(solution)/shard_map/pallas_call | solution.py:34
  4.0 1.6 %collective-permute-start = (bf16[16,8192]{1,0:T(8,128)(2,1)S(1)}, bf16[16,8192]{1,0:T(8,128)(2,1)S(1)}, u32[]{:S(2)}, u32[]{:S(2)}) collective-permute-start(bf16[16,8192]{1,0:T(8,128)(2,1)S(1)} %bitcast.9), channel_id=1, source_target_pairs={{0,1},{1,2},{2,3},{3,0},{4,5},{5,6},{6,7},{7,4},{8,9},{9,10},{10,1... | collective-permute-start | bytes 786440 | tf_op jit(solution)/shard_map/ppermute | solution.py:50
  5.7 1.6 %collective-permute-start.3 = (bf16[32,1280]{1,0:T(8,128)(2,1)S(1)}, bf16[32,1280]{1,0:T(8,128)(2,1)S(1)}, u32[]{:S(2)}, u32[]{:S(2)}) collective-permute-start(bf16[32,1280]{1,0:T(8,128)(2,1)S(1)} %get-tuple-element.32), channel_id=1, source_target_pairs={{0,1},{1,2},{2,3},{3,0},{4,5},{5,6},{6,7},{7,4},{8,9},{9,10},{10,1... | collective-permute-start | bytes 245768 | tf_op jit(solution)/shard_map/ppermute | solution.py:50
  7.3 1.2 %collective-permute-start.4 = (bf16[32,1280]{1,0:T(8,128)(2,1)S(1)}, bf16[32,1280]{1,0:T(8,128)(2,1)S(1)}, u32[]{:S(2)}, u32[]{:S(2)}) collective-permute-start(bf16[32,1280]{1,0:T(8,128)(2,1)S(1)} %get-tuple-element.33), channel_id=1, source_target_pairs={{0,2},{1,3},{2,0},{3,1},{4,6},{5,7},{6,4},{7,5},{8,10},{9,11},{10,... | collective-permute-start | bytes 245768 | tf_op jit(solution)/shard_map/ppermute | solution.py:50
  8.6 1.8 %collective-permute-start.5 = (bf16[32,1280]{1,0:T(8,128)(2,1)S(1)}, bf16[32,1280]{1,0:T(8,128)(2,1)S(1)}, u32[]{:S(2)}, u32[]{:S(2)}) collective-permute-start(bf16[32,1280]{1,0:T(8,128)(2,1)S(1)} %get-tuple-element.34), channel_id=1, source_target_pairs={{0,3},{1,0},{2,1},{3,2},{4,7},{5,4},{6,5},{7,6},{8,11},{9,8},{10,9... | collective-permute-start | bytes 245768 | tf_op jit(solution)/shard_map/ppermute | solution.py:50
  10.3 2.8 %collective-permute-done.refs_0_.refs_4_ = bf16[16,8192]{1,0:T(8,128)(2,1)S(1)} collective-permute-done((bf16[16,8192]{1,0:T(8,128)(2,1)S(1)}, bf16[16,8192]{1,0:T(8,128)(2,1)S(1)}, u32[]{:S(2)}, u32[]{:S(2)}) %collective-permute-start) | collective-permute-done | bytes 262176 | tf_op jit(solution)/shard_map/ppermute | solution.py:50
  13.2 4.2 %collective-permute-done.3.refs_4_ = bf16[32,1280]{1,0:T(8,128)(2,1)S(1)} collective-permute-done((bf16[32,1280]{1,0:T(8,128)(2,1)S(1)}, bf16[32,1280]{1,0:T(8,128)(2,1)S(1)}, u32[]{:S(2)}, u32[]{:S(2)}) %collective-permute-start.3) | collective-permute-done | bytes 81952 | tf_op jit(solution)/shard_map/ppermute | solution.py:50
  17.4 1.4 %collective-permute-done.4.refs_5_ = bf16[32,1280]{1,0:T(8,128)(2,1)S(1)} collective-permute-done((bf16[32,1280]{1,0:T(8,128)(2,1)S(1)}, bf16[32,1280]{1,0:T(8,128)(2,1)S(1)}, u32[]{:S(2)}, u32[]{:S(2)}) %collective-permute-start.4) | collective-permute-done | bytes 81952 | tf_op jit(solution)/shard_map/ppermute | solution.py:50
  18.8 1.8 %collective-permute-done.5.refs_6_ = bf16[32,1280]{1,0:T(8,128)(2,1)S(1)} collective-permute-done((bf16[32,1280]{1,0:T(8,128)(2,1)S(1)}, bf16[32,1280]{1,0:T(8,128)(2,1)S(1)}, u32[]{:S(2)}, u32[]{:S(2)}) %collective-permute-start.5) | collective-permute-done | bytes 81952 | tf_op jit(solution)/shard_map/ppermute | solution.py:50
  20.8 2.2 %collective-permute-start.7 = (bf16[32,1280]{1,0:T(8,128)(2,1)S(1)}, bf16[32,1280]{1,0:T(8,128)(2,1)S(1)}, u32[]{:S(2)}, u32[]{:S(2)}) collective-permute-start(bf16[32,1280]{1,0:T(8,128)(2,1)S(1)} %shard_map.165.refs_2_), channel_id=1, source_target_pairs={{0,2},{1,3},{2,0},{3,1},{4,6},{5,7},{6,4},{7,5},{8,10},{9,11},{10,... | collective-permute-start | bytes 245768 | tf_op jit(solution)/shard_map/ppermute | solution.py:50
  23.0 1.4 %collective-permute-start.8 = (bf16[32,1280]{1,0:T(8,128)(2,1)S(1)}, bf16[32,1280]{1,0:T(8,128)(2,1)S(1)}, u32[]{:S(2)}, u32[]{:S(2)}) collective-permute-start(bf16[32,1280]{1,0:T(8,128)(2,1)S(1)} %shard_map.165.refs_2_), channel_id=1, source_target_pairs={{0,3},{1,0},{2,1},{3,2},{4,7},{5,4},{6,5},{7,6},{8,11},{9,8},{10,9... | collective-permute-start | bytes 245768 | tf_op jit(solution)/shard_map/ppermute | solution.py:50
  24.4 1.7 %collective-permute-done.6.refs_3_ = bf16[32,1280]{1,0:T(8,128)(2,1)S(1)} collective-permute-done((bf16[32,1280]{1,0:T(8,128)(2,1)S(1)}, bf16[32,1280]{1,0:T(8,128)(2,1)S(1)}, u32[]{:S(2)}, u32[]{:S(2)}) %collective-permute-start.6) | collective-permute-done | bytes 81952 | tf_op jit(solution)/shard_map/ppermute | solution.py:50
  26.1 2.2 %collective-permute-done.7.refs_4_ = bf16[32,1280]{1,0:T(8,128)(2,1)S(1)} collective-permute-done((bf16[32,1280]{1,0:T(8,128)(2,1)S(1)}, bf16[32,1280]{1,0:T(8,128)(2,1)S(1)}, u32[]{:S(2)}, u32[]{:S(2)}) %collective-permute-start.7) | collective-permute-done | bytes 81952 | tf_op jit(solution)/shard_map/ppermute | solution.py:50
  28.3 2.3 %collective-permute-done.8.refs_5_ = bf16[32,1280]{1,0:T(8,128)(2,1)S(1)} collective-permute-done((bf16[32,1280]{1,0:T(8,128)(2,1)S(1)}, bf16[32,1280]{1,0:T(8,128)(2,1)S(1)}, u32[]{:S(2)}, u32[]{:S(2)}) %collective-permute-start.8) | collective-permute-done | bytes 81952 | tf_op jit(solution)/shard_map/ppermute | solution.py:50
  30.6 1.2 %collective-permute-done.12.refs_9_ = bf16[32,1280]{1,0:T(8,128)(2,1)S(1)} collective-permute-done((bf16[32,1280]{1,0:T(8,128)(2,1)S(1)}, bf16[32,1280]{1,0:T(8,128)(2,1)S(1)}, u32[]{:S(2)}, u32[]{:S(2)}) %collective-permute-start.12) | collective-permute-done | bytes 81952 | tf_op jit(solution)/shard_map/ppermute | solution.py:305
  31.8 1.1 %shard_map.166.refs_0_ = bf16[64,320]{1,0:T(8,128)(2,1)S(1)} custom-call(bf16[320,5120]{1,0:T(8,128)(2,1)S(1)} %get-tuple-element.25.refs_0_, f32[320]{0:T(512)S(1)} %get-tuple-element.26.refs_1_, bf16[32,1280]{1,0:T(8,128)(2,1)S(1)} %shard_map.165.refs_2_, bf16[32,1280]{1,0:T(8,128)(2,1)S(1)} %collective-permute-done.6.refs_3_, ...), custom_call_target="tpu_custom_call" | custom-call | flops 209715200 | bytes 3974400 | tf_op jit(solution)/shard_map/pallas_call | solution.py:34
  34.6 7.8 %collective-permute-done.1.refs_0_.refs_6_ = bf16[16,8192]{1,0:T(8,128)(2,1)S(1)} collective-permute-done((bf16[16,8192]{1,0:T(8,128)(2,1)S(1)}, bf16[16,8192]{1,0:T(8,128)(2,1)S(1)}, u32[]{:S(2)}, u32[]{:S(2)}) %collective-permute-start.1) | collective-permute-done | bytes 262176 | tf_op jit(solution)/shard_map/ppermute | solution.py:50
  42.6 3.1 %collective-permute-start.17 = (bf16[16,8192]{1,0:T(8,128)(2,1)S(1)}, bf16[16,8192]{1,0:T(8,128)(2,1)S(1)}, u32[]{:S(2)}, u32[]{:S(2)}) collective-permute-start(bf16[16,8192]{1,0:T(8,128)(2,1)S(1)} %bitcast.11), channel_id=1, source_target_pairs={{0,2},{1,3},{2,0},{3,1},{4,6},{5,7},{6,4},{7,5},{8,10},{9,11},{10,... | collective-permute-start | bytes 786440 | tf_op jit(solution)/shard_map/ppermute | solution.py:50
  46.3 1.5 %collective-permute-done.14.refs_2_ = bf16[64,1024]{1,0:T(8,128)(2,1)S(1)} collective-permute-done((bf16[64,1024]{1,0:T(8,128)(2,1)S(1)}, bf16[64,1024]{1,0:T(8,128)(2,1)S(1)}, u32[]{:S(2)}, u32[]{:S(2)}) %collective-permute-start.14) | collective-permute-done | bytes 131104 | tf_op jit(solution)/shard_map/ppermute | solution.py:50
  47.8 3.8 %collective-permute-start.16 = (bf16[64,1024]{1,0:T(8,128)(2,1)S(1)}, bf16[64,1024]{1,0:T(8,128)(2,1)S(1)}, u32[]{:S(2)}, u32[]{:S(2)}) collective-permute-start(bf16[64,1024]{1,0:T(8,128)(2,1)S(1)} %get-tuple-element.38), channel_id=1, source_target_pairs={{0,3},{1,0},{2,1},{3,2},{4,7},{5,4},{6,5},{7,6},{8,11},{9,8},{10,9... | collective-permute-start | bytes 393224 | tf_op jit(solution)/shard_map/ppermute | solution.py:50
  51.6 13.4 %collective-permute-done.15.refs_3_ = bf16[64,1024]{1,0:T(8,128)(2,1)S(1)} collective-permute-done((bf16[64,1024]{1,0:T(8,128)(2,1)S(1)}, bf16[64,1024]{1,0:T(8,128)(2,1)S(1)}, u32[]{:S(2)}, u32[]{:S(2)}) %collective-permute-start.15) | collective-permute-done | bytes 131104 | tf_op jit(solution)/shard_map/ppermute | solution.py:50
  65.0 3.3 %collective-permute-done.16.refs_4_ = bf16[64,1024]{1,0:T(8,128)(2,1)S(1)} collective-permute-done((bf16[64,1024]{1,0:T(8,128)(2,1)S(1)}, bf16[64,1024]{1,0:T(8,128)(2,1)S(1)}, u32[]{:S(2)}, u32[]{:S(2)}) %collective-permute-start.16) | collective-permute-done | bytes 131104 | tf_op jit(solution)/shard_map/ppermute | solution.py:50
  68.5 1.5 %collective-permute-start.23 = (bf16[64,1024]{1,0:T(8,128)(2,1)S(1)}, bf16[64,1024]{1,0:T(8,128)(2,1)S(1)}, u32[]{:S(2)}, u32[]{:S(2)}) collective-permute-start(bf16[64,1024]{1,0:T(8,128)(2,1)S(1)} %shard_map.170.refs_0_.refs_4_), channel_id=1, source_target_pairs={{0,2},{1,3},{2,0},{3,1},{4,6},{5,7},{6,4},{7,5},{8,10},{9,11},{10,... | collective-permute-start | bytes 393224 | tf_op jit(solution)/shard_map/ppermute | solution.py:50
  70.1 1.0 %collective-permute-start.24 = (bf16[64,1024]{1,0:T(8,128)(2,1)S(1)}, bf16[64,1024]{1,0:T(8,128)(2,1)S(1)}, u32[]{:S(2)}, u32[]{:S(2)}) collective-permute-start(bf16[64,1024]{1,0:T(8,128)(2,1)S(1)} %shard_map.170.refs_0_.refs_4_), channel_id=1, source_target_pairs={{0,3},{1,0},{2,1},{3,2},{4,7},{5,4},{6,5},{7,6},{8,11},{9,8},{10,9... | collective-permute-start | bytes 393224 | tf_op jit(solution)/shard_map/ppermute | solution.py:50
  71.1 3.7 %collective-permute-done.22.refs_5_ = bf16[64,1024]{1,0:T(8,128)(2,1)S(1)} collective-permute-done((bf16[64,1024]{1,0:T(8,128)(2,1)S(1)}, bf16[64,1024]{1,0:T(8,128)(2,1)S(1)}, u32[]{:S(2)}, u32[]{:S(2)}) %collective-permute-start.22) | collective-permute-done | bytes 131104 | tf_op jit(solution)/shard_map/ppermute | solution.py:50
  74.8 5.8 %collective-permute-done.23.refs_6_ = bf16[64,1024]{1,0:T(8,128)(2,1)S(1)} collective-permute-done((bf16[64,1024]{1,0:T(8,128)(2,1)S(1)}, bf16[64,1024]{1,0:T(8,128)(2,1)S(1)}, u32[]{:S(2)}, u32[]{:S(2)}) %collective-permute-start.23) | collective-permute-done | bytes 131104 | tf_op jit(solution)/shard_map/ppermute | solution.py:50
  80.6 1.3 %collective-permute-done.24.refs_7_ = bf16[64,1024]{1,0:T(8,128)(2,1)S(1)} collective-permute-done((bf16[64,1024]{1,0:T(8,128)(2,1)S(1)}, bf16[64,1024]{1,0:T(8,128)(2,1)S(1)}, u32[]{:S(2)}, u32[]{:S(2)}) %collective-permute-start.24) | collective-permute-done | bytes 131104 | tf_op jit(solution)/shard_map/ppermute | solution.py:50
  84.2 1.5 %collective-permute-start.29 = (bf16[192,256]{1,0:T(8,128)(2,1)S(1)}, bf16[192,256]{1,0:T(8,128)(2,1)S(1)}, u32[]{:S(2)}, u32[]{:S(2)}) collective-permute-start(bf16[192,256]{1,0:T(8,128)(2,1)S(1)} %shard_map.173.refs_2_), channel_id=1, source_target_pairs={{0,4},{4,8},{8,12},{12,0},{1,5},{5,9},{9,13},{13,1},{2,6},{6,10},{... | collective-permute-start | bytes 294920 | tf_op jit(solution)/shard_map/ppermute | solution.py:50
  86.3 1.5 %collective-permute-start.31 = (bf16[192,256]{1,0:T(8,128)(2,1)S(1)}, bf16[192,256]{1,0:T(8,128)(2,1)S(1)}, u32[]{:S(2)}, u32[]{:S(2)}) collective-permute-start(bf16[192,256]{1,0:T(8,128)(2,1)S(1)} %shard_map.173.refs_2_), channel_id=1, source_target_pairs={{0,12},{4,0},{8,4},{12,8},{1,13},{5,1},{9,5},{13,9},{2,14},{6,2},{... | collective-permute-start | bytes 294920 | tf_op jit(solution)/shard_map/ppermute | solution.py:50
  87.8 1.3 %collective-permute-done.29.refs_3_ = bf16[192,256]{1,0:T(8,128)(2,1)S(1)} collective-permute-done((bf16[192,256]{1,0:T(8,128)(2,1)S(1)}, bf16[192,256]{1,0:T(8,128)(2,1)S(1)}, u32[]{:S(2)}, u32[]{:S(2)}) %collective-permute-start.29) | collective-permute-done | bytes 98336 | tf_op jit(solution)/shard_map/ppermute | solution.py:50
  89.2 3.3 %collective-permute-done.30.refs_4_ = bf16[192,256]{1,0:T(8,128)(2,1)S(1)} collective-permute-done((bf16[192,256]{1,0:T(8,128)(2,1)S(1)}, bf16[192,256]{1,0:T(8,128)(2,1)S(1)}, u32[]{:S(2)}, u32[]{:S(2)}) %collective-permute-start.30) | collective-permute-done | bytes 98336 | tf_op jit(solution)/shard_map/ppermute | solution.py:50
  92.5 1.7 %shard_map.174 = bf16[4,32,256]{2,1,0:T(8,128)(2,1)} custom-call(s32[4,4]{1,0:T(4,128)S(1)} %copy-done.3, s32[4,4,16]{2,1,0:T(4,128)S(1)} %copy-done.2, bf16[192,256]{1,0:T(8,128)(2,1)S(1)} %shard_map.173.refs_2_, bf16[192,256]{1,0:T(8,128)(2,1)S(1)} %collective-permute-done.29.refs_3_, bf16[192,256]{1,0:T(8,128)(2,1)S(1)} %collective-permute-done.30.refs_4_, ...), custom_call_target="tpu_custom_call" | custom-call | bytes 459840 | tf_op jit(solution)/shard_map/pallas_call | solution.py:34
  (57 shorter events, 5.8 us)
Async XLA Ops:
  3.9 1.7 %collective-permute-start.2 = (bf16[128,1280]{1,0:T(8,128)(2,1)S(1)}, bf16[128,1280]{1,0:T(8,128)(2,1)S(1)}, u32[]{:S(2)}, u32[]{:S(2)}) collective-permute-start(bf16[128,1280]{1,0:T(8,128)(2,1)S(1)} %get-tuple-element.30), channel_id=1, source_target_pairs={{0,16},{16,0},{1,17},{17,1},{2,18},{18,2},{3,19},{19,3},{4,20},{20... | collective-permute-start | bytes 983048 | tf_op jit(solution)/shard_map/ppermute | solution.py:305
  4.0 9.2 %collective-permute-start = (bf16[16,8192]{1,0:T(8,128)(2,1)S(1)}, bf16[16,8192]{1,0:T(8,128)(2,1)S(1)}, u32[]{:S(2)}, u32[]{:S(2)}) collective-permute-start(bf16[16,8192]{1,0:T(8,128)(2,1)S(1)} %bitcast.9), channel_id=1, source_target_pairs={{0,1},{1,2},{2,3},{3,0},{4,5},{5,6},{6,7},{7,4},{8,9},{9,10},{10,1... | collective-permute-start | bytes 786440 | tf_op jit(solution)/shard_map/ppermute | solution.py:50
  5.7 11.7 %collective-permute-start.3 = (bf16[32,1280]{1,0:T(8,128)(2,1)S(1)}, bf16[32,1280]{1,0:T(8,128)(2,1)S(1)}, u32[]{:S(2)}, u32[]{:S(2)}) collective-permute-start(bf16[32,1280]{1,0:T(8,128)(2,1)S(1)} %get-tuple-element.32), channel_id=1, source_target_pairs={{0,1},{1,2},{2,3},{3,0},{4,5},{5,6},{6,7},{7,4},{8,9},{9,10},{10,1... | collective-permute-start | bytes 245768 | tf_op jit(solution)/shard_map/ppermute | solution.py:50
  7.3 11.5 %collective-permute-start.4 = (bf16[32,1280]{1,0:T(8,128)(2,1)S(1)}, bf16[32,1280]{1,0:T(8,128)(2,1)S(1)}, u32[]{:S(2)}, u32[]{:S(2)}) collective-permute-start(bf16[32,1280]{1,0:T(8,128)(2,1)S(1)} %get-tuple-element.33), channel_id=1, source_target_pairs={{0,2},{1,3},{2,0},{3,1},{4,6},{5,7},{6,4},{7,5},{8,10},{9,11},{10,... | collective-permute-start | bytes 245768 | tf_op jit(solution)/shard_map/ppermute | solution.py:50
  8.6 12.0 %collective-permute-start.5 = (bf16[32,1280]{1,0:T(8,128)(2,1)S(1)}, bf16[32,1280]{1,0:T(8,128)(2,1)S(1)}, u32[]{:S(2)}, u32[]{:S(2)}) collective-permute-start(bf16[32,1280]{1,0:T(8,128)(2,1)S(1)} %get-tuple-element.34), channel_id=1, source_target_pairs={{0,3},{1,0},{2,1},{3,2},{4,7},{5,4},{6,5},{7,6},{8,11},{9,8},{10,9... | collective-permute-start | bytes 245768 | tf_op jit(solution)/shard_map/ppermute | solution.py:50
  20.7 5.4 %collective-permute-start.6 = (bf16[32,1280]{1,0:T(8,128)(2,1)S(1)}, bf16[32,1280]{1,0:T(8,128)(2,1)S(1)}, u32[]{:S(2)}, u32[]{:S(2)}) collective-permute-start(bf16[32,1280]{1,0:T(8,128)(2,1)S(1)} %shard_map.165.refs_2_), channel_id=1, source_target_pairs={{0,1},{1,2},{2,3},{3,0},{4,5},{5,6},{6,7},{7,4},{8,9},{9,10},{10,1... | collective-permute-start | bytes 245768 | tf_op jit(solution)/shard_map/ppermute | solution.py:50
  20.8 7.5 %collective-permute-start.7 = (bf16[32,1280]{1,0:T(8,128)(2,1)S(1)}, bf16[32,1280]{1,0:T(8,128)(2,1)S(1)}, u32[]{:S(2)}, u32[]{:S(2)}) collective-permute-start(bf16[32,1280]{1,0:T(8,128)(2,1)S(1)} %shard_map.165.refs_2_), channel_id=1, source_target_pairs={{0,2},{1,3},{2,0},{3,1},{4,6},{5,7},{6,4},{7,5},{8,10},{9,11},{10,... | collective-permute-start | bytes 245768 | tf_op jit(solution)/shard_map/ppermute | solution.py:50
  23.0 7.6 %collective-permute-start.8 = (bf16[32,1280]{1,0:T(8,128)(2,1)S(1)}, bf16[32,1280]{1,0:T(8,128)(2,1)S(1)}, u32[]{:S(2)}, u32[]{:S(2)}) collective-permute-start(bf16[32,1280]{1,0:T(8,128)(2,1)S(1)} %shard_map.165.refs_2_), channel_id=1, source_target_pairs={{0,3},{1,0},{2,1},{3,2},{4,7},{5,4},{6,5},{7,6},{8,11},{9,8},{10,9... | collective-permute-start | bytes 245768 | tf_op jit(solution)/shard_map/ppermute | solution.py:50
  24.4 6.1 %collective-permute-start.9 = (bf16[32,1280]{1,0:T(8,128)(2,1)S(1)}, bf16[32,1280]{1,0:T(8,128)(2,1)S(1)}, u32[]{:S(2)}, u32[]{:S(2)}) collective-permute-start(bf16[32,1280]{1,0:T(8,128)(2,1)S(1)} %shard_map.165.refs_2_), channel_id=1, source_target_pairs={{0,16},{16,0},{1,17},{17,1},{2,18},{18,2},{3,19},{19,3},{4,20},{20... | collective-permute-start | bytes 245768 | tf_op jit(solution)/shard_map/ppermute | solution.py:305
  26.1 4.4 %collective-permute-start.10 = (bf16[32,1280]{1,0:T(8,128)(2,1)S(1)}, bf16[32,1280]{1,0:T(8,128)(2,1)S(1)}, u32[]{:S(2)}, u32[]{:S(2)}) collective-permute-start(bf16[32,1280]{1,0:T(8,128)(2,1)S(1)} %collective-permute-done.6.refs_3_), channel_id=1, source_target_pairs={{0,16},{16,0},{1,17},{17,1},{2,18},{18,2},{3,19},{19,3},{4,20},{20... | collective-permute-start | bytes 245768 | tf_op jit(solution)/shard_map/ppermute | solution.py:305
  28.3 2.3 %collective-permute-start.11 = (bf16[32,1280]{1,0:T(8,128)(2,1)S(1)}, bf16[32,1280]{1,0:T(8,128)(2,1)S(1)}, u32[]{:S(2)}, u32[]{:S(2)}) collective-permute-start(bf16[32,1280]{1,0:T(8,128)(2,1)S(1)} %collective-permute-done.7.refs_4_), channel_id=1, source_target_pairs={{0,16},{16,0},{1,17},{17,1},{2,18},{18,2},{3,19},{19,3},{4,20},{20... | collective-permute-start | bytes 245768 | tf_op jit(solution)/shard_map/ppermute | solution.py:305
  30.5 1.3 %collective-permute-start.12 = (bf16[32,1280]{1,0:T(8,128)(2,1)S(1)}, bf16[32,1280]{1,0:T(8,128)(2,1)S(1)}, u32[]{:S(2)}, u32[]{:S(2)}) collective-permute-start(bf16[32,1280]{1,0:T(8,128)(2,1)S(1)} %collective-permute-done.8.refs_5_), channel_id=1, source_target_pairs={{0,16},{16,0},{1,17},{17,1},{2,18},{18,2},{3,19},{19,3},{4,20},{20... | collective-permute-start | bytes 245768 | tf_op jit(solution)/shard_map/ppermute | solution.py:305
  33.6 8.8 %collective-permute-start.13 = (bf16[64,4096]{1,0:T(8,128)(2,1)S(1)}, bf16[64,4096]{1,0:T(8,128)(2,1)S(1)}, u32[]{:S(2)}, u32[]{:S(2)}) collective-permute-start(bf16[64,4096]{1,0:T(8,128)(2,1)S(1)} %shard_map.168), channel_id=1, source_target_pairs={{0,16},{16,0},{1,17},{17,1},{2,18},{18,2},{3,19},{19,3},{4,20},{20... | collective-permute-start | bytes 1572872 | tf_op jit(solution)/shard_map/ppermute | solution.py:305
  33.8 8.6 %collective-permute-start.1 = (bf16[16,8192]{1,0:T(8,128)(2,1)S(1)}, bf16[16,8192]{1,0:T(8,128)(2,1)S(1)}, u32[]{:S(2)}, u32[]{:S(2)}) collective-permute-start(bf16[16,8192]{1,0:T(8,128)(2,1)S(1)} %bitcast.10), channel_id=1, source_target_pairs={{0,3},{1,0},{2,1},{3,2},{4,7},{5,4},{6,5},{7,6},{8,11},{9,8},{10,9... | collective-permute-start | bytes 786440 | tf_op jit(solution)/shard_map/ppermute | solution.py:50
  42.5 5.3 %collective-permute-start.14 = (bf16[64,1024]{1,0:T(8,128)(2,1)S(1)}, bf16[64,1024]{1,0:T(8,128)(2,1)S(1)}, u32[]{:S(2)}, u32[]{:S(2)}) collective-permute-start(bf16[64,1024]{1,0:T(8,128)(2,1)S(1)} %get-tuple-element.36), channel_id=1, source_target_pairs={{0,1},{1,2},{2,3},{3,0},{4,5},{5,6},{6,7},{7,4},{8,9},{9,10},{10,1... | collective-permute-start | bytes 393224 | tf_op jit(solution)/shard_map/ppermute | solution.py:50
  42.6 25.7 %collective-permute-start.17 = (bf16[16,8192]{1,0:T(8,128)(2,1)S(1)}, bf16[16,8192]{1,0:T(8,128)(2,1)S(1)}, u32[]{:S(2)}, u32[]{:S(2)}) collective-permute-start(bf16[16,8192]{1,0:T(8,128)(2,1)S(1)} %bitcast.11), channel_id=1, source_target_pairs={{0,2},{1,3},{2,0},{3,1},{4,6},{5,7},{6,4},{7,5},{8,10},{9,11},{10,... | collective-permute-start | bytes 786440 | tf_op jit(solution)/shard_map/ppermute | solution.py:50
  45.7 19.3 %collective-permute-start.15 = (bf16[64,1024]{1,0:T(8,128)(2,1)S(1)}, bf16[64,1024]{1,0:T(8,128)(2,1)S(1)}, u32[]{:S(2)}, u32[]{:S(2)}) collective-permute-start(bf16[64,1024]{1,0:T(8,128)(2,1)S(1)} %get-tuple-element.37), channel_id=1, source_target_pairs={{0,2},{1,3},{2,0},{3,1},{4,6},{5,7},{6,4},{7,5},{8,10},{9,11},{10,... | collective-permute-start | bytes 393224 | tf_op jit(solution)/shard_map/ppermute | solution.py:50
  45.8 22.8 %collective-permute-start.18 = (bf16[16,8192]{1,0:T(8,128)(2,1)S(1)}, bf16[16,8192]{1,0:T(8,128)(2,1)S(1)}, u32[]{:S(2)}, u32[]{:S(2)}) collective-permute-start(bf16[16,8192]{1,0:T(8,128)(2,1)S(1)} %bitcast.12), channel_id=1, source_target_pairs={{0,16},{16,0},{1,17},{17,1},{2,18},{18,2},{3,19},{19,3},{4,20},{20... | collective-permute-start | bytes 786440 | tf_op jit(solution)/shard_map/ppermute | solution.py:305
  45.8 24.3 %collective-permute-start.19 = (bf16[16,8192]{1,0:T(8,128)(2,1)S(1)}, bf16[16,8192]{1,0:T(8,128)(2,1)S(1)}, u32[]{:S(2)}, u32[]{:S(2)}) collective-permute-start(bf16[16,8192]{1,0:T(8,128)(2,1)S(1)} %collective-permute-done.refs_0_.refs_4_), channel_id=1, source_target_pairs={{0,16},{16,0},{1,17},{17,1},{2,18},{18,2},{3,19},{19,3},{4,20},{20... | collective-permute-start | bytes 786440 | tf_op jit(solution)/shard_map/ppermute | solution.py:305
  47.8 20.5 %collective-permute-start.16 = (bf16[64,1024]{1,0:T(8,128)(2,1)S(1)}, bf16[64,1024]{1,0:T(8,128)(2,1)S(1)}, u32[]{:S(2)}, u32[]{:S(2)}) collective-permute-start(bf16[64,1024]{1,0:T(8,128)(2,1)S(1)} %get-tuple-element.38), channel_id=1, source_target_pairs={{0,3},{1,0},{2,1},{3,2},{4,7},{5,4},{6,5},{7,6},{8,11},{9,8},{10,9... | collective-permute-start | bytes 393224 | tf_op jit(solution)/shard_map/ppermute | solution.py:50
  65.0 6.1 %collective-permute-start.21 = (bf16[16,8192]{1,0:T(8,128)(2,1)S(1)}, bf16[16,8192]{1,0:T(8,128)(2,1)S(1)}, u32[]{:S(2)}, u32[]{:S(2)}) collective-permute-start(bf16[16,8192]{1,0:T(8,128)(2,1)S(1)} %collective-permute-done.1.refs_0_.refs_6_), channel_id=1, source_target_pairs={{0,16},{16,0},{1,17},{17,1},{2,18},{18,2},{3,19},{19,3},{4,20},{20... | collective-permute-start | bytes 786440 | tf_op jit(solution)/shard_map/ppermute | solution.py:305
  68.4 13.6 %collective-permute-start.20 = (bf16[16,8192]{1,0:T(8,128)(2,1)S(1)}, bf16[16,8192]{1,0:T(8,128)(2,1)S(1)}, u32[]{:S(2)}, u32[]{:S(2)}) collective-permute-start(bf16[16,8192]{1,0:T(8,128)(2,1)S(1)} %shard_map.171.refs_5_), channel_id=1, source_target_pairs={{0,16},{16,0},{1,17},{17,1},{2,18},{18,2},{3,19},{19,3},{4,20},{20... | collective-permute-start | bytes 786440 | tf_op jit(solution)/shard_map/ppermute | solution.py:305
  68.5 6.3 %collective-permute-start.22 = (bf16[64,1024]{1,0:T(8,128)(2,1)S(1)}, bf16[64,1024]{1,0:T(8,128)(2,1)S(1)}, u32[]{:S(2)}, u32[]{:S(2)}) collective-permute-start(bf16[64,1024]{1,0:T(8,128)(2,1)S(1)} %shard_map.170.refs_0_.refs_4_), channel_id=1, source_target_pairs={{0,1},{1,2},{2,3},{3,0},{4,5},{5,6},{6,7},{7,4},{8,9},{9,10},{10,1... | collective-permute-start | bytes 393224 | tf_op jit(solution)/shard_map/ppermute | solution.py:50
  68.5 12.1 %collective-permute-start.23 = (bf16[64,1024]{1,0:T(8,128)(2,1)S(1)}, bf16[64,1024]{1,0:T(8,128)(2,1)S(1)}, u32[]{:S(2)}, u32[]{:S(2)}) collective-permute-start(bf16[64,1024]{1,0:T(8,128)(2,1)S(1)} %shard_map.170.refs_0_.refs_4_), channel_id=1, source_target_pairs={{0,2},{1,3},{2,0},{3,1},{4,6},{5,7},{6,4},{7,5},{8,10},{9,11},{10,... | collective-permute-start | bytes 393224 | tf_op jit(solution)/shard_map/ppermute | solution.py:50
  70.1 11.9 %collective-permute-start.24 = (bf16[64,1024]{1,0:T(8,128)(2,1)S(1)}, bf16[64,1024]{1,0:T(8,128)(2,1)S(1)}, u32[]{:S(2)}, u32[]{:S(2)}) collective-permute-start(bf16[64,1024]{1,0:T(8,128)(2,1)S(1)} %shard_map.170.refs_0_.refs_4_), channel_id=1, source_target_pairs={{0,3},{1,0},{2,1},{3,2},{4,7},{5,4},{6,5},{7,6},{8,11},{9,8},{10,9... | collective-permute-start | bytes 393224 | tf_op jit(solution)/shard_map/ppermute | solution.py:50
  71.1 11.8 %collective-permute-start.25 = (bf16[64,1024]{1,0:T(8,128)(2,1)S(1)}, bf16[64,1024]{1,0:T(8,128)(2,1)S(1)}, u32[]{:S(2)}, u32[]{:S(2)}) collective-permute-start(bf16[64,1024]{1,0:T(8,128)(2,1)S(1)} %shard_map.170.refs_0_.refs_4_), channel_id=1, source_target_pairs={{0,16},{16,0},{1,17},{17,1},{2,18},{18,2},{3,19},{19,3},{4,20},{20... | collective-permute-start | bytes 393224 | tf_op jit(solution)/shard_map/ppermute | solution.py:305
  74.8 8.1 %collective-permute-start.26 = (bf16[64,1024]{1,0:T(8,128)(2,1)S(1)}, bf16[64,1024]{1,0:T(8,128)(2,1)S(1)}, u32[]{:S(2)}, u32[]{:S(2)}) collective-permute-start(bf16[64,1024]{1,0:T(8,128)(2,1)S(1)} %collective-permute-done.22.refs_5_), channel_id=1, source_target_pairs={{0,16},{16,0},{1,17},{17,1},{2,18},{18,2},{3,19},{19,3},{4,20},{20... | collective-permute-start | bytes 393224 | tf_op jit(solution)/shard_map/ppermute | solution.py:305
  80.6 2.4 %collective-permute-start.27 = (bf16[64,1024]{1,0:T(8,128)(2,1)S(1)}, bf16[64,1024]{1,0:T(8,128)(2,1)S(1)}, u32[]{:S(2)}, u32[]{:S(2)}) collective-permute-start(bf16[64,1024]{1,0:T(8,128)(2,1)S(1)} %collective-permute-done.23.refs_6_), channel_id=1, source_target_pairs={{0,16},{16,0},{1,17},{17,1},{2,18},{18,2},{3,19},{19,3},{4,20},{20... | collective-permute-start | bytes 393224 | tf_op jit(solution)/shard_map/ppermute | solution.py:305
  81.9 1.3 %collective-permute-start.28 = (bf16[64,1024]{1,0:T(8,128)(2,1)S(1)}, bf16[64,1024]{1,0:T(8,128)(2,1)S(1)}, u32[]{:S(2)}, u32[]{:S(2)}) collective-permute-start(bf16[64,1024]{1,0:T(8,128)(2,1)S(1)} %collective-permute-done.24.refs_7_), channel_id=1, source_target_pairs={{0,16},{16,0},{1,17},{17,1},{2,18},{18,2},{3,19},{19,3},{4,20},{20... | collective-permute-start | bytes 393224 | tf_op jit(solution)/shard_map/ppermute | solution.py:305
  84.2 4.9 %collective-permute-start.29 = (bf16[192,256]{1,0:T(8,128)(2,1)S(1)}, bf16[192,256]{1,0:T(8,128)(2,1)S(1)}, u32[]{:S(2)}, u32[]{:S(2)}) collective-permute-start(bf16[192,256]{1,0:T(8,128)(2,1)S(1)} %shard_map.173.refs_2_), channel_id=1, source_target_pairs={{0,4},{4,8},{8,12},{12,0},{1,5},{5,9},{9,13},{13,1},{2,6},{6,10},{... | collective-permute-start | bytes 294920 | tf_op jit(solution)/shard_map/ppermute | solution.py:50
  85.8 6.7 %collective-permute-start.30 = (bf16[192,256]{1,0:T(8,128)(2,1)S(1)}, bf16[192,256]{1,0:T(8,128)(2,1)S(1)}, u32[]{:S(2)}, u32[]{:S(2)}) collective-permute-start(bf16[192,256]{1,0:T(8,128)(2,1)S(1)} %shard_map.173.refs_2_), channel_id=1, source_target_pairs={{0,8},{4,12},{8,0},{12,4},{1,9},{5,13},{9,1},{13,5},{2,10},{6,14},... | collective-permute-start | bytes 294920 | tf_op jit(solution)/shard_map/ppermute | solution.py:50
  86.3 6.2 %collective-permute-start.31 = (bf16[192,256]{1,0:T(8,128)(2,1)S(1)}, bf16[192,256]{1,0:T(8,128)(2,1)S(1)}, u32[]{:S(2)}, u32[]{:S(2)}) collective-permute-start(bf16[192,256]{1,0:T(8,128)(2,1)S(1)} %shard_map.173.refs_2_), channel_id=1, source_target_pairs={{0,12},{4,0},{8,4},{12,8},{1,13},{5,1},{9,5},{13,9},{2,14},{6,2},{... | collective-permute-start | bytes 294920 | tf_op jit(solution)/shard_map/ppermute | solution.py:50
  (6 other events, 137.4 us)

commit v3 on v2

--- a/solution.py
+++ b/solution.py
@@ -216,31 +216,39 @@
     out_ref[prompt:, :] = (acc * scale + b_ref[...][None, :]).astype(BF16)
 
 
-def relay_kernel(in_ref, out_ref):
-    out_ref[...] = in_ref[...]
-
-
-def text_keyval_kernel(n_z, gain_ref, w_ref, b_ref, *refs):
-    c, z = lax.axis_index("section"), lax.axis_index("mp")
+def relay_kernel(n_z, linear, *refs):
+    z = lax.axis_index("mp")
     pieces, out_ref = refs[:-1], refs[-1]
-    block, model = pieces[0].shape
+    if not linear:
+        for k, piece in enumerate(pieces):
+            out_ref[lax.rem(z - k + n_z, n_z)] = piece[...]
+        return
+    own, near, mid_first, mid_second, far_first, far_second = pieces
+    low = z < 2
+    out_ref[z] = own[...]
+    out_ref[z + 1 - 2 * lax.rem(z, 2)] = near[...]
+    inner = (z == 1) | (z == 2)
+    out_ref[jnp.where(low, 2, 1)] = jnp.where(inner, mid_first[...], far_first[...])
+    out_ref[jnp.where(low, 3, 0)] = jnp.where(inner, mid_second[...], far_second[...])
+
+
+def text_keyval_kernel(gain_ref, w_ref, b_ref, here_ref, there_ref, out_ref):
+    c = lax.axis_index("section")
+    blocks, rows, model = here_ref.shape
+    half = blocks * rows
     acc = jnp.zeros(out_ref.shape, F32)
     squares = jnp.zeros((out_ref.shape[0], 1), F32)
     step = 1024
     for first in range(0, model, step):
-        x = jnp.concatenate([p[:, first:first + step] for p in pieces], axis=0).astype(F32)
+        at = slice(first, first + step)
+        x = jnp.concatenate([r[i, :, at] for r in (here_ref, there_ref) for i in range(blocks)], axis=0).astype(F32)
         squares += jnp.sum(x * x, axis=-1, keepdims=True)
-        y = (x * gain_ref[first:first + step][None, :]).astype(BF16)
-        acc += jnp.dot(y, w_ref[first:first + step, :], preferred_element_type=F32)
+        y = (x * gain_ref[at][None, :]).astype(BF16)
+        acc += jnp.dot(y, w_ref[at, :], preferred_element_type=F32)
     scale = lax.rsqrt(squares * (1.0 / model) + NORM_EPS)
-    acc = acc * scale + b_ref[...][None, :]
-    for side in range(2):
-        section = c if side == 0 else 1 - c
-        for k in range(n_z):
-            d = section * n_z + lax.rem(z - k + n_z, n_z)
-            at = pl.ds(pl.multiple_of(d * block, block), block)
-            i = side * n_z + k
-            out_ref[at, :] = acc[i * block:(i + 1) * block].astype(BF16)
+    acc = (acc * scale + b_ref[...][None, :]).astype(BF16)
+    out_ref[pl.ds(pl.multiple_of(c * half, half), half), :] = acc[:half]
+    out_ref[pl.ds(pl.multiple_of((1 - c) * half, half), half), :] = acc[half:]
 
 
 def place_kernel(n_s, slot_map, place_ref, *refs):
@@ -309,7 +317,21 @@
         return here + [swap(v) for v in here]
 
     text_own = text[0]
-    text_at = {k: shifted(text_own, "mp", n_z, k) for k in range(1, n_z)}
+    linear = n_z == 4
+    if linear:
+        def near(v):
+            return lax.ppermute(v, "mp", [(0, 1), (1, 0), (2, 3), (3, 2)])
+
+        def middle(v):
+            return lax.ppermute(v, "mp", [(0, 0), (1, 2), (2, 1), (3, 3)])
+
+        first = [near(text_own), middle(text_own)]
+        second = [middle(first[0])]
+        third = [near(first[1]), near(second[0])]
+        text_pieces = [text_own, *first, *second, *third]
+    else:
+        text_pieces = [text_own] + [shifted(text_own, "mp", n_z, k) for k in range(1, n_z)]
+        first, second = text_pieces[1:2], text_pieces[2:3]
 
     w = qkv_weight.transpose(1, 2, 0).reshape(3 * head_width, width)
     later = [merge_gain, merge_up.T, merge_up_bias, merge_down_bias, input_gain, kv_bias]
@@ -336,7 +358,7 @@
     )
     sums = [parts[0]] + [shifted(parts[k], "mp", n_z, k) for k in range(1, n_z)]
     merged, = call(
-        resid_kernel, [struct((block, width), BF16)], [base, gain] + sums, after=[text_at[1]])
+        resid_kernel, [struct((block, width), BF16)], [base, gain] + sums, after=first)
     pieces = spread(merged)
 
     hidden, = call(
@@ -351,6 +373,7 @@
             functools.partial(down_kernel, other),
             [struct((units, model // 2), BF16)],
             [hidden, merge_down],
+            after=second if other else (),
             flops=units * merge_down.size,
             grant=16,
         )[0]
@@ -361,21 +384,19 @@
         functools.partial(pair_columns_kernel, n_z, columns),
         [struct((units, columns), F32)] + [struct((units, columns), BF16)] * (n_z - 1),
         [keep, got],
-        after=[text_at[n_z - 1]],
     )
     sums = [parts[0]] + [shifted(parts[k], "mp", n_z, k) for k in range(1, n_z)]
     image, = call(
         functools.partial(image_kernel, n_z), [struct((units, columns), BF16)], [down_bias] + sums)
     image_pieces = spread(image)
 
-    for k in range(2, n_z - 1):
-        text_at[k] = call(relay_kernel, [struct(text_own.shape, BF16)], [text_at[k]], after=[image])[0]
-    text_here = [text_own] + [text_at[k] for k in range(1, n_z)]
+    line, = call(
+        functools.partial(relay_kernel, n_z, linear), [struct((n_z,) + text_own.shape, BF16)], text_pieces, after=[image])
     prompt = n_d * text.shape[1]
     text_keyval, = call(
-        functools.partial(text_keyval_kernel, n_z),
+        text_keyval_kernel,
         [struct((prompt, kv_width), BF16)],
-        [text_gain, kv_weight, bias] + text_here + [swap(v) for v in text_here],
+        [text_gain, kv_weight, bias, line, swap(line)],
         flops=2 * prompt * model * kv_width,
         grant=16,
     )

time: 94.4 us -> 89.3 us (0.946)
  waiting for transfers between devices: 59.5 us -> 45.6 us
  starting transfers between devices: 24.3 us -> 33 us
    ppermute x18 -> x15, waiting for transfers between devices: 57.9 us -> 39.1 us  [shifted(): return lax.ppermute(x, axis, [(i, (i + k) % count) for i in range(count)])]
    ppermute x0 -> x5, starting transfers between devices: none -> 10.6 us  [the longest x2 8.08 us: middle(): return lax.ppermute(v, 'mp', [(0, 0), (1, 2), (2, 1), (3, 3)])]
    ppermute x0 -> x5, waiting for transfers between devices: none -> 4.92 us  [the longest x2 3.06 us: middle(): return lax.ppermute(v, 'mp', [(0, 0), (1, 2), (2, 1), (3, 3)])]
    ppermute x18 -> x15, starting transfers between devices: 23.3 us -> 21.9 us  [shifted(): return lax.ppermute(x, axis, [(i, (i + k) % count) for i in range(count)])]
  transfers between devices with their start and end apart: 32 -> 31, of which waited for: 18 -> 18; matrix products, arithmetic and copies ran while one was open for 0% -> 0% of each run, Pallas kernels for 2% -> 3%
where the time goes in v3:
time: 89.3 us; the launch traced here: 89.1 us
  waiting for transfers between devices  45.6 us (51%)
  starting transfers between devices  33 us (37%)
  Pallas kernels  10.3 us (12%)
    ppermute x15, waiting for transfers between devices, shifted(): return lax.ppermute(x, axis, [(i, (i + k) % count) for i in range(count)])  39.1 us
    ppermute x15, starting transfers between devices, shifted(): return lax.ppermute(x, axis, [(i, (i + k) % count) for i in range(count)])  21.9 us
    pallas_call x12, Pallas kernels, call(): pl.pallas_call(body, out_shape=outs, in_specs=[unread] * count + [scalar]...  10.3 us
    ppermute x2, starting transfers between devices, middle(): return lax.ppermute(v, 'mp', [(0, 0), (1, 2), (2, 1), (3, 3)])  8.08 us
    ppermute x2, waiting for transfers between devices, middle(): return lax.ppermute(v, 'mp', [(0, 0), (1, 2), (2, 1), (3, 3)])  3.06 us
    ppermute x3, starting transfers between devices, near(): return lax.ppermute(v, 'mp', [(0, 1), (1, 0), (2, 3), (3, 2)])  2.55 us
    ppermute x3, waiting for transfers between devices, near(): return lax.ppermute(v, 'mp', [(0, 1), (1, 0), (2, 3), (3, 2)])  1.86 us
  transfers between devices with their start and end apart: 31, of which 18 were waited for; matrix products, arithmetic and copies ran while one was open for 0% of the time, Pallas kernels for 3%

profile of v3, /device:TPU:10, one launch (start us, length us, event | category | flops | bytes accessed | tf_op | source)
XLA Modules:
  0.0 89.1 jit_solution(3812843710559865350)
XLA Ops:
  0.0 3.8 %shard_map.163 = (bf16[128,1280]{1,0:T(8,128)(2,1)S(1)}, bf16[128,1280]{1,0:T(8,128)(2,1)S(1)}, f32[32,1280]{1,0:T(8,128)S(1)}, f32[1280]{0:T(1024)S(1)}, bf16[3...) custom-call(s32[4,4,16]{2,1,0:T(4,128)} %refs_1_.5, ...), custom_call_target="tpu_custom_call" | custom-call | flops 419430400 | bytes 9825664 | tf_op jit(solution)/shard_map/pallas_call | solution.py:34
  4.4 4.6 %collective-permute-start.1 = (bf16[16,8192]{1,0:T(8,128)(2,1)S(1)}, bf16[16,8192]{1,0:T(8,128)(2,1)S(1)}, u32[]{:S(2)}, u32[]{:S(2)}) collective-permute-start(bf16[16,8192]{1,0:T(8,128)(2,1)S(1)} %bitcast.8), channel_id=1, source_target_pairs={{0,0},{1,2},{2,1},{3,3},{4,4},{5,6},{6,5},{7,7},{8,8},{9,10},{10,9... | collective-permute-start | bytes 786440 | tf_op jit(solution)/shard_map/ppermute | solution.py:326
  9.3 1.9 %collective-permute-start.5 = (bf16[32,1280]{1,0:T(8,128)(2,1)S(1)}, bf16[32,1280]{1,0:T(8,128)(2,1)S(1)}, u32[]{:S(2)}, u32[]{:S(2)}) collective-permute-start(bf16[32,1280]{1,0:T(8,128)(2,1)S(1)} %get-tuple-element.34), channel_id=1, source_target_pairs={{0,3},{1,0},{2,1},{3,2},{4,7},{5,4},{6,5},{7,6},{8,11},{9,8},{10,9... | collective-permute-start | bytes 245768 | tf_op jit(solution)/shard_map/ppermute | solution.py:50
  11.2 1.9 %collective-permute-done.refs_0_.refs_2_ = bf16[16,8192]{1,0:T(8,128)(2,1)S(1)} collective-permute-done((bf16[16,8192]{1,0:T(8,128)(2,1)S(1)}, bf16[16,8192]{1,0:T(8,128)(2,1)S(1)}, u32[]{:S(2)}, u32[]{:S(2)}) %collective-permute-start) | collective-permute-done | bytes 262176 | tf_op jit(solution)/shard_map/ppermute | solution.py:323
  13.1 3.5 %collective-permute-start.13 = (bf16[16,8192]{1,0:T(8,128)(2,1)S(1)}, bf16[16,8192]{1,0:T(8,128)(2,1)S(1)}, u32[]{:S(2)}, u32[]{:S(2)}) collective-permute-start(bf16[16,8192]{1,0:T(8,128)(2,1)S(1)} %collective-permute-done.refs_0_.refs_2_), channel_id=1, source_target_pairs={{0,0},{1,2},{2,1},{3,3},{4,4},{5,6},{6,5},{7,7},{8,8},{9,10},{10,9... | collective-permute-start | bytes 786440 | tf_op jit(solution)/shard_map/ppermute | solution.py:326
  16.5 3.1 %collective-permute-done.1.refs_1_.refs_3_ = bf16[16,8192]{1,0:T(8,128)(2,1)S(1)} collective-permute-done((bf16[16,8192]{1,0:T(8,128)(2,1)S(1)}, bf16[16,8192]{1,0:T(8,128)(2,1)S(1)}, u32[]{:S(2)}, u32[]{:S(2)}) %collective-permute-start.1) | collective-permute-done | bytes 262176 | tf_op jit(solution)/shard_map/ppermute | solution.py:326
  19.6 1.3 %collective-permute-done.3.refs_5_ = bf16[32,1280]{1,0:T(8,128)(2,1)S(1)} collective-permute-done((bf16[32,1280]{1,0:T(8,128)(2,1)S(1)}, bf16[32,1280]{1,0:T(8,128)(2,1)S(1)}, u32[]{:S(2)}, u32[]{:S(2)}) %collective-permute-start.3) | collective-permute-done | bytes 81952 | tf_op jit(solution)/shard_map/ppermute | solution.py:50
  20.9 1.8 %collective-permute-done.4.refs_6_ = bf16[32,1280]{1,0:T(8,128)(2,1)S(1)} collective-permute-done((bf16[32,1280]{1,0:T(8,128)(2,1)S(1)}, bf16[32,1280]{1,0:T(8,128)(2,1)S(1)}, u32[]{:S(2)}, u32[]{:S(2)}) %collective-permute-start.4) | collective-permute-done | bytes 81952 | tf_op jit(solution)/shard_map/ppermute | solution.py:50
  23.6 2.7 %collective-permute-start.7 = (bf16[32,1280]{1,0:T(8,128)(2,1)S(1)}, bf16[32,1280]{1,0:T(8,128)(2,1)S(1)}, u32[]{:S(2)}, u32[]{:S(2)}) collective-permute-start(bf16[32,1280]{1,0:T(8,128)(2,1)S(1)} %shard_map.165.refs_2_), channel_id=1, source_target_pairs={{0,2},{1,3},{2,0},{3,1},{4,6},{5,7},{6,4},{7,5},{8,10},{9,11},{10,... | collective-permute-start | bytes 245768 | tf_op jit(solution)/shard_map/ppermute | solution.py:50
  26.3 1.9 %collective-permute-start.8 = (bf16[32,1280]{1,0:T(8,128)(2,1)S(1)}, bf16[32,1280]{1,0:T(8,128)(2,1)S(1)}, u32[]{:S(2)}, u32[]{:S(2)}) collective-permute-start(bf16[32,1280]{1,0:T(8,128)(2,1)S(1)} %shard_map.165.refs_2_), channel_id=1, source_target_pairs={{0,3},{1,0},{2,1},{3,2},{4,7},{5,4},{6,5},{7,6},{8,11},{9,8},{10,9... | collective-permute-start | bytes 245768 | tf_op jit(solution)/shard_map/ppermute | solution.py:50
  28.3 5.3 %collective-permute-done.6.refs_3_ = bf16[32,1280]{1,0:T(8,128)(2,1)S(1)} collective-permute-done((bf16[32,1280]{1,0:T(8,128)(2,1)S(1)}, bf16[32,1280]{1,0:T(8,128)(2,1)S(1)}, u32[]{:S(2)}, u32[]{:S(2)}) %collective-permute-start.6) | collective-permute-done | bytes 81952 | tf_op jit(solution)/shard_map/ppermute | solution.py:50
  33.6 1.0 %collective-permute-done.7.refs_4_ = bf16[32,1280]{1,0:T(8,128)(2,1)S(1)} collective-permute-done((bf16[32,1280]{1,0:T(8,128)(2,1)S(1)}, bf16[32,1280]{1,0:T(8,128)(2,1)S(1)}, u32[]{:S(2)}, u32[]{:S(2)}) %collective-permute-start.7) | collective-permute-done | bytes 81952 | tf_op jit(solution)/shard_map/ppermute | solution.py:50
  36.6 1.1 %shard_map.166.refs_0_.refs_1_ = bf16[64,320]{1,0:T(8,128)(2,1)S(1)} custom-call(bf16[320,5120]{1,0:T(8,128)(2,1)S(1)} %get-tuple-element.25.refs_0_, f32[320]{0:T(512)S(1)} %get-tuple-element.26.refs_1_, bf16[32,1280]{1,0:T(8,128)(2,1)S(1)} %shard_map.165.refs_2_, bf16[32,1280]{1,0:T(8,128)(2,1)S(1)} %collective-permute-done.6.refs_3_, ...), custom_call_target="tpu_custom_call" | custom-call | flops 209715200 | bytes 3974400 | tf_op jit(solution)/shard_map/pallas_call | solution.py:34
  39.1 1.6 %collective-permute-start.19 = (bf16[16,8192]{1,0:T(8,128)(2,1)S(1)}, bf16[16,8192]{1,0:T(8,128)(2,1)S(1)}, u32[]{:S(2)}, u32[]{:S(2)}) collective-permute-start(bf16[16,8192]{1,0:T(8,128)(2,1)S(1)} %collective-permute-done.13.refs_0_.refs_4_), channel_id=1, source_target_pairs={{0,1},{1,0},{2,3},{3,2},{4,5},{5,4},{6,7},{7,6},{8,9},{9,8},{10,11... | collective-permute-start | bytes 786440 | tf_op jit(solution)/shard_map/ppermute | solution.py:323
  41.4 1.6 %collective-permute-start.15 = (bf16[64,1024]{1,0:T(8,128)(2,1)S(1)}, bf16[64,1024]{1,0:T(8,128)(2,1)S(1)}, u32[]{:S(2)}, u32[]{:S(2)}) collective-permute-start(bf16[64,1024]{1,0:T(8,128)(2,1)S(1)} %get-tuple-element.36), channel_id=1, source_target_pairs={{0,1},{1,2},{2,3},{3,0},{4,5},{5,6},{6,7},{7,4},{8,9},{9,10},{10,1... | collective-permute-start | bytes 393224 | tf_op jit(solution)/shard_map/ppermute | solution.py:50
  43.0 1.5 %collective-permute-start.16 = (bf16[64,1024]{1,0:T(8,128)(2,1)S(1)}, bf16[64,1024]{1,0:T(8,128)(2,1)S(1)}, u32[]{:S(2)}, u32[]{:S(2)}) collective-permute-start(bf16[64,1024]{1,0:T(8,128)(2,1)S(1)} %get-tuple-element.37), channel_id=1, source_target_pairs={{0,2},{1,3},{2,0},{3,1},{4,6},{5,7},{6,4},{7,5},{8,10},{9,11},{10,... | collective-permute-start | bytes 393224 | tf_op jit(solution)/shard_map/ppermute | solution.py:50
  44.5 1.9 %collective-permute-start.17 = (bf16[64,1024]{1,0:T(8,128)(2,1)S(1)}, bf16[64,1024]{1,0:T(8,128)(2,1)S(1)}, u32[]{:S(2)}, u32[]{:S(2)}) collective-permute-start(bf16[64,1024]{1,0:T(8,128)(2,1)S(1)} %get-tuple-element.38), channel_id=1, source_target_pairs={{0,3},{1,0},{2,1},{3,2},{4,7},{5,4},{6,5},{7,6},{8,11},{9,8},{10,9... | collective-permute-start | bytes 393224 | tf_op jit(solution)/shard_map/ppermute | solution.py:50
  46.4 9.7 %collective-permute-done.15.refs_2_ = bf16[64,1024]{1,0:T(8,128)(2,1)S(1)} collective-permute-done((bf16[64,1024]{1,0:T(8,128)(2,1)S(1)}, bf16[64,1024]{1,0:T(8,128)(2,1)S(1)}, u32[]{:S(2)}, u32[]{:S(2)}) %collective-permute-start.15) | collective-permute-done | bytes 131104 | tf_op jit(solution)/shard_map/ppermute | solution.py:50
  56.2 3.7 %collective-permute-done.16.refs_3_ = bf16[64,1024]{1,0:T(8,128)(2,1)S(1)} collective-permute-done((bf16[64,1024]{1,0:T(8,128)(2,1)S(1)}, bf16[64,1024]{1,0:T(8,128)(2,1)S(1)}, u32[]{:S(2)}, u32[]{:S(2)}) %collective-permute-start.16) | collective-permute-done | bytes 131104 | tf_op jit(solution)/shard_map/ppermute | solution.py:50
  60.2 3.0 %collective-permute-start.21 = (bf16[64,1024]{1,0:T(8,128)(2,1)S(1)}, bf16[64,1024]{1,0:T(8,128)(2,1)S(1)}, u32[]{:S(2)}, u32[]{:S(2)}) collective-permute-start(bf16[64,1024]{1,0:T(8,128)(2,1)S(1)} %shard_map.170.refs_0_.refs_4_), channel_id=1, source_target_pairs={{0,1},{1,2},{2,3},{3,0},{4,5},{5,6},{6,7},{7,4},{8,9},{9,10},{10,1... | collective-permute-start | bytes 393224 | tf_op jit(solution)/shard_map/ppermute | solution.py:50
  63.2 1.3 %collective-permute-start.22 = (bf16[64,1024]{1,0:T(8,128)(2,1)S(1)}, bf16[64,1024]{1,0:T(8,128)(2,1)S(1)}, u32[]{:S(2)}, u32[]{:S(2)}) collective-permute-start(bf16[64,1024]{1,0:T(8,128)(2,1)S(1)} %shard_map.170.refs_0_.refs_4_), channel_id=1, source_target_pairs={{0,2},{1,3},{2,0},{3,1},{4,6},{5,7},{6,4},{7,5},{8,10},{9,11},{10,... | collective-permute-start | bytes 393224 | tf_op jit(solution)/shard_map/ppermute | solution.py:50
  64.4 1.9 %collective-permute-start.23 = (bf16[64,1024]{1,0:T(8,128)(2,1)S(1)}, bf16[64,1024]{1,0:T(8,128)(2,1)S(1)}, u32[]{:S(2)}, u32[]{:S(2)}) collective-permute-start(bf16[64,1024]{1,0:T(8,128)(2,1)S(1)} %shard_map.170.refs_0_.refs_4_), channel_id=1, source_target_pairs={{0,3},{1,0},{2,1},{3,2},{4,7},{5,4},{6,5},{7,6},{8,11},{9,8},{10,9... | collective-permute-start | bytes 393224 | tf_op jit(solution)/shard_map/ppermute | solution.py:50
  66.4 6.1 %collective-permute-done.21.refs_5_ = bf16[64,1024]{1,0:T(8,128)(2,1)S(1)} collective-permute-done((bf16[64,1024]{1,0:T(8,128)(2,1)S(1)}, bf16[64,1024]{1,0:T(8,128)(2,1)S(1)}, u32[]{:S(2)}, u32[]{:S(2)}) %collective-permute-start.21) | collective-permute-done | bytes 131104 | tf_op jit(solution)/shard_map/ppermute | solution.py:50
  72.4 2.5 %collective-permute-done.22.refs_6_ = bf16[64,1024]{1,0:T(8,128)(2,1)S(1)} collective-permute-done((bf16[64,1024]{1,0:T(8,128)(2,1)S(1)}, bf16[64,1024]{1,0:T(8,128)(2,1)S(1)}, u32[]{:S(2)}, u32[]{:S(2)}) %collective-permute-start.22) | collective-permute-done | bytes 131104 | tf_op jit(solution)/shard_map/ppermute | solution.py:50
  74.9 1.9 %collective-permute-done.23.refs_7_ = bf16[64,1024]{1,0:T(8,128)(2,1)S(1)} collective-permute-done((bf16[64,1024]{1,0:T(8,128)(2,1)S(1)}, bf16[64,1024]{1,0:T(8,128)(2,1)S(1)}, u32[]{:S(2)}, u32[]{:S(2)}) %collective-permute-start.23) | collective-permute-done | bytes 131104 | tf_op jit(solution)/shard_map/ppermute | solution.py:50
  76.9 0.9 %shard_map.172.refs_0_ = bf16[128,256]{1,0:T(8,128)(2,1)S(1)} custom-call(f32[8192]{0:T(1024)S(1)} %get-tuple-element.22.refs_0_.refs_1_, bf16[8192,256]{1,0:T(8,128)(2,1)S(1)} %copy-done.1, f32[256]{0:T(256)S(1)} %get-tuple-element.23.refs_2_.refs_3_, bf16[4,16,8192]{2,1,0:T(8,128)(2,1)S(1)} %shard_map.171.refs_3_, ...), custom_call_target="tpu_custom_call" | custom-call | flops 536870912 | bytes 6390784 | tf_op jit(solution)/shard_map/pallas_call | solution.py:34
  78.2 0.9 %shard_map.173.refs_2_ = bf16[192,256]{1,0:T(8,128)(2,1)S(1)} custom-call(bf16[128,256]{1,0:T(8,128)(2,1)S(1)} %shard_map.172.refs_0_, f32[8192]{0:T(1024)S(1)} %get-tuple-element.22.refs_0_.refs_1_, bf16[8192,256]{1,0:T(8,128)(2,1)S(1)} %copy-done.1, f32[256]{0:T(256)S(1)} %get-tuple-element.23.refs_2_.refs_3_, ...), custom_call_target="tpu_custom_call" | custom-call | flops 268435456 | bytes 5440512 | tf_op jit(solution)/shard_map/pallas_call | solution.py:34
  79.2 1.5 %collective-permute-start.28 = (bf16[192,256]{1,0:T(8,128)(2,1)S(1)}, bf16[192,256]{1,0:T(8,128)(2,1)S(1)}, u32[]{:S(2)}, u32[]{:S(2)}) collective-permute-start(bf16[192,256]{1,0:T(8,128)(2,1)S(1)} %shard_map.173.refs_2_), channel_id=1, source_target_pairs={{0,4},{4,8},{8,12},{12,0},{1,5},{5,9},{9,13},{13,1},{2,6},{6,10},{... | collective-permute-start | bytes 294920 | tf_op jit(solution)/shard_map/ppermute | solution.py:50
  81.2 1.5 %collective-permute-start.30 = (bf16[192,256]{1,0:T(8,128)(2,1)S(1)}, bf16[192,256]{1,0:T(8,128)(2,1)S(1)}, u32[]{:S(2)}, u32[]{:S(2)}) collective-permute-start(bf16[192,256]{1,0:T(8,128)(2,1)S(1)} %shard_map.173.refs_2_), channel_id=1, source_target_pairs={{0,12},{4,0},{8,4},{12,8},{1,13},{5,1},{9,5},{13,9},{2,14},{6,2},{... | collective-permute-start | bytes 294920 | tf_op jit(solution)/shard_map/ppermute | solution.py:50
  82.7 1.4 %collective-permute-done.28.refs_3_ = bf16[192,256]{1,0:T(8,128)(2,1)S(1)} collective-permute-done((bf16[192,256]{1,0:T(8,128)(2,1)S(1)}, bf16[192,256]{1,0:T(8,128)(2,1)S(1)}, u32[]{:S(2)}, u32[]{:S(2)}) %collective-permute-start.28) | collective-permute-done | bytes 98336 | tf_op jit(solution)/shard_map/ppermute | solution.py:50
  84.1 3.3 %collective-permute-done.29.refs_4_ = bf16[192,256]{1,0:T(8,128)(2,1)S(1)} collective-permute-done((bf16[192,256]{1,0:T(8,128)(2,1)S(1)}, bf16[192,256]{1,0:T(8,128)(2,1)S(1)}, u32[]{:S(2)}, u32[]{:S(2)}) %collective-permute-start.29) | collective-permute-done | bytes 98336 | tf_op jit(solution)/shard_map/ppermute | solution.py:50
  87.4 1.7 %shard_map.174 = bf16[4,32,256]{2,1,0:T(8,128)(2,1)} custom-call(s32[4,4]{1,0:T(4,128)S(1)} %copy-done.4, s32[4,4,16]{2,1,0:T(4,128)S(1)} %copy-done.3, bf16[192,256]{1,0:T(8,128)(2,1)S(1)} %shard_map.173.refs_2_, bf16[192,256]{1,0:T(8,128)(2,1)S(1)} %collective-permute-done.28.refs_3_, bf16[192,256]{1,0:T(8,128)(2,1)S(1)} %collective-permute-done.29.refs_4_, ...), custom_call_target="tpu_custom_call" | custom-call | bytes 459840 | tf_op jit(solution)/shard_map/pallas_call | solution.py:34
  (52 shorter events, 7.1 us)
Async XLA Ops:
  3.8 5.2 %collective-permute-start.2 = (bf16[128,1280]{1,0:T(8,128)(2,1)S(1)}, bf16[128,1280]{1,0:T(8,128)(2,1)S(1)}, u32[]{:S(2)}, u32[]{:S(2)}) collective-permute-start(bf16[128,1280]{1,0:T(8,128)(2,1)S(1)} %get-tuple-element.30), channel_id=1, source_target_pairs={{0,16},{16,0},{1,17},{17,1},{2,18},{18,2},{3,19},{19,3},{4,20},{20... | collective-permute-start | bytes 983048 | tf_op jit(solution)/shard_map/ppermute | solution.py:313
  3.9 9.2 %collective-permute-start = (bf16[16,8192]{1,0:T(8,128)(2,1)S(1)}, bf16[16,8192]{1,0:T(8,128)(2,1)S(1)}, u32[]{:S(2)}, u32[]{:S(2)}) collective-permute-start(bf16[16,8192]{1,0:T(8,128)(2,1)S(1)} %bitcast.7), channel_id=1, source_target_pairs={{0,1},{1,0},{2,3},{3,2},{4,5},{5,4},{6,7},{7,6},{8,9},{9,8},{10,11... | collective-permute-start | bytes 786440 | tf_op jit(solution)/shard_map/ppermute | solution.py:323
  4.4 15.2 %collective-permute-start.1 = (bf16[16,8192]{1,0:T(8,128)(2,1)S(1)}, bf16[16,8192]{1,0:T(8,128)(2,1)S(1)}, u32[]{:S(2)}, u32[]{:S(2)}) collective-permute-start(bf16[16,8192]{1,0:T(8,128)(2,1)S(1)} %bitcast.8), channel_id=1, source_target_pairs={{0,0},{1,2},{2,1},{3,3},{4,4},{5,6},{6,5},{7,7},{8,8},{9,10},{10,9... | collective-permute-start | bytes 786440 | tf_op jit(solution)/shard_map/ppermute | solution.py:326
  9.1 11.8 %collective-permute-start.3 = (bf16[32,1280]{1,0:T(8,128)(2,1)S(1)}, bf16[32,1280]{1,0:T(8,128)(2,1)S(1)}, u32[]{:S(2)}, u32[]{:S(2)}) collective-permute-start(bf16[32,1280]{1,0:T(8,128)(2,1)S(1)} %get-tuple-element.32), channel_id=1, source_target_pairs={{0,1},{1,2},{2,3},{3,0},{4,5},{5,6},{6,7},{7,4},{8,9},{9,10},{10,1... | collective-permute-start | bytes 245768 | tf_op jit(solution)/shard_map/ppermute | solution.py:50
  9.2 13.5 %collective-permute-start.4 = (bf16[32,1280]{1,0:T(8,128)(2,1)S(1)}, bf16[32,1280]{1,0:T(8,128)(2,1)S(1)}, u32[]{:S(2)}, u32[]{:S(2)}) collective-permute-start(bf16[32,1280]{1,0:T(8,128)(2,1)S(1)} %get-tuple-element.33), channel_id=1, source_target_pairs={{0,2},{1,3},{2,0},{3,1},{4,6},{5,7},{6,4},{7,5},{8,10},{9,11},{10,... | collective-permute-start | bytes 245768 | tf_op jit(solution)/shard_map/ppermute | solution.py:50
  9.3 13.8 %collective-permute-start.5 = (bf16[32,1280]{1,0:T(8,128)(2,1)S(1)}, bf16[32,1280]{1,0:T(8,128)(2,1)S(1)}, u32[]{:S(2)}, u32[]{:S(2)}) collective-permute-start(bf16[32,1280]{1,0:T(8,128)(2,1)S(1)} %get-tuple-element.34), channel_id=1, source_target_pairs={{0,3},{1,0},{2,1},{3,2},{4,7},{5,4},{6,5},{7,6},{8,11},{9,8},{10,9... | collective-permute-start | bytes 245768 | tf_op jit(solution)/shard_map/ppermute | solution.py:50
  13.1 24.6 %collective-permute-start.13 = (bf16[16,8192]{1,0:T(8,128)(2,1)S(1)}, bf16[16,8192]{1,0:T(8,128)(2,1)S(1)}, u32[]{:S(2)}, u32[]{:S(2)}) collective-permute-start(bf16[16,8192]{1,0:T(8,128)(2,1)S(1)} %collective-permute-done.refs_0_.refs_2_), channel_id=1, source_target_pairs={{0,0},{1,2},{2,1},{3,3},{4,4},{5,6},{6,5},{7,7},{8,8},{9,10},{10,9... | collective-permute-start | bytes 786440 | tf_op jit(solution)/shard_map/ppermute | solution.py:326
  23.3 10.3 %collective-permute-start.6 = (bf16[32,1280]{1,0:T(8,128)(2,1)S(1)}, bf16[32,1280]{1,0:T(8,128)(2,1)S(1)}, u32[]{:S(2)}, u32[]{:S(2)}) collective-permute-start(bf16[32,1280]{1,0:T(8,128)(2,1)S(1)} %shard_map.165.refs_2_), channel_id=1, source_target_pairs={{0,1},{1,2},{2,3},{3,0},{4,5},{5,6},{6,7},{7,4},{8,9},{9,10},{10,1... | collective-permute-start | bytes 245768 | tf_op jit(solution)/shard_map/ppermute | solution.py:50
  23.6 10.9 %collective-permute-start.7 = (bf16[32,1280]{1,0:T(8,128)(2,1)S(1)}, bf16[32,1280]{1,0:T(8,128)(2,1)S(1)}, u32[]{:S(2)}, u32[]{:S(2)}) collective-permute-start(bf16[32,1280]{1,0:T(8,128)(2,1)S(1)} %shard_map.165.refs_2_), channel_id=1, source_target_pairs={{0,2},{1,3},{2,0},{3,1},{4,6},{5,7},{6,4},{7,5},{8,10},{9,11},{10,... | collective-permute-start | bytes 245768 | tf_op jit(solution)/shard_map/ppermute | solution.py:50
  26.3 8.9 %collective-permute-start.8 = (bf16[32,1280]{1,0:T(8,128)(2,1)S(1)}, bf16[32,1280]{1,0:T(8,128)(2,1)S(1)}, u32[]{:S(2)}, u32[]{:S(2)}) collective-permute-start(bf16[32,1280]{1,0:T(8,128)(2,1)S(1)} %shard_map.165.refs_2_), channel_id=1, source_target_pairs={{0,3},{1,0},{2,1},{3,2},{4,7},{5,4},{6,5},{7,6},{8,11},{9,8},{10,9... | collective-permute-start | bytes 245768 | tf_op jit(solution)/shard_map/ppermute | solution.py:50
  28.3 7.0 %collective-permute-start.9 = (bf16[32,1280]{1,0:T(8,128)(2,1)S(1)}, bf16[32,1280]{1,0:T(8,128)(2,1)S(1)}, u32[]{:S(2)}, u32[]{:S(2)}) collective-permute-start(bf16[32,1280]{1,0:T(8,128)(2,1)S(1)} %shard_map.165.refs_2_), channel_id=1, source_target_pairs={{0,16},{16,0},{1,17},{17,1},{2,18},{18,2},{3,19},{19,3},{4,20},{20... | collective-permute-start | bytes 245768 | tf_op jit(solution)/shard_map/ppermute | solution.py:313
  33.6 1.7 %collective-permute-start.10 = (bf16[32,1280]{1,0:T(8,128)(2,1)S(1)}, bf16[32,1280]{1,0:T(8,128)(2,1)S(1)}, u32[]{:S(2)}, u32[]{:S(2)}) collective-permute-start(bf16[32,1280]{1,0:T(8,128)(2,1)S(1)} %collective-permute-done.6.refs_3_), channel_id=1, source_target_pairs={{0,16},{16,0},{1,17},{17,1},{2,18},{18,2},{3,19},{19,3},{4,20},{20... | collective-permute-start | bytes 245768 | tf_op jit(solution)/shard_map/ppermute | solution.py:313
  34.5 1.3 %collective-permute-start.11 = (bf16[32,1280]{1,0:T(8,128)(2,1)S(1)}, bf16[32,1280]{1,0:T(8,128)(2,1)S(1)}, u32[]{:S(2)}, u32[]{:S(2)}) collective-permute-start(bf16[32,1280]{1,0:T(8,128)(2,1)S(1)} %collective-permute-done.7.refs_4_), channel_id=1, source_target_pairs={{0,16},{16,0},{1,17},{17,1},{2,18},{18,2},{3,19},{19,3},{4,20},{20... | collective-permute-start | bytes 245768 | tf_op jit(solution)/shard_map/ppermute | solution.py:313
  35.3 1.3 %collective-permute-start.12 = (bf16[32,1280]{1,0:T(8,128)(2,1)S(1)}, bf16[32,1280]{1,0:T(8,128)(2,1)S(1)}, u32[]{:S(2)}, u32[]{:S(2)}) collective-permute-start(bf16[32,1280]{1,0:T(8,128)(2,1)S(1)} %collective-permute-done.8.refs_5_), channel_id=1, source_target_pairs={{0,16},{16,0},{1,17},{17,1},{2,18},{18,2},{3,19},{19,3},{4,20},{20... | collective-permute-start | bytes 245768 | tf_op jit(solution)/shard_map/ppermute | solution.py:313
  38.4 2.9 %collective-permute-start.14 = (bf16[64,4096]{1,0:T(8,128)(2,1)S(1)}, bf16[64,4096]{1,0:T(8,128)(2,1)S(1)}, u32[]{:S(2)}, u32[]{:S(2)}) collective-permute-start(bf16[64,4096]{1,0:T(8,128)(2,1)S(1)} %shard_map.168), channel_id=1, source_target_pairs={{0,16},{16,0},{1,17},{17,1},{2,18},{18,2},{3,19},{19,3},{4,20},{20... | collective-permute-start | bytes 1572872 | tf_op jit(solution)/shard_map/ppermute | solution.py:313
  38.6 21.4 %collective-permute-start.18 = (bf16[16,8192]{1,0:T(8,128)(2,1)S(1)}, bf16[16,8192]{1,0:T(8,128)(2,1)S(1)}, u32[]{:S(2)}, u32[]{:S(2)}) collective-permute-start(bf16[16,8192]{1,0:T(8,128)(2,1)S(1)} %collective-permute-done.1.refs_1_.refs_3_), channel_id=1, source_target_pairs={{0,1},{1,0},{2,3},{3,2},{4,5},{5,4},{6,7},{7,6},{8,9},{9,8},{10,11... | collective-permute-start | bytes 786440 | tf_op jit(solution)/shard_map/ppermute | solution.py:323
  39.1 20.9 %collective-permute-start.19 = (bf16[16,8192]{1,0:T(8,128)(2,1)S(1)}, bf16[16,8192]{1,0:T(8,128)(2,1)S(1)}, u32[]{:S(2)}, u32[]{:S(2)}) collective-permute-start(bf16[16,8192]{1,0:T(8,128)(2,1)S(1)} %collective-permute-done.13.refs_0_.refs_4_), channel_id=1, source_target_pairs={{0,1},{1,0},{2,3},{3,2},{4,5},{5,4},{6,7},{7,6},{8,9},{9,8},{10,11... | collective-permute-start | bytes 786440 | tf_op jit(solution)/shard_map/ppermute | solution.py:323
  41.3 35.7 %copy-start.1 = (bf16[8192,256]{1,0:T(8,128)(2,1)S(1)}, bf16[8192,256]{1,0:T(8,128)(2,1)}, u32[]{:S(2)}) copy-start(bf16[8192,256]{1,0:T(8,128)(2,1)} %refs_2_.5) | copy-start | bytes 12582916
  41.4 14.7 %collective-permute-start.15 = (bf16[64,1024]{1,0:T(8,128)(2,1)S(1)}, bf16[64,1024]{1,0:T(8,128)(2,1)S(1)}, u32[]{:S(2)}, u32[]{:S(2)}) collective-permute-start(bf16[64,1024]{1,0:T(8,128)(2,1)S(1)} %get-tuple-element.36), channel_id=1, source_target_pairs={{0,1},{1,2},{2,3},{3,0},{4,5},{5,6},{6,7},{7,4},{8,9},{9,10},{10,1... | collective-permute-start | bytes 393224 | tf_op jit(solution)/shard_map/ppermute | solution.py:50
  43.0 16.9 %collective-permute-start.16 = (bf16[64,1024]{1,0:T(8,128)(2,1)S(1)}, bf16[64,1024]{1,0:T(8,128)(2,1)S(1)}, u32[]{:S(2)}, u32[]{:S(2)}) collective-permute-start(bf16[64,1024]{1,0:T(8,128)(2,1)S(1)} %get-tuple-element.37), channel_id=1, source_target_pairs={{0,2},{1,3},{2,0},{3,1},{4,6},{5,7},{6,4},{7,5},{8,10},{9,11},{10,... | collective-permute-start | bytes 393224 | tf_op jit(solution)/shard_map/ppermute | solution.py:50
  44.5 15.4 %collective-permute-start.17 = (bf16[64,1024]{1,0:T(8,128)(2,1)S(1)}, bf16[64,1024]{1,0:T(8,128)(2,1)S(1)}, u32[]{:S(2)}, u32[]{:S(2)}) collective-permute-start(bf16[64,1024]{1,0:T(8,128)(2,1)S(1)} %get-tuple-element.38), channel_id=1, source_target_pairs={{0,3},{1,0},{2,1},{3,2},{4,7},{5,4},{6,5},{7,6},{8,11},{9,8},{10,9... | collective-permute-start | bytes 393224 | tf_op jit(solution)/shard_map/ppermute | solution.py:50
  60.1 16.9 %collective-permute-start.20 = (bf16[4,16,8192]{2,1,0:T(8,128)(2,1)S(1)}, bf16[4,16,8192]{2,1,0:T(8,128)(2,1)S(1)}, u32[]{:S(2)}, u32[]{:S(2)}) collective-permute-start(bf16[4,16,8192]{2,1,0:T(8,128)(2,1)S(1)} %shard_map.171.refs_3_), channel_id=1, source_target_pairs={{0,16},{16,0},{1,17},{17,1},{2,18},{18,2},{3,19},{19,3},{4,20},{20... | collective-permute-start | bytes 3145736 | tf_op jit(solution)/shard_map/ppermute | solution.py:313
  60.2 12.3 %collective-permute-start.21 = (bf16[64,1024]{1,0:T(8,128)(2,1)S(1)}, bf16[64,1024]{1,0:T(8,128)(2,1)S(1)}, u32[]{:S(2)}, u32[]{:S(2)}) collective-permute-start(bf16[64,1024]{1,0:T(8,128)(2,1)S(1)} %shard_map.170.refs_0_.refs_4_), channel_id=1, source_target_pairs={{0,1},{1,2},{2,3},{3,0},{4,5},{5,6},{6,7},{7,4},{8,9},{9,10},{10,1... | collective-permute-start | bytes 393224 | tf_op jit(solution)/shard_map/ppermute | solution.py:50
  63.2 11.8 %collective-permute-start.22 = (bf16[64,1024]{1,0:T(8,128)(2,1)S(1)}, bf16[64,1024]{1,0:T(8,128)(2,1)S(1)}, u32[]{:S(2)}, u32[]{:S(2)}) collective-permute-start(bf16[64,1024]{1,0:T(8,128)(2,1)S(1)} %shard_map.170.refs_0_.refs_4_), channel_id=1, source_target_pairs={{0,2},{1,3},{2,0},{3,1},{4,6},{5,7},{6,4},{7,5},{8,10},{9,11},{10,... | collective-permute-start | bytes 393224 | tf_op jit(solution)/shard_map/ppermute | solution.py:50
  64.4 12.4 %collective-permute-start.23 = (bf16[64,1024]{1,0:T(8,128)(2,1)S(1)}, bf16[64,1024]{1,0:T(8,128)(2,1)S(1)}, u32[]{:S(2)}, u32[]{:S(2)}) collective-permute-start(bf16[64,1024]{1,0:T(8,128)(2,1)S(1)} %shard_map.170.refs_0_.refs_4_), channel_id=1, source_target_pairs={{0,3},{1,0},{2,1},{3,2},{4,7},{5,4},{6,5},{7,6},{8,11},{9,8},{10,9... | collective-permute-start | bytes 393224 | tf_op jit(solution)/shard_map/ppermute | solution.py:50
  66.4 11.5 %collective-permute-start.24 = (bf16[64,1024]{1,0:T(8,128)(2,1)S(1)}, bf16[64,1024]{1,0:T(8,128)(2,1)S(1)}, u32[]{:S(2)}, u32[]{:S(2)}) collective-permute-start(bf16[64,1024]{1,0:T(8,128)(2,1)S(1)} %shard_map.170.refs_0_.refs_4_), channel_id=1, source_target_pairs={{0,16},{16,0},{1,17},{17,1},{2,18},{18,2},{3,19},{19,3},{4,20},{20... | collective-permute-start | bytes 393224 | tf_op jit(solution)/shard_map/ppermute | solution.py:313
  72.4 5.5 %collective-permute-start.25 = (bf16[64,1024]{1,0:T(8,128)(2,1)S(1)}, bf16[64,1024]{1,0:T(8,128)(2,1)S(1)}, u32[]{:S(2)}, u32[]{:S(2)}) collective-permute-start(bf16[64,1024]{1,0:T(8,128)(2,1)S(1)} %collective-permute-done.21.refs_5_), channel_id=1, source_target_pairs={{0,16},{16,0},{1,17},{17,1},{2,18},{18,2},{3,19},{19,3},{4,20},{20... | collective-permute-start | bytes 393224 | tf_op jit(solution)/shard_map/ppermute | solution.py:313
  74.9 3.0 %collective-permute-start.26 = (bf16[64,1024]{1,0:T(8,128)(2,1)S(1)}, bf16[64,1024]{1,0:T(8,128)(2,1)S(1)}, u32[]{:S(2)}, u32[]{:S(2)}) collective-permute-start(bf16[64,1024]{1,0:T(8,128)(2,1)S(1)} %collective-permute-done.22.refs_6_), channel_id=1, source_target_pairs={{0,16},{16,0},{1,17},{17,1},{2,18},{18,2},{3,19},{19,3},{4,20},{20... | collective-permute-start | bytes 393224 | tf_op jit(solution)/shard_map/ppermute | solution.py:313
  76.9 1.3 %collective-permute-start.27 = (bf16[64,1024]{1,0:T(8,128)(2,1)S(1)}, bf16[64,1024]{1,0:T(8,128)(2,1)S(1)}, u32[]{:S(2)}, u32[]{:S(2)}) collective-permute-start(bf16[64,1024]{1,0:T(8,128)(2,1)S(1)} %collective-permute-done.23.refs_7_), channel_id=1, source_target_pairs={{0,16},{16,0},{1,17},{17,1},{2,18},{18,2},{3,19},{19,3},{4,20},{20... | collective-permute-start | bytes 393224 | tf_op jit(solution)/shard_map/ppermute | solution.py:313
  79.2 4.9 %collective-permute-start.28 = (bf16[192,256]{1,0:T(8,128)(2,1)S(1)}, bf16[192,256]{1,0:T(8,128)(2,1)S(1)}, u32[]{:S(2)}, u32[]{:S(2)}) collective-permute-start(bf16[192,256]{1,0:T(8,128)(2,1)S(1)} %shard_map.173.refs_2_), channel_id=1, source_target_pairs={{0,4},{4,8},{8,12},{12,0},{1,5},{5,9},{9,13},{13,1},{2,6},{6,10},{... | collective-permute-start | bytes 294920 | tf_op jit(solution)/shard_map/ppermute | solution.py:50
  80.6 6.7 %collective-permute-start.29 = (bf16[192,256]{1,0:T(8,128)(2,1)S(1)}, bf16[192,256]{1,0:T(8,128)(2,1)S(1)}, u32[]{:S(2)}, u32[]{:S(2)}) collective-permute-start(bf16[192,256]{1,0:T(8,128)(2,1)S(1)} %shard_map.173.refs_2_), channel_id=1, source_target_pairs={{0,8},{4,12},{8,0},{12,4},{1,9},{5,13},{9,1},{13,5},{2,10},{6,14},... | collective-permute-start | bytes 294920 | tf_op jit(solution)/shard_map/ppermute | solution.py:50
  81.2 6.2 %collective-permute-start.30 = (bf16[192,256]{1,0:T(8,128)(2,1)S(1)}, bf16[192,256]{1,0:T(8,128)(2,1)S(1)}, u32[]{:S(2)}, u32[]{:S(2)}) collective-permute-start(bf16[192,256]{1,0:T(8,128)(2,1)S(1)} %shard_map.173.refs_2_), channel_id=1, source_target_pairs={{0,12},{4,0},{8,4},{12,8},{1,13},{5,1},{9,5},{13,9},{2,14},{6,2},{... | collective-permute-start | bytes 294920 | tf_op jit(solution)/shard_map/ppermute | solution.py:50
  (4 other events, 56.8 us)

commit v4 on v3

--- a/solution.py
+++ b/solution.py
@@ -56,7 +56,8 @@
 
 def front_kernel(n_z, block, kept, place_hbm, x_hbm, gain_hbm, w_hbm, b_hbm, wo_hbm, ob_hbm, *refs):
     later, refs = refs[:kept], refs[kept:]
-    (keep_ref, send_ref, base_ref), held, refs = refs[:3], refs[3:3 + kept], refs[3 + kept:]
+    (keep_ref, base_ref), sends, refs = refs[:2], refs[2:2 + n_z], refs[2 + n_z:]
+    held, refs = refs[:kept], refs[kept:]
     hf, place, x_ref, gain_ref, w_ref, b_ref, wo_ref, ob_ref, sems = refs
     brought = (
         (x_hbm, x_ref), (gain_hbm, gain_ref), (w_hbm, w_ref), (b_hbm, b_ref),
@@ -124,22 +125,31 @@
     copies[6].wait()
     wo = wo_ref[...]
     heads = hf[...]
-    for section, out in ((1 - c, send_ref), (c, keep_ref)):
-        order = picked(section, 0, rows // 2)
-        chosen = jnp.dot(order, heads, preferred_element_type=F32).astype(BF16)
-        out[...] = jnp.dot(chosen, wo, preferred_element_type=F32).astype(BF16)
+    def summed(section):
+        chosen = jnp.dot(picked(section, 0, rows // 2), heads, preferred_element_type=F32).astype(BF16)
+        return jnp.dot(chosen, wo, preferred_element_type=F32).astype(BF16)
+
+    other = summed(1 - c)
+    for zz, out in enumerate(sends):
+        out[...] = other[zz * block:(zz + 1) * block, :]
+    keep_ref[...] = summed(c)
     own = jnp.dot(picked(c, z, block), x_ref[...], preferred_element_type=F32)
     base_ref[...] = own + ob_ref[...][None, :]
     for copy in copies[7:]:
         copy.wait()
 
 
-def pair_rows_kernel(n_z, block, keep_ref, got_ref, *outs):
+def pair_rows_kernel(n_z, block, keep_ref, *refs):
     z = lax.axis_index("mp")
+    gots, outs = refs[:n_z], refs[n_z:]
     for k in range(n_z):
-        at = pl.ds(pl.multiple_of(lax.rem(z + k, n_z) * block, block), block)
-        total = keep_ref[at, :].astype(F32) + got_ref[at, :].astype(F32)
-        outs[k][...] = total.astype(outs[k].dtype)
+        mine = lax.rem(z + k, n_z)
+        keep = keep_ref[pl.ds(pl.multiple_of(mine * block, block), block), :].astype(F32)
+        for zz in range(n_z):
+
+            @pl.when(mine == zz)
+            def _():
+                outs[k][...] = (keep + gots[zz][...].astype(F32)).astype(outs[k].dtype)
 
 
 def resid_kernel(base_ref, gain_ref, own_ref, *refs):
@@ -170,19 +180,26 @@
     out_ref[...] = (0.5 * acc * (1.0 + lax.erf(acc * (1.0 / math.sqrt(2.0))))).astype(BF16)
 
 
-def down_kernel(other, hidden_ref, down_ref, out_ref):
+def down_kernel(other, hidden_ref, down_ref, *outs):
     c = lax.axis_index("section")
-    half = out_ref.shape[1]
-    at = pl.ds(pl.multiple_of((1 - c if other else c) * half, half), half)
-    out_ref[...] = jnp.dot(hidden_ref[...], down_ref[:, at], preferred_element_type=F32).astype(BF16)
-
-
-def pair_columns_kernel(n_z, block, keep_ref, got_ref, *outs):
+    width = outs[0].shape[1]
+    first = (1 - c if other else c) * len(outs) * width
+    for i, out in enumerate(outs):
+        at = pl.ds(pl.multiple_of(first + i * width, width), width)
+        out[...] = jnp.dot(hidden_ref[...], down_ref[:, at], preferred_element_type=F32).astype(BF16)
+
+
+def pair_columns_kernel(n_z, *refs):
     z = lax.axis_index("mp")
+    keeps, gots, outs = refs[:n_z], refs[n_z:2 * n_z], refs[2 * n_z:]
     for k in range(n_z):
-        at = pl.ds(pl.multiple_of(lax.rem(z + k, n_z) * block, block), block)
-        total = keep_ref[:, at].astype(F32) + got_ref[:, at].astype(F32)
-        outs[k][...] = total.astype(outs[k].dtype)
+        mine = lax.rem(z + k, n_z)
+        for zz in range(n_z):
+
+            @pl.when(mine == zz)
+            def _():
+                total = keeps[zz][...].astype(F32) + gots[zz][...].astype(F32)
+                outs[k][...] = total.astype(outs[k].dtype)
 
 
 def image_kernel(n_z, bias_ref, own_ref, *refs):
@@ -253,30 +270,33 @@
 
 def place_kernel(n_s, slot_map, place_ref, *refs):
     s = lax.axis_index("seq")
-    keyvals, (out_ref, held) = refs[:n_s], refs[n_s:]
+    keyvals, (out_ref, held, texts) = refs[:n_s], refs[n_s:]
     units = place_ref.shape[2]
     prompt = n_s * CTX
     for k in range(n_s):
         held[lax.rem(s - k + n_s, n_s)] = keyvals[k][prompt:, :]
     position = lax.broadcasted_iota(jnp.int32, (CTX, units), 0)
     for k in range(n_s):
-        j = lax.rem(s - k + n_s, n_s)
-
-        def one(i, carry):
-            slot = slot_map[j, i] - s * n_s
-
-            @pl.when((slot >= 0) & (slot < n_s))
-            def _():
-                chosen = position == place_ref[i, pl.ds(j, 1), :]
-                covered = jnp.sum(chosen.astype(F32), axis=1, keepdims=True) > 0.5
-                rows = held[i, pl.ds(pl.multiple_of(j * units, units), units), :]
-                image = jnp.dot(chosen.astype(BF16), rows, preferred_element_type=F32)
-                text = keyvals[k][pl.ds(pl.multiple_of(i * CTX, CTX), CTX), :]
-                out_ref[slot] = jnp.where(covered, image, text.astype(F32)).astype(BF16)
-
-            return carry
-
-        lax.fori_loop(0, n_s, one, 0)
+        texts[lax.rem(s - k + n_s, n_s)] = keyvals[k][:prompt, :]
+
+    def source(t):
+        def look(n, found):
+            return jnp.where(slot_map[n // n_s, n % n_s] == s * n_s + t, n, found)
+
+        found = lax.fori_loop(0, n_s * n_s, look, 0, unroll=n_s == 4)
+        return found // n_s, found % n_s
+
+    def one(t):
+        j, i = source(t)
+        chosen = position == place_ref[i, pl.ds(j, 1), :]
+        covered = jnp.sum(chosen.astype(F32), axis=1, keepdims=True) > 0.5
+        rows = held[i, pl.ds(pl.multiple_of(j * units, units), units), :]
+        image = jnp.dot(chosen.astype(BF16), rows, preferred_element_type=F32)
+        text = texts[j, pl.ds(pl.multiple_of(i * CTX, CTX), CTX), :]
+        out_ref[t] = jnp.where(covered, image, text.astype(F32)).astype(BF16)
+
+    for t in range(n_s):
+        one(t)
 
 
 def shards(
@@ -325,19 +345,19 @@
         def middle(v):
             return lax.ppermute(v, "mp", [(0, 0), (1, 2), (2, 1), (3, 3)])
 
-        first = [near(text_own), middle(text_own)]
-        second = [middle(first[0])]
-        third = [near(first[1]), near(second[0])]
-        text_pieces = [text_own, *first, *second, *third]
+        near_own, middle_own = near(text_own), middle(text_own)
+        middle_near, near_middle = middle(near_own), near(middle_own)
+        near_last = near(middle_near)
+        text_pieces = [text_own, near_own, middle_own, middle_near, near_middle, near_last]
     else:
         text_pieces = [text_own] + [shifted(text_own, "mp", n_z, k) for k in range(1, n_z)]
-        first, second = text_pieces[1:2], text_pieces[2:3]
 
     w = qkv_weight.transpose(1, 2, 0).reshape(3 * head_width, width)
     later = [merge_gain, merge_up.T, merge_up_bias, merge_down_bias, input_gain, kv_bias]
-    keep, send, base, gain, up, up_bias, down_bias, text_gain, bias = call(
+    keep, base, *rest = call(
         functools.partial(front_kernel, n_z, block, len(later)),
-        [struct((rows // 2, width), BF16)] * 2 + [struct((block, width), F32)]
+        [struct((rows // 2, width), BF16), struct((block, width), F32)]
+        + [struct((block, width), BF16)] * n_z
         + [struct(v.shape, v.dtype) for v in later],
         [image_place, x, vision_gain, w, qkv_bias, out_weight, out_bias] + later,
         scratch=[
@@ -350,15 +370,15 @@
         grant=24,
         flops=2 * rows * width * 4 * head_width,
     )
-    got = swap(send)
+    sends, (gain, up, up_bias, down_bias, text_gain, bias) = rest[:n_z], rest[n_z:]
     parts = call(
         functools.partial(pair_rows_kernel, n_z, block),
         [struct((block, width), F32)] + [struct((block, width), BF16)] * (n_z - 1),
-        [keep, got],
+        [keep] + [swap(v) for v in sends],
     )
     sums = [parts[0]] + [shifted(parts[k], "mp", n_z, k) for k in range(1, n_z)]
     merged, = call(
-        resid_kernel, [struct((block, width), BF16)], [base, gain] + sums, after=first)
+        resid_kernel, [struct((block, width), BF16)], [base, gain] + sums)
     pieces = spread(merged)
 
     hidden, = call(
@@ -368,22 +388,20 @@
         scratch=[pltpu.VMEM((JOIN, units, width), BF16)],
         flops=2 * units * merge_up.size,
     )
-    send, keep = (
+    sends, keeps = (
         call(
             functools.partial(down_kernel, other),
-            [struct((units, model // 2), BF16)],
+            [struct((units, columns), BF16)] * n_z,
             [hidden, merge_down],
-            after=second if other else (),
             flops=units * merge_down.size,
             grant=16,
-        )[0]
+        )
         for other in (True, False)
     )
-    got = swap(send)
     parts = call(
-        functools.partial(pair_columns_kernel, n_z, columns),
+        functools.partial(pair_columns_kernel, n_z),
         [struct((units, columns), F32)] + [struct((units, columns), BF16)] * (n_z - 1),
-        [keep, got],
+        [*keeps, *(swap(v) for v in sends)],
     )
     sums = [parts[0]] + [shifted(parts[k], "mp", n_z, k) for k in range(1, n_z)]
     image, = call(
@@ -413,7 +431,7 @@
         functools.partial(place_kernel, n_s),
         [struct((n_s, CTX, kv_width), BF16)],
         [slot_map, image_place] + keyvals,
-        scratch=[pltpu.VMEM((n_s, units, kv_width), BF16)],
+        scratch=[pltpu.VMEM((n_s, units, kv_width), BF16), pltpu.VMEM((n_s, prompt, kv_width), BF16)],
         smem=1,
         grant=16,
     )

time: 89.3 us -> 83.8 us (0.938)
  waiting for transfers between devices: 45.6 us -> 41.1 us
  starting transfers between devices: 33 us -> 32 us
    ppermute x15, waiting for transfers between devices: 39.1 us -> 32.5 us  [shifted(): return lax.ppermute(x, axis, [(i, (i + k) % count) for i in range(count)])]
    ppermute x2, waiting for transfers between devices: 3.06 us -> 6.23 us  [middle(): return lax.ppermute(v, 'mp', [(0, 0), (1, 2), (2, 1), (3, 3)])]
    ppermute x2, starting transfers between devices: 8.08 us -> 5.83 us  [middle(): return lax.ppermute(v, 'mp', [(0, 0), (1, 2), (2, 1), (3, 3)])]
    ppermute x11 -> x17, starting transfers between devices: 0.45 us -> 2.62 us  [swap(): return lax.ppermute(v, 'section', [(0, 1), (1, 0)])]
    ppermute x3, starting transfers between devices: 2.55 us -> 0.45 us  [near(): return lax.ppermute(v, 'mp', [(0, 1), (1, 0), (2, 3), (3, 2)])]
    ppermute x3, waiting for transfers between devices: 1.86 us -> 0.01 us  [near(): return lax.ppermute(v, 'mp', [(0, 1), (1, 0), (2, 3), (3, 2)])]
    ppermute x15, starting transfers between devices: 21.9 us -> 23.1 us  [shifted(): return lax.ppermute(x, axis, [(i, (i + k) % count) for i in range(count)])]
    ppermute x11 -> x17, waiting for transfers between devices: 1.57 us -> 2.42 us  [swap(): return lax.ppermute(v, 'section', [(0, 1), (1, 0)])]
  transfers between devices with their start and end apart: 31 -> 37, of which waited for: 18 -> 22; matrix products, arithmetic and copies ran while one was open for 0% -> 0% of each run, Pallas kernels for 3% -> 9%
where the time goes in v4:
time: 83.8 us; the launch traced here: 83.6 us
  waiting for transfers between devices  41.1 us (49%)
  starting transfers between devices  32 us (38%)
  Pallas kernels  10.2 us (12%)
    ppermute x15, waiting for transfers between devices, shifted(): return lax.ppermute(x, axis, [(i, (i + k) % count) for i in range(count)])  32.5 us
    ppermute x15, starting transfers between devices, shifted(): return lax.ppermute(x, axis, [(i, (i + k) % count) for i in range(count)])  23.1 us
    pallas_call x12, Pallas kernels, call(): pl.pallas_call(body, out_shape=outs, in_specs=[unread] * count + [scalar]...  10.2 us
    ppermute x2, waiting for transfers between devices, middle(): return lax.ppermute(v, 'mp', [(0, 0), (1, 2), (2, 1), (3, 3)])  6.23 us
    ppermute x2, starting transfers between devices, middle(): return lax.ppermute(v, 'mp', [(0, 0), (1, 2), (2, 1), (3, 3)])  5.83 us
    ppermute x17, starting transfers between devices, swap(): return lax.ppermute(v, 'section', [(0, 1), (1, 0)])  2.62 us
    ppermute x17, waiting for transfers between devices, swap(): return lax.ppermute(v, 'section', [(0, 1), (1, 0)])  2.42 us
  transfers between devices with their start and end apart: 37, of which 22 were waited for; matrix products, arithmetic and copies ran while one was open for 0% of the time, Pallas kernels for 9%

profile of v4, /device:TPU:10, one launch (start us, length us, event | category | flops | bytes accessed | tf_op | source)
XLA Modules:
  0.0 83.6 jit_solution(11040166125397828385)
XLA Ops:
  0.5 3.9 %shard_map.163 = (bf16[128,1280]{1,0:T(8,128)(2,1)S(1)}, f32[32,1280]{1,0:T(8,128)S(1)}, bf16[32,1280]{1,0:T(8,128)(2,1)S(1)}, bf16[32,1280]{1,0:T(8,128)(2,1)S(...) custom-call(s32[4,4,16]{2,1,0:T(4,128)} %refs_1_.7, ...), custom_call_target="tpu_custom_call" | custom-call | flops 419430400 | bytes 9825664 | tf_op jit(solution)/shard_map/pallas_call | solution.py:34
  6.5 2.8 %collective-permute-start.4 = (bf16[32,1280]{1,0:T(8,128)(2,1)S(1)}, bf16[32,1280]{1,0:T(8,128)(2,1)S(1)}, u32[]{:S(2)}, u32[]{:S(2)}) collective-permute-start(bf16[32,1280]{1,0:T(8,128)(2,1)S(1)} %get-tuple-element.46), channel_id=1, source_target_pairs={{0,1},{1,2},{2,3},{3,0},{4,5},{5,6},{6,7},{7,4},{8,9},{9,10},{10,1... | collective-permute-start | bytes 245768 | tf_op jit(solution)/shard_map/ppermute | solution.py:50
  9.3 1.2 %collective-permute-start.5 = (bf16[32,1280]{1,0:T(8,128)(2,1)S(1)}, bf16[32,1280]{1,0:T(8,128)(2,1)S(1)}, u32[]{:S(2)}, u32[]{:S(2)}) collective-permute-start(bf16[32,1280]{1,0:T(8,128)(2,1)S(1)} %get-tuple-element.47), channel_id=1, source_target_pairs={{0,2},{1,3},{2,0},{3,1},{4,6},{5,7},{6,4},{7,5},{8,10},{9,11},{10,... | collective-permute-start | bytes 245768 | tf_op jit(solution)/shard_map/ppermute | solution.py:50
  10.5 0.7 collective-permute-start.6
  11.2 4.2 %collective-permute-done.4.refs_3_ = bf16[32,1280]{1,0:T(8,128)(2,1)S(1)} collective-permute-done((bf16[32,1280]{1,0:T(8,128)(2,1)S(1)}, bf16[32,1280]{1,0:T(8,128)(2,1)S(1)}, u32[]{:S(2)}, u32[]{:S(2)}) %collective-permute-start.4) | collective-permute-done | bytes 81952 | tf_op jit(solution)/shard_map/ppermute | solution.py:50
  15.4 1.3 %collective-permute-done.5.refs_4_ = bf16[32,1280]{1,0:T(8,128)(2,1)S(1)} collective-permute-done((bf16[32,1280]{1,0:T(8,128)(2,1)S(1)}, bf16[32,1280]{1,0:T(8,128)(2,1)S(1)}, u32[]{:S(2)}, u32[]{:S(2)}) %collective-permute-start.5) | collective-permute-done | bytes 81952 | tf_op jit(solution)/shard_map/ppermute | solution.py:50
  16.7 1.0 %collective-permute-done.6.refs_5_ = bf16[32,1280]{1,0:T(8,128)(2,1)S(1)} collective-permute-done((bf16[32,1280]{1,0:T(8,128)(2,1)S(1)}, bf16[32,1280]{1,0:T(8,128)(2,1)S(1)}, u32[]{:S(2)}, u32[]{:S(2)}) %collective-permute-start.6) | collective-permute-done | bytes 81952 | tf_op jit(solution)/shard_map/ppermute | solution.py:50
  18.2 2.6 %collective-permute-start.8 = (bf16[32,1280]{1,0:T(8,128)(2,1)S(1)}, bf16[32,1280]{1,0:T(8,128)(2,1)S(1)}, u32[]{:S(2)}, u32[]{:S(2)}) collective-permute-start(bf16[32,1280]{1,0:T(8,128)(2,1)S(1)} %shard_map.165.refs_2_), channel_id=1, source_target_pairs={{0,2},{1,3},{2,0},{3,1},{4,6},{5,7},{6,4},{7,5},{8,10},{9,11},{10,... | collective-permute-start | bytes 245768 | tf_op jit(solution)/shard_map/ppermute | solution.py:50
  20.8 1.6 %collective-permute-start.9 = (bf16[32,1280]{1,0:T(8,128)(2,1)S(1)}, bf16[32,1280]{1,0:T(8,128)(2,1)S(1)}, u32[]{:S(2)}, u32[]{:S(2)}) collective-permute-start(bf16[32,1280]{1,0:T(8,128)(2,1)S(1)} %shard_map.165.refs_2_), channel_id=1, source_target_pairs={{0,3},{1,0},{2,1},{3,2},{4,7},{5,4},{6,5},{7,6},{8,11},{9,8},{10,9... | collective-permute-start | bytes 245768 | tf_op jit(solution)/shard_map/ppermute | solution.py:50
  22.5 2.8 %collective-permute-start.22 = (bf16[16,8192]{1,0:T(8,128)(2,1)S(1)}, bf16[16,8192]{1,0:T(8,128)(2,1)S(1)}, u32[]{:S(2)}, u32[]{:S(2)}) collective-permute-start(bf16[16,8192]{1,0:T(8,128)(2,1)S(1)} %bitcast.10), channel_id=1, source_target_pairs={{0,0},{1,2},{2,1},{3,3},{4,4},{5,6},{6,5},{7,7},{8,8},{9,10},{10,9... | collective-permute-start | bytes 786440 | tf_op jit(solution)/shard_map/ppermute | solution.py:346
  25.3 3.1 %collective-permute-start.23 = (bf16[16,8192]{1,0:T(8,128)(2,1)S(1)}, bf16[16,8192]{1,0:T(8,128)(2,1)S(1)}, u32[]{:S(2)}, u32[]{:S(2)}) collective-permute-start(bf16[16,8192]{1,0:T(8,128)(2,1)S(1)} %collective-permute-done.21.refs_2_), channel_id=1, source_target_pairs={{0,0},{1,2},{2,1},{3,3},{4,4},{5,6},{6,5},{7,7},{8,8},{9,10},{10,9... | collective-permute-start | bytes 786440 | tf_op jit(solution)/shard_map/ppermute | solution.py:346
  29.1 0.7 collective-permute-done.11.refs_7_
  30.3 1.1 %shard_map.166.refs_0_ = bf16[64,320]{1,0:T(8,128)(2,1)S(1)} custom-call(bf16[320,5120]{1,0:T(8,128)(2,1)S(1)} %get-tuple-element.36.refs_0_, f32[320]{0:T(512)S(1)} %get-tuple-element.37.refs_1_, bf16[32,1280]{1,0:T(8,128)(2,1)S(1)} %shard_map.165.refs_2_, bf16[32,1280]{1,0:T(8,128)(2,1)S(1)} %collective-permute-done.7.refs_3_, ...), custom_call_target="tpu_custom_call" | custom-call | flops 209715200 | bytes 3974400 | tf_op jit(solution)/shard_map/pallas_call | solution.py:34
  32.8 0.9 %collective-permute-done.22.refs_3_ = bf16[16,8192]{1,0:T(8,128)(2,1)S(1)} collective-permute-done((bf16[16,8192]{1,0:T(8,128)(2,1)S(1)}, bf16[16,8192]{1,0:T(8,128)(2,1)S(1)}, u32[]{:S(2)}, u32[]{:S(2)}) %collective-permute-start.22) | collective-permute-done | bytes 262176 | tf_op jit(solution)/shard_map/ppermute | solution.py:346
  33.7 5.4 %collective-permute-done.23.refs_4_ = bf16[16,8192]{1,0:T(8,128)(2,1)S(1)} collective-permute-done((bf16[16,8192]{1,0:T(8,128)(2,1)S(1)}, bf16[16,8192]{1,0:T(8,128)(2,1)S(1)}, u32[]{:S(2)}, u32[]{:S(2)}) %collective-permute-start.23) | collective-permute-done | bytes 262176 | tf_op jit(solution)/shard_map/ppermute | solution.py:346
  40.4 4.0 %collective-permute-start.19 = (bf16[64,1024]{1,0:T(8,128)(2,1)S(1)}, bf16[64,1024]{1,0:T(8,128)(2,1)S(1)}, u32[]{:S(2)}, u32[]{:S(2)}) collective-permute-start(bf16[64,1024]{1,0:T(8,128)(2,1)S(1)} %get-tuple-element.59), channel_id=1, source_target_pairs={{0,2},{1,3},{2,0},{3,1},{4,6},{5,7},{6,4},{7,5},{8,10},{9,11},{10,... | collective-permute-start | bytes 393224 | tf_op jit(solution)/shard_map/ppermute | solution.py:50
  44.4 6.8 %collective-permute-done.18.refs_2_ = bf16[64,1024]{1,0:T(8,128)(2,1)S(1)} collective-permute-done((bf16[64,1024]{1,0:T(8,128)(2,1)S(1)}, bf16[64,1024]{1,0:T(8,128)(2,1)S(1)}, u32[]{:S(2)}, u32[]{:S(2)}) %collective-permute-start.18) | collective-permute-done | bytes 131104 | tf_op jit(solution)/shard_map/ppermute | solution.py:50
  51.2 3.1 %collective-permute-done.19.refs_3_ = bf16[64,1024]{1,0:T(8,128)(2,1)S(1)} collective-permute-done((bf16[64,1024]{1,0:T(8,128)(2,1)S(1)}, bf16[64,1024]{1,0:T(8,128)(2,1)S(1)}, u32[]{:S(2)}, u32[]{:S(2)}) %collective-permute-start.19) | collective-permute-done | bytes 131104 | tf_op jit(solution)/shard_map/ppermute | solution.py:50
  54.3 0.7 collective-permute-done.20.refs_4_
  55.3 2.4 %collective-permute-start.27 = (bf16[64,1024]{1,0:T(8,128)(2,1)S(1)}, bf16[64,1024]{1,0:T(8,128)(2,1)S(1)}, u32[]{:S(2)}, u32[]{:S(2)}) collective-permute-start(bf16[64,1024]{1,0:T(8,128)(2,1)S(1)} %shard_map.170.refs_0_.refs_4_), channel_id=1, source_target_pairs={{0,1},{1,2},{2,3},{3,0},{4,5},{5,6},{6,7},{7,4},{8,9},{9,10},{10,1... | collective-permute-start | bytes 393224 | tf_op jit(solution)/shard_map/ppermute | solution.py:50
  57.7 1.8 %collective-permute-start.28 = (bf16[64,1024]{1,0:T(8,128)(2,1)S(1)}, bf16[64,1024]{1,0:T(8,128)(2,1)S(1)}, u32[]{:S(2)}, u32[]{:S(2)}) collective-permute-start(bf16[64,1024]{1,0:T(8,128)(2,1)S(1)} %shard_map.170.refs_0_.refs_4_), channel_id=1, source_target_pairs={{0,2},{1,3},{2,0},{3,1},{4,6},{5,7},{6,4},{7,5},{8,10},{9,11},{10,... | collective-permute-start | bytes 393224 | tf_op jit(solution)/shard_map/ppermute | solution.py:50
  59.4 1.7 %collective-permute-start.29 = (bf16[64,1024]{1,0:T(8,128)(2,1)S(1)}, bf16[64,1024]{1,0:T(8,128)(2,1)S(1)}, u32[]{:S(2)}, u32[]{:S(2)}) collective-permute-start(bf16[64,1024]{1,0:T(8,128)(2,1)S(1)} %shard_map.170.refs_0_.refs_4_), channel_id=1, source_target_pairs={{0,3},{1,0},{2,1},{3,2},{4,7},{5,4},{6,5},{7,6},{8,11},{9,8},{10,9... | collective-permute-start | bytes 393224 | tf_op jit(solution)/shard_map/ppermute | solution.py:50
  61.2 5.8 %collective-permute-done.27.refs_5_ = bf16[64,1024]{1,0:T(8,128)(2,1)S(1)} collective-permute-done((bf16[64,1024]{1,0:T(8,128)(2,1)S(1)}, bf16[64,1024]{1,0:T(8,128)(2,1)S(1)}, u32[]{:S(2)}, u32[]{:S(2)}) %collective-permute-start.27) | collective-permute-done | bytes 131104 | tf_op jit(solution)/shard_map/ppermute | solution.py:50
  66.9 2.5 %collective-permute-done.28.refs_6_ = bf16[64,1024]{1,0:T(8,128)(2,1)S(1)} collective-permute-done((bf16[64,1024]{1,0:T(8,128)(2,1)S(1)}, bf16[64,1024]{1,0:T(8,128)(2,1)S(1)}, u32[]{:S(2)}, u32[]{:S(2)}) %collective-permute-start.28) | collective-permute-done | bytes 131104 | tf_op jit(solution)/shard_map/ppermute | solution.py:50
  69.5 2.2 %collective-permute-done.29.refs_7_ = bf16[64,1024]{1,0:T(8,128)(2,1)S(1)} collective-permute-done((bf16[64,1024]{1,0:T(8,128)(2,1)S(1)}, bf16[64,1024]{1,0:T(8,128)(2,1)S(1)}, u32[]{:S(2)}, u32[]{:S(2)}) %collective-permute-start.29) | collective-permute-done | bytes 131104 | tf_op jit(solution)/shard_map/ppermute | solution.py:50
  71.7 0.9 %shard_map.172.refs_0_ = bf16[128,256]{1,0:T(8,128)(2,1)S(1)} custom-call(f32[8192]{0:T(1024)S(1)} %get-tuple-element.33.refs_0_.refs_1_, bf16[8192,256]{1,0:T(8,128)(2,1)S(1)} %copy-done, f32[256]{0:T(256)S(1)} %get-tuple-element.34.refs_2_.refs_3_, bf16[4,16,8192]{2,1,0:T(8,128)(2,1)S(1)} %shard_map.171.refs_3_, ...), custom_call_target="tpu_custom_call" | custom-call | flops 536870912 | bytes 6390784 | tf_op jit(solution)/shard_map/pallas_call | solution.py:34
  73.0 0.9 %shard_map.173.refs_2_ = bf16[192,256]{1,0:T(8,128)(2,1)S(1)} custom-call(bf16[128,256]{1,0:T(8,128)(2,1)S(1)} %shard_map.172.refs_0_, f32[8192]{0:T(1024)S(1)} %get-tuple-element.33.refs_0_.refs_1_, bf16[8192,256]{1,0:T(8,128)(2,1)S(1)} %copy-done, f32[256]{0:T(256)S(1)} %get-tuple-element.34.refs_2_.refs_3_, ...), custom_call_target="tpu_custom_call" | custom-call | flops 268435456 | bytes 5440512 | tf_op jit(solution)/shard_map/pallas_call | solution.py:34
  74.0 1.5 %collective-permute-start.34 = (bf16[192,256]{1,0:T(8,128)(2,1)S(1)}, bf16[192,256]{1,0:T(8,128)(2,1)S(1)}, u32[]{:S(2)}, u32[]{:S(2)}) collective-permute-start(bf16[192,256]{1,0:T(8,128)(2,1)S(1)} %shard_map.173.refs_2_), channel_id=1, source_target_pairs={{0,4},{4,8},{8,12},{12,0},{1,5},{5,9},{9,13},{13,1},{2,6},{6,10},{... | collective-permute-start | bytes 294920 | tf_op jit(solution)/shard_map/ppermute | solution.py:50
  75.9 1.7 %collective-permute-start.36 = (bf16[192,256]{1,0:T(8,128)(2,1)S(1)}, bf16[192,256]{1,0:T(8,128)(2,1)S(1)}, u32[]{:S(2)}, u32[]{:S(2)}) collective-permute-start(bf16[192,256]{1,0:T(8,128)(2,1)S(1)} %shard_map.173.refs_2_), channel_id=1, source_target_pairs={{0,12},{4,0},{8,4},{12,8},{1,13},{5,1},{9,5},{13,9},{2,14},{6,2},{... | collective-permute-start | bytes 294920 | tf_op jit(solution)/shard_map/ppermute | solution.py:50
  77.6 1.3 %collective-permute-done.34.refs_3_ = bf16[192,256]{1,0:T(8,128)(2,1)S(1)} collective-permute-done((bf16[192,256]{1,0:T(8,128)(2,1)S(1)}, bf16[192,256]{1,0:T(8,128)(2,1)S(1)}, u32[]{:S(2)}, u32[]{:S(2)}) %collective-permute-start.34) | collective-permute-done | bytes 98336 | tf_op jit(solution)/shard_map/ppermute | solution.py:50
  78.9 3.3 %collective-permute-done.35.refs_4_ = bf16[192,256]{1,0:T(8,128)(2,1)S(1)} collective-permute-done((bf16[192,256]{1,0:T(8,128)(2,1)S(1)}, bf16[192,256]{1,0:T(8,128)(2,1)S(1)}, u32[]{:S(2)}, u32[]{:S(2)}) %collective-permute-start.35) | collective-permute-done | bytes 98336 | tf_op jit(solution)/shard_map/ppermute | solution.py:50
  82.2 1.4 %shard_map.174 = bf16[4,32,256]{2,1,0:T(8,128)(2,1)} custom-call(s32[4,4]{1,0:T(4,128)S(1)} %copy-done.3, s32[4,4,16]{2,1,0:T(4,128)S(1)} %copy-done.2, bf16[192,256]{1,0:T(8,128)(2,1)S(1)} %shard_map.173.refs_2_, bf16[192,256]{1,0:T(8,128)(2,1)S(1)} %collective-permute-done.34.refs_3_, bf16[192,256]{1,0:T(8,128)(2,1)S(1)} %collective-permute-done.35.refs_4_, ...), custom_call_target="tpu_custom_call" | custom-call | bytes 459840 | tf_op jit(solution)/shard_map/pallas_call | solution.py:34
  (67 shorter events, 8.2 us)
Async XLA Ops:
  0.0 25.3 %collective-permute-start.21 = (bf16[16,8192]{1,0:T(8,128)(2,1)}, bf16[16,8192]{1,0:T(8,128)(2,1)S(1)}, u32[]{:S(2)}, u32[]{:S(2)}) collective-permute-start(bf16[16,8192]{1,0:T(8,128)(2,1)} %bitcast.9), channel_id=1, source_target_pairs={{0,1},{1,0},{2,3},{3,2},{4,5},{5,4},{6,7},{7,6},{8,9},{9,8},{10,11... | collective-permute-start | bytes 786440 | tf_op jit(solution)/shard_map/ppermute | solution.py:343
  4.4 1.4 %collective-permute-start.1 = (bf16[32,1280]{1,0:T(8,128)(2,1)S(1)}, bf16[32,1280]{1,0:T(8,128)(2,1)S(1)}, u32[]{:S(2)}, u32[]{:S(2)}) collective-permute-start(bf16[32,1280]{1,0:T(8,128)(2,1)S(1)} %get-tuple-element.42), channel_id=1, source_target_pairs={{0,16},{16,0},{1,17},{17,1},{2,18},{18,2},{3,19},{19,3},{4,20},{20... | collective-permute-start | bytes 245768 | tf_op jit(solution)/shard_map/ppermute | solution.py:333
  5.0 1.4 %collective-permute-start.3 = (bf16[32,1280]{1,0:T(8,128)(2,1)S(1)}, bf16[32,1280]{1,0:T(8,128)(2,1)S(1)}, u32[]{:S(2)}, u32[]{:S(2)}) collective-permute-start(bf16[32,1280]{1,0:T(8,128)(2,1)S(1)} %get-tuple-element.44), channel_id=1, source_target_pairs={{0,16},{16,0},{1,17},{17,1},{2,18},{18,2},{3,19},{19,3},{4,20},{20... | collective-permute-start | bytes 245768 | tf_op jit(solution)/shard_map/ppermute | solution.py:333
  6.5 8.9 %collective-permute-start.4 = (bf16[32,1280]{1,0:T(8,128)(2,1)S(1)}, bf16[32,1280]{1,0:T(8,128)(2,1)S(1)}, u32[]{:S(2)}, u32[]{:S(2)}) collective-permute-start(bf16[32,1280]{1,0:T(8,128)(2,1)S(1)} %get-tuple-element.46), channel_id=1, source_target_pairs={{0,1},{1,2},{2,3},{3,0},{4,5},{5,6},{6,7},{7,4},{8,9},{9,10},{10,1... | collective-permute-start | bytes 245768 | tf_op jit(solution)/shard_map/ppermute | solution.py:50
  9.3 7.5 %collective-permute-start.5 = (bf16[32,1280]{1,0:T(8,128)(2,1)S(1)}, bf16[32,1280]{1,0:T(8,128)(2,1)S(1)}, u32[]{:S(2)}, u32[]{:S(2)}) collective-permute-start(bf16[32,1280]{1,0:T(8,128)(2,1)S(1)} %get-tuple-element.47), channel_id=1, source_target_pairs={{0,2},{1,3},{2,0},{3,1},{4,6},{5,7},{6,4},{7,5},{8,10},{9,11},{10,... | collective-permute-start | bytes 245768 | tf_op jit(solution)/shard_map/ppermute | solution.py:50
  10.5 7.2 %collective-permute-start.6 = (bf16[32,1280]{1,0:T(8,128)(2,1)S(1)}, bf16[32,1280]{1,0:T(8,128)(2,1)S(1)}, u32[]{:S(2)}, u32[]{:S(2)}) collective-permute-start(bf16[32,1280]{1,0:T(8,128)(2,1)S(1)} %get-tuple-element.48), channel_id=1, source_target_pairs={{0,3},{1,0},{2,1},{3,2},{4,7},{5,4},{6,5},{7,6},{8,11},{9,8},{10,9... | collective-permute-start | bytes 245768 | tf_op jit(solution)/shard_map/ppermute | solution.py:50
  17.9 4.7 %collective-permute-start.7 = (bf16[32,1280]{1,0:T(8,128)(2,1)S(1)}, bf16[32,1280]{1,0:T(8,128)(2,1)S(1)}, u32[]{:S(2)}, u32[]{:S(2)}) collective-permute-start(bf16[32,1280]{1,0:T(8,128)(2,1)S(1)} %shard_map.165.refs_2_), channel_id=1, source_target_pairs={{0,1},{1,2},{2,3},{3,0},{4,5},{5,6},{6,7},{7,4},{8,9},{9,10},{10,1... | collective-permute-start | bytes 245768 | tf_op jit(solution)/shard_map/ppermute | solution.py:50
  18.2 10.2 %collective-permute-start.8 = (bf16[32,1280]{1,0:T(8,128)(2,1)S(1)}, bf16[32,1280]{1,0:T(8,128)(2,1)S(1)}, u32[]{:S(2)}, u32[]{:S(2)}) collective-permute-start(bf16[32,1280]{1,0:T(8,128)(2,1)S(1)} %shard_map.165.refs_2_), channel_id=1, source_target_pairs={{0,2},{1,3},{2,0},{3,1},{4,6},{5,7},{6,4},{7,5},{8,10},{9,11},{10,... | collective-permute-start | bytes 245768 | tf_op jit(solution)/shard_map/ppermute | solution.py:50
  20.8 7.7 %collective-permute-start.9 = (bf16[32,1280]{1,0:T(8,128)(2,1)S(1)}, bf16[32,1280]{1,0:T(8,128)(2,1)S(1)}, u32[]{:S(2)}, u32[]{:S(2)}) collective-permute-start(bf16[32,1280]{1,0:T(8,128)(2,1)S(1)} %shard_map.165.refs_2_), channel_id=1, source_target_pairs={{0,3},{1,0},{2,1},{3,2},{4,7},{5,4},{6,5},{7,6},{8,11},{9,8},{10,9... | collective-permute-start | bytes 245768 | tf_op jit(solution)/shard_map/ppermute | solution.py:50
  22.4 6.6 %collective-permute-start.10 = (bf16[32,1280]{1,0:T(8,128)(2,1)S(1)}, bf16[32,1280]{1,0:T(8,128)(2,1)S(1)}, u32[]{:S(2)}, u32[]{:S(2)}) collective-permute-start(bf16[32,1280]{1,0:T(8,128)(2,1)S(1)} %shard_map.165.refs_2_), channel_id=1, source_target_pairs={{0,16},{16,0},{1,17},{17,1},{2,18},{18,2},{3,19},{19,3},{4,20},{20... | collective-permute-start | bytes 245768 | tf_op jit(solution)/shard_map/ppermute | solution.py:333
  22.5 11.1 %collective-permute-start.22 = (bf16[16,8192]{1,0:T(8,128)(2,1)S(1)}, bf16[16,8192]{1,0:T(8,128)(2,1)S(1)}, u32[]{:S(2)}, u32[]{:S(2)}) collective-permute-start(bf16[16,8192]{1,0:T(8,128)(2,1)S(1)} %bitcast.10), channel_id=1, source_target_pairs={{0,0},{1,2},{2,1},{3,3},{4,4},{5,6},{6,5},{7,7},{8,8},{9,10},{10,9... | collective-permute-start | bytes 786440 | tf_op jit(solution)/shard_map/ppermute | solution.py:346
  25.3 13.7 %collective-permute-start.23 = (bf16[16,8192]{1,0:T(8,128)(2,1)S(1)}, bf16[16,8192]{1,0:T(8,128)(2,1)S(1)}, u32[]{:S(2)}, u32[]{:S(2)}) collective-permute-start(bf16[16,8192]{1,0:T(8,128)(2,1)S(1)} %collective-permute-done.21.refs_2_), channel_id=1, source_target_pairs={{0,0},{1,2},{2,1},{3,3},{4,4},{5,6},{6,5},{7,7},{8,8},{9,10},{10,9... | collective-permute-start | bytes 786440 | tf_op jit(solution)/shard_map/ppermute | solution.py:346
  28.5 1.4 %collective-permute-start.12 = (bf16[32,1280]{1,0:T(8,128)(2,1)S(1)}, bf16[32,1280]{1,0:T(8,128)(2,1)S(1)}, u32[]{:S(2)}, u32[]{:S(2)}) collective-permute-start(bf16[32,1280]{1,0:T(8,128)(2,1)S(1)} %collective-permute-done.8.refs_4_), channel_id=1, source_target_pairs={{0,16},{16,0},{1,17},{17,1},{2,18},{18,2},{3,19},{19,3},{4,20},{20... | collective-permute-start | bytes 245768 | tf_op jit(solution)/shard_map/ppermute | solution.py:333
  32.0 1.6 %collective-permute-start.14 = (bf16[64,1024]{1,0:T(8,128)(2,1)S(1)}, bf16[64,1024]{1,0:T(8,128)(2,1)S(1)}, u32[]{:S(2)}, u32[]{:S(2)}) collective-permute-start(bf16[64,1024]{1,0:T(8,128)(2,1)S(1)} %get-tuple-element.53), channel_id=1, source_target_pairs={{0,16},{16,0},{1,17},{17,1},{2,18},{18,2},{3,19},{19,3},{4,20},{20... | collective-permute-start | bytes 393224 | tf_op jit(solution)/shard_map/ppermute | solution.py:333
  32.3 7.4 %collective-permute-start.15 = (bf16[64,1024]{1,0:T(8,128)(2,1)S(1)}, bf16[64,1024]{1,0:T(8,128)(2,1)S(1)}, u32[]{:S(2)}, u32[]{:S(2)}) collective-permute-start(bf16[64,1024]{1,0:T(8,128)(2,1)S(1)} %get-tuple-element.54), channel_id=1, source_target_pairs={{0,16},{16,0},{1,17},{17,1},{2,18},{18,2},{3,19},{19,3},{4,20},{20... | collective-permute-start | bytes 393224 | tf_op jit(solution)/shard_map/ppermute | solution.py:333
  32.6 7.1 %collective-permute-start.16 = (bf16[64,1024]{1,0:T(8,128)(2,1)S(1)}, bf16[64,1024]{1,0:T(8,128)(2,1)S(1)}, u32[]{:S(2)}, u32[]{:S(2)}) collective-permute-start(bf16[64,1024]{1,0:T(8,128)(2,1)S(1)} %get-tuple-element.55), channel_id=1, source_target_pairs={{0,16},{16,0},{1,17},{17,1},{2,18},{18,2},{3,19},{19,3},{4,20},{20... | collective-permute-start | bytes 393224 | tf_op jit(solution)/shard_map/ppermute | solution.py:333
  33.7 6.0 %collective-permute-start.17 = (bf16[64,1024]{1,0:T(8,128)(2,1)S(1)}, bf16[64,1024]{1,0:T(8,128)(2,1)S(1)}, u32[]{:S(2)}, u32[]{:S(2)}) collective-permute-start(bf16[64,1024]{1,0:T(8,128)(2,1)S(1)} %get-tuple-element.56), channel_id=1, source_target_pairs={{0,16},{16,0},{1,17},{17,1},{2,18},{18,2},{3,19},{19,3},{4,20},{20... | collective-permute-start | bytes 393224 | tf_op jit(solution)/shard_map/ppermute | solution.py:333
  33.7 21.4 %collective-permute-start.24 = (bf16[16,8192]{1,0:T(8,128)(2,1)S(1)}, bf16[16,8192]{1,0:T(8,128)(2,1)S(1)}, u32[]{:S(2)}, u32[]{:S(2)}) collective-permute-start(bf16[16,8192]{1,0:T(8,128)(2,1)S(1)} %collective-permute-done.22.refs_3_), channel_id=1, source_target_pairs={{0,1},{1,0},{2,3},{3,2},{4,5},{5,4},{6,7},{7,6},{8,9},{9,8},{10,11... | collective-permute-start | bytes 786440 | tf_op jit(solution)/shard_map/ppermute | solution.py:343
  39.0 16.0 %collective-permute-start.25 = (bf16[16,8192]{1,0:T(8,128)(2,1)S(1)}, bf16[16,8192]{1,0:T(8,128)(2,1)S(1)}, u32[]{:S(2)}, u32[]{:S(2)}) collective-permute-start(bf16[16,8192]{1,0:T(8,128)(2,1)S(1)} %collective-permute-done.23.refs_4_), channel_id=1, source_target_pairs={{0,1},{1,0},{2,3},{3,2},{4,5},{5,4},{6,7},{7,6},{8,9},{9,8},{10,11... | collective-permute-start | bytes 786440 | tf_op jit(solution)/shard_map/ppermute | solution.py:343
  39.9 11.3 %collective-permute-start.18 = (bf16[64,1024]{1,0:T(8,128)(2,1)S(1)}, bf16[64,1024]{1,0:T(8,128)(2,1)S(1)}, u32[]{:S(2)}, u32[]{:S(2)}) collective-permute-start(bf16[64,1024]{1,0:T(8,128)(2,1)S(1)} %get-tuple-element.58), channel_id=1, source_target_pairs={{0,1},{1,2},{2,3},{3,0},{4,5},{5,6},{6,7},{7,4},{8,9},{9,10},{10,1... | collective-permute-start | bytes 393224 | tf_op jit(solution)/shard_map/ppermute | solution.py:50
  40.4 13.9 %collective-permute-start.19 = (bf16[64,1024]{1,0:T(8,128)(2,1)S(1)}, bf16[64,1024]{1,0:T(8,128)(2,1)S(1)}, u32[]{:S(2)}, u32[]{:S(2)}) collective-permute-start(bf16[64,1024]{1,0:T(8,128)(2,1)S(1)} %get-tuple-element.59), channel_id=1, source_target_pairs={{0,2},{1,3},{2,0},{3,1},{4,6},{5,7},{6,4},{7,5},{8,10},{9,11},{10,... | collective-permute-start | bytes 393224 | tf_op jit(solution)/shard_map/ppermute | solution.py:50
  44.4 10.6 %collective-permute-start.20 = (bf16[64,1024]{1,0:T(8,128)(2,1)S(1)}, bf16[64,1024]{1,0:T(8,128)(2,1)S(1)}, u32[]{:S(2)}, u32[]{:S(2)}) collective-permute-start(bf16[64,1024]{1,0:T(8,128)(2,1)S(1)} %get-tuple-element.60), channel_id=1, source_target_pairs={{0,3},{1,0},{2,1},{3,2},{4,7},{5,4},{6,5},{7,6},{8,11},{9,8},{10,9... | collective-permute-start | bytes 393224 | tf_op jit(solution)/shard_map/ppermute | solution.py:50
  55.2 16.6 %collective-permute-start.26 = (bf16[4,16,8192]{2,1,0:T(8,128)(2,1)S(1)}, bf16[4,16,8192]{2,1,0:T(8,128)(2,1)S(1)}, u32[]{:S(2)}, u32[]{:S(2)}) collective-permute-start(bf16[4,16,8192]{2,1,0:T(8,128)(2,1)S(1)} %shard_map.171.refs_3_), channel_id=1, source_target_pairs={{0,16},{16,0},{1,17},{17,1},{2,18},{18,2},{3,19},{19,3},{4,20},{20... | collective-permute-start | bytes 3145736 | tf_op jit(solution)/shard_map/ppermute | solution.py:333
  55.3 11.7 %collective-permute-start.27 = (bf16[64,1024]{1,0:T(8,128)(2,1)S(1)}, bf16[64,1024]{1,0:T(8,128)(2,1)S(1)}, u32[]{:S(2)}, u32[]{:S(2)}) collective-permute-start(bf16[64,1024]{1,0:T(8,128)(2,1)S(1)} %shard_map.170.refs_0_.refs_4_), channel_id=1, source_target_pairs={{0,1},{1,2},{2,3},{3,0},{4,5},{5,6},{6,7},{7,4},{8,9},{9,10},{10,1... | collective-permute-start | bytes 393224 | tf_op jit(solution)/shard_map/ppermute | solution.py:50
  57.7 11.8 %collective-permute-start.28 = (bf16[64,1024]{1,0:T(8,128)(2,1)S(1)}, bf16[64,1024]{1,0:T(8,128)(2,1)S(1)}, u32[]{:S(2)}, u32[]{:S(2)}) collective-permute-start(bf16[64,1024]{1,0:T(8,128)(2,1)S(1)} %shard_map.170.refs_0_.refs_4_), channel_id=1, source_target_pairs={{0,2},{1,3},{2,0},{3,1},{4,6},{5,7},{6,4},{7,5},{8,10},{9,11},{10,... | collective-permute-start | bytes 393224 | tf_op jit(solution)/shard_map/ppermute | solution.py:50
  59.4 12.2 %collective-permute-start.29 = (bf16[64,1024]{1,0:T(8,128)(2,1)S(1)}, bf16[64,1024]{1,0:T(8,128)(2,1)S(1)}, u32[]{:S(2)}, u32[]{:S(2)}) collective-permute-start(bf16[64,1024]{1,0:T(8,128)(2,1)S(1)} %shard_map.170.refs_0_.refs_4_), channel_id=1, source_target_pairs={{0,3},{1,0},{2,1},{3,2},{4,7},{5,4},{6,5},{7,6},{8,11},{9,8},{10,9... | collective-permute-start | bytes 393224 | tf_op jit(solution)/shard_map/ppermute | solution.py:50
  61.2 11.5 %collective-permute-start.30 = (bf16[64,1024]{1,0:T(8,128)(2,1)S(1)}, bf16[64,1024]{1,0:T(8,128)(2,1)S(1)}, u32[]{:S(2)}, u32[]{:S(2)}) collective-permute-start(bf16[64,1024]{1,0:T(8,128)(2,1)S(1)} %shard_map.170.refs_0_.refs_4_), channel_id=1, source_target_pairs={{0,16},{16,0},{1,17},{17,1},{2,18},{18,2},{3,19},{19,3},{4,20},{20... | collective-permute-start | bytes 393224 | tf_op jit(solution)/shard_map/ppermute | solution.py:333
  66.9 5.8 %collective-permute-start.31 = (bf16[64,1024]{1,0:T(8,128)(2,1)S(1)}, bf16[64,1024]{1,0:T(8,128)(2,1)S(1)}, u32[]{:S(2)}, u32[]{:S(2)}) collective-permute-start(bf16[64,1024]{1,0:T(8,128)(2,1)S(1)} %collective-permute-done.27.refs_5_), channel_id=1, source_target_pairs={{0,16},{16,0},{1,17},{17,1},{2,18},{18,2},{3,19},{19,3},{4,20},{20... | collective-permute-start | bytes 393224 | tf_op jit(solution)/shard_map/ppermute | solution.py:333
  69.4 3.3 %collective-permute-start.32 = (bf16[64,1024]{1,0:T(8,128)(2,1)S(1)}, bf16[64,1024]{1,0:T(8,128)(2,1)S(1)}, u32[]{:S(2)}, u32[]{:S(2)}) collective-permute-start(bf16[64,1024]{1,0:T(8,128)(2,1)S(1)} %collective-permute-done.28.refs_6_), channel_id=1, source_target_pairs={{0,16},{16,0},{1,17},{17,1},{2,18},{18,2},{3,19},{19,3},{4,20},{20... | collective-permute-start | bytes 393224 | tf_op jit(solution)/shard_map/ppermute | solution.py:333
  74.0 4.9 %collective-permute-start.34 = (bf16[192,256]{1,0:T(8,128)(2,1)S(1)}, bf16[192,256]{1,0:T(8,128)(2,1)S(1)}, u32[]{:S(2)}, u32[]{:S(2)}) collective-permute-start(bf16[192,256]{1,0:T(8,128)(2,1)S(1)} %shard_map.173.refs_2_), channel_id=1, source_target_pairs={{0,4},{4,8},{8,12},{12,0},{1,5},{5,9},{9,13},{13,1},{2,6},{6,10},{... | collective-permute-start | bytes 294920 | tf_op jit(solution)/shard_map/ppermute | solution.py:50
  75.5 6.7 %collective-permute-start.35 = (bf16[192,256]{1,0:T(8,128)(2,1)S(1)}, bf16[192,256]{1,0:T(8,128)(2,1)S(1)}, u32[]{:S(2)}, u32[]{:S(2)}) collective-permute-start(bf16[192,256]{1,0:T(8,128)(2,1)S(1)} %shard_map.173.refs_2_), channel_id=1, source_target_pairs={{0,8},{4,12},{8,0},{12,4},{1,9},{5,13},{9,1},{13,5},{2,10},{6,14},... | collective-permute-start | bytes 294920 | tf_op jit(solution)/shard_map/ppermute | solution.py:50
  75.9 6.3 %collective-permute-start.36 = (bf16[192,256]{1,0:T(8,128)(2,1)S(1)}, bf16[192,256]{1,0:T(8,128)(2,1)S(1)}, u32[]{:S(2)}, u32[]{:S(2)}) collective-permute-start(bf16[192,256]{1,0:T(8,128)(2,1)S(1)} %shard_map.173.refs_2_), channel_id=1, source_target_pairs={{0,12},{4,0},{8,4},{12,8},{1,13},{5,1},{9,5},{13,9},{2,14},{6,2},{... | collective-permute-start | bytes 294920 | tf_op jit(solution)/shard_map/ppermute | solution.py:50
  (11 other events, 141.7 us)

commit v5 on v4

--- a/solution.py
+++ b/solution.py
@@ -240,13 +240,10 @@
         for k, piece in enumerate(pieces):
             out_ref[lax.rem(z - k + n_z, n_z)] = piece[...]
         return
-    own, near, mid_first, mid_second, far_first, far_second = pieces
-    low = z < 2
-    out_ref[z] = own[...]
-    out_ref[z + 1 - 2 * lax.rem(z, 2)] = near[...]
-    inner = (z == 1) | (z == 2)
-    out_ref[jnp.where(low, 2, 1)] = jnp.where(inner, mid_first[...], far_first[...])
-    out_ref[jnp.where(low, 3, 0)] = jnp.where(inner, mid_second[...], far_second[...])
+    pair = 1 - 2 * lax.rem(z, 2)
+    far = lax.rem(z + 2, n_z)
+    for at, piece in zip((z, z + pair, far, far + pair), pieces):
+        out_ref[at] = piece[...]
 
 
 def text_keyval_kernel(gain_ref, w_ref, b_ref, here_ref, there_ref, out_ref):
@@ -342,15 +339,16 @@
         def near(v):
             return lax.ppermute(v, "mp", [(0, 1), (1, 0), (2, 3), (3, 2)])
 
-        def middle(v):
-            return lax.ppermute(v, "mp", [(0, 0), (1, 2), (2, 1), (3, 3)])
-
-        near_own, middle_own = near(text_own), middle(text_own)
-        middle_near, near_middle = middle(near_own), near(middle_own)
-        near_last = near(middle_near)
-        text_pieces = [text_own, near_own, middle_own, middle_near, near_middle, near_last]
+        def across(v):
+            return lax.ppermute(v, "mp", [(0, 2), (2, 0), (1, 3), (3, 1)])
+
+        across_own, near_own = across(text_own), near(text_own)
+        near_across = near(across_own)
+        text_pieces = [text_own, near_own, across_own, near_across]
+        early, late = [across_own, near_own], [near_across]
     else:
         text_pieces = [text_own] + [shifted(text_own, "mp", n_z, k) for k in range(1, n_z)]
+        early, late = text_pieces[1:2], text_pieces[2:3]
 
     w = qkv_weight.transpose(1, 2, 0).reshape(3 * head_width, width)
     later = [merge_gain, merge_up.T, merge_up_bias, merge_down_bias, input_gain, kv_bias]
@@ -378,7 +376,7 @@
     )
     sums = [parts[0]] + [shifted(parts[k], "mp", n_z, k) for k in range(1, n_z)]
     merged, = call(
-        resid_kernel, [struct((block, width), BF16)], [base, gain] + sums)
+        resid_kernel, [struct((block, width), BF16)], [base, gain] + sums, after=early)
     pieces = spread(merged)
 
     hidden, = call(
@@ -393,6 +391,7 @@
             functools.partial(down_kernel, other),
             [struct((units, columns), BF16)] * n_z,
             [hidden, merge_down],
+            after=late if other else (),
             flops=units * merge_down.size,
             grant=16,
         )

time: 83.8 us -> 78.4 us (0.936)
  starting transfers between devices: 32 us -> 26.5 us
    ppermute x2 -> x1, waiting for transfers between devices: 6.23 us -> 0.56 us  [across(): return lax.ppermute(v, 'mp', [(0, 2), (2, 0), (1, 3), (3, 1)])]
    ppermute x15, waiting for transfers between devices: 32.5 us -> 37.2 us  [shifted(): return lax.ppermute(x, axis, [(i, (i + k) % count) for i in range(count)])]
    ppermute x2 -> x1, starting transfers between devices: 5.83 us -> 2.59 us  [across(): return lax.ppermute(v, 'mp', [(0, 2), (2, 0), (1, 3), (3, 1)])]
    ppermute x15, starting transfers between devices: 23.1 us -> 20 us  [shifted(): return lax.ppermute(x, axis, [(i, (i + k) % count) for i in range(count)])]
    ppermute x3 -> x2, starting transfers between devices: 0.45 us -> 1.84 us  [near(): return lax.ppermute(v, 'mp', [(0, 1), (1, 0), (2, 3), (3, 2)])]
    ppermute x17, waiting for transfers between devices: 2.42 us -> 3.8 us  [swap(): return lax.ppermute(v, 'section', [(0, 1), (1, 0)])]
  transfers between devices with their start and end apart: 37 -> 35, of which waited for: 22 -> 21; matrix products, arithmetic and copies ran while one was open for 0% -> 0% of each run, Pallas kernels for 9% -> 8%
where the time goes in v5:
time: 78.4 us; the launch traced here: 78.3 us
  waiting for transfers between devices  41.6 us (53%)
  starting transfers between devices  26.5 us (34%)
  Pallas kernels  9.92 us (13%)
    ppermute x15, waiting for transfers between devices, shifted(): return lax.ppermute(x, axis, [(i, (i + k) % count) for i in range(count)])  37.2 us
    ppermute x15, starting transfers between devices, shifted(): return lax.ppermute(x, axis, [(i, (i + k) % count) for i in range(count)])  20 us
    pallas_call x12, Pallas kernels, call(): pl.pallas_call(body, out_shape=outs, in_specs=[unread] * count + [scalar]...  9.92 us
    ppermute x17, waiting for transfers between devices, swap(): return lax.ppermute(v, 'section', [(0, 1), (1, 0)])  3.8 us
    ppermute x1, starting transfers between devices, across(): return lax.ppermute(v, 'mp', [(0, 2), (2, 0), (1, 3), (3, 1)])  2.59 us
    ppermute x17, starting transfers between devices, swap(): return lax.ppermute(v, 'section', [(0, 1), (1, 0)])  2.04 us
    ppermute x2, starting transfers between devices, near(): return lax.ppermute(v, 'mp', [(0, 1), (1, 0), (2, 3), (3, 2)])  1.84 us
  transfers between devices with their start and end apart: 35, of which 21 were waited for; matrix products, arithmetic and copies ran while one was open for 0% of the time, Pallas kernels for 8%

profile of v5, /device:TPU:10, one launch (start us, length us, event | category | flops | bytes accessed | tf_op | source)
XLA Modules:
  0.0 78.3 jit_solution(3161159868704781836)
XLA Ops:
  0.0 2.6 %collective-permute-start = (bf16[16,8192]{1,0:T(8,128)(2,1)}, bf16[16,8192]{1,0:T(8,128)(2,1)S(1)}, u32[]{:S(2)}, u32[]{:S(2)}) collective-permute-start(bf16[16,8192]{1,0:T(8,128)(2,1)} %bitcast.7), channel_id=1, source_target_pairs={{0,2},{2,0},{1,3},{3,1},{4,6},{6,4},{5,7},{7,5},{8,10},{10,8},{9,1... | collective-permute-start | bytes 786440 | tf_op jit(solution)/shard_map/ppermute | solution.py:343
  3.0 3.7 %shard_map.163 = (bf16[128,1280]{1,0:T(8,128)(2,1)S(1)}, f32[32,1280]{1,0:T(8,128)S(1)}, bf16[32,1280]{1,0:T(8,128)(2,1)S(1)}, bf16[32,1280]{1,0:T(8,128)(2,1)S(...) custom-call(s32[4,4,16]{2,1,0:T(4,128)} %refs_1_.5, ...), custom_call_target="tpu_custom_call" | custom-call | flops 419430400 | bytes 9825664 | tf_op jit(solution)/shard_map/pallas_call | solution.py:34
  7.4 0.7 collective-permute-done.2.refs_1_
  8.6 0.8 collective-permute-done.5.refs_4_
  10.1 3.5 %collective-permute-start.7 = (bf16[32,1280]{1,0:T(8,128)(2,1)S(1)}, bf16[32,1280]{1,0:T(8,128)(2,1)S(1)}, u32[]{:S(2)}, u32[]{:S(2)}) collective-permute-start(bf16[32,1280]{1,0:T(8,128)(2,1)S(1)} %get-tuple-element.47), channel_id=1, source_target_pairs={{0,2},{1,3},{2,0},{3,1},{4,6},{5,7},{6,4},{7,5},{8,10},{9,11},{10,... | collective-permute-start | bytes 245768 | tf_op jit(solution)/shard_map/ppermute | solution.py:50
  14.1 1.4 %collective-permute-start.16 = (bf16[16,8192]{1,0:T(8,128)(2,1)S(1)}, bf16[16,8192]{1,0:T(8,128)(2,1)S(1)}, u32[]{:S(2)}, u32[]{:S(2)}) collective-permute-start(bf16[16,8192]{1,0:T(8,128)(2,1)S(1)} %collective-permute-done.refs_0_.refs_3_), channel_id=1, source_target_pairs={{0,1},{1,0},{2,3},{3,2},{4,5},{5,4},{6,7},{7,6},{8,9},{9,8},{10,11... | collective-permute-start | bytes 786440 | tf_op jit(solution)/shard_map/ppermute | solution.py:340
  15.5 2.3 %collective-permute-done.6.refs_5_ = bf16[32,1280]{1,0:T(8,128)(2,1)S(1)} collective-permute-done((bf16[32,1280]{1,0:T(8,128)(2,1)S(1)}, bf16[32,1280]{1,0:T(8,128)(2,1)S(1)}, u32[]{:S(2)}, u32[]{:S(2)}) %collective-permute-start.6) | collective-permute-done | bytes 81952 | tf_op jit(solution)/shard_map/ppermute | solution.py:50
  17.8 3.1 %collective-permute-done.7.refs_6_ = bf16[32,1280]{1,0:T(8,128)(2,1)S(1)} collective-permute-done((bf16[32,1280]{1,0:T(8,128)(2,1)S(1)}, bf16[32,1280]{1,0:T(8,128)(2,1)S(1)}, u32[]{:S(2)}, u32[]{:S(2)}) %collective-permute-start.7) | collective-permute-done | bytes 81952 | tf_op jit(solution)/shard_map/ppermute | solution.py:50
  21.4 3.3 %collective-permute-start.10 = (bf16[32,1280]{1,0:T(8,128)(2,1)S(1)}, bf16[32,1280]{1,0:T(8,128)(2,1)S(1)}, u32[]{:S(2)}, u32[]{:S(2)}) collective-permute-start(bf16[32,1280]{1,0:T(8,128)(2,1)S(1)} %shard_map.165.refs_2_), channel_id=1, source_target_pairs={{0,2},{1,3},{2,0},{3,1},{4,6},{5,7},{6,4},{7,5},{8,10},{9,11},{10,... | collective-permute-start | bytes 245768 | tf_op jit(solution)/shard_map/ppermute | solution.py:50
  24.7 1.9 %collective-permute-start.11 = (bf16[32,1280]{1,0:T(8,128)(2,1)S(1)}, bf16[32,1280]{1,0:T(8,128)(2,1)S(1)}, u32[]{:S(2)}, u32[]{:S(2)}) collective-permute-start(bf16[32,1280]{1,0:T(8,128)(2,1)S(1)} %shard_map.165.refs_2_), channel_id=1, source_target_pairs={{0,3},{1,0},{2,1},{3,2},{4,7},{5,4},{6,5},{7,6},{8,11},{9,8},{10,9... | collective-permute-start | bytes 245768 | tf_op jit(solution)/shard_map/ppermute | solution.py:50
  26.6 1.7 %collective-permute-done.9.refs_3_ = bf16[32,1280]{1,0:T(8,128)(2,1)S(1)} collective-permute-done((bf16[32,1280]{1,0:T(8,128)(2,1)S(1)}, bf16[32,1280]{1,0:T(8,128)(2,1)S(1)}, u32[]{:S(2)}, u32[]{:S(2)}) %collective-permute-start.9) | collective-permute-done | bytes 81952 | tf_op jit(solution)/shard_map/ppermute | solution.py:50
  28.3 1.3 %collective-permute-done.10.refs_4_ = bf16[32,1280]{1,0:T(8,128)(2,1)S(1)} collective-permute-done((bf16[32,1280]{1,0:T(8,128)(2,1)S(1)}, bf16[32,1280]{1,0:T(8,128)(2,1)S(1)}, u32[]{:S(2)}, u32[]{:S(2)}) %collective-permute-start.10) | collective-permute-done | bytes 81952 | tf_op jit(solution)/shard_map/ppermute | solution.py:50
  29.6 2.9 %collective-permute-done.11.refs_5_ = bf16[32,1280]{1,0:T(8,128)(2,1)S(1)} collective-permute-done((bf16[32,1280]{1,0:T(8,128)(2,1)S(1)}, bf16[32,1280]{1,0:T(8,128)(2,1)S(1)}, u32[]{:S(2)}, u32[]{:S(2)}) %collective-permute-start.11) | collective-permute-done | bytes 81952 | tf_op jit(solution)/shard_map/ppermute | solution.py:50
  32.6 1.3 %collective-permute-done.15.refs_9_ = bf16[32,1280]{1,0:T(8,128)(2,1)S(1)} collective-permute-done((bf16[32,1280]{1,0:T(8,128)(2,1)S(1)}, bf16[32,1280]{1,0:T(8,128)(2,1)S(1)}, u32[]{:S(2)}, u32[]{:S(2)}) %collective-permute-start.15) | collective-permute-done | bytes 81952 | tf_op jit(solution)/shard_map/ppermute | solution.py:330
  33.9 1.1 %shard_map.166.refs_0_.refs_1_ = bf16[64,320]{1,0:T(8,128)(2,1)S(1)} custom-call(bf16[320,5120]{1,0:T(8,128)(2,1)S(1)} %get-tuple-element.36.refs_0_, f32[320]{0:T(512)S(1)} %get-tuple-element.37.refs_1_, bf16[32,1280]{1,0:T(8,128)(2,1)S(1)} %shard_map.165.refs_2_, bf16[32,1280]{1,0:T(8,128)(2,1)S(1)} %collective-permute-done.9.refs_3_, ...), custom_call_target="tpu_custom_call" | custom-call | flops 209715200 | bytes 3974400 | tf_op jit(solution)/shard_map/pallas_call | solution.py:34
  38.2 2.5 %collective-permute-start.22 = (bf16[64,1024]{1,0:T(8,128)(2,1)S(1)}, bf16[64,1024]{1,0:T(8,128)(2,1)S(1)}, u32[]{:S(2)}, u32[]{:S(2)}) collective-permute-start(bf16[64,1024]{1,0:T(8,128)(2,1)S(1)} %get-tuple-element.59), channel_id=1, source_target_pairs={{0,2},{1,3},{2,0},{3,1},{4,6},{5,7},{6,4},{7,5},{8,10},{9,11},{10,... | collective-permute-start | bytes 393224 | tf_op jit(solution)/shard_map/ppermute | solution.py:50
  40.7 1.5 %collective-permute-start.23 = (bf16[64,1024]{1,0:T(8,128)(2,1)S(1)}, bf16[64,1024]{1,0:T(8,128)(2,1)S(1)}, u32[]{:S(2)}, u32[]{:S(2)}) collective-permute-start(bf16[64,1024]{1,0:T(8,128)(2,1)S(1)} %get-tuple-element.60), channel_id=1, source_target_pairs={{0,3},{1,0},{2,1},{3,2},{4,7},{5,4},{6,5},{7,6},{8,11},{9,8},{10,9... | collective-permute-start | bytes 393224 | tf_op jit(solution)/shard_map/ppermute | solution.py:50
  42.2 2.2 %collective-permute-done.21.refs_2_ = bf16[64,1024]{1,0:T(8,128)(2,1)S(1)} collective-permute-done((bf16[64,1024]{1,0:T(8,128)(2,1)S(1)}, bf16[64,1024]{1,0:T(8,128)(2,1)S(1)}, u32[]{:S(2)}, u32[]{:S(2)}) %collective-permute-start.21) | collective-permute-done | bytes 131104 | tf_op jit(solution)/shard_map/ppermute | solution.py:50
  44.3 5.6 %collective-permute-done.22.refs_3_ = bf16[64,1024]{1,0:T(8,128)(2,1)S(1)} collective-permute-done((bf16[64,1024]{1,0:T(8,128)(2,1)S(1)}, bf16[64,1024]{1,0:T(8,128)(2,1)S(1)}, u32[]{:S(2)}, u32[]{:S(2)}) %collective-permute-start.22) | collective-permute-done | bytes 131104 | tf_op jit(solution)/shard_map/ppermute | solution.py:50
  50.0 2.7 %collective-permute-done.23.refs_4_ = bf16[64,1024]{1,0:T(8,128)(2,1)S(1)} collective-permute-done((bf16[64,1024]{1,0:T(8,128)(2,1)S(1)}, bf16[64,1024]{1,0:T(8,128)(2,1)S(1)}, u32[]{:S(2)}, u32[]{:S(2)}) %collective-permute-start.23) | collective-permute-done | bytes 131104 | tf_op jit(solution)/shard_map/ppermute | solution.py:50
  53.0 1.1 %collective-permute-start.26 = (bf16[64,1024]{1,0:T(8,128)(2,1)S(1)}, bf16[64,1024]{1,0:T(8,128)(2,1)S(1)}, u32[]{:S(2)}, u32[]{:S(2)}) collective-permute-start(bf16[64,1024]{1,0:T(8,128)(2,1)S(1)} %shard_map.170.refs_0_.refs_4_), channel_id=1, source_target_pairs={{0,2},{1,3},{2,0},{3,1},{4,6},{5,7},{6,4},{7,5},{8,10},{9,11},{10,... | collective-permute-start | bytes 393224 | tf_op jit(solution)/shard_map/ppermute | solution.py:50
  54.1 1.6 %collective-permute-start.27 = (bf16[64,1024]{1,0:T(8,128)(2,1)S(1)}, bf16[64,1024]{1,0:T(8,128)(2,1)S(1)}, u32[]{:S(2)}, u32[]{:S(2)}) collective-permute-start(bf16[64,1024]{1,0:T(8,128)(2,1)S(1)} %shard_map.170.refs_0_.refs_4_), channel_id=1, source_target_pairs={{0,3},{1,0},{2,1},{3,2},{4,7},{5,4},{6,5},{7,6},{8,11},{9,8},{10,9... | collective-permute-start | bytes 393224 | tf_op jit(solution)/shard_map/ppermute | solution.py:50
  55.7 3.6 %collective-permute-done.25.refs_5_ = bf16[64,1024]{1,0:T(8,128)(2,1)S(1)} collective-permute-done((bf16[64,1024]{1,0:T(8,128)(2,1)S(1)}, bf16[64,1024]{1,0:T(8,128)(2,1)S(1)}, u32[]{:S(2)}, u32[]{:S(2)}) %collective-permute-start.25) | collective-permute-done | bytes 131104 | tf_op jit(solution)/shard_map/ppermute | solution.py:50
  59.3 5.8 %collective-permute-done.26.refs_6_ = bf16[64,1024]{1,0:T(8,128)(2,1)S(1)} collective-permute-done((bf16[64,1024]{1,0:T(8,128)(2,1)S(1)}, bf16[64,1024]{1,0:T(8,128)(2,1)S(1)}, u32[]{:S(2)}, u32[]{:S(2)}) %collective-permute-start.26) | collective-permute-done | bytes 131104 | tf_op jit(solution)/shard_map/ppermute | solution.py:50
  65.1 1.3 %collective-permute-done.27.refs_7_ = bf16[64,1024]{1,0:T(8,128)(2,1)S(1)} collective-permute-done((bf16[64,1024]{1,0:T(8,128)(2,1)S(1)}, bf16[64,1024]{1,0:T(8,128)(2,1)S(1)}, u32[]{:S(2)}, u32[]{:S(2)}) %collective-permute-start.27) | collective-permute-done | bytes 131104 | tf_op jit(solution)/shard_map/ppermute | solution.py:50
  66.4 0.9 %shard_map.172.refs_0_ = bf16[128,256]{1,0:T(8,128)(2,1)S(1)} custom-call(f32[8192]{0:T(1024)S(1)} %get-tuple-element.33.refs_0_.refs_1_, bf16[8192,256]{1,0:T(8,128)(2,1)S(1)} %copy-done.1, f32[256]{0:T(256)S(1)} %get-tuple-element.34.refs_2_.refs_3_, bf16[4,16,8192]{2,1,0:T(8,128)(2,1)S(1)} %shard_map.171.refs_3_, ...), custom_call_target="tpu_custom_call" | custom-call | flops 536870912 | bytes 6390784 | tf_op jit(solution)/shard_map/pallas_call | solution.py:34
  67.7 0.9 %shard_map.173.refs_2_ = bf16[192,256]{1,0:T(8,128)(2,1)S(1)} custom-call(bf16[128,256]{1,0:T(8,128)(2,1)S(1)} %shard_map.172.refs_0_, f32[8192]{0:T(1024)S(1)} %get-tuple-element.33.refs_0_.refs_1_, bf16[8192,256]{1,0:T(8,128)(2,1)S(1)} %copy-done.1, f32[256]{0:T(256)S(1)} %get-tuple-element.34.refs_2_.refs_3_, ...), custom_call_target="tpu_custom_call" | custom-call | flops 268435456 | bytes 5440512 | tf_op jit(solution)/shard_map/pallas_call | solution.py:34
  68.6 1.5 %collective-permute-start.32 = (bf16[192,256]{1,0:T(8,128)(2,1)S(1)}, bf16[192,256]{1,0:T(8,128)(2,1)S(1)}, u32[]{:S(2)}, u32[]{:S(2)}) collective-permute-start(bf16[192,256]{1,0:T(8,128)(2,1)S(1)} %shard_map.173.refs_2_), channel_id=1, source_target_pairs={{0,4},{4,8},{8,12},{12,0},{1,5},{5,9},{9,13},{13,1},{2,6},{6,10},{... | collective-permute-start | bytes 294920 | tf_op jit(solution)/shard_map/ppermute | solution.py:50
  70.6 1.6 %collective-permute-start.34 = (bf16[192,256]{1,0:T(8,128)(2,1)S(1)}, bf16[192,256]{1,0:T(8,128)(2,1)S(1)}, u32[]{:S(2)}, u32[]{:S(2)}) collective-permute-start(bf16[192,256]{1,0:T(8,128)(2,1)S(1)} %shard_map.173.refs_2_), channel_id=1, source_target_pairs={{0,12},{4,0},{8,4},{12,8},{1,13},{5,1},{9,5},{13,9},{2,14},{6,2},{... | collective-permute-start | bytes 294920 | tf_op jit(solution)/shard_map/ppermute | solution.py:50
  72.2 1.3 %collective-permute-done.32.refs_3_ = bf16[192,256]{1,0:T(8,128)(2,1)S(1)} collective-permute-done((bf16[192,256]{1,0:T(8,128)(2,1)S(1)}, bf16[192,256]{1,0:T(8,128)(2,1)S(1)}, u32[]{:S(2)}, u32[]{:S(2)}) %collective-permute-start.32) | collective-permute-done | bytes 98336 | tf_op jit(solution)/shard_map/ppermute | solution.py:50
  73.5 3.4 %collective-permute-done.33.refs_4_ = bf16[192,256]{1,0:T(8,128)(2,1)S(1)} collective-permute-done((bf16[192,256]{1,0:T(8,128)(2,1)S(1)}, bf16[192,256]{1,0:T(8,128)(2,1)S(1)}, u32[]{:S(2)}, u32[]{:S(2)}) %collective-permute-start.33) | collective-permute-done | bytes 98336 | tf_op jit(solution)/shard_map/ppermute | solution.py:50
  76.8 1.4 %shard_map.174 = bf16[4,32,256]{2,1,0:T(8,128)(2,1)} custom-call(s32[4,4]{1,0:T(4,128)S(1)} %copy-done.4, s32[4,4,16]{2,1,0:T(4,128)S(1)} %copy-done.3, bf16[192,256]{1,0:T(8,128)(2,1)S(1)} %shard_map.173.refs_2_, bf16[192,256]{1,0:T(8,128)(2,1)S(1)} %collective-permute-done.32.refs_3_, bf16[192,256]{1,0:T(8,128)(2,1)S(1)} %collective-permute-done.33.refs_4_, ...), custom_call_target="tpu_custom_call" | custom-call | bytes 459840 | tf_op jit(solution)/shard_map/pallas_call | solution.py:34
  (60 shorter events, 7.6 us)
Async XLA Ops:
  0.0 14.1 %collective-permute-start = (bf16[16,8192]{1,0:T(8,128)(2,1)}, bf16[16,8192]{1,0:T(8,128)(2,1)S(1)}, u32[]{:S(2)}, u32[]{:S(2)}) collective-permute-start(bf16[16,8192]{1,0:T(8,128)(2,1)} %bitcast.7), channel_id=1, source_target_pairs={{0,2},{2,0},{1,3},{3,1},{4,6},{6,4},{5,7},{7,5},{8,10},{10,8},{9,1... | collective-permute-start | bytes 786440 | tf_op jit(solution)/shard_map/ppermute | solution.py:343
  2.6 18.4 %collective-permute-start.1 = (bf16[16,8192]{1,0:T(8,128)(2,1)}, bf16[16,8192]{1,0:T(8,128)(2,1)S(1)}, u32[]{:S(2)}, u32[]{:S(2)}) collective-permute-start(bf16[16,8192]{1,0:T(8,128)(2,1)} %bitcast.8), channel_id=1, source_target_pairs={{0,1},{1,0},{2,3},{3,2},{4,5},{5,4},{6,7},{7,6},{8,9},{9,8},{10,11... | collective-permute-start | bytes 786440 | tf_op jit(solution)/shard_map/ppermute | solution.py:340
  6.8 1.3 %collective-permute-start.2 = (bf16[32,1280]{1,0:T(8,128)(2,1)S(1)}, bf16[32,1280]{1,0:T(8,128)(2,1)S(1)}, u32[]{:S(2)}, u32[]{:S(2)}) collective-permute-start(bf16[32,1280]{1,0:T(8,128)(2,1)S(1)} %get-tuple-element.41), channel_id=1, source_target_pairs={{0,16},{16,0},{1,17},{17,1},{2,18},{18,2},{3,19},{19,3},{4,20},{20... | collective-permute-start | bytes 245768 | tf_op jit(solution)/shard_map/ppermute | solution.py:330
  6.9 1.4 %collective-permute-start.3 = (bf16[32,1280]{1,0:T(8,128)(2,1)S(1)}, bf16[32,1280]{1,0:T(8,128)(2,1)S(1)}, u32[]{:S(2)}, u32[]{:S(2)}) collective-permute-start(bf16[32,1280]{1,0:T(8,128)(2,1)S(1)} %get-tuple-element.42), channel_id=1, source_target_pairs={{0,16},{16,0},{1,17},{17,1},{2,18},{18,2},{3,19},{19,3},{4,20},{20... | collective-permute-start | bytes 245768 | tf_op jit(solution)/shard_map/ppermute | solution.py:330
  9.6 8.3 %collective-permute-start.6 = (bf16[32,1280]{1,0:T(8,128)(2,1)S(1)}, bf16[32,1280]{1,0:T(8,128)(2,1)S(1)}, u32[]{:S(2)}, u32[]{:S(2)}) collective-permute-start(bf16[32,1280]{1,0:T(8,128)(2,1)S(1)} %get-tuple-element.46), channel_id=1, source_target_pairs={{0,1},{1,2},{2,3},{3,0},{4,5},{5,6},{6,7},{7,4},{8,9},{9,10},{10,1... | collective-permute-start | bytes 245768 | tf_op jit(solution)/shard_map/ppermute | solution.py:50
  10.1 10.9 %collective-permute-start.7 = (bf16[32,1280]{1,0:T(8,128)(2,1)S(1)}, bf16[32,1280]{1,0:T(8,128)(2,1)S(1)}, u32[]{:S(2)}, u32[]{:S(2)}) collective-permute-start(bf16[32,1280]{1,0:T(8,128)(2,1)S(1)} %get-tuple-element.47), channel_id=1, source_target_pairs={{0,2},{1,3},{2,0},{3,1},{4,6},{5,7},{6,4},{7,5},{8,10},{9,11},{10,... | collective-permute-start | bytes 245768 | tf_op jit(solution)/shard_map/ppermute | solution.py:50
  13.5 7.4 %collective-permute-start.8 = (bf16[32,1280]{1,0:T(8,128)(2,1)S(1)}, bf16[32,1280]{1,0:T(8,128)(2,1)S(1)}, u32[]{:S(2)}, u32[]{:S(2)}) collective-permute-start(bf16[32,1280]{1,0:T(8,128)(2,1)S(1)} %get-tuple-element.48), channel_id=1, source_target_pairs={{0,3},{1,0},{2,1},{3,2},{4,7},{5,4},{6,5},{7,6},{8,11},{9,8},{10,9... | collective-permute-start | bytes 245768 | tf_op jit(solution)/shard_map/ppermute | solution.py:50
  14.1 20.9 %collective-permute-start.16 = (bf16[16,8192]{1,0:T(8,128)(2,1)S(1)}, bf16[16,8192]{1,0:T(8,128)(2,1)S(1)}, u32[]{:S(2)}, u32[]{:S(2)}) collective-permute-start(bf16[16,8192]{1,0:T(8,128)(2,1)S(1)} %collective-permute-done.refs_0_.refs_3_), channel_id=1, source_target_pairs={{0,1},{1,0},{2,3},{3,2},{4,5},{5,4},{6,7},{7,6},{8,9},{9,8},{10,11... | collective-permute-start | bytes 786440 | tf_op jit(solution)/shard_map/ppermute | solution.py:340
  21.1 7.2 %collective-permute-start.9 = (bf16[32,1280]{1,0:T(8,128)(2,1)S(1)}, bf16[32,1280]{1,0:T(8,128)(2,1)S(1)}, u32[]{:S(2)}, u32[]{:S(2)}) collective-permute-start(bf16[32,1280]{1,0:T(8,128)(2,1)S(1)} %shard_map.165.refs_2_), channel_id=1, source_target_pairs={{0,1},{1,2},{2,3},{3,0},{4,5},{5,6},{6,7},{7,4},{8,9},{9,10},{10,1... | collective-permute-start | bytes 245768 | tf_op jit(solution)/shard_map/ppermute | solution.py:50
  21.4 8.3 %collective-permute-start.10 = (bf16[32,1280]{1,0:T(8,128)(2,1)S(1)}, bf16[32,1280]{1,0:T(8,128)(2,1)S(1)}, u32[]{:S(2)}, u32[]{:S(2)}) collective-permute-start(bf16[32,1280]{1,0:T(8,128)(2,1)S(1)} %shard_map.165.refs_2_), channel_id=1, source_target_pairs={{0,2},{1,3},{2,0},{3,1},{4,6},{5,7},{6,4},{7,5},{8,10},{9,11},{10,... | collective-permute-start | bytes 245768 | tf_op jit(solution)/shard_map/ppermute | solution.py:50
  24.7 7.9 %collective-permute-start.11 = (bf16[32,1280]{1,0:T(8,128)(2,1)S(1)}, bf16[32,1280]{1,0:T(8,128)(2,1)S(1)}, u32[]{:S(2)}, u32[]{:S(2)}) collective-permute-start(bf16[32,1280]{1,0:T(8,128)(2,1)S(1)} %shard_map.165.refs_2_), channel_id=1, source_target_pairs={{0,3},{1,0},{2,1},{3,2},{4,7},{5,4},{6,5},{7,6},{8,11},{9,8},{10,9... | collective-permute-start | bytes 245768 | tf_op jit(solution)/shard_map/ppermute | solution.py:50
  26.6 6.0 %collective-permute-start.12 = (bf16[32,1280]{1,0:T(8,128)(2,1)S(1)}, bf16[32,1280]{1,0:T(8,128)(2,1)S(1)}, u32[]{:S(2)}, u32[]{:S(2)}) collective-permute-start(bf16[32,1280]{1,0:T(8,128)(2,1)S(1)} %shard_map.165.refs_2_), channel_id=1, source_target_pairs={{0,16},{16,0},{1,17},{17,1},{2,18},{18,2},{3,19},{19,3},{4,20},{20... | collective-permute-start | bytes 245768 | tf_op jit(solution)/shard_map/ppermute | solution.py:330
  28.3 4.3 %collective-permute-start.13 = (bf16[32,1280]{1,0:T(8,128)(2,1)S(1)}, bf16[32,1280]{1,0:T(8,128)(2,1)S(1)}, u32[]{:S(2)}, u32[]{:S(2)}) collective-permute-start(bf16[32,1280]{1,0:T(8,128)(2,1)S(1)} %collective-permute-done.9.refs_3_), channel_id=1, source_target_pairs={{0,16},{16,0},{1,17},{17,1},{2,18},{18,2},{3,19},{19,3},{4,20},{20... | collective-permute-start | bytes 245768 | tf_op jit(solution)/shard_map/ppermute | solution.py:330
  29.6 3.0 %collective-permute-start.14 = (bf16[32,1280]{1,0:T(8,128)(2,1)S(1)}, bf16[32,1280]{1,0:T(8,128)(2,1)S(1)}, u32[]{:S(2)}, u32[]{:S(2)}) collective-permute-start(bf16[32,1280]{1,0:T(8,128)(2,1)S(1)} %collective-permute-done.10.refs_4_), channel_id=1, source_target_pairs={{0,16},{16,0},{1,17},{17,1},{2,18},{18,2},{3,19},{19,3},{4,20},{20... | collective-permute-start | bytes 245768 | tf_op jit(solution)/shard_map/ppermute | solution.py:330
  35.6 1.7 %collective-permute-start.17 = (bf16[64,1024]{1,0:T(8,128)(2,1)S(1)}, bf16[64,1024]{1,0:T(8,128)(2,1)S(1)}, u32[]{:S(2)}, u32[]{:S(2)}) collective-permute-start(bf16[64,1024]{1,0:T(8,128)(2,1)S(1)} %get-tuple-element.53), channel_id=1, source_target_pairs={{0,16},{16,0},{1,17},{17,1},{2,18},{18,2},{3,19},{19,3},{4,20},{20... | collective-permute-start | bytes 393224 | tf_op jit(solution)/shard_map/ppermute | solution.py:330
  35.9 1.5 %collective-permute-start.18 = (bf16[64,1024]{1,0:T(8,128)(2,1)S(1)}, bf16[64,1024]{1,0:T(8,128)(2,1)S(1)}, u32[]{:S(2)}, u32[]{:S(2)}) collective-permute-start(bf16[64,1024]{1,0:T(8,128)(2,1)S(1)} %get-tuple-element.54), channel_id=1, source_target_pairs={{0,16},{16,0},{1,17},{17,1},{2,18},{18,2},{3,19},{19,3},{4,20},{20... | collective-permute-start | bytes 393224 | tf_op jit(solution)/shard_map/ppermute | solution.py:330
  36.2 1.3 %collective-permute-start.19 = (bf16[64,1024]{1,0:T(8,128)(2,1)S(1)}, bf16[64,1024]{1,0:T(8,128)(2,1)S(1)}, u32[]{:S(2)}, u32[]{:S(2)}) collective-permute-start(bf16[64,1024]{1,0:T(8,128)(2,1)S(1)} %get-tuple-element.55), channel_id=1, source_target_pairs={{0,16},{16,0},{1,17},{17,1},{2,18},{18,2},{3,19},{19,3},{4,20},{20... | collective-permute-start | bytes 393224 | tf_op jit(solution)/shard_map/ppermute | solution.py:330
  36.4 1.4 %collective-permute-start.20 = (bf16[64,1024]{1,0:T(8,128)(2,1)S(1)}, bf16[64,1024]{1,0:T(8,128)(2,1)S(1)}, u32[]{:S(2)}, u32[]{:S(2)}) collective-permute-start(bf16[64,1024]{1,0:T(8,128)(2,1)S(1)} %get-tuple-element.56), channel_id=1, source_target_pairs={{0,16},{16,0},{1,17},{17,1},{2,18},{18,2},{3,19},{19,3},{4,20},{20... | collective-permute-start | bytes 393224 | tf_op jit(solution)/shard_map/ppermute | solution.py:330
  37.9 6.4 %collective-permute-start.21 = (bf16[64,1024]{1,0:T(8,128)(2,1)S(1)}, bf16[64,1024]{1,0:T(8,128)(2,1)S(1)}, u32[]{:S(2)}, u32[]{:S(2)}) collective-permute-start(bf16[64,1024]{1,0:T(8,128)(2,1)S(1)} %get-tuple-element.58), channel_id=1, source_target_pairs={{0,1},{1,2},{2,3},{3,0},{4,5},{5,6},{6,7},{7,4},{8,9},{9,10},{10,1... | collective-permute-start | bytes 393224 | tf_op jit(solution)/shard_map/ppermute | solution.py:50
  38.2 11.7 %collective-permute-start.22 = (bf16[64,1024]{1,0:T(8,128)(2,1)S(1)}, bf16[64,1024]{1,0:T(8,128)(2,1)S(1)}, u32[]{:S(2)}, u32[]{:S(2)}) collective-permute-start(bf16[64,1024]{1,0:T(8,128)(2,1)S(1)} %get-tuple-element.59), channel_id=1, source_target_pairs={{0,2},{1,3},{2,0},{3,1},{4,6},{5,7},{6,4},{7,5},{8,10},{9,11},{10,... | collective-permute-start | bytes 393224 | tf_op jit(solution)/shard_map/ppermute | solution.py:50
  40.7 12.0 %collective-permute-start.23 = (bf16[64,1024]{1,0:T(8,128)(2,1)S(1)}, bf16[64,1024]{1,0:T(8,128)(2,1)S(1)}, u32[]{:S(2)}, u32[]{:S(2)}) collective-permute-start(bf16[64,1024]{1,0:T(8,128)(2,1)S(1)} %get-tuple-element.60), channel_id=1, source_target_pairs={{0,3},{1,0},{2,1},{3,2},{4,7},{5,4},{6,5},{7,6},{8,11},{9,8},{10,9... | collective-permute-start | bytes 393224 | tf_op jit(solution)/shard_map/ppermute | solution.py:50
  52.8 13.5 %collective-permute-start.24 = (bf16[4,16,8192]{2,1,0:T(8,128)(2,1)S(1)}, bf16[4,16,8192]{2,1,0:T(8,128)(2,1)S(1)}, u32[]{:S(2)}, u32[]{:S(2)}) collective-permute-start(bf16[4,16,8192]{2,1,0:T(8,128)(2,1)S(1)} %shard_map.171.refs_3_), channel_id=1, source_target_pairs={{0,16},{16,0},{1,17},{17,1},{2,18},{18,2},{3,19},{19,3},{4,20},{20... | collective-permute-start | bytes 3145736 | tf_op jit(solution)/shard_map/ppermute | solution.py:330
  52.9 6.3 %collective-permute-start.25 = (bf16[64,1024]{1,0:T(8,128)(2,1)S(1)}, bf16[64,1024]{1,0:T(8,128)(2,1)S(1)}, u32[]{:S(2)}, u32[]{:S(2)}) collective-permute-start(bf16[64,1024]{1,0:T(8,128)(2,1)S(1)} %shard_map.170.refs_0_.refs_4_), channel_id=1, source_target_pairs={{0,1},{1,2},{2,3},{3,0},{4,5},{5,6},{6,7},{7,4},{8,9},{9,10},{10,1... | collective-permute-start | bytes 393224 | tf_op jit(solution)/shard_map/ppermute | solution.py:50
  53.0 12.1 %collective-permute-start.26 = (bf16[64,1024]{1,0:T(8,128)(2,1)S(1)}, bf16[64,1024]{1,0:T(8,128)(2,1)S(1)}, u32[]{:S(2)}, u32[]{:S(2)}) collective-permute-start(bf16[64,1024]{1,0:T(8,128)(2,1)S(1)} %shard_map.170.refs_0_.refs_4_), channel_id=1, source_target_pairs={{0,2},{1,3},{2,0},{3,1},{4,6},{5,7},{6,4},{7,5},{8,10},{9,11},{10,... | collective-permute-start | bytes 393224 | tf_op jit(solution)/shard_map/ppermute | solution.py:50
  54.1 12.2 %collective-permute-start.27 = (bf16[64,1024]{1,0:T(8,128)(2,1)S(1)}, bf16[64,1024]{1,0:T(8,128)(2,1)S(1)}, u32[]{:S(2)}, u32[]{:S(2)}) collective-permute-start(bf16[64,1024]{1,0:T(8,128)(2,1)S(1)} %shard_map.170.refs_0_.refs_4_), channel_id=1, source_target_pairs={{0,3},{1,0},{2,1},{3,2},{4,7},{5,4},{6,5},{7,6},{8,11},{9,8},{10,9... | collective-permute-start | bytes 393224 | tf_op jit(solution)/shard_map/ppermute | solution.py:50
  55.7 11.6 %collective-permute-start.28 = (bf16[64,1024]{1,0:T(8,128)(2,1)S(1)}, bf16[64,1024]{1,0:T(8,128)(2,1)S(1)}, u32[]{:S(2)}, u32[]{:S(2)}) collective-permute-start(bf16[64,1024]{1,0:T(8,128)(2,1)S(1)} %shard_map.170.refs_0_.refs_4_), channel_id=1, source_target_pairs={{0,16},{16,0},{1,17},{17,1},{2,18},{18,2},{3,19},{19,3},{4,20},{20... | collective-permute-start | bytes 393224 | tf_op jit(solution)/shard_map/ppermute | solution.py:330
  59.3 8.0 %collective-permute-start.29 = (bf16[64,1024]{1,0:T(8,128)(2,1)S(1)}, bf16[64,1024]{1,0:T(8,128)(2,1)S(1)}, u32[]{:S(2)}, u32[]{:S(2)}) collective-permute-start(bf16[64,1024]{1,0:T(8,128)(2,1)S(1)} %collective-permute-done.25.refs_5_), channel_id=1, source_target_pairs={{0,16},{16,0},{1,17},{17,1},{2,18},{18,2},{3,19},{19,3},{4,20},{20... | collective-permute-start | bytes 393224 | tf_op jit(solution)/shard_map/ppermute | solution.py:330
  65.0 2.3 %collective-permute-start.30 = (bf16[64,1024]{1,0:T(8,128)(2,1)S(1)}, bf16[64,1024]{1,0:T(8,128)(2,1)S(1)}, u32[]{:S(2)}, u32[]{:S(2)}) collective-permute-start(bf16[64,1024]{1,0:T(8,128)(2,1)S(1)} %collective-permute-done.26.refs_6_), channel_id=1, source_target_pairs={{0,16},{16,0},{1,17},{17,1},{2,18},{18,2},{3,19},{19,3},{4,20},{20... | collective-permute-start | bytes 393224 | tf_op jit(solution)/shard_map/ppermute | solution.py:330
  66.3 1.3 %collective-permute-start.31 = (bf16[64,1024]{1,0:T(8,128)(2,1)S(1)}, bf16[64,1024]{1,0:T(8,128)(2,1)S(1)}, u32[]{:S(2)}, u32[]{:S(2)}) collective-permute-start(bf16[64,1024]{1,0:T(8,128)(2,1)S(1)} %collective-permute-done.27.refs_7_), channel_id=1, source_target_pairs={{0,16},{16,0},{1,17},{17,1},{2,18},{18,2},{3,19},{19,3},{4,20},{20... | collective-permute-start | bytes 393224 | tf_op jit(solution)/shard_map/ppermute | solution.py:330
  68.6 4.9 %collective-permute-start.32 = (bf16[192,256]{1,0:T(8,128)(2,1)S(1)}, bf16[192,256]{1,0:T(8,128)(2,1)S(1)}, u32[]{:S(2)}, u32[]{:S(2)}) collective-permute-start(bf16[192,256]{1,0:T(8,128)(2,1)S(1)} %shard_map.173.refs_2_), channel_id=1, source_target_pairs={{0,4},{4,8},{8,12},{12,0},{1,5},{5,9},{9,13},{13,1},{2,6},{6,10},{... | collective-permute-start | bytes 294920 | tf_op jit(solution)/shard_map/ppermute | solution.py:50
  70.1 6.7 %collective-permute-start.33 = (bf16[192,256]{1,0:T(8,128)(2,1)S(1)}, bf16[192,256]{1,0:T(8,128)(2,1)S(1)}, u32[]{:S(2)}, u32[]{:S(2)}) collective-permute-start(bf16[192,256]{1,0:T(8,128)(2,1)S(1)} %shard_map.173.refs_2_), channel_id=1, source_target_pairs={{0,8},{4,12},{8,0},{12,4},{1,9},{5,13},{9,1},{13,5},{2,10},{6,14},... | collective-permute-start | bytes 294920 | tf_op jit(solution)/shard_map/ppermute | solution.py:50
  70.6 6.2 %collective-permute-start.34 = (bf16[192,256]{1,0:T(8,128)(2,1)S(1)}, bf16[192,256]{1,0:T(8,128)(2,1)S(1)}, u32[]{:S(2)}, u32[]{:S(2)}) collective-permute-start(bf16[192,256]{1,0:T(8,128)(2,1)S(1)} %shard_map.173.refs_2_), channel_id=1, source_target_pairs={{0,12},{4,0},{8,4},{12,8},{1,13},{5,1},{9,5},{13,9},{2,14},{6,2},{... | collective-permute-start | bytes 294920 | tf_op jit(solution)/shard_map/ppermute | solution.py:50
  (8 other events, 97.2 us)

commit v6 on v5

--- a/solution.py
+++ b/solution.py
@@ -48,6 +48,10 @@
 
 def shifted(x, axis, count, k):
     return lax.ppermute(x, axis, [(i, (i + k) % count) for i in range(count)])
+
+
+def origin(z, k, n_z):
+    return lax.rem(z - k + n_z, n_z)
 
 
 def chunk_of(section, z, n_z):
@@ -169,7 +173,7 @@
     for side in range(2):
         section = c if side == 0 else 1 - c
         for k in range(n_z):
-            zz = lax.rem(z - k + n_z, n_z)
+            zz = origin(z, k, n_z)
             chunk = chunk_of(section, zz, n_z)
             at = pl.ds(pl.multiple_of(chunk * block, block), block)
             xs[lax.rem(zz, JOIN), at, :] = pieces[side * n_z + k][...]
@@ -213,24 +217,28 @@
     out_ref[...] = (total + bias_ref[at][None, :]).astype(BF16)
 
 
-def image_keyval_kernel(n_z, text_ref, gain_ref, w_ref, b_ref, *refs):
+def image_part_kernel(n_z, which, gain_ref, w_ref, *refs):
     c, z = lax.axis_index("section"), lax.axis_index("mp")
-    pieces, out_ref = refs[:-1], refs[-1]
+    pieces, (acc_ref, squares_ref) = refs[:-2], refs[-2:]
     rows, block = pieces[0].shape
-    prompt = text_ref.shape[0]
-    out_ref[:prompt, :] = text_ref[...]
-    acc = jnp.zeros((rows, out_ref.shape[1]), F32)
+    acc = jnp.zeros(acc_ref.shape, F32)
     squares = jnp.zeros((rows, 1), F32)
-    for side in range(2):
-        section = c if side == 0 else 1 - c
-        for k in range(n_z):
-            d = section * n_z + lax.rem(z - k + n_z, n_z)
-            at = pl.ds(pl.multiple_of(d * block, block), block)
-            x = pieces[side * n_z + k][...].astype(F32)
-            squares += jnp.sum(x * x, axis=-1, keepdims=True)
-            acc += jnp.dot((x * gain_ref[at][None, :]).astype(BF16), w_ref[at, :], preferred_element_type=F32)
-    scale = lax.rsqrt(squares * (1.0 / w_ref.shape[0]) + NORM_EPS)
-    out_ref[prompt:, :] = (acc * scale + b_ref[...][None, :]).astype(BF16)
+    for (side, k), piece in zip(which, pieces):
+        d = (c if side == 0 else 1 - c) * n_z + origin(z, k, n_z)
+        at = pl.ds(pl.multiple_of(d * block, block), block)
+        x = piece[...].astype(F32)
+        squares += jnp.sum(x * x, axis=-1, keepdims=True)
+        acc += jnp.dot((x * gain_ref[at][None, :]).astype(BF16), w_ref[at, :], preferred_element_type=F32)
+    acc_ref[...] = acc
+    squares_ref[...] = jnp.broadcast_to(squares, squares_ref.shape)
+
+
+def image_keyval_kernel(n_z, which, gain_ref, w_ref, b_ref, acc_ref, squares_ref, *refs):
+    pieces, (out_ref, acc, squares) = refs[:-3], refs[-3:]
+    image_part_kernel(n_z, which, gain_ref, w_ref, *pieces, acc, squares)
+    total = squares[:, :1] + squares_ref[:, :1]
+    scale = lax.rsqrt(total * (1.0 / w_ref.shape[0]) + NORM_EPS)
+    out_ref[...] = ((acc[...] + acc_ref[...]) * scale + b_ref[...][None, :]).astype(BF16)
 
 
 def relay_kernel(n_z, linear, *refs):
@@ -265,16 +273,16 @@
     out_ref[pl.ds(pl.multiple_of((1 - c) * half, half), half), :] = acc[half:]
 
 
-def place_kernel(n_s, slot_map, place_ref, *refs):
+def text_place_kernel(n_s, slot_map, place_ref, *refs):
     s = lax.axis_index("seq")
-    keyvals, (out_ref, held, texts) = refs[:n_s], refs[n_s:]
+    keyvals, (out_ref, pick_ref, held) = refs[:n_s], refs[n_s:]
     units = place_ref.shape[2]
-    prompt = n_s * CTX
+    group, width = n_s * units, pick_ref.shape[1]
     for k in range(n_s):
-        held[lax.rem(s - k + n_s, n_s)] = keyvals[k][prompt:, :]
+        held[lax.rem(s - k + n_s, n_s)] = keyvals[k][...]
     position = lax.broadcasted_iota(jnp.int32, (CTX, units), 0)
-    for k in range(n_s):
-        texts[lax.rem(s - k + n_s, n_s)] = keyvals[k][:prompt, :]
+    unit = lax.broadcasted_iota(jnp.int32, (units, width), 0)
+    lane = lax.broadcasted_iota(jnp.int32, (units, width), 1)
 
     def source(t):
         def look(n, found):
@@ -283,17 +291,23 @@
         found = lax.fori_loop(0, n_s * n_s, look, 0, unroll=n_s == 4)
         return found // n_s, found % n_s
 
-    def one(t):
+    for t in range(n_s):
         j, i = source(t)
-        chosen = position == place_ref[i, pl.ds(j, 1), :]
-        covered = jnp.sum(chosen.astype(F32), axis=1, keepdims=True) > 0.5
-        rows = held[i, pl.ds(pl.multiple_of(j * units, units), units), :]
-        image = jnp.dot(chosen.astype(BF16), rows, preferred_element_type=F32)
-        text = texts[j, pl.ds(pl.multiple_of(i * CTX, CTX), CTX), :]
-        out_ref[t] = jnp.where(covered, image, text.astype(F32)).astype(BF16)
-
-    for t in range(n_s):
-        one(t)
+        rows = slice(t * CTX, (t + 1) * CTX)
+        chosen = (position == place_ref[i, pl.ds(j, 1), :]).astype(F32)
+        covered = jnp.sum(chosen, axis=1, keepdims=True) > 0.5
+        text = held[j, pl.ds(pl.multiple_of(i * CTX, CTX), CTX), :]
+        out_ref[rows, :] = jnp.where(covered, 0.0, text.astype(F32))
+        shift = lax.rem(s - i + n_s, n_s)
+        spot = (lane == shift * group + j * units + unit).astype(BF16)
+        pick_ref[rows, :] = jnp.dot(chosen.astype(BF16), spot, preferred_element_type=F32).astype(BF16)
+
+
+def place_kernel(text_ref, pick_ref, *refs):
+    keyvals, out_ref = refs[:-1], refs[-1]
+    rows = jnp.concatenate([r[...] for r in keyvals], axis=0)
+    total = text_ref[...] + jnp.dot(pick_ref[...], rows, preferred_element_type=F32)
+    out_ref[...] = total.astype(BF16).reshape(out_ref.shape)
 
 
 def shards(
@@ -329,19 +343,21 @@
     def swap(v):
         return lax.ppermute(v, "section", [(0, 1), (1, 0)])
 
+    linear = n_z == 4
+
+    def near(v):
+        return lax.ppermute(v, "mp", [(0, 1), (1, 0), (2, 3), (3, 2)])
+
+    def across(v):
+        return lax.ppermute(v, "mp", [(0, 2), (2, 0), (1, 3), (3, 1)])
+
     def spread(own):
         here = [own] + [shifted(own, "mp", n_z, k) for k in range(1, n_z)]
         return here + [swap(v) for v in here]
 
     text_own = text[0]
-    linear = n_z == 4
+
     if linear:
-        def near(v):
-            return lax.ppermute(v, "mp", [(0, 1), (1, 0), (2, 3), (3, 2)])
-
-        def across(v):
-            return lax.ppermute(v, "mp", [(0, 2), (2, 0), (1, 3), (3, 1)])
-
         across_own, near_own = across(text_own), near(text_own)
         near_across = near(across_own)
         text_pieces = [text_own, near_own, across_own, near_across]
@@ -403,12 +419,8 @@
         [*keeps, *(swap(v) for v in sends)],
     )
     sums = [parts[0]] + [shifted(parts[k], "mp", n_z, k) for k in range(1, n_z)]
-    image, = call(
-        functools.partial(image_kernel, n_z), [struct((units, columns), BF16)], [down_bias] + sums)
-    image_pieces = spread(image)
-
     line, = call(
-        functools.partial(relay_kernel, n_z, linear), [struct((n_z,) + text_own.shape, BF16)], text_pieces, after=[image])
+        functools.partial(relay_kernel, n_z, linear), [struct((n_z,) + text_own.shape, BF16)], text_pieces, after=parts[:1])
     prompt = n_d * text.shape[1]
     text_keyval, = call(
         text_keyval_kernel,
@@ -417,23 +429,39 @@
         flops=2 * prompt * model * kv_width,
         grant=16,
     )
-
+    texts = [text_keyval] + [shifted(text_keyval, "seq", n_s, k) for k in range(1, n_s)]
+    image, = call(
+        functools.partial(image_kernel, n_z), [struct((units, columns), BF16)], [down_bias] + sums, after=texts[1:])
+    image_pieces = spread(image)
+
+    text_placed, pick = call(
+        functools.partial(text_place_kernel, n_s),
+        [struct((n_s * CTX, kv_width), F32), struct((n_s * CTX, n_s * units), BF16)],
+        [slot_map, image_place] + texts,
+        scratch=[pltpu.VMEM((n_s, prompt, kv_width), BF16)],
+        smem=1,
+        grant=24,
+    )
+
+    sides = [(i // n_z, i % n_z) for i in range(2 * n_z)]
+    first, last = ([s for s in sides if (s[1] == n_z - 1) == end] for end in (False, True))
+    acc, squares = call(
+        functools.partial(image_part_kernel, n_z, first),
+        [struct((units, kv_width), F32), struct((units, 128), F32)],
+        [text_gain, kv_weight] + [image_pieces[side * n_z + k] for side, k in first],
+        flops=units * model * kv_width,
+        grant=16,
+    )
     keyval, = call(
-        functools.partial(image_keyval_kernel, n_z),
-        [struct((prompt + units, kv_width), BF16)],
-        [text_keyval, text_gain, kv_weight, bias] + image_pieces,
-        flops=2 * units * model * kv_width,
+        functools.partial(image_keyval_kernel, n_z, last),
+        [struct((units, kv_width), BF16)],
+        [text_gain, kv_weight, bias, acc, squares] + [image_pieces[side * n_z + k] for side, k in last],
+        scratch=[pltpu.VMEM((units, kv_width), F32), pltpu.VMEM((units, 128), F32)],
         grant=16,
     )
     keyvals = [keyval] + [shifted(keyval, "seq", n_s, k) for k in range(1, n_s)]
     cache, = call(
-        functools.partial(place_kernel, n_s),
-        [struct((n_s, CTX, kv_width), BF16)],
-        [slot_map, image_place] + keyvals,
-        scratch=[pltpu.VMEM((n_s, units, kv_width), BF16), pltpu.VMEM((n_s, prompt, kv_width), BF16)],
-        smem=1,
-        grant=16,
-    )
+        place_kernel, [struct((n_s, CTX, kv_width), BF16)], [text_placed, pick] + keyvals, grant=24)
     return cache[None]
 
 

time: 78.4 us -> 76.2 us (0.972)
  waiting for transfers between devices: 41.6 us -> 34.8 us
  starting transfers between devices: 26.5 us -> 30.1 us
    ppermute x15 -> x18, waiting for transfers between devices: 37.2 us -> 30.2 us  [shifted(): return lax.ppermute(x, axis, [(i, (i + k) % count) for i in range(count)])]
    ppermute x15 -> x18, starting transfers between devices: 20 us -> 23.4 us  [shifted(): return lax.ppermute(x, axis, [(i, (i + k) % count) for i in range(count)])]
    pallas_call x12 -> x14, Pallas kernels: 9.92 us -> 10.2 us  [call(): pl.pallas_call(body, out_shape=outs, in_specs=[unread] * count + [scalar]...]
  transfers between devices with their start and end apart: 35 -> 38, of which waited for: 21 -> 21; matrix products, arithmetic and copies ran while one was open for 0% -> 0% of each run, Pallas kernels for 8% -> 11%
where the time goes in v6:
time: 76.2 us; the launch traced here: 75.4 us
  waiting for transfers between devices  34.8 us (46%)
  starting transfers between devices  30.1 us (40%)
  Pallas kernels  10.2 us (13%)
    ppermute x18, waiting for transfers between devices, shifted(): return lax.ppermute(x, axis, [(i, (i + k) % count) for i in range(count)])  30.2 us
    ppermute x18, starting transfers between devices, shifted(): return lax.ppermute(x, axis, [(i, (i + k) % count) for i in range(count)])  23.4 us
    pallas_call x14, Pallas kernels, call(): pl.pallas_call(body, out_shape=outs, in_specs=[unread] * count + [scalar]...  10.2 us
    ppermute x17, waiting for transfers between devices, swap(): return lax.ppermute(v, 'section', [(0, 1), (1, 0)])  4.03 us
    ppermute x1, starting transfers between devices, across(): return lax.ppermute(v, 'mp', [(0, 2), (2, 0), (1, 3), (3, 1)])  2.59 us
    ppermute x17, starting transfers between devices, swap(): return lax.ppermute(v, 'section', [(0, 1), (1, 0)])  2.31 us
    ppermute x2, starting transfers between devices, near(): return lax.ppermute(v, 'mp', [(0, 1), (1, 0), (2, 3), (3, 2)])  1.84 us
  transfers between devices with their start and end apart: 38, of which 21 were waited for; matrix products, arithmetic and copies ran while one was open for 0% of the time, Pallas kernels for 11%

profile of v6, /device:TPU:10, one launch (start us, length us, event | category | flops | bytes accessed | tf_op | source)
XLA Modules:
  0.0 75.4 jit_solution(10628676140195095546)
XLA Ops:
  0.0 2.6 %collective-permute-start = (bf16[16,8192]{1,0:T(8,128)(2,1)}, bf16[16,8192]{1,0:T(8,128)(2,1)S(1)}, u32[]{:S(2)}, u32[]{:S(2)}) collective-permute-start(bf16[16,8192]{1,0:T(8,128)(2,1)} %bitcast.7), channel_id=1, source_target_pairs={{0,2},{2,0},{1,3},{3,1},{4,6},{6,4},{5,7},{7,5},{8,10},{10,8},{9,1... | collective-permute-start | bytes 786440 | tf_op jit(solution)/shard_map/ppermute | solution.py:352
  3.0 3.7 %shard_map.163 = (bf16[128,1280]{1,0:T(8,128)(2,1)S(1)}, f32[32,1280]{1,0:T(8,128)S(1)}, bf16[32,1280]{1,0:T(8,128)(2,1)S(1)}, bf16[32,1280]{1,0:T(8,128)(2,1)S(...) custom-call(s32[4,4,16]{2,1,0:T(4,128)} %refs_1_.7, ...), custom_call_target="tpu_custom_call" | custom-call | flops 419430400 | bytes 9825664 | tf_op jit(solution)/shard_map/pallas_call | solution.py:34
  8.6 0.8 %collective-permute-done.5.refs_4_ = bf16[32,1280]{1,0:T(8,128)(2,1)S(1)} collective-permute-done((bf16[32,1280]{1,0:T(8,128)(2,1)S(1)}, bf16[32,1280]{1,0:T(8,128)(2,1)S(1)}, u32[]{:S(2)}, u32[]{:S(2)}) %collective-permute-start.5) | collective-permute-done | bytes 81952 | tf_op jit(solution)/shard_map/ppermute | solution.py:344
  10.1 3.5 %collective-permute-start.7 = (bf16[32,1280]{1,0:T(8,128)(2,1)S(1)}, bf16[32,1280]{1,0:T(8,128)(2,1)S(1)}, u32[]{:S(2)}, u32[]{:S(2)}) collective-permute-start(bf16[32,1280]{1,0:T(8,128)(2,1)S(1)} %get-tuple-element.50), channel_id=1, source_target_pairs={{0,2},{1,3},{2,0},{3,1},{4,6},{5,7},{6,4},{7,5},{8,10},{9,11},{10,... | collective-permute-start | bytes 245768 | tf_op jit(solution)/shard_map/ppermute | solution.py:50
  14.1 1.4 %collective-permute-start.16 = (bf16[16,8192]{1,0:T(8,128)(2,1)S(1)}, bf16[16,8192]{1,0:T(8,128)(2,1)S(1)}, u32[]{:S(2)}, u32[]{:S(2)}) collective-permute-start(bf16[16,8192]{1,0:T(8,128)(2,1)S(1)} %collective-permute-done.refs_0_.refs_3_), channel_id=1, source_target_pairs={{0,1},{1,0},{2,3},{3,2},{4,5},{5,4},{6,7},{7,6},{8,9},{9,8},{10,11... | collective-permute-start | bytes 786440 | tf_op jit(solution)/shard_map/ppermute | solution.py:349
  15.5 2.3 %collective-permute-done.6.refs_5_ = bf16[32,1280]{1,0:T(8,128)(2,1)S(1)} collective-permute-done((bf16[32,1280]{1,0:T(8,128)(2,1)S(1)}, bf16[32,1280]{1,0:T(8,128)(2,1)S(1)}, u32[]{:S(2)}, u32[]{:S(2)}) %collective-permute-start.6) | collective-permute-done | bytes 81952 | tf_op jit(solution)/shard_map/ppermute | solution.py:50
  17.8 3.1 %collective-permute-done.7.refs_6_ = bf16[32,1280]{1,0:T(8,128)(2,1)S(1)} collective-permute-done((bf16[32,1280]{1,0:T(8,128)(2,1)S(1)}, bf16[32,1280]{1,0:T(8,128)(2,1)S(1)}, u32[]{:S(2)}, u32[]{:S(2)}) %collective-permute-start.7) | collective-permute-done | bytes 81952 | tf_op jit(solution)/shard_map/ppermute | solution.py:50
  21.4 3.3 %collective-permute-start.10 = (bf16[32,1280]{1,0:T(8,128)(2,1)S(1)}, bf16[32,1280]{1,0:T(8,128)(2,1)S(1)}, u32[]{:S(2)}, u32[]{:S(2)}) collective-permute-start(bf16[32,1280]{1,0:T(8,128)(2,1)S(1)} %shard_map.165.refs_2_), channel_id=1, source_target_pairs={{0,2},{1,3},{2,0},{3,1},{4,6},{5,7},{6,4},{7,5},{8,10},{9,11},{10,... | collective-permute-start | bytes 245768 | tf_op jit(solution)/shard_map/ppermute | solution.py:50
  24.7 1.9 %collective-permute-start.11 = (bf16[32,1280]{1,0:T(8,128)(2,1)S(1)}, bf16[32,1280]{1,0:T(8,128)(2,1)S(1)}, u32[]{:S(2)}, u32[]{:S(2)}) collective-permute-start(bf16[32,1280]{1,0:T(8,128)(2,1)S(1)} %shard_map.165.refs_2_), channel_id=1, source_target_pairs={{0,3},{1,0},{2,1},{3,2},{4,7},{5,4},{6,5},{7,6},{8,11},{9,8},{10,9... | collective-permute-start | bytes 245768 | tf_op jit(solution)/shard_map/ppermute | solution.py:50
  26.6 1.7 %collective-permute-done.9.refs_3_ = bf16[32,1280]{1,0:T(8,128)(2,1)S(1)} collective-permute-done((bf16[32,1280]{1,0:T(8,128)(2,1)S(1)}, bf16[32,1280]{1,0:T(8,128)(2,1)S(1)}, u32[]{:S(2)}, u32[]{:S(2)}) %collective-permute-start.9) | collective-permute-done | bytes 81952 | tf_op jit(solution)/shard_map/ppermute | solution.py:50
  28.3 1.3 %collective-permute-done.10.refs_4_ = bf16[32,1280]{1,0:T(8,128)(2,1)S(1)} collective-permute-done((bf16[32,1280]{1,0:T(8,128)(2,1)S(1)}, bf16[32,1280]{1,0:T(8,128)(2,1)S(1)}, u32[]{:S(2)}, u32[]{:S(2)}) %collective-permute-start.10) | collective-permute-done | bytes 81952 | tf_op jit(solution)/shard_map/ppermute | solution.py:50
  29.7 2.9 %collective-permute-done.11.refs_5_ = bf16[32,1280]{1,0:T(8,128)(2,1)S(1)} collective-permute-done((bf16[32,1280]{1,0:T(8,128)(2,1)S(1)}, bf16[32,1280]{1,0:T(8,128)(2,1)S(1)}, u32[]{:S(2)}, u32[]{:S(2)}) %collective-permute-start.11) | collective-permute-done | bytes 81952 | tf_op jit(solution)/shard_map/ppermute | solution.py:50
  32.6 1.3 %collective-permute-done.15.refs_9_ = bf16[32,1280]{1,0:T(8,128)(2,1)S(1)} collective-permute-done((bf16[32,1280]{1,0:T(8,128)(2,1)S(1)}, bf16[32,1280]{1,0:T(8,128)(2,1)S(1)}, u32[]{:S(2)}, u32[]{:S(2)}) %collective-permute-start.15) | collective-permute-done | bytes 81952 | tf_op jit(solution)/shard_map/ppermute | solution.py:344
  33.9 1.1 %shard_map.166.refs_0_.refs_1_ = bf16[64,320]{1,0:T(8,128)(2,1)S(1)} custom-call(bf16[320,5120]{1,0:T(8,128)(2,1)S(1)} %get-tuple-element.39.refs_0_, f32[320]{0:T(512)S(1)} %get-tuple-element.40.refs_1_, bf16[32,1280]{1,0:T(8,128)(2,1)S(1)} %shard_map.165.refs_2_, bf16[32,1280]{1,0:T(8,128)(2,1)S(1)} %collective-permute-done.9.refs_3_, ...), custom_call_target="tpu_custom_call" | custom-call | flops 209715200 | bytes 3974400 | tf_op jit(solution)/shard_map/pallas_call | solution.py:34
  38.7 2.3 %collective-permute-start.26 = (bf16[64,1024]{1,0:T(8,128)(2,1)S(1)}, bf16[64,1024]{1,0:T(8,128)(2,1)S(1)}, u32[]{:S(2)}, u32[]{:S(2)}) collective-permute-start(bf16[64,1024]{1,0:T(8,128)(2,1)S(1)} %get-tuple-element.65), channel_id=1, source_target_pairs={{0,2},{1,3},{2,0},{3,1},{4,6},{5,7},{6,4},{7,5},{8,10},{9,11},{10,... | collective-permute-start | bytes 393224 | tf_op jit(solution)/shard_map/ppermute | solution.py:50
  41.0 1.6 %collective-permute-start.27 = (bf16[64,1024]{1,0:T(8,128)(2,1)S(1)}, bf16[64,1024]{1,0:T(8,128)(2,1)S(1)}, u32[]{:S(2)}, u32[]{:S(2)}) collective-permute-start(bf16[64,1024]{1,0:T(8,128)(2,1)S(1)} %get-tuple-element.66), channel_id=1, source_target_pairs={{0,3},{1,0},{2,1},{3,2},{4,7},{5,4},{6,5},{7,6},{8,11},{9,8},{10,9... | collective-permute-start | bytes 393224 | tf_op jit(solution)/shard_map/ppermute | solution.py:50
  42.6 0.9 %shard_map.171.refs_2_ = bf16[128,256]{1,0:T(8,128)(2,1)S(1)} custom-call(f32[8192]{0:T(1024)S(1)} %get-tuple-element.37.refs_0_, bf16[8192,256]{1,0:T(8,128)(2,1)S(1)} %copy-done, f32[256]{0:T(256)S(1)} %get-tuple-element.38.refs_2_, bf16[4,16,8192]{2,1,0:T(8,128)(2,1)S(1)} %shard_map.170.refs_3_, bf16[4,16,8192]{2,1,0:T(8,128)(2,1)S(1)} %collective-permute-done.21.refs_4_), custom_call_target="tpu_custom_call" | custom-call | flops 536870912 | bytes 6390784 | tf_op jit(solution)/shard_map/pallas_call | solution.py:34
  43.5 1.5 %collective-permute-start.22 = (bf16[128,256]{1,0:T(8,128)(2,1)S(1)}, bf16[128,256]{1,0:T(8,128)(2,1)S(1)}, u32[]{:S(2)}, u32[]{:S(2)}) collective-permute-start(bf16[128,256]{1,0:T(8,128)(2,1)S(1)} %shard_map.171.refs_2_), channel_id=1, source_target_pairs={{0,4},{4,8},{8,12},{12,0},{1,5},{5,9},{9,13},{13,1},{2,6},{6,10},{... | collective-permute-start | bytes 196616 | tf_op jit(solution)/shard_map/ppermute | solution.py:50
  45.6 1.5 %collective-permute-start.24 = (bf16[128,256]{1,0:T(8,128)(2,1)S(1)}, bf16[128,256]{1,0:T(8,128)(2,1)S(1)}, u32[]{:S(2)}, u32[]{:S(2)}) collective-permute-start(bf16[128,256]{1,0:T(8,128)(2,1)S(1)} %shard_map.171.refs_2_), channel_id=1, source_target_pairs={{0,12},{4,0},{8,4},{12,8},{1,13},{5,1},{9,5},{13,9},{2,14},{6,2},{... | collective-permute-start | bytes 196616 | tf_op jit(solution)/shard_map/ppermute | solution.py:50
  47.1 3.2 %collective-permute-done.26.refs_6_ = bf16[64,1024]{1,0:T(8,128)(2,1)S(1)} collective-permute-done((bf16[64,1024]{1,0:T(8,128)(2,1)S(1)}, bf16[64,1024]{1,0:T(8,128)(2,1)S(1)}, u32[]{:S(2)}, u32[]{:S(2)}) %collective-permute-start.26) | collective-permute-done | bytes 131104 | tf_op jit(solution)/shard_map/ppermute | solution.py:50
  50.3 2.8 %collective-permute-done.27.refs_7_ = bf16[64,1024]{1,0:T(8,128)(2,1)S(1)} collective-permute-done((bf16[64,1024]{1,0:T(8,128)(2,1)S(1)}, bf16[64,1024]{1,0:T(8,128)(2,1)S(1)}, u32[]{:S(2)}, u32[]{:S(2)}) %collective-permute-start.27) | collective-permute-done | bytes 131104 | tf_op jit(solution)/shard_map/ppermute | solution.py:50
  53.3 1.2 %collective-permute-start.29 = (bf16[64,1024]{1,0:T(8,128)(2,1)S(1)}, bf16[64,1024]{1,0:T(8,128)(2,1)S(1)}, u32[]{:S(2)}, u32[]{:S(2)}) collective-permute-start(bf16[64,1024]{1,0:T(8,128)(2,1)S(1)} %shard_map.173.refs_2_), channel_id=1, source_target_pairs={{0,2},{1,3},{2,0},{3,1},{4,6},{5,7},{6,4},{7,5},{8,10},{9,11},{10,... | collective-permute-start | bytes 393224 | tf_op jit(solution)/shard_map/ppermute | solution.py:50
  54.5 1.3 %collective-permute-start.33 = (bf16[64,1024]{1,0:T(8,128)(2,1)S(1)}, bf16[64,1024]{1,0:T(8,128)(2,1)S(1)}, u32[]{:S(2)}, u32[]{:S(2)}) collective-permute-start(bf16[64,1024]{1,0:T(8,128)(2,1)S(1)} %shard_map.173.refs_2_), channel_id=1, source_target_pairs={{0,3},{1,0},{2,1},{3,2},{4,7},{5,4},{6,5},{7,6},{8,11},{9,8},{10,9... | collective-permute-start | bytes 393224 | tf_op jit(solution)/shard_map/ppermute | solution.py:50
  55.8 3.8 %collective-permute-done.28.refs_3_ = bf16[64,1024]{1,0:T(8,128)(2,1)S(1)} collective-permute-done((bf16[64,1024]{1,0:T(8,128)(2,1)S(1)}, bf16[64,1024]{1,0:T(8,128)(2,1)S(1)}, u32[]{:S(2)}, u32[]{:S(2)}) %collective-permute-start.28) | collective-permute-done | bytes 131104 | tf_op jit(solution)/shard_map/ppermute | solution.py:50
  59.6 5.3 %collective-permute-done.29.refs_4_ = bf16[64,1024]{1,0:T(8,128)(2,1)S(1)} collective-permute-done((bf16[64,1024]{1,0:T(8,128)(2,1)S(1)}, bf16[64,1024]{1,0:T(8,128)(2,1)S(1)}, u32[]{:S(2)}, u32[]{:S(2)}) %collective-permute-start.29) | collective-permute-done | bytes 131104 | tf_op jit(solution)/shard_map/ppermute | solution.py:50
  64.9 1.2 %collective-permute-done.33.refs_5_ = bf16[64,1024]{1,0:T(8,128)(2,1)S(1)} collective-permute-done((bf16[64,1024]{1,0:T(8,128)(2,1)S(1)}, bf16[64,1024]{1,0:T(8,128)(2,1)S(1)}, u32[]{:S(2)}, u32[]{:S(2)}) %collective-permute-start.33) | collective-permute-done | bytes 131104 | tf_op jit(solution)/shard_map/ppermute | solution.py:50
  67.8 1.5 %collective-permute-start.35 = (bf16[64,256]{1,0:T(8,128)(2,1)S(1)}, bf16[64,256]{1,0:T(8,128)(2,1)S(1)}, u32[]{:S(2)}, u32[]{:S(2)}) collective-permute-start(bf16[64,256]{1,0:T(8,128)(2,1)S(1)} %shard_map.175.refs_2_), channel_id=1, source_target_pairs={{0,4},{4,8},{8,12},{12,0},{1,5},{5,9},{9,13},{13,1},{2,6},{6,10},{... | collective-permute-start | bytes 98312 | tf_op jit(solution)/shard_map/ppermute | solution.py:50
  69.8 1.5 %collective-permute-start.37 = (bf16[64,256]{1,0:T(8,128)(2,1)S(1)}, bf16[64,256]{1,0:T(8,128)(2,1)S(1)}, u32[]{:S(2)}, u32[]{:S(2)}) collective-permute-start(bf16[64,256]{1,0:T(8,128)(2,1)S(1)} %shard_map.175.refs_2_), channel_id=1, source_target_pairs={{0,12},{4,0},{8,4},{12,8},{1,13},{5,1},{9,5},{13,9},{2,14},{6,2},{... | collective-permute-start | bytes 98312 | tf_op jit(solution)/shard_map/ppermute | solution.py:50
  71.4 0.8 %shard_map.172 = (f32[128,256]{1,0:T(8,128)S(1)}, bf16[128,256]{1,0:T(8,128)(2,1)S(1)}) custom-call(s32[4,4]{1,0:T(4,128)S(1)} %copy-done.4, s32[4,4,16]{2,1,0:T(4,128)S(1)} %copy-done.3, bf16[128,256]{1,0:T(8,128)(2,1)S(1)} %shard_map.171.refs_2_, bf16[128,256]{1,0:T(8,128)(2,1)S(1)} %collective-permute-done.22.refs_3_.refs_0_, ...), custom_call_target="tpu_custom_call" | custom-call | bytes 459840 | tf_op jit(solution)/shard_map/pallas_call | solution.py:34
  72.2 1.4 %collective-permute-done.36.refs_4_ = bf16[64,256]{1,0:T(8,128)(2,1)S(1)} collective-permute-done((bf16[64,256]{1,0:T(8,128)(2,1)S(1)}, bf16[64,256]{1,0:T(8,128)(2,1)S(1)}, u32[]{:S(2)}, u32[]{:S(2)}) %collective-permute-start.36) | collective-permute-done | bytes 32800 | tf_op jit(solution)/shard_map/ppermute | solution.py:50
  73.6 1.1 %collective-permute-done.37.refs_5_ = bf16[64,256]{1,0:T(8,128)(2,1)S(1)} collective-permute-done((bf16[64,256]{1,0:T(8,128)(2,1)S(1)}, bf16[64,256]{1,0:T(8,128)(2,1)S(1)}, u32[]{:S(2)}, u32[]{:S(2)}) %collective-permute-start.37) | collective-permute-done | bytes 32800 | tf_op jit(solution)/shard_map/ppermute | solution.py:50
  74.6 0.8 %shard_map.176 = bf16[4,32,256]{2,1,0:T(8,128)(2,1)} custom-call(f32[128,256]{1,0:T(8,128)S(1)} %get-tuple-element.61.refs_0_, bf16[128,256]{1,0:T(8,128)(2,1)S(1)} %get-tuple-element.62.refs_1_, bf16[64,256]{1,0:T(8,128)(2,1)S(1)} %shard_map.175.refs_2_, bf16[64,256]{1,0:T(8,128)(2,1)S(1)} %collective-permute-done.35.refs_3_, ...), custom_call_target="tpu_custom_call" | custom-call | bytes 393216 | tf_op jit(solution)/shard_map/pallas_call | solution.py:34
  (68 shorter events, 10.3 us)
Async XLA Ops:
  0.0 14.1 %collective-permute-start = (bf16[16,8192]{1,0:T(8,128)(2,1)}, bf16[16,8192]{1,0:T(8,128)(2,1)S(1)}, u32[]{:S(2)}, u32[]{:S(2)}) collective-permute-start(bf16[16,8192]{1,0:T(8,128)(2,1)} %bitcast.7), channel_id=1, source_target_pairs={{0,2},{2,0},{1,3},{3,1},{4,6},{6,4},{5,7},{7,5},{8,10},{10,8},{9,1... | collective-permute-start | bytes 786440 | tf_op jit(solution)/shard_map/ppermute | solution.py:352
  2.6 18.4 %collective-permute-start.1 = (bf16[16,8192]{1,0:T(8,128)(2,1)}, bf16[16,8192]{1,0:T(8,128)(2,1)S(1)}, u32[]{:S(2)}, u32[]{:S(2)}) collective-permute-start(bf16[16,8192]{1,0:T(8,128)(2,1)} %bitcast.8), channel_id=1, source_target_pairs={{0,1},{1,0},{2,3},{3,2},{4,5},{5,4},{6,7},{7,6},{8,9},{9,8},{10,11... | collective-permute-start | bytes 786440 | tf_op jit(solution)/shard_map/ppermute | solution.py:349
  6.9 1.4 %collective-permute-start.3 = (bf16[32,1280]{1,0:T(8,128)(2,1)S(1)}, bf16[32,1280]{1,0:T(8,128)(2,1)S(1)}, u32[]{:S(2)}, u32[]{:S(2)}) collective-permute-start(bf16[32,1280]{1,0:T(8,128)(2,1)S(1)} %get-tuple-element.45), channel_id=1, source_target_pairs={{0,16},{16,0},{1,17},{17,1},{2,18},{18,2},{3,19},{19,3},{4,20},{20... | collective-permute-start | bytes 245768 | tf_op jit(solution)/shard_map/ppermute | solution.py:344
  9.6 8.3 %collective-permute-start.6 = (bf16[32,1280]{1,0:T(8,128)(2,1)S(1)}, bf16[32,1280]{1,0:T(8,128)(2,1)S(1)}, u32[]{:S(2)}, u32[]{:S(2)}) collective-permute-start(bf16[32,1280]{1,0:T(8,128)(2,1)S(1)} %get-tuple-element.49), channel_id=1, source_target_pairs={{0,1},{1,2},{2,3},{3,0},{4,5},{5,6},{6,7},{7,4},{8,9},{9,10},{10,1... | collective-permute-start | bytes 245768 | tf_op jit(solution)/shard_map/ppermute | solution.py:50
  10.1 10.9 %collective-permute-start.7 = (bf16[32,1280]{1,0:T(8,128)(2,1)S(1)}, bf16[32,1280]{1,0:T(8,128)(2,1)S(1)}, u32[]{:S(2)}, u32[]{:S(2)}) collective-permute-start(bf16[32,1280]{1,0:T(8,128)(2,1)S(1)} %get-tuple-element.50), channel_id=1, source_target_pairs={{0,2},{1,3},{2,0},{3,1},{4,6},{5,7},{6,4},{7,5},{8,10},{9,11},{10,... | collective-permute-start | bytes 245768 | tf_op jit(solution)/shard_map/ppermute | solution.py:50
  13.5 7.4 %collective-permute-start.8 = (bf16[32,1280]{1,0:T(8,128)(2,1)S(1)}, bf16[32,1280]{1,0:T(8,128)(2,1)S(1)}, u32[]{:S(2)}, u32[]{:S(2)}) collective-permute-start(bf16[32,1280]{1,0:T(8,128)(2,1)S(1)} %get-tuple-element.51), channel_id=1, source_target_pairs={{0,3},{1,0},{2,1},{3,2},{4,7},{5,4},{6,5},{7,6},{8,11},{9,8},{10,9... | collective-permute-start | bytes 245768 | tf_op jit(solution)/shard_map/ppermute | solution.py:50
  14.1 20.9 %collective-permute-start.16 = (bf16[16,8192]{1,0:T(8,128)(2,1)S(1)}, bf16[16,8192]{1,0:T(8,128)(2,1)S(1)}, u32[]{:S(2)}, u32[]{:S(2)}) collective-permute-start(bf16[16,8192]{1,0:T(8,128)(2,1)S(1)} %collective-permute-done.refs_0_.refs_3_), channel_id=1, source_target_pairs={{0,1},{1,0},{2,3},{3,2},{4,5},{5,4},{6,7},{7,6},{8,9},{9,8},{10,11... | collective-permute-start | bytes 786440 | tf_op jit(solution)/shard_map/ppermute | solution.py:349
  21.1 7.2 %collective-permute-start.9 = (bf16[32,1280]{1,0:T(8,128)(2,1)S(1)}, bf16[32,1280]{1,0:T(8,128)(2,1)S(1)}, u32[]{:S(2)}, u32[]{:S(2)}) collective-permute-start(bf16[32,1280]{1,0:T(8,128)(2,1)S(1)} %shard_map.165.refs_2_), channel_id=1, source_target_pairs={{0,1},{1,2},{2,3},{3,0},{4,5},{5,6},{6,7},{7,4},{8,9},{9,10},{10,1... | collective-permute-start | bytes 245768 | tf_op jit(solution)/shard_map/ppermute | solution.py:50
  21.4 8.3 %collective-permute-start.10 = (bf16[32,1280]{1,0:T(8,128)(2,1)S(1)}, bf16[32,1280]{1,0:T(8,128)(2,1)S(1)}, u32[]{:S(2)}, u32[]{:S(2)}) collective-permute-start(bf16[32,1280]{1,0:T(8,128)(2,1)S(1)} %shard_map.165.refs_2_), channel_id=1, source_target_pairs={{0,2},{1,3},{2,0},{3,1},{4,6},{5,7},{6,4},{7,5},{8,10},{9,11},{10,... | collective-permute-start | bytes 245768 | tf_op jit(solution)/shard_map/ppermute | solution.py:50
  24.7 7.9 %collective-permute-start.11 = (bf16[32,1280]{1,0:T(8,128)(2,1)S(1)}, bf16[32,1280]{1,0:T(8,128)(2,1)S(1)}, u32[]{:S(2)}, u32[]{:S(2)}) collective-permute-start(bf16[32,1280]{1,0:T(8,128)(2,1)S(1)} %shard_map.165.refs_2_), channel_id=1, source_target_pairs={{0,3},{1,0},{2,1},{3,2},{4,7},{5,4},{6,5},{7,6},{8,11},{9,8},{10,9... | collective-permute-start | bytes 245768 | tf_op jit(solution)/shard_map/ppermute | solution.py:50
  26.6 6.0 %collective-permute-start.12 = (bf16[32,1280]{1,0:T(8,128)(2,1)S(1)}, bf16[32,1280]{1,0:T(8,128)(2,1)S(1)}, u32[]{:S(2)}, u32[]{:S(2)}) collective-permute-start(bf16[32,1280]{1,0:T(8,128)(2,1)S(1)} %shard_map.165.refs_2_), channel_id=1, source_target_pairs={{0,16},{16,0},{1,17},{17,1},{2,18},{18,2},{3,19},{19,3},{4,20},{20... | collective-permute-start | bytes 245768 | tf_op jit(solution)/shard_map/ppermute | solution.py:344
  28.3 4.3 %collective-permute-start.13 = (bf16[32,1280]{1,0:T(8,128)(2,1)S(1)}, bf16[32,1280]{1,0:T(8,128)(2,1)S(1)}, u32[]{:S(2)}, u32[]{:S(2)}) collective-permute-start(bf16[32,1280]{1,0:T(8,128)(2,1)S(1)} %collective-permute-done.9.refs_3_), channel_id=1, source_target_pairs={{0,16},{16,0},{1,17},{17,1},{2,18},{18,2},{3,19},{19,3},{4,20},{20... | collective-permute-start | bytes 245768 | tf_op jit(solution)/shard_map/ppermute | solution.py:344
  29.6 3.0 %collective-permute-start.14 = (bf16[32,1280]{1,0:T(8,128)(2,1)S(1)}, bf16[32,1280]{1,0:T(8,128)(2,1)S(1)}, u32[]{:S(2)}, u32[]{:S(2)}) collective-permute-start(bf16[32,1280]{1,0:T(8,128)(2,1)S(1)} %collective-permute-done.10.refs_4_), channel_id=1, source_target_pairs={{0,16},{16,0},{1,17},{17,1},{2,18},{18,2},{3,19},{19,3},{4,20},{20... | collective-permute-start | bytes 245768 | tf_op jit(solution)/shard_map/ppermute | solution.py:344
  35.7 1.7 %collective-permute-start.17 = (bf16[64,1024]{1,0:T(8,128)(2,1)S(1)}, bf16[64,1024]{1,0:T(8,128)(2,1)S(1)}, u32[]{:S(2)}, u32[]{:S(2)}) collective-permute-start(bf16[64,1024]{1,0:T(8,128)(2,1)S(1)} %get-tuple-element.56), channel_id=1, source_target_pairs={{0,16},{16,0},{1,17},{17,1},{2,18},{18,2},{3,19},{19,3},{4,20},{20... | collective-permute-start | bytes 393224 | tf_op jit(solution)/shard_map/ppermute | solution.py:344
  35.9 1.5 %collective-permute-start.18 = (bf16[64,1024]{1,0:T(8,128)(2,1)S(1)}, bf16[64,1024]{1,0:T(8,128)(2,1)S(1)}, u32[]{:S(2)}, u32[]{:S(2)}) collective-permute-start(bf16[64,1024]{1,0:T(8,128)(2,1)S(1)} %get-tuple-element.57), channel_id=1, source_target_pairs={{0,16},{16,0},{1,17},{17,1},{2,18},{18,2},{3,19},{19,3},{4,20},{20... | collective-permute-start | bytes 393224 | tf_op jit(solution)/shard_map/ppermute | solution.py:344
  36.2 1.3 %collective-permute-start.19 = (bf16[64,1024]{1,0:T(8,128)(2,1)S(1)}, bf16[64,1024]{1,0:T(8,128)(2,1)S(1)}, u32[]{:S(2)}, u32[]{:S(2)}) collective-permute-start(bf16[64,1024]{1,0:T(8,128)(2,1)S(1)} %get-tuple-element.58), channel_id=1, source_target_pairs={{0,16},{16,0},{1,17},{17,1},{2,18},{18,2},{3,19},{19,3},{4,20},{20... | collective-permute-start | bytes 393224 | tf_op jit(solution)/shard_map/ppermute | solution.py:344
  36.4 1.4 %collective-permute-start.20 = (bf16[64,1024]{1,0:T(8,128)(2,1)S(1)}, bf16[64,1024]{1,0:T(8,128)(2,1)S(1)}, u32[]{:S(2)}, u32[]{:S(2)}) collective-permute-start(bf16[64,1024]{1,0:T(8,128)(2,1)S(1)} %get-tuple-element.59), channel_id=1, source_target_pairs={{0,16},{16,0},{1,17},{17,1},{2,18},{18,2},{3,19},{19,3},{4,20},{20... | collective-permute-start | bytes 393224 | tf_op jit(solution)/shard_map/ppermute | solution.py:344
  38.1 4.5 %collective-permute-start.21 = (bf16[4,16,8192]{2,1,0:T(8,128)(2,1)S(1)}, bf16[4,16,8192]{2,1,0:T(8,128)(2,1)S(1)}, u32[]{:S(2)}, u32[]{:S(2)}) collective-permute-start(bf16[4,16,8192]{2,1,0:T(8,128)(2,1)S(1)} %shard_map.170.refs_3_), channel_id=1, source_target_pairs={{0,16},{16,0},{1,17},{17,1},{2,18},{18,2},{3,19},{19,3},{4,20},{20... | collective-permute-start | bytes 3145736 | tf_op jit(solution)/shard_map/ppermute | solution.py:344
  38.4 7.1 %collective-permute-start.25 = (bf16[64,1024]{1,0:T(8,128)(2,1)S(1)}, bf16[64,1024]{1,0:T(8,128)(2,1)S(1)}, u32[]{:S(2)}, u32[]{:S(2)}) collective-permute-start(bf16[64,1024]{1,0:T(8,128)(2,1)S(1)} %get-tuple-element.64), channel_id=1, source_target_pairs={{0,1},{1,2},{2,3},{3,0},{4,5},{5,6},{6,7},{7,4},{8,9},{9,10},{10,1... | collective-permute-start | bytes 393224 | tf_op jit(solution)/shard_map/ppermute | solution.py:50
  38.7 11.6 %collective-permute-start.26 = (bf16[64,1024]{1,0:T(8,128)(2,1)S(1)}, bf16[64,1024]{1,0:T(8,128)(2,1)S(1)}, u32[]{:S(2)}, u32[]{:S(2)}) collective-permute-start(bf16[64,1024]{1,0:T(8,128)(2,1)S(1)} %get-tuple-element.65), channel_id=1, source_target_pairs={{0,2},{1,3},{2,0},{3,1},{4,6},{5,7},{6,4},{7,5},{8,10},{9,11},{10,... | collective-permute-start | bytes 393224 | tf_op jit(solution)/shard_map/ppermute | solution.py:50
  41.0 12.1 %collective-permute-start.27 = (bf16[64,1024]{1,0:T(8,128)(2,1)S(1)}, bf16[64,1024]{1,0:T(8,128)(2,1)S(1)}, u32[]{:S(2)}, u32[]{:S(2)}) collective-permute-start(bf16[64,1024]{1,0:T(8,128)(2,1)S(1)} %get-tuple-element.66), channel_id=1, source_target_pairs={{0,3},{1,0},{2,1},{3,2},{4,7},{5,4},{6,5},{7,6},{8,11},{9,8},{10,9... | collective-permute-start | bytes 393224 | tf_op jit(solution)/shard_map/ppermute | solution.py:50
  43.5 9.6 %collective-permute-start.22 = (bf16[128,256]{1,0:T(8,128)(2,1)S(1)}, bf16[128,256]{1,0:T(8,128)(2,1)S(1)}, u32[]{:S(2)}, u32[]{:S(2)}) collective-permute-start(bf16[128,256]{1,0:T(8,128)(2,1)S(1)} %shard_map.171.refs_2_), channel_id=1, source_target_pairs={{0,4},{4,8},{8,12},{12,0},{1,5},{5,9},{9,13},{13,1},{2,6},{6,10},{... | collective-permute-start | bytes 196616 | tf_op jit(solution)/shard_map/ppermute | solution.py:50
  45.0 8.1 %collective-permute-start.23 = (bf16[128,256]{1,0:T(8,128)(2,1)S(1)}, bf16[128,256]{1,0:T(8,128)(2,1)S(1)}, u32[]{:S(2)}, u32[]{:S(2)}) collective-permute-start(bf16[128,256]{1,0:T(8,128)(2,1)S(1)} %shard_map.171.refs_2_), channel_id=1, source_target_pairs={{0,8},{4,12},{8,0},{12,4},{1,9},{5,13},{9,1},{13,5},{2,10},{6,14},... | collective-permute-start | bytes 196616 | tf_op jit(solution)/shard_map/ppermute | solution.py:50
  45.6 7.6 %collective-permute-start.24 = (bf16[128,256]{1,0:T(8,128)(2,1)S(1)}, bf16[128,256]{1,0:T(8,128)(2,1)S(1)}, u32[]{:S(2)}, u32[]{:S(2)}) collective-permute-start(bf16[128,256]{1,0:T(8,128)(2,1)S(1)} %shard_map.171.refs_2_), channel_id=1, source_target_pairs={{0,12},{4,0},{8,4},{12,8},{1,13},{5,1},{9,5},{13,9},{2,14},{6,2},{... | collective-permute-start | bytes 196616 | tf_op jit(solution)/shard_map/ppermute | solution.py:50
  53.2 6.4 %collective-permute-start.28 = (bf16[64,1024]{1,0:T(8,128)(2,1)S(1)}, bf16[64,1024]{1,0:T(8,128)(2,1)S(1)}, u32[]{:S(2)}, u32[]{:S(2)}) collective-permute-start(bf16[64,1024]{1,0:T(8,128)(2,1)S(1)} %shard_map.173.refs_2_), channel_id=1, source_target_pairs={{0,1},{1,2},{2,3},{3,0},{4,5},{5,6},{6,7},{7,4},{8,9},{9,10},{10,1... | collective-permute-start | bytes 393224 | tf_op jit(solution)/shard_map/ppermute | solution.py:50
  53.3 11.6 %collective-permute-start.29 = (bf16[64,1024]{1,0:T(8,128)(2,1)S(1)}, bf16[64,1024]{1,0:T(8,128)(2,1)S(1)}, u32[]{:S(2)}, u32[]{:S(2)}) collective-permute-start(bf16[64,1024]{1,0:T(8,128)(2,1)S(1)} %shard_map.173.refs_2_), channel_id=1, source_target_pairs={{0,2},{1,3},{2,0},{3,1},{4,6},{5,7},{6,4},{7,5},{8,10},{9,11},{10,... | collective-permute-start | bytes 393224 | tf_op jit(solution)/shard_map/ppermute | solution.py:50
  54.5 11.6 %collective-permute-start.33 = (bf16[64,1024]{1,0:T(8,128)(2,1)S(1)}, bf16[64,1024]{1,0:T(8,128)(2,1)S(1)}, u32[]{:S(2)}, u32[]{:S(2)}) collective-permute-start(bf16[64,1024]{1,0:T(8,128)(2,1)S(1)} %shard_map.173.refs_2_), channel_id=1, source_target_pairs={{0,3},{1,0},{2,1},{3,2},{4,7},{5,4},{6,5},{7,6},{8,11},{9,8},{10,9... | collective-permute-start | bytes 393224 | tf_op jit(solution)/shard_map/ppermute | solution.py:50
  55.8 10.3 %collective-permute-start.30 = (bf16[64,1024]{1,0:T(8,128)(2,1)S(1)}, bf16[64,1024]{1,0:T(8,128)(2,1)S(1)}, u32[]{:S(2)}, u32[]{:S(2)}) collective-permute-start(bf16[64,1024]{1,0:T(8,128)(2,1)S(1)} %shard_map.173.refs_2_), channel_id=1, source_target_pairs={{0,16},{16,0},{1,17},{17,1},{2,18},{18,2},{3,19},{19,3},{4,20},{20... | collective-permute-start | bytes 393224 | tf_op jit(solution)/shard_map/ppermute | solution.py:344
  59.6 6.5 %collective-permute-start.31 = (bf16[64,1024]{1,0:T(8,128)(2,1)S(1)}, bf16[64,1024]{1,0:T(8,128)(2,1)S(1)}, u32[]{:S(2)}, u32[]{:S(2)}) collective-permute-start(bf16[64,1024]{1,0:T(8,128)(2,1)S(1)} %collective-permute-done.28.refs_3_), channel_id=1, source_target_pairs={{0,16},{16,0},{1,17},{17,1},{2,18},{18,2},{3,19},{19,3},{4,20},{20... | collective-permute-start | bytes 393224 | tf_op jit(solution)/shard_map/ppermute | solution.py:344
  67.8 4.4 %collective-permute-start.35 = (bf16[64,256]{1,0:T(8,128)(2,1)S(1)}, bf16[64,256]{1,0:T(8,128)(2,1)S(1)}, u32[]{:S(2)}, u32[]{:S(2)}) collective-permute-start(bf16[64,256]{1,0:T(8,128)(2,1)S(1)} %shard_map.175.refs_2_), channel_id=1, source_target_pairs={{0,4},{4,8},{8,12},{12,0},{1,5},{5,9},{9,13},{13,1},{2,6},{6,10},{... | collective-permute-start | bytes 98312 | tf_op jit(solution)/shard_map/ppermute | solution.py:50
  69.3 4.3 %collective-permute-start.36 = (bf16[64,256]{1,0:T(8,128)(2,1)S(1)}, bf16[64,256]{1,0:T(8,128)(2,1)S(1)}, u32[]{:S(2)}, u32[]{:S(2)}) collective-permute-start(bf16[64,256]{1,0:T(8,128)(2,1)S(1)} %shard_map.175.refs_2_), channel_id=1, source_target_pairs={{0,8},{4,12},{8,0},{12,4},{1,9},{5,13},{9,1},{13,5},{2,10},{6,14},... | collective-permute-start | bytes 98312 | tf_op jit(solution)/shard_map/ppermute | solution.py:50
  69.8 4.8 %collective-permute-start.37 = (bf16[64,256]{1,0:T(8,128)(2,1)S(1)}, bf16[64,256]{1,0:T(8,128)(2,1)S(1)}, u32[]{:S(2)}, u32[]{:S(2)}) collective-permute-start(bf16[64,256]{1,0:T(8,128)(2,1)S(1)} %shard_map.175.refs_2_), channel_id=1, source_target_pairs={{0,12},{4,0},{8,4},{12,8},{1,13},{5,1},{9,5},{13,9},{2,14},{6,2},{... | collective-permute-start | bytes 98312 | tf_op jit(solution)/shard_map/ppermute | solution.py:50
  (11 other events, 53.4 us)

commit v7 on v6

--- a/solution.py
+++ b/solution.py
@@ -50,8 +50,8 @@
     return lax.ppermute(x, axis, [(i, (i + k) % count) for i in range(count)])
 
 
-def origin(z, k, n_z):
-    return lax.rem(z - k + n_z, n_z)
+def origin(z, k, n_z, hops):
+    return lax.bitwise_xor(z, jnp.int32(k)) if hops and n_z == 4 else lax.rem(z - k + n_z, n_z)
 
 
 def chunk_of(section, z, n_z):
@@ -173,7 +173,7 @@
     for side in range(2):
         section = c if side == 0 else 1 - c
         for k in range(n_z):
-            zz = origin(z, k, n_z)
+            zz = origin(z, k, n_z, False)
             chunk = chunk_of(section, zz, n_z)
             at = pl.ds(pl.multiple_of(chunk * block, block), block)
             xs[lax.rem(zz, JOIN), at, :] = pieces[side * n_z + k][...]
@@ -224,7 +224,7 @@
     acc = jnp.zeros(acc_ref.shape, F32)
     squares = jnp.zeros((rows, 1), F32)
     for (side, k), piece in zip(which, pieces):
-        d = (c if side == 0 else 1 - c) * n_z + origin(z, k, n_z)
+        d = (c if side == 0 else 1 - c) * n_z + origin(z, k, n_z, True)
         at = pl.ds(pl.multiple_of(d * block, block), block)
         x = piece[...].astype(F32)
         squares += jnp.sum(x * x, axis=-1, keepdims=True)
@@ -351,8 +351,15 @@
     def across(v):
         return lax.ppermute(v, "mp", [(0, 2), (2, 0), (1, 3), (3, 1)])
 
-    def spread(own):
-        here = [own] + [shifted(own, "mp", n_z, k) for k in range(1, n_z)]
+    def spread(own, hops):
+        if linear and hops:
+            far, beside = across(own), near(own)
+            here = [own, beside, far]
+            swapped = [swap(v) for v in here]
+            last = near(far)
+            return here + [last] + swapped + [swap(last)]
+        else:
+            here = [own] + [shifted(own, "mp", n_z, k) for k in range(1, n_z)]
         return here + [swap(v) for v in here]
 
     text_own = text[0]
@@ -393,7 +400,7 @@
     sums = [parts[0]] + [shifted(parts[k], "mp", n_z, k) for k in range(1, n_z)]
     merged, = call(
         resid_kernel, [struct((block, width), BF16)], [base, gain] + sums, after=early)
-    pieces = spread(merged)
+    pieces = spread(merged, False)
 
     hidden, = call(
         functools.partial(hidden_kernel, n_z, block),
@@ -432,7 +439,7 @@
     texts = [text_keyval] + [shifted(text_keyval, "seq", n_s, k) for k in range(1, n_s)]
     image, = call(
         functools.partial(image_kernel, n_z), [struct((units, columns), BF16)], [down_bias] + sums, after=texts[1:])
-    image_pieces = spread(image)
+    image_pieces = spread(image, True)
 
     text_placed, pick = call(
         functools.partial(text_place_kernel, n_s),

time: 76.2 us -> 76.1 us (level)
  starting transfers between devices: 30.1 us -> 29.2 us
    ppermute x18 -> x15, waiting for transfers between devices: 30.2 us -> 19.9 us  [shifted(): return lax.ppermute(x, axis, [(i, (i + k) % count) for i in range(count)])]
    ppermute x1 -> x2, waiting for transfers between devices: 0.56 us -> 6.81 us  [across(): return lax.ppermute(v, 'mp', [(0, 2), (2, 0), (1, 3), (3, 1)])]
    ppermute x2 -> x4, waiting for transfers between devices: 0.01 us -> 4.39 us  [near(): return lax.ppermute(v, 'mp', [(0, 1), (1, 0), (2, 3), (3, 2)])]
    ppermute x18 -> x15, starting transfers between devices: 23.4 us -> 20.8 us  [shifted(): return lax.ppermute(x, axis, [(i, (i + k) % count) for i in range(count)])]
    ppermute x1 -> x2, starting transfers between devices: 2.59 us -> 3.2 us  [across(): return lax.ppermute(v, 'mp', [(0, 2), (2, 0), (1, 3), (3, 1)])]
    ppermute x2 -> x4, starting transfers between devices: 1.84 us -> 2.31 us  [near(): return lax.ppermute(v, 'mp', [(0, 1), (1, 0), (2, 3), (3, 2)])]
  transfers between devices with their start and end apart: 38 -> 38, of which waited for: 21 -> 19; matrix products, arithmetic and copies ran while one was open for 0% -> 0% of each run, Pallas kernels for 11% -> 11%
where the time goes in v7:
time: 76.1 us; the launch traced here: 74.8 us
  waiting for transfers between devices  35.2 us (46%)
  starting transfers between devices  29.2 us (38%)
  Pallas kernels  10.2 us (13%)
    ppermute x15, starting transfers between devices, shifted(): return lax.ppermute(x, axis, [(i, (i + k) % count) for i in range(count)])  20.8 us
    ppermute x15, waiting for transfers between devices, shifted(): return lax.ppermute(x, axis, [(i, (i + k) % count) for i in range(count)])  19.9 us
    pallas_call x14, Pallas kernels, call(): pl.pallas_call(body, out_shape=outs, in_specs=[unread] * count + [scalar]...  10.2 us
    ppermute x2, waiting for transfers between devices, across(): return lax.ppermute(v, 'mp', [(0, 2), (2, 0), (1, 3), (3, 1)])  6.81 us
    ppermute x4, waiting for transfers between devices, near(): return lax.ppermute(v, 'mp', [(0, 1), (1, 0), (2, 3), (3, 2)])  4.39 us
    ppermute x17, waiting for transfers between devices, swap(): return lax.ppermute(v, 'section', [(0, 1), (1, 0)])  4.04 us
    ppermute x2, starting transfers between devices, across(): return lax.ppermute(v, 'mp', [(0, 2), (2, 0), (1, 3), (3, 1)])  3.2 us
    ppermute x17, starting transfers between devices, swap(): return lax.ppermute(v, 'section', [(0, 1), (1, 0)])  2.87 us
  transfers between devices with their start and end apart: 38, of which 19 were waited for; matrix products, arithmetic and copies ran while one was open for 0% of the time, Pallas kernels for 11%

profile of v7, /device:TPU:10, one launch (start us, length us, event | category | flops | bytes accessed | tf_op | source)
XLA Modules:
  0.0 74.8 jit_solution(11370281416733029351)
XLA Ops:
  0.0 2.6 %collective-permute-start = (bf16[16,8192]{1,0:T(8,128)(2,1)}, bf16[16,8192]{1,0:T(8,128)(2,1)S(1)}, u32[]{:S(2)}, u32[]{:S(2)}) collective-permute-start(bf16[16,8192]{1,0:T(8,128)(2,1)} %bitcast.7), channel_id=1, source_target_pairs={{0,2},{2,0},{1,3},{3,1},{4,6},{6,4},{5,7},{7,5},{8,10},{10,8},{9,1... | collective-permute-start | bytes 786440 | tf_op jit(solution)/shard_map/ppermute | solution.py:352
  3.0 3.7 %shard_map.163 = (bf16[128,1280]{1,0:T(8,128)(2,1)S(1)}, f32[32,1280]{1,0:T(8,128)S(1)}, bf16[32,1280]{1,0:T(8,128)(2,1)S(1)}, bf16[32,1280]{1,0:T(8,128)(2,1)S(...) custom-call(s32[4,4,16]{2,1,0:T(4,128)} %refs_1_.7, ...), custom_call_target="tpu_custom_call" | custom-call | flops 419430400 | bytes 9825664 | tf_op jit(solution)/shard_map/pallas_call | solution.py:34
  7.4 0.7 collective-permute-done.2.refs_1_
  8.6 0.8 %collective-permute-done.5.refs_4_ = bf16[32,1280]{1,0:T(8,128)(2,1)S(1)} collective-permute-done((bf16[32,1280]{1,0:T(8,128)(2,1)S(1)}, bf16[32,1280]{1,0:T(8,128)(2,1)S(1)}, u32[]{:S(2)}, u32[]{:S(2)}) %collective-permute-start.5) | collective-permute-done | bytes 81952 | tf_op jit(solution)/shard_map/ppermute | solution.py:344
  10.1 3.5 %collective-permute-start.7 = (bf16[32,1280]{1,0:T(8,128)(2,1)S(1)}, bf16[32,1280]{1,0:T(8,128)(2,1)S(1)}, u32[]{:S(2)}, u32[]{:S(2)}) collective-permute-start(bf16[32,1280]{1,0:T(8,128)(2,1)S(1)} %get-tuple-element.50), channel_id=1, source_target_pairs={{0,2},{1,3},{2,0},{3,1},{4,6},{5,7},{6,4},{7,5},{8,10},{9,11},{10,... | collective-permute-start | bytes 245768 | tf_op jit(solution)/shard_map/ppermute | solution.py:50
  14.1 1.4 %collective-permute-start.16 = (bf16[16,8192]{1,0:T(8,128)(2,1)S(1)}, bf16[16,8192]{1,0:T(8,128)(2,1)S(1)}, u32[]{:S(2)}, u32[]{:S(2)}) collective-permute-start(bf16[16,8192]{1,0:T(8,128)(2,1)S(1)} %collective-permute-done.refs_0_.refs_3_), channel_id=1, source_target_pairs={{0,1},{1,0},{2,3},{3,2},{4,5},{5,4},{6,7},{7,6},{8,9},{9,8},{10,11... | collective-permute-start | bytes 786440 | tf_op jit(solution)/shard_map/ppermute | solution.py:349
  15.5 2.3 %collective-permute-done.6.refs_5_ = bf16[32,1280]{1,0:T(8,128)(2,1)S(1)} collective-permute-done((bf16[32,1280]{1,0:T(8,128)(2,1)S(1)}, bf16[32,1280]{1,0:T(8,128)(2,1)S(1)}, u32[]{:S(2)}, u32[]{:S(2)}) %collective-permute-start.6) | collective-permute-done | bytes 81952 | tf_op jit(solution)/shard_map/ppermute | solution.py:50
  17.8 3.1 %collective-permute-done.7.refs_6_ = bf16[32,1280]{1,0:T(8,128)(2,1)S(1)} collective-permute-done((bf16[32,1280]{1,0:T(8,128)(2,1)S(1)}, bf16[32,1280]{1,0:T(8,128)(2,1)S(1)}, u32[]{:S(2)}, u32[]{:S(2)}) %collective-permute-start.7) | collective-permute-done | bytes 81952 | tf_op jit(solution)/shard_map/ppermute | solution.py:50
  21.4 3.3 %collective-permute-start.10 = (bf16[32,1280]{1,0:T(8,128)(2,1)S(1)}, bf16[32,1280]{1,0:T(8,128)(2,1)S(1)}, u32[]{:S(2)}, u32[]{:S(2)}) collective-permute-start(bf16[32,1280]{1,0:T(8,128)(2,1)S(1)} %shard_map.165.refs_2_), channel_id=1, source_target_pairs={{0,2},{1,3},{2,0},{3,1},{4,6},{5,7},{6,4},{7,5},{8,10},{9,11},{10,... | collective-permute-start | bytes 245768 | tf_op jit(solution)/shard_map/ppermute | solution.py:50
  24.7 1.9 %collective-permute-start.11 = (bf16[32,1280]{1,0:T(8,128)(2,1)S(1)}, bf16[32,1280]{1,0:T(8,128)(2,1)S(1)}, u32[]{:S(2)}, u32[]{:S(2)}) collective-permute-start(bf16[32,1280]{1,0:T(8,128)(2,1)S(1)} %shard_map.165.refs_2_), channel_id=1, source_target_pairs={{0,3},{1,0},{2,1},{3,2},{4,7},{5,4},{6,5},{7,6},{8,11},{9,8},{10,9... | collective-permute-start | bytes 245768 | tf_op jit(solution)/shard_map/ppermute | solution.py:50
  26.6 1.7 %collective-permute-done.9.refs_3_ = bf16[32,1280]{1,0:T(8,128)(2,1)S(1)} collective-permute-done((bf16[32,1280]{1,0:T(8,128)(2,1)S(1)}, bf16[32,1280]{1,0:T(8,128)(2,1)S(1)}, u32[]{:S(2)}, u32[]{:S(2)}) %collective-permute-start.9) | collective-permute-done | bytes 81952 | tf_op jit(solution)/shard_map/ppermute | solution.py:50
  28.3 1.3 %collective-permute-done.10.refs_4_ = bf16[32,1280]{1,0:T(8,128)(2,1)S(1)} collective-permute-done((bf16[32,1280]{1,0:T(8,128)(2,1)S(1)}, bf16[32,1280]{1,0:T(8,128)(2,1)S(1)}, u32[]{:S(2)}, u32[]{:S(2)}) %collective-permute-start.10) | collective-permute-done | bytes 81952 | tf_op jit(solution)/shard_map/ppermute | solution.py:50
  29.7 2.9 %collective-permute-done.11.refs_5_ = bf16[32,1280]{1,0:T(8,128)(2,1)S(1)} collective-permute-done((bf16[32,1280]{1,0:T(8,128)(2,1)S(1)}, bf16[32,1280]{1,0:T(8,128)(2,1)S(1)}, u32[]{:S(2)}, u32[]{:S(2)}) %collective-permute-start.11) | collective-permute-done | bytes 81952 | tf_op jit(solution)/shard_map/ppermute | solution.py:50
  32.6 1.3 %collective-permute-done.15.refs_9_ = bf16[32,1280]{1,0:T(8,128)(2,1)S(1)} collective-permute-done((bf16[32,1280]{1,0:T(8,128)(2,1)S(1)}, bf16[32,1280]{1,0:T(8,128)(2,1)S(1)}, u32[]{:S(2)}, u32[]{:S(2)}) %collective-permute-start.15) | collective-permute-done | bytes 81952 | tf_op jit(solution)/shard_map/ppermute | solution.py:344
  33.9 1.1 %shard_map.166.refs_0_.refs_1_ = bf16[64,320]{1,0:T(8,128)(2,1)S(1)} custom-call(bf16[320,5120]{1,0:T(8,128)(2,1)S(1)} %get-tuple-element.39.refs_0_, f32[320]{0:T(512)S(1)} %get-tuple-element.40.refs_1_, bf16[32,1280]{1,0:T(8,128)(2,1)S(1)} %shard_map.165.refs_2_, bf16[32,1280]{1,0:T(8,128)(2,1)S(1)} %collective-permute-done.9.refs_3_, ...), custom_call_target="tpu_custom_call" | custom-call | flops 209715200 | bytes 3974400 | tf_op jit(solution)/shard_map/pallas_call | solution.py:34
  35.0 0.6 shard_map.168
  38.7 2.3 %collective-permute-start.26 = (bf16[64,1024]{1,0:T(8,128)(2,1)S(1)}, bf16[64,1024]{1,0:T(8,128)(2,1)S(1)}, u32[]{:S(2)}, u32[]{:S(2)}) collective-permute-start(bf16[64,1024]{1,0:T(8,128)(2,1)S(1)} %get-tuple-element.65), channel_id=1, source_target_pairs={{0,2},{1,3},{2,0},{3,1},{4,6},{5,7},{6,4},{7,5},{8,10},{9,11},{10,... | collective-permute-start | bytes 393224 | tf_op jit(solution)/shard_map/ppermute | solution.py:50
  41.0 1.6 %collective-permute-start.27 = (bf16[64,1024]{1,0:T(8,128)(2,1)S(1)}, bf16[64,1024]{1,0:T(8,128)(2,1)S(1)}, u32[]{:S(2)}, u32[]{:S(2)}) collective-permute-start(bf16[64,1024]{1,0:T(8,128)(2,1)S(1)} %get-tuple-element.66), channel_id=1, source_target_pairs={{0,3},{1,0},{2,1},{3,2},{4,7},{5,4},{6,5},{7,6},{8,11},{9,8},{10,9... | collective-permute-start | bytes 393224 | tf_op jit(solution)/shard_map/ppermute | solution.py:50
  42.6 0.9 %shard_map.171.refs_2_ = bf16[128,256]{1,0:T(8,128)(2,1)S(1)} custom-call(f32[8192]{0:T(1024)S(1)} %get-tuple-element.37.refs_0_, bf16[8192,256]{1,0:T(8,128)(2,1)S(1)} %copy-done, f32[256]{0:T(256)S(1)} %get-tuple-element.38.refs_2_, bf16[4,16,8192]{2,1,0:T(8,128)(2,1)S(1)} %shard_map.170.refs_3_, bf16[4,16,8192]{2,1,0:T(8,128)(2,1)S(1)} %collective-permute-done.21.refs_4_), custom_call_target="tpu_custom_call" | custom-call | flops 536870912 | bytes 6390784 | tf_op jit(solution)/shard_map/pallas_call | solution.py:34
  43.5 1.5 %collective-permute-start.22 = (bf16[128,256]{1,0:T(8,128)(2,1)S(1)}, bf16[128,256]{1,0:T(8,128)(2,1)S(1)}, u32[]{:S(2)}, u32[]{:S(2)}) collective-permute-start(bf16[128,256]{1,0:T(8,128)(2,1)S(1)} %shard_map.171.refs_2_), channel_id=1, source_target_pairs={{0,4},{4,8},{8,12},{12,0},{1,5},{5,9},{9,13},{13,1},{2,6},{6,10},{... | collective-permute-start | bytes 196616 | tf_op jit(solution)/shard_map/ppermute | solution.py:50
  45.6 1.5 %collective-permute-start.24 = (bf16[128,256]{1,0:T(8,128)(2,1)S(1)}, bf16[128,256]{1,0:T(8,128)(2,1)S(1)}, u32[]{:S(2)}, u32[]{:S(2)}) collective-permute-start(bf16[128,256]{1,0:T(8,128)(2,1)S(1)} %shard_map.171.refs_2_), channel_id=1, source_target_pairs={{0,12},{4,0},{8,4},{12,8},{1,13},{5,1},{9,5},{13,9},{2,14},{6,2},{... | collective-permute-start | bytes 196616 | tf_op jit(solution)/shard_map/ppermute | solution.py:50
  47.1 3.2 %collective-permute-done.26.refs_6_ = bf16[64,1024]{1,0:T(8,128)(2,1)S(1)} collective-permute-done((bf16[64,1024]{1,0:T(8,128)(2,1)S(1)}, bf16[64,1024]{1,0:T(8,128)(2,1)S(1)}, u32[]{:S(2)}, u32[]{:S(2)}) %collective-permute-start.26) | collective-permute-done | bytes 131104 | tf_op jit(solution)/shard_map/ppermute | solution.py:50
  50.3 2.8 %collective-permute-done.27.refs_7_ = bf16[64,1024]{1,0:T(8,128)(2,1)S(1)} collective-permute-done((bf16[64,1024]{1,0:T(8,128)(2,1)S(1)}, bf16[64,1024]{1,0:T(8,128)(2,1)S(1)}, u32[]{:S(2)}, u32[]{:S(2)}) %collective-permute-start.27) | collective-permute-done | bytes 131104 | tf_op jit(solution)/shard_map/ppermute | solution.py:50
  54.3 6.2 %collective-permute-done.29.refs_4_ = bf16[64,1024]{1,0:T(8,128)(2,1)S(1)} collective-permute-done((bf16[64,1024]{1,0:T(8,128)(2,1)S(1)}, bf16[64,1024]{1,0:T(8,128)(2,1)S(1)}, u32[]{:S(2)}, u32[]{:S(2)}) %collective-permute-start.29) | collective-permute-done | bytes 131104 | tf_op jit(solution)/shard_map/ppermute | solution.py:352
  61.1 4.4 %collective-permute-done.33.refs_5_ = bf16[64,1024]{1,0:T(8,128)(2,1)S(1)} collective-permute-done((bf16[64,1024]{1,0:T(8,128)(2,1)S(1)}, bf16[64,1024]{1,0:T(8,128)(2,1)S(1)}, u32[]{:S(2)}, u32[]{:S(2)}) %collective-permute-start.33) | collective-permute-done | bytes 131104 | tf_op jit(solution)/shard_map/ppermute | solution.py:349
  65.5 0.7 shard_map.174
  67.2 1.5 %collective-permute-start.35 = (bf16[64,256]{1,0:T(8,128)(2,1)S(1)}, bf16[64,256]{1,0:T(8,128)(2,1)S(1)}, u32[]{:S(2)}, u32[]{:S(2)}) collective-permute-start(bf16[64,256]{1,0:T(8,128)(2,1)S(1)} %shard_map.175.refs_2_), channel_id=1, source_target_pairs={{0,4},{4,8},{8,12},{12,0},{1,5},{5,9},{9,13},{13,1},{2,6},{6,10},{... | collective-permute-start | bytes 98312 | tf_op jit(solution)/shard_map/ppermute | solution.py:50
  69.2 1.5 %collective-permute-start.37 = (bf16[64,256]{1,0:T(8,128)(2,1)S(1)}, bf16[64,256]{1,0:T(8,128)(2,1)S(1)}, u32[]{:S(2)}, u32[]{:S(2)}) collective-permute-start(bf16[64,256]{1,0:T(8,128)(2,1)S(1)} %shard_map.175.refs_2_), channel_id=1, source_target_pairs={{0,12},{4,0},{8,4},{12,8},{1,13},{5,1},{9,5},{13,9},{2,14},{6,2},{... | collective-permute-start | bytes 98312 | tf_op jit(solution)/shard_map/ppermute | solution.py:50
  70.8 0.8 %shard_map.172 = (f32[128,256]{1,0:T(8,128)S(1)}, bf16[128,256]{1,0:T(8,128)(2,1)S(1)}) custom-call(s32[4,4]{1,0:T(4,128)S(1)} %copy-done.4, s32[4,4,16]{2,1,0:T(4,128)S(1)} %copy-done.3, bf16[128,256]{1,0:T(8,128)(2,1)S(1)} %shard_map.171.refs_2_, bf16[128,256]{1,0:T(8,128)(2,1)S(1)} %collective-permute-done.22.refs_3_.refs_0_, ...), custom_call_target="tpu_custom_call" | custom-call | bytes 459840 | tf_op jit(solution)/shard_map/pallas_call | solution.py:34
  71.5 1.4 %collective-permute-done.36.refs_4_ = bf16[64,256]{1,0:T(8,128)(2,1)S(1)} collective-permute-done((bf16[64,256]{1,0:T(8,128)(2,1)S(1)}, bf16[64,256]{1,0:T(8,128)(2,1)S(1)}, u32[]{:S(2)}, u32[]{:S(2)}) %collective-permute-start.36) | collective-permute-done | bytes 32800 | tf_op jit(solution)/shard_map/ppermute | solution.py:50
  73.0 1.1 %collective-permute-done.37.refs_5_ = bf16[64,256]{1,0:T(8,128)(2,1)S(1)} collective-permute-done((bf16[64,256]{1,0:T(8,128)(2,1)S(1)}, bf16[64,256]{1,0:T(8,128)(2,1)S(1)}, u32[]{:S(2)}, u32[]{:S(2)}) %collective-permute-start.37) | collective-permute-done | bytes 32800 | tf_op jit(solution)/shard_map/ppermute | solution.py:50
  74.0 0.8 %shard_map.176 = bf16[4,32,256]{2,1,0:T(8,128)(2,1)} custom-call(f32[128,256]{1,0:T(8,128)S(1)} %get-tuple-element.61.refs_0_, bf16[128,256]{1,0:T(8,128)(2,1)S(1)} %get-tuple-element.62.refs_1_, bf16[64,256]{1,0:T(8,128)(2,1)S(1)} %shard_map.175.refs_2_, bf16[64,256]{1,0:T(8,128)(2,1)S(1)} %collective-permute-done.35.refs_3_, ...), custom_call_target="tpu_custom_call" | custom-call | bytes 393216 | tf_op jit(solution)/shard_map/pallas_call | solution.py:34
  (68 shorter events, 9.9 us)
Async XLA Ops:
  0.0 14.1 %collective-permute-start = (bf16[16,8192]{1,0:T(8,128)(2,1)}, bf16[16,8192]{1,0:T(8,128)(2,1)S(1)}, u32[]{:S(2)}, u32[]{:S(2)}) collective-permute-start(bf16[16,8192]{1,0:T(8,128)(2,1)} %bitcast.7), channel_id=1, source_target_pairs={{0,2},{2,0},{1,3},{3,1},{4,6},{6,4},{5,7},{7,5},{8,10},{10,8},{9,1... | collective-permute-start | bytes 786440 | tf_op jit(solution)/shard_map/ppermute | solution.py:352
  2.6 18.4 %collective-permute-start.1 = (bf16[16,8192]{1,0:T(8,128)(2,1)}, bf16[16,8192]{1,0:T(8,128)(2,1)S(1)}, u32[]{:S(2)}, u32[]{:S(2)}) collective-permute-start(bf16[16,8192]{1,0:T(8,128)(2,1)} %bitcast.8), channel_id=1, source_target_pairs={{0,1},{1,0},{2,3},{3,2},{4,5},{5,4},{6,7},{7,6},{8,9},{9,8},{10,11... | collective-permute-start | bytes 786440 | tf_op jit(solution)/shard_map/ppermute | solution.py:349
  6.9 1.4 %collective-permute-start.3 = (bf16[32,1280]{1,0:T(8,128)(2,1)S(1)}, bf16[32,1280]{1,0:T(8,128)(2,1)S(1)}, u32[]{:S(2)}, u32[]{:S(2)}) collective-permute-start(bf16[32,1280]{1,0:T(8,128)(2,1)S(1)} %get-tuple-element.45), channel_id=1, source_target_pairs={{0,16},{16,0},{1,17},{17,1},{2,18},{18,2},{3,19},{19,3},{4,20},{20... | collective-permute-start | bytes 245768 | tf_op jit(solution)/shard_map/ppermute | solution.py:344
  9.6 8.3 %collective-permute-start.6 = (bf16[32,1280]{1,0:T(8,128)(2,1)S(1)}, bf16[32,1280]{1,0:T(8,128)(2,1)S(1)}, u32[]{:S(2)}, u32[]{:S(2)}) collective-permute-start(bf16[32,1280]{1,0:T(8,128)(2,1)S(1)} %get-tuple-element.49), channel_id=1, source_target_pairs={{0,1},{1,2},{2,3},{3,0},{4,5},{5,6},{6,7},{7,4},{8,9},{9,10},{10,1... | collective-permute-start | bytes 245768 | tf_op jit(solution)/shard_map/ppermute | solution.py:50
  10.1 10.9 %collective-permute-start.7 = (bf16[32,1280]{1,0:T(8,128)(2,1)S(1)}, bf16[32,1280]{1,0:T(8,128)(2,1)S(1)}, u32[]{:S(2)}, u32[]{:S(2)}) collective-permute-start(bf16[32,1280]{1,0:T(8,128)(2,1)S(1)} %get-tuple-element.50), channel_id=1, source_target_pairs={{0,2},{1,3},{2,0},{3,1},{4,6},{5,7},{6,4},{7,5},{8,10},{9,11},{10,... | collective-permute-start | bytes 245768 | tf_op jit(solution)/shard_map/ppermute | solution.py:50
  13.5 7.4 %collective-permute-start.8 = (bf16[32,1280]{1,0:T(8,128)(2,1)S(1)}, bf16[32,1280]{1,0:T(8,128)(2,1)S(1)}, u32[]{:S(2)}, u32[]{:S(2)}) collective-permute-start(bf16[32,1280]{1,0:T(8,128)(2,1)S(1)} %get-tuple-element.51), channel_id=1, source_target_pairs={{0,3},{1,0},{2,1},{3,2},{4,7},{5,4},{6,5},{7,6},{8,11},{9,8},{10,9... | collective-permute-start | bytes 245768 | tf_op jit(solution)/shard_map/ppermute | solution.py:50
  14.1 20.9 %collective-permute-start.16 = (bf16[16,8192]{1,0:T(8,128)(2,1)S(1)}, bf16[16,8192]{1,0:T(8,128)(2,1)S(1)}, u32[]{:S(2)}, u32[]{:S(2)}) collective-permute-start(bf16[16,8192]{1,0:T(8,128)(2,1)S(1)} %collective-permute-done.refs_0_.refs_3_), channel_id=1, source_target_pairs={{0,1},{1,0},{2,3},{3,2},{4,5},{5,4},{6,7},{7,6},{8,9},{9,8},{10,11... | collective-permute-start | bytes 786440 | tf_op jit(solution)/shard_map/ppermute | solution.py:349
  21.1 7.2 %collective-permute-start.9 = (bf16[32,1280]{1,0:T(8,128)(2,1)S(1)}, bf16[32,1280]{1,0:T(8,128)(2,1)S(1)}, u32[]{:S(2)}, u32[]{:S(2)}) collective-permute-start(bf16[32,1280]{1,0:T(8,128)(2,1)S(1)} %shard_map.165.refs_2_), channel_id=1, source_target_pairs={{0,1},{1,2},{2,3},{3,0},{4,5},{5,6},{6,7},{7,4},{8,9},{9,10},{10,1... | collective-permute-start | bytes 245768 | tf_op jit(solution)/shard_map/ppermute | solution.py:50
  21.4 8.3 %collective-permute-start.10 = (bf16[32,1280]{1,0:T(8,128)(2,1)S(1)}, bf16[32,1280]{1,0:T(8,128)(2,1)S(1)}, u32[]{:S(2)}, u32[]{:S(2)}) collective-permute-start(bf16[32,1280]{1,0:T(8,128)(2,1)S(1)} %shard_map.165.refs_2_), channel_id=1, source_target_pairs={{0,2},{1,3},{2,0},{3,1},{4,6},{5,7},{6,4},{7,5},{8,10},{9,11},{10,... | collective-permute-start | bytes 245768 | tf_op jit(solution)/shard_map/ppermute | solution.py:50
  24.7 7.9 %collective-permute-start.11 = (bf16[32,1280]{1,0:T(8,128)(2,1)S(1)}, bf16[32,1280]{1,0:T(8,128)(2,1)S(1)}, u32[]{:S(2)}, u32[]{:S(2)}) collective-permute-start(bf16[32,1280]{1,0:T(8,128)(2,1)S(1)} %shard_map.165.refs_2_), channel_id=1, source_target_pairs={{0,3},{1,0},{2,1},{3,2},{4,7},{5,4},{6,5},{7,6},{8,11},{9,8},{10,9... | collective-permute-start | bytes 245768 | tf_op jit(solution)/shard_map/ppermute | solution.py:50
  26.6 6.0 %collective-permute-start.12 = (bf16[32,1280]{1,0:T(8,128)(2,1)S(1)}, bf16[32,1280]{1,0:T(8,128)(2,1)S(1)}, u32[]{:S(2)}, u32[]{:S(2)}) collective-permute-start(bf16[32,1280]{1,0:T(8,128)(2,1)S(1)} %shard_map.165.refs_2_), channel_id=1, source_target_pairs={{0,16},{16,0},{1,17},{17,1},{2,18},{18,2},{3,19},{19,3},{4,20},{20... | collective-permute-start | bytes 245768 | tf_op jit(solution)/shard_map/ppermute | solution.py:344
  28.3 4.3 %collective-permute-start.13 = (bf16[32,1280]{1,0:T(8,128)(2,1)S(1)}, bf16[32,1280]{1,0:T(8,128)(2,1)S(1)}, u32[]{:S(2)}, u32[]{:S(2)}) collective-permute-start(bf16[32,1280]{1,0:T(8,128)(2,1)S(1)} %collective-permute-done.9.refs_3_), channel_id=1, source_target_pairs={{0,16},{16,0},{1,17},{17,1},{2,18},{18,2},{3,19},{19,3},{4,20},{20... | collective-permute-start | bytes 245768 | tf_op jit(solution)/shard_map/ppermute | solution.py:344
  29.6 3.0 %collective-permute-start.14 = (bf16[32,1280]{1,0:T(8,128)(2,1)S(1)}, bf16[32,1280]{1,0:T(8,128)(2,1)S(1)}, u32[]{:S(2)}, u32[]{:S(2)}) collective-permute-start(bf16[32,1280]{1,0:T(8,128)(2,1)S(1)} %collective-permute-done.10.refs_4_), channel_id=1, source_target_pairs={{0,16},{16,0},{1,17},{17,1},{2,18},{18,2},{3,19},{19,3},{4,20},{20... | collective-permute-start | bytes 245768 | tf_op jit(solution)/shard_map/ppermute | solution.py:344
  35.7 1.7 %collective-permute-start.17 = (bf16[64,1024]{1,0:T(8,128)(2,1)S(1)}, bf16[64,1024]{1,0:T(8,128)(2,1)S(1)}, u32[]{:S(2)}, u32[]{:S(2)}) collective-permute-start(bf16[64,1024]{1,0:T(8,128)(2,1)S(1)} %get-tuple-element.56), channel_id=1, source_target_pairs={{0,16},{16,0},{1,17},{17,1},{2,18},{18,2},{3,19},{19,3},{4,20},{20... | collective-permute-start | bytes 393224 | tf_op jit(solution)/shard_map/ppermute | solution.py:344
  35.9 1.5 %collective-permute-start.18 = (bf16[64,1024]{1,0:T(8,128)(2,1)S(1)}, bf16[64,1024]{1,0:T(8,128)(2,1)S(1)}, u32[]{:S(2)}, u32[]{:S(2)}) collective-permute-start(bf16[64,1024]{1,0:T(8,128)(2,1)S(1)} %get-tuple-element.57), channel_id=1, source_target_pairs={{0,16},{16,0},{1,17},{17,1},{2,18},{18,2},{3,19},{19,3},{4,20},{20... | collective-permute-start | bytes 393224 | tf_op jit(solution)/shard_map/ppermute | solution.py:344
  36.4 1.4 %collective-permute-start.20 = (bf16[64,1024]{1,0:T(8,128)(2,1)S(1)}, bf16[64,1024]{1,0:T(8,128)(2,1)S(1)}, u32[]{:S(2)}, u32[]{:S(2)}) collective-permute-start(bf16[64,1024]{1,0:T(8,128)(2,1)S(1)} %get-tuple-element.59), channel_id=1, source_target_pairs={{0,16},{16,0},{1,17},{17,1},{2,18},{18,2},{3,19},{19,3},{4,20},{20... | collective-permute-start | bytes 393224 | tf_op jit(solution)/shard_map/ppermute | solution.py:344
  38.1 4.5 %collective-permute-start.21 = (bf16[4,16,8192]{2,1,0:T(8,128)(2,1)S(1)}, bf16[4,16,8192]{2,1,0:T(8,128)(2,1)S(1)}, u32[]{:S(2)}, u32[]{:S(2)}) collective-permute-start(bf16[4,16,8192]{2,1,0:T(8,128)(2,1)S(1)} %shard_map.170.refs_3_), channel_id=1, source_target_pairs={{0,16},{16,0},{1,17},{17,1},{2,18},{18,2},{3,19},{19,3},{4,20},{20... | collective-permute-start | bytes 3145736 | tf_op jit(solution)/shard_map/ppermute | solution.py:344
  38.4 7.1 %collective-permute-start.25 = (bf16[64,1024]{1,0:T(8,128)(2,1)S(1)}, bf16[64,1024]{1,0:T(8,128)(2,1)S(1)}, u32[]{:S(2)}, u32[]{:S(2)}) collective-permute-start(bf16[64,1024]{1,0:T(8,128)(2,1)S(1)} %get-tuple-element.64), channel_id=1, source_target_pairs={{0,1},{1,2},{2,3},{3,0},{4,5},{5,6},{6,7},{7,4},{8,9},{9,10},{10,1... | collective-permute-start | bytes 393224 | tf_op jit(solution)/shard_map/ppermute | solution.py:50
  38.7 11.6 %collective-permute-start.26 = (bf16[64,1024]{1,0:T(8,128)(2,1)S(1)}, bf16[64,1024]{1,0:T(8,128)(2,1)S(1)}, u32[]{:S(2)}, u32[]{:S(2)}) collective-permute-start(bf16[64,1024]{1,0:T(8,128)(2,1)S(1)} %get-tuple-element.65), channel_id=1, source_target_pairs={{0,2},{1,3},{2,0},{3,1},{4,6},{5,7},{6,4},{7,5},{8,10},{9,11},{10,... | collective-permute-start | bytes 393224 | tf_op jit(solution)/shard_map/ppermute | solution.py:50
  41.0 12.1 %collective-permute-start.27 = (bf16[64,1024]{1,0:T(8,128)(2,1)S(1)}, bf16[64,1024]{1,0:T(8,128)(2,1)S(1)}, u32[]{:S(2)}, u32[]{:S(2)}) collective-permute-start(bf16[64,1024]{1,0:T(8,128)(2,1)S(1)} %get-tuple-element.66), channel_id=1, source_target_pairs={{0,3},{1,0},{2,1},{3,2},{4,7},{5,4},{6,5},{7,6},{8,11},{9,8},{10,9... | collective-permute-start | bytes 393224 | tf_op jit(solution)/shard_map/ppermute | solution.py:50
  43.5 9.6 %collective-permute-start.22 = (bf16[128,256]{1,0:T(8,128)(2,1)S(1)}, bf16[128,256]{1,0:T(8,128)(2,1)S(1)}, u32[]{:S(2)}, u32[]{:S(2)}) collective-permute-start(bf16[128,256]{1,0:T(8,128)(2,1)S(1)} %shard_map.171.refs_2_), channel_id=1, source_target_pairs={{0,4},{4,8},{8,12},{12,0},{1,5},{5,9},{9,13},{13,1},{2,6},{6,10},{... | collective-permute-start | bytes 196616 | tf_op jit(solution)/shard_map/ppermute | solution.py:50
  45.0 8.1 %collective-permute-start.23 = (bf16[128,256]{1,0:T(8,128)(2,1)S(1)}, bf16[128,256]{1,0:T(8,128)(2,1)S(1)}, u32[]{:S(2)}, u32[]{:S(2)}) collective-permute-start(bf16[128,256]{1,0:T(8,128)(2,1)S(1)} %shard_map.171.refs_2_), channel_id=1, source_target_pairs={{0,8},{4,12},{8,0},{12,4},{1,9},{5,13},{9,1},{13,5},{2,10},{6,14},... | collective-permute-start | bytes 196616 | tf_op jit(solution)/shard_map/ppermute | solution.py:50
  45.6 7.6 %collective-permute-start.24 = (bf16[128,256]{1,0:T(8,128)(2,1)S(1)}, bf16[128,256]{1,0:T(8,128)(2,1)S(1)}, u32[]{:S(2)}, u32[]{:S(2)}) collective-permute-start(bf16[128,256]{1,0:T(8,128)(2,1)S(1)} %shard_map.171.refs_2_), channel_id=1, source_target_pairs={{0,12},{4,0},{8,4},{12,8},{1,13},{5,1},{9,5},{13,9},{2,14},{6,2},{... | collective-permute-start | bytes 196616 | tf_op jit(solution)/shard_map/ppermute | solution.py:50
  53.2 7.3 %collective-permute-start.29 = (bf16[64,1024]{1,0:T(8,128)(2,1)S(1)}, bf16[64,1024]{1,0:T(8,128)(2,1)S(1)}, u32[]{:S(2)}, u32[]{:S(2)}) collective-permute-start(bf16[64,1024]{1,0:T(8,128)(2,1)S(1)} %shard_map.173.refs_2_), channel_id=1, source_target_pairs={{0,2},{2,0},{1,3},{3,1},{4,6},{6,4},{5,7},{7,5},{8,10},{10,8},{9,1... | collective-permute-start | bytes 393224 | tf_op jit(solution)/shard_map/ppermute | solution.py:352
  53.8 6.7 %collective-permute-start.28 = (bf16[64,1024]{1,0:T(8,128)(2,1)S(1)}, bf16[64,1024]{1,0:T(8,128)(2,1)S(1)}, u32[]{:S(2)}, u32[]{:S(2)}) collective-permute-start(bf16[64,1024]{1,0:T(8,128)(2,1)S(1)} %shard_map.173.refs_2_), channel_id=1, source_target_pairs={{0,1},{1,0},{2,3},{3,2},{4,5},{5,4},{6,7},{7,6},{8,9},{9,8},{10,11... | collective-permute-start | bytes 393224 | tf_op jit(solution)/shard_map/ppermute | solution.py:349
  60.5 5.0 %collective-permute-start.33 = (bf16[64,1024]{1,0:T(8,128)(2,1)S(1)}, bf16[64,1024]{1,0:T(8,128)(2,1)S(1)}, u32[]{:S(2)}, u32[]{:S(2)}) collective-permute-start(bf16[64,1024]{1,0:T(8,128)(2,1)S(1)} %collective-permute-done.29.refs_4_), channel_id=1, source_target_pairs={{0,1},{1,0},{2,3},{3,2},{4,5},{5,4},{6,7},{7,6},{8,9},{9,8},{10,11... | collective-permute-start | bytes 393224 | tf_op jit(solution)/shard_map/ppermute | solution.py:349
  60.5 5.0 %collective-permute-start.30 = (bf16[64,1024]{1,0:T(8,128)(2,1)S(1)}, bf16[64,1024]{1,0:T(8,128)(2,1)S(1)}, u32[]{:S(2)}, u32[]{:S(2)}) collective-permute-start(bf16[64,1024]{1,0:T(8,128)(2,1)S(1)} %shard_map.173.refs_2_), channel_id=1, source_target_pairs={{0,16},{16,0},{1,17},{17,1},{2,18},{18,2},{3,19},{19,3},{4,20},{20... | collective-permute-start | bytes 393224 | tf_op jit(solution)/shard_map/ppermute | solution.py:344
  60.5 5.0 %collective-permute-start.31 = (bf16[64,1024]{1,0:T(8,128)(2,1)S(1)}, bf16[64,1024]{1,0:T(8,128)(2,1)S(1)}, u32[]{:S(2)}, u32[]{:S(2)}) collective-permute-start(bf16[64,1024]{1,0:T(8,128)(2,1)S(1)} %collective-permute-done.28.refs_3_), channel_id=1, source_target_pairs={{0,16},{16,0},{1,17},{17,1},{2,18},{18,2},{3,19},{19,3},{4,20},{20... | collective-permute-start | bytes 393224 | tf_op jit(solution)/shard_map/ppermute | solution.py:344
  61.0 4.5 %collective-permute-start.32 = (bf16[64,1024]{1,0:T(8,128)(2,1)S(1)}, bf16[64,1024]{1,0:T(8,128)(2,1)S(1)}, u32[]{:S(2)}, u32[]{:S(2)}) collective-permute-start(bf16[64,1024]{1,0:T(8,128)(2,1)S(1)} %collective-permute-done.29.refs_4_), channel_id=1, source_target_pairs={{0,16},{16,0},{1,17},{17,1},{2,18},{18,2},{3,19},{19,3},{4,20},{20... | collective-permute-start | bytes 393224 | tf_op jit(solution)/shard_map/ppermute | solution.py:344
  67.2 4.4 %collective-permute-start.35 = (bf16[64,256]{1,0:T(8,128)(2,1)S(1)}, bf16[64,256]{1,0:T(8,128)(2,1)S(1)}, u32[]{:S(2)}, u32[]{:S(2)}) collective-permute-start(bf16[64,256]{1,0:T(8,128)(2,1)S(1)} %shard_map.175.refs_2_), channel_id=1, source_target_pairs={{0,4},{4,8},{8,12},{12,0},{1,5},{5,9},{9,13},{13,1},{2,6},{6,10},{... | collective-permute-start | bytes 98312 | tf_op jit(solution)/shard_map/ppermute | solution.py:50
  68.7 4.3 %collective-permute-start.36 = (bf16[64,256]{1,0:T(8,128)(2,1)S(1)}, bf16[64,256]{1,0:T(8,128)(2,1)S(1)}, u32[]{:S(2)}, u32[]{:S(2)}) collective-permute-start(bf16[64,256]{1,0:T(8,128)(2,1)S(1)} %shard_map.175.refs_2_), channel_id=1, source_target_pairs={{0,8},{4,12},{8,0},{12,4},{1,9},{5,13},{9,1},{13,5},{2,10},{6,14},... | collective-permute-start | bytes 98312 | tf_op jit(solution)/shard_map/ppermute | solution.py:50
  69.2 4.8 %collective-permute-start.37 = (bf16[64,256]{1,0:T(8,128)(2,1)S(1)}, bf16[64,256]{1,0:T(8,128)(2,1)S(1)}, u32[]{:S(2)}, u32[]{:S(2)}) collective-permute-start(bf16[64,256]{1,0:T(8,128)(2,1)S(1)} %shard_map.175.refs_2_), channel_id=1, source_target_pairs={{0,12},{4,0},{8,4},{12,8},{1,13},{5,1},{9,5},{13,9},{2,14},{6,2},{... | collective-permute-start | bytes 98312 | tf_op jit(solution)/shard_map/ppermute | solution.py:50
  (11 other events, 53.6 us)

commit v8 on v6

--- a/solution.py
+++ b/solution.py
@@ -76,14 +76,22 @@
     units = place.shape[2]
     tile = 256
     per_tile = tile // WIN
-    for copy in copies[:5]:
-        copy.wait()
+    single = rows == tile
+
+    def wait(*which, inside=True):
+        if inside == single:
+            for i in which:
+                copies[i].wait()
+
+    wait(0, 1, 2, 3, 4, inside=False)
 
     def one(t, carry):
         at = pl.ds(pl.multiple_of(t * tile, tile), tile)
+        wait(0, 1)
         x = x_ref[at, :].astype(F32)
         scale = lax.rsqrt(jnp.mean(x * x, axis=-1, keepdims=True) + NORM_EPS)
         y = (x * scale * gain_ref[...][None, :]).astype(BF16)
+        wait(2, 3)
         parts = []
         for i in range(3):
             w = w_ref[i * head_width:(i + 1) * head_width, :]
@@ -93,6 +101,7 @@
         key = lax.broadcasted_iota(jnp.int32, (tile, tile), 1)
         row = lax.broadcasted_iota(jnp.int32, (tile, tile), 0)
         same = key // WIN == row // WIN
+        wait(4)
         end = jnp.zeros((tile, tile), jnp.int32)
         for j in range(per_tile):
             count = jnp.int32(0)
@@ -113,7 +122,7 @@
         hf[at, :] = total.astype(BF16)
         return carry
 
-    if rows == tile:
+    if single:
         one(0, 0)
     else:
         lax.fori_loop(0, rows // tile, one, 0)

time: 76.2 us -> 76.2 us (level)
  no operation moved by 1% of the time
where the time goes in v8:
time: 76.2 us; the launch traced here: 75.4 us
  waiting for transfers between devices  34.8 us (46%)
  starting transfers between devices  30 us (39%)
  Pallas kernels  10.4 us (14%)
    ppermute x18, waiting for transfers between devices, shifted(): return lax.ppermute(x, axis, [(i, (i + k) % count) for i in range(count)])  30.3 us
    ppermute x18, starting transfers between devices, shifted(): return lax.ppermute(x, axis, [(i, (i + k) % count) for i in range(count)])  23.4 us
    pallas_call x14, Pallas kernels, call(): pl.pallas_call(body, out_shape=outs, in_specs=[unread] * count + [scalar]...  10.4 us
    ppermute x17, waiting for transfers between devices, swap(): return lax.ppermute(v, 'section', [(0, 1), (1, 0)])  4.03 us
    ppermute x1, starting transfers between devices, across(): return lax.ppermute(v, 'mp', [(0, 2), (2, 0), (1, 3), (3, 1)])  2.59 us
    ppermute x17, starting transfers between devices, swap(): return lax.ppermute(v, 'section', [(0, 1), (1, 0)])  2.31 us
    ppermute x2, starting transfers between devices, near(): return lax.ppermute(v, 'mp', [(0, 1), (1, 0), (2, 3), (3, 2)])  1.7 us
  transfers between devices with their start and end apart: 38, of which 21 were waited for; matrix products, arithmetic and copies ran while one was open for 0% of the time, Pallas kernels for 11%

profile of v8, /device:TPU:10, one launch (start us, length us, event | category | flops | bytes accessed | tf_op | source)
XLA Modules:
  0.0 75.4 jit_solution(4114001061923538019)
XLA Ops:
  0.0 2.6 %collective-permute-start = (bf16[16,8192]{1,0:T(8,128)(2,1)}, bf16[16,8192]{1,0:T(8,128)(2,1)S(1)}, u32[]{:S(2)}, u32[]{:S(2)}) collective-permute-start(bf16[16,8192]{1,0:T(8,128)(2,1)} %bitcast.7), channel_id=1, source_target_pairs={{0,2},{2,0},{1,3},{3,1},{4,6},{6,4},{5,7},{7,5},{8,10},{10,8},{9,1... | collective-permute-start | bytes 786440 | tf_op jit(solution)/shard_map/ppermute | solution.py:361
  3.0 3.9 %shard_map.163 = (bf16[128,1280]{1,0:T(8,128)(2,1)S(1)}, f32[32,1280]{1,0:T(8,128)S(1)}, bf16[32,1280]{1,0:T(8,128)(2,1)S(1)}, bf16[32,1280]{1,0:T(8,128)(2,1)S(...) custom-call(s32[4,4,16]{2,1,0:T(4,128)} %refs_1_.7, ...), custom_call_target="tpu_custom_call" | custom-call | flops 419430400 | bytes 9825664 | tf_op jit(solution)/shard_map/pallas_call | solution.py:34
  8.8 0.8 %collective-permute-done.5.refs_4_ = bf16[32,1280]{1,0:T(8,128)(2,1)S(1)} collective-permute-done((bf16[32,1280]{1,0:T(8,128)(2,1)S(1)}, bf16[32,1280]{1,0:T(8,128)(2,1)S(1)}, u32[]{:S(2)}, u32[]{:S(2)}) %collective-permute-start.5) | collective-permute-done | bytes 81952 | tf_op jit(solution)/shard_map/ppermute | solution.py:353
  10.2 3.5 %collective-permute-start.7 = (bf16[32,1280]{1,0:T(8,128)(2,1)S(1)}, bf16[32,1280]{1,0:T(8,128)(2,1)S(1)}, u32[]{:S(2)}, u32[]{:S(2)}) collective-permute-start(bf16[32,1280]{1,0:T(8,128)(2,1)S(1)} %get-tuple-element.50), channel_id=1, source_target_pairs={{0,2},{1,3},{2,0},{3,1},{4,6},{5,7},{6,4},{7,5},{8,10},{9,11},{10,... | collective-permute-start | bytes 245768 | tf_op jit(solution)/shard_map/ppermute | solution.py:50
  14.1 1.2 %collective-permute-start.16 = (bf16[16,8192]{1,0:T(8,128)(2,1)S(1)}, bf16[16,8192]{1,0:T(8,128)(2,1)S(1)}, u32[]{:S(2)}, u32[]{:S(2)}) collective-permute-start(bf16[16,8192]{1,0:T(8,128)(2,1)S(1)} %collective-permute-done.refs_0_.refs_3_), channel_id=1, source_target_pairs={{0,1},{1,0},{2,3},{3,2},{4,5},{5,4},{6,7},{7,6},{8,9},{9,8},{10,11... | collective-permute-start | bytes 786440 | tf_op jit(solution)/shard_map/ppermute | solution.py:358
  15.4 2.5 %collective-permute-done.6.refs_5_ = bf16[32,1280]{1,0:T(8,128)(2,1)S(1)} collective-permute-done((bf16[32,1280]{1,0:T(8,128)(2,1)S(1)}, bf16[32,1280]{1,0:T(8,128)(2,1)S(1)}, u32[]{:S(2)}, u32[]{:S(2)}) %collective-permute-start.6) | collective-permute-done | bytes 81952 | tf_op jit(solution)/shard_map/ppermute | solution.py:50
  17.8 3.1 %collective-permute-done.7.refs_6_ = bf16[32,1280]{1,0:T(8,128)(2,1)S(1)} collective-permute-done((bf16[32,1280]{1,0:T(8,128)(2,1)S(1)}, bf16[32,1280]{1,0:T(8,128)(2,1)S(1)}, u32[]{:S(2)}, u32[]{:S(2)}) %collective-permute-start.7) | collective-permute-done | bytes 81952 | tf_op jit(solution)/shard_map/ppermute | solution.py:50
  21.3 3.4 %collective-permute-start.10 = (bf16[32,1280]{1,0:T(8,128)(2,1)S(1)}, bf16[32,1280]{1,0:T(8,128)(2,1)S(1)}, u32[]{:S(2)}, u32[]{:S(2)}) collective-permute-start(bf16[32,1280]{1,0:T(8,128)(2,1)S(1)} %shard_map.165.refs_2_), channel_id=1, source_target_pairs={{0,2},{1,3},{2,0},{3,1},{4,6},{5,7},{6,4},{7,5},{8,10},{9,11},{10,... | collective-permute-start | bytes 245768 | tf_op jit(solution)/shard_map/ppermute | solution.py:50
  24.7 1.9 %collective-permute-start.11 = (bf16[32,1280]{1,0:T(8,128)(2,1)S(1)}, bf16[32,1280]{1,0:T(8,128)(2,1)S(1)}, u32[]{:S(2)}, u32[]{:S(2)}) collective-permute-start(bf16[32,1280]{1,0:T(8,128)(2,1)S(1)} %shard_map.165.refs_2_), channel_id=1, source_target_pairs={{0,3},{1,0},{2,1},{3,2},{4,7},{5,4},{6,5},{7,6},{8,11},{9,8},{10,9... | collective-permute-start | bytes 245768 | tf_op jit(solution)/shard_map/ppermute | solution.py:50
  26.6 1.7 %collective-permute-done.9.refs_3_ = bf16[32,1280]{1,0:T(8,128)(2,1)S(1)} collective-permute-done((bf16[32,1280]{1,0:T(8,128)(2,1)S(1)}, bf16[32,1280]{1,0:T(8,128)(2,1)S(1)}, u32[]{:S(2)}, u32[]{:S(2)}) %collective-permute-start.9) | collective-permute-done | bytes 81952 | tf_op jit(solution)/shard_map/ppermute | solution.py:50
  28.3 1.3 %collective-permute-done.10.refs_4_ = bf16[32,1280]{1,0:T(8,128)(2,1)S(1)} collective-permute-done((bf16[32,1280]{1,0:T(8,128)(2,1)S(1)}, bf16[32,1280]{1,0:T(8,128)(2,1)S(1)}, u32[]{:S(2)}, u32[]{:S(2)}) %collective-permute-start.10) | collective-permute-done | bytes 81952 | tf_op jit(solution)/shard_map/ppermute | solution.py:50
  29.6 2.9 %collective-permute-done.11.refs_5_ = bf16[32,1280]{1,0:T(8,128)(2,1)S(1)} collective-permute-done((bf16[32,1280]{1,0:T(8,128)(2,1)S(1)}, bf16[32,1280]{1,0:T(8,128)(2,1)S(1)}, u32[]{:S(2)}, u32[]{:S(2)}) %collective-permute-start.11) | collective-permute-done | bytes 81952 | tf_op jit(solution)/shard_map/ppermute | solution.py:50
  32.6 1.3 %collective-permute-done.15.refs_9_ = bf16[32,1280]{1,0:T(8,128)(2,1)S(1)} collective-permute-done((bf16[32,1280]{1,0:T(8,128)(2,1)S(1)}, bf16[32,1280]{1,0:T(8,128)(2,1)S(1)}, u32[]{:S(2)}, u32[]{:S(2)}) %collective-permute-start.15) | collective-permute-done | bytes 81952 | tf_op jit(solution)/shard_map/ppermute | solution.py:353
  33.9 1.1 %shard_map.166.refs_0_.refs_1_ = bf16[64,320]{1,0:T(8,128)(2,1)S(1)} custom-call(bf16[320,5120]{1,0:T(8,128)(2,1)S(1)} %get-tuple-element.39.refs_0_, f32[320]{0:T(512)S(1)} %get-tuple-element.40.refs_1_, bf16[32,1280]{1,0:T(8,128)(2,1)S(1)} %shard_map.165.refs_2_, bf16[32,1280]{1,0:T(8,128)(2,1)S(1)} %collective-permute-done.9.refs_3_, ...), custom_call_target="tpu_custom_call" | custom-call | flops 209715200 | bytes 3974400 | tf_op jit(solution)/shard_map/pallas_call | solution.py:34
  38.7 2.3 %collective-permute-start.26 = (bf16[64,1024]{1,0:T(8,128)(2,1)S(1)}, bf16[64,1024]{1,0:T(8,128)(2,1)S(1)}, u32[]{:S(2)}, u32[]{:S(2)}) collective-permute-start(bf16[64,1024]{1,0:T(8,128)(2,1)S(1)} %get-tuple-element.65), channel_id=1, source_target_pairs={{0,2},{1,3},{2,0},{3,1},{4,6},{5,7},{6,4},{7,5},{8,10},{9,11},{10,... | collective-permute-start | bytes 393224 | tf_op jit(solution)/shard_map/ppermute | solution.py:50
  41.0 1.6 %collective-permute-start.27 = (bf16[64,1024]{1,0:T(8,128)(2,1)S(1)}, bf16[64,1024]{1,0:T(8,128)(2,1)S(1)}, u32[]{:S(2)}, u32[]{:S(2)}) collective-permute-start(bf16[64,1024]{1,0:T(8,128)(2,1)S(1)} %get-tuple-element.66), channel_id=1, source_target_pairs={{0,3},{1,0},{2,1},{3,2},{4,7},{5,4},{6,5},{7,6},{8,11},{9,8},{10,9... | collective-permute-start | bytes 393224 | tf_op jit(solution)/shard_map/ppermute | solution.py:50
  42.6 0.9 %shard_map.171.refs_2_ = bf16[128,256]{1,0:T(8,128)(2,1)S(1)} custom-call(f32[8192]{0:T(1024)S(1)} %get-tuple-element.37.refs_0_, bf16[8192,256]{1,0:T(8,128)(2,1)S(1)} %copy-done, f32[256]{0:T(256)S(1)} %get-tuple-element.38.refs_2_, bf16[4,16,8192]{2,1,0:T(8,128)(2,1)S(1)} %shard_map.170.refs_3_, bf16[4,16,8192]{2,1,0:T(8,128)(2,1)S(1)} %collective-permute-done.21.refs_4_), custom_call_target="tpu_custom_call" | custom-call | flops 536870912 | bytes 6390784 | tf_op jit(solution)/shard_map/pallas_call | solution.py:34
  43.5 1.5 %collective-permute-start.22 = (bf16[128,256]{1,0:T(8,128)(2,1)S(1)}, bf16[128,256]{1,0:T(8,128)(2,1)S(1)}, u32[]{:S(2)}, u32[]{:S(2)}) collective-permute-start(bf16[128,256]{1,0:T(8,128)(2,1)S(1)} %shard_map.171.refs_2_), channel_id=1, source_target_pairs={{0,4},{4,8},{8,12},{12,0},{1,5},{5,9},{9,13},{13,1},{2,6},{6,10},{... | collective-permute-start | bytes 196616 | tf_op jit(solution)/shard_map/ppermute | solution.py:50
  45.6 1.5 %collective-permute-start.24 = (bf16[128,256]{1,0:T(8,128)(2,1)S(1)}, bf16[128,256]{1,0:T(8,128)(2,1)S(1)}, u32[]{:S(2)}, u32[]{:S(2)}) collective-permute-start(bf16[128,256]{1,0:T(8,128)(2,1)S(1)} %shard_map.171.refs_2_), channel_id=1, source_target_pairs={{0,12},{4,0},{8,4},{12,8},{1,13},{5,1},{9,5},{13,9},{2,14},{6,2},{... | collective-permute-start | bytes 196616 | tf_op jit(solution)/shard_map/ppermute | solution.py:50
  47.1 3.2 %collective-permute-done.26.refs_6_ = bf16[64,1024]{1,0:T(8,128)(2,1)S(1)} collective-permute-done((bf16[64,1024]{1,0:T(8,128)(2,1)S(1)}, bf16[64,1024]{1,0:T(8,128)(2,1)S(1)}, u32[]{:S(2)}, u32[]{:S(2)}) %collective-permute-start.26) | collective-permute-done | bytes 131104 | tf_op jit(solution)/shard_map/ppermute | solution.py:50
  50.3 2.8 %collective-permute-done.27.refs_7_ = bf16[64,1024]{1,0:T(8,128)(2,1)S(1)} collective-permute-done((bf16[64,1024]{1,0:T(8,128)(2,1)S(1)}, bf16[64,1024]{1,0:T(8,128)(2,1)S(1)}, u32[]{:S(2)}, u32[]{:S(2)}) %collective-permute-start.27) | collective-permute-done | bytes 131104 | tf_op jit(solution)/shard_map/ppermute | solution.py:50
  53.3 1.2 %collective-permute-start.29 = (bf16[64,1024]{1,0:T(8,128)(2,1)S(1)}, bf16[64,1024]{1,0:T(8,128)(2,1)S(1)}, u32[]{:S(2)}, u32[]{:S(2)}) collective-permute-start(bf16[64,1024]{1,0:T(8,128)(2,1)S(1)} %shard_map.173.refs_2_), channel_id=1, source_target_pairs={{0,2},{1,3},{2,0},{3,1},{4,6},{5,7},{6,4},{7,5},{8,10},{9,11},{10,... | collective-permute-start | bytes 393224 | tf_op jit(solution)/shard_map/ppermute | solution.py:50
  54.5 1.3 %collective-permute-start.33 = (bf16[64,1024]{1,0:T(8,128)(2,1)S(1)}, bf16[64,1024]{1,0:T(8,128)(2,1)S(1)}, u32[]{:S(2)}, u32[]{:S(2)}) collective-permute-start(bf16[64,1024]{1,0:T(8,128)(2,1)S(1)} %shard_map.173.refs_2_), channel_id=1, source_target_pairs={{0,3},{1,0},{2,1},{3,2},{4,7},{5,4},{6,5},{7,6},{8,11},{9,8},{10,9... | collective-permute-start | bytes 393224 | tf_op jit(solution)/shard_map/ppermute | solution.py:50
  55.8 3.8 %collective-permute-done.28.refs_3_ = bf16[64,1024]{1,0:T(8,128)(2,1)S(1)} collective-permute-done((bf16[64,1024]{1,0:T(8,128)(2,1)S(1)}, bf16[64,1024]{1,0:T(8,128)(2,1)S(1)}, u32[]{:S(2)}, u32[]{:S(2)}) %collective-permute-start.28) | collective-permute-done | bytes 131104 | tf_op jit(solution)/shard_map/ppermute | solution.py:50
  59.6 5.3 %collective-permute-done.29.refs_4_ = bf16[64,1024]{1,0:T(8,128)(2,1)S(1)} collective-permute-done((bf16[64,1024]{1,0:T(8,128)(2,1)S(1)}, bf16[64,1024]{1,0:T(8,128)(2,1)S(1)}, u32[]{:S(2)}, u32[]{:S(2)}) %collective-permute-start.29) | collective-permute-done | bytes 131104 | tf_op jit(solution)/shard_map/ppermute | solution.py:50
  64.9 1.2 %collective-permute-done.33.refs_5_ = bf16[64,1024]{1,0:T(8,128)(2,1)S(1)} collective-permute-done((bf16[64,1024]{1,0:T(8,128)(2,1)S(1)}, bf16[64,1024]{1,0:T(8,128)(2,1)S(1)}, u32[]{:S(2)}, u32[]{:S(2)}) %collective-permute-start.33) | collective-permute-done | bytes 131104 | tf_op jit(solution)/shard_map/ppermute | solution.py:50
  67.8 1.5 %collective-permute-start.35 = (bf16[64,256]{1,0:T(8,128)(2,1)S(1)}, bf16[64,256]{1,0:T(8,128)(2,1)S(1)}, u32[]{:S(2)}, u32[]{:S(2)}) collective-permute-start(bf16[64,256]{1,0:T(8,128)(2,1)S(1)} %shard_map.175.refs_2_), channel_id=1, source_target_pairs={{0,4},{4,8},{8,12},{12,0},{1,5},{5,9},{9,13},{13,1},{2,6},{6,10},{... | collective-permute-start | bytes 98312 | tf_op jit(solution)/shard_map/ppermute | solution.py:50
  69.8 1.5 %collective-permute-start.37 = (bf16[64,256]{1,0:T(8,128)(2,1)S(1)}, bf16[64,256]{1,0:T(8,128)(2,1)S(1)}, u32[]{:S(2)}, u32[]{:S(2)}) collective-permute-start(bf16[64,256]{1,0:T(8,128)(2,1)S(1)} %shard_map.175.refs_2_), channel_id=1, source_target_pairs={{0,12},{4,0},{8,4},{12,8},{1,13},{5,1},{9,5},{13,9},{2,14},{6,2},{... | collective-permute-start | bytes 98312 | tf_op jit(solution)/shard_map/ppermute | solution.py:50
  71.4 0.8 %shard_map.172 = (f32[128,256]{1,0:T(8,128)S(1)}, bf16[128,256]{1,0:T(8,128)(2,1)S(1)}) custom-call(s32[4,4]{1,0:T(4,128)S(1)} %copy-done.4, s32[4,4,16]{2,1,0:T(4,128)S(1)} %copy-done.3, bf16[128,256]{1,0:T(8,128)(2,1)S(1)} %shard_map.171.refs_2_, bf16[128,256]{1,0:T(8,128)(2,1)S(1)} %collective-permute-done.22.refs_3_.refs_0_, ...), custom_call_target="tpu_custom_call" | custom-call | bytes 459840 | tf_op jit(solution)/shard_map/pallas_call | solution.py:34
  72.2 1.4 %collective-permute-done.36.refs_4_ = bf16[64,256]{1,0:T(8,128)(2,1)S(1)} collective-permute-done((bf16[64,256]{1,0:T(8,128)(2,1)S(1)}, bf16[64,256]{1,0:T(8,128)(2,1)S(1)}, u32[]{:S(2)}, u32[]{:S(2)}) %collective-permute-start.36) | collective-permute-done | bytes 32800 | tf_op jit(solution)/shard_map/ppermute | solution.py:50
  73.6 1.1 %collective-permute-done.37.refs_5_ = bf16[64,256]{1,0:T(8,128)(2,1)S(1)} collective-permute-done((bf16[64,256]{1,0:T(8,128)(2,1)S(1)}, bf16[64,256]{1,0:T(8,128)(2,1)S(1)}, u32[]{:S(2)}, u32[]{:S(2)}) %collective-permute-start.37) | collective-permute-done | bytes 32800 | tf_op jit(solution)/shard_map/ppermute | solution.py:50
  74.6 0.8 %shard_map.176 = bf16[4,32,256]{2,1,0:T(8,128)(2,1)} custom-call(f32[128,256]{1,0:T(8,128)S(1)} %get-tuple-element.61.refs_0_, bf16[128,256]{1,0:T(8,128)(2,1)S(1)} %get-tuple-element.62.refs_1_, bf16[64,256]{1,0:T(8,128)(2,1)S(1)} %shard_map.175.refs_2_, bf16[64,256]{1,0:T(8,128)(2,1)S(1)} %collective-permute-done.35.refs_3_, ...), custom_call_target="tpu_custom_call" | custom-call | bytes 393216 | tf_op jit(solution)/shard_map/pallas_call | solution.py:34
  (68 shorter events, 10.1 us)
Async XLA Ops:
  0.0 14.1 %collective-permute-start = (bf16[16,8192]{1,0:T(8,128)(2,1)}, bf16[16,8192]{1,0:T(8,128)(2,1)S(1)}, u32[]{:S(2)}, u32[]{:S(2)}) collective-permute-start(bf16[16,8192]{1,0:T(8,128)(2,1)} %bitcast.7), channel_id=1, source_target_pairs={{0,2},{2,0},{1,3},{3,1},{4,6},{6,4},{5,7},{7,5},{8,10},{10,8},{9,1... | collective-permute-start | bytes 786440 | tf_op jit(solution)/shard_map/ppermute | solution.py:361
  2.6 18.4 %collective-permute-start.1 = (bf16[16,8192]{1,0:T(8,128)(2,1)}, bf16[16,8192]{1,0:T(8,128)(2,1)S(1)}, u32[]{:S(2)}, u32[]{:S(2)}) collective-permute-start(bf16[16,8192]{1,0:T(8,128)(2,1)} %bitcast.8), channel_id=1, source_target_pairs={{0,1},{1,0},{2,3},{3,2},{4,5},{5,4},{6,7},{7,6},{8,9},{9,8},{10,11... | collective-permute-start | bytes 786440 | tf_op jit(solution)/shard_map/ppermute | solution.py:358
  7.0 1.4 %collective-permute-start.3 = (bf16[32,1280]{1,0:T(8,128)(2,1)S(1)}, bf16[32,1280]{1,0:T(8,128)(2,1)S(1)}, u32[]{:S(2)}, u32[]{:S(2)}) collective-permute-start(bf16[32,1280]{1,0:T(8,128)(2,1)S(1)} %get-tuple-element.45), channel_id=1, source_target_pairs={{0,16},{16,0},{1,17},{17,1},{2,18},{18,2},{3,19},{19,3},{4,20},{20... | collective-permute-start | bytes 245768 | tf_op jit(solution)/shard_map/ppermute | solution.py:353
  9.7 8.1 %collective-permute-start.6 = (bf16[32,1280]{1,0:T(8,128)(2,1)S(1)}, bf16[32,1280]{1,0:T(8,128)(2,1)S(1)}, u32[]{:S(2)}, u32[]{:S(2)}) collective-permute-start(bf16[32,1280]{1,0:T(8,128)(2,1)S(1)} %get-tuple-element.49), channel_id=1, source_target_pairs={{0,1},{1,2},{2,3},{3,0},{4,5},{5,6},{6,7},{7,4},{8,9},{9,10},{10,1... | collective-permute-start | bytes 245768 | tf_op jit(solution)/shard_map/ppermute | solution.py:50
  10.2 10.8 %collective-permute-start.7 = (bf16[32,1280]{1,0:T(8,128)(2,1)S(1)}, bf16[32,1280]{1,0:T(8,128)(2,1)S(1)}, u32[]{:S(2)}, u32[]{:S(2)}) collective-permute-start(bf16[32,1280]{1,0:T(8,128)(2,1)S(1)} %get-tuple-element.50), channel_id=1, source_target_pairs={{0,2},{1,3},{2,0},{3,1},{4,6},{5,7},{6,4},{7,5},{8,10},{9,11},{10,... | collective-permute-start | bytes 245768 | tf_op jit(solution)/shard_map/ppermute | solution.py:50
  13.7 7.3 %collective-permute-start.8 = (bf16[32,1280]{1,0:T(8,128)(2,1)S(1)}, bf16[32,1280]{1,0:T(8,128)(2,1)S(1)}, u32[]{:S(2)}, u32[]{:S(2)}) collective-permute-start(bf16[32,1280]{1,0:T(8,128)(2,1)S(1)} %get-tuple-element.51), channel_id=1, source_target_pairs={{0,3},{1,0},{2,1},{3,2},{4,7},{5,4},{6,5},{7,6},{8,11},{9,8},{10,9... | collective-permute-start | bytes 245768 | tf_op jit(solution)/shard_map/ppermute | solution.py:50
  14.1 20.9 %collective-permute-start.16 = (bf16[16,8192]{1,0:T(8,128)(2,1)S(1)}, bf16[16,8192]{1,0:T(8,128)(2,1)S(1)}, u32[]{:S(2)}, u32[]{:S(2)}) collective-permute-start(bf16[16,8192]{1,0:T(8,128)(2,1)S(1)} %collective-permute-done.refs_0_.refs_3_), channel_id=1, source_target_pairs={{0,1},{1,0},{2,3},{3,2},{4,5},{5,4},{6,7},{7,6},{8,9},{9,8},{10,11... | collective-permute-start | bytes 786440 | tf_op jit(solution)/shard_map/ppermute | solution.py:358
  21.1 7.2 %collective-permute-start.9 = (bf16[32,1280]{1,0:T(8,128)(2,1)S(1)}, bf16[32,1280]{1,0:T(8,128)(2,1)S(1)}, u32[]{:S(2)}, u32[]{:S(2)}) collective-permute-start(bf16[32,1280]{1,0:T(8,128)(2,1)S(1)} %shard_map.165.refs_2_), channel_id=1, source_target_pairs={{0,1},{1,2},{2,3},{3,0},{4,5},{5,6},{6,7},{7,4},{8,9},{9,10},{10,1... | collective-permute-start | bytes 245768 | tf_op jit(solution)/shard_map/ppermute | solution.py:50
  21.3 8.3 %collective-permute-start.10 = (bf16[32,1280]{1,0:T(8,128)(2,1)S(1)}, bf16[32,1280]{1,0:T(8,128)(2,1)S(1)}, u32[]{:S(2)}, u32[]{:S(2)}) collective-permute-start(bf16[32,1280]{1,0:T(8,128)(2,1)S(1)} %shard_map.165.refs_2_), channel_id=1, source_target_pairs={{0,2},{1,3},{2,0},{3,1},{4,6},{5,7},{6,4},{7,5},{8,10},{9,11},{10,... | collective-permute-start | bytes 245768 | tf_op jit(solution)/shard_map/ppermute | solution.py:50
  24.7 7.9 %collective-permute-start.11 = (bf16[32,1280]{1,0:T(8,128)(2,1)S(1)}, bf16[32,1280]{1,0:T(8,128)(2,1)S(1)}, u32[]{:S(2)}, u32[]{:S(2)}) collective-permute-start(bf16[32,1280]{1,0:T(8,128)(2,1)S(1)} %shard_map.165.refs_2_), channel_id=1, source_target_pairs={{0,3},{1,0},{2,1},{3,2},{4,7},{5,4},{6,5},{7,6},{8,11},{9,8},{10,9... | collective-permute-start | bytes 245768 | tf_op jit(solution)/shard_map/ppermute | solution.py:50
  26.6 6.0 %collective-permute-start.12 = (bf16[32,1280]{1,0:T(8,128)(2,1)S(1)}, bf16[32,1280]{1,0:T(8,128)(2,1)S(1)}, u32[]{:S(2)}, u32[]{:S(2)}) collective-permute-start(bf16[32,1280]{1,0:T(8,128)(2,1)S(1)} %shard_map.165.refs_2_), channel_id=1, source_target_pairs={{0,16},{16,0},{1,17},{17,1},{2,18},{18,2},{3,19},{19,3},{4,20},{20... | collective-permute-start | bytes 245768 | tf_op jit(solution)/shard_map/ppermute | solution.py:353
  28.3 4.3 %collective-permute-start.13 = (bf16[32,1280]{1,0:T(8,128)(2,1)S(1)}, bf16[32,1280]{1,0:T(8,128)(2,1)S(1)}, u32[]{:S(2)}, u32[]{:S(2)}) collective-permute-start(bf16[32,1280]{1,0:T(8,128)(2,1)S(1)} %collective-permute-done.9.refs_3_), channel_id=1, source_target_pairs={{0,16},{16,0},{1,17},{17,1},{2,18},{18,2},{3,19},{19,3},{4,20},{20... | collective-permute-start | bytes 245768 | tf_op jit(solution)/shard_map/ppermute | solution.py:353
  29.6 3.0 %collective-permute-start.14 = (bf16[32,1280]{1,0:T(8,128)(2,1)S(1)}, bf16[32,1280]{1,0:T(8,128)(2,1)S(1)}, u32[]{:S(2)}, u32[]{:S(2)}) collective-permute-start(bf16[32,1280]{1,0:T(8,128)(2,1)S(1)} %collective-permute-done.10.refs_4_), channel_id=1, source_target_pairs={{0,16},{16,0},{1,17},{17,1},{2,18},{18,2},{3,19},{19,3},{4,20},{20... | collective-permute-start | bytes 245768 | tf_op jit(solution)/shard_map/ppermute | solution.py:353
  35.7 1.7 %collective-permute-start.17 = (bf16[64,1024]{1,0:T(8,128)(2,1)S(1)}, bf16[64,1024]{1,0:T(8,128)(2,1)S(1)}, u32[]{:S(2)}, u32[]{:S(2)}) collective-permute-start(bf16[64,1024]{1,0:T(8,128)(2,1)S(1)} %get-tuple-element.56), channel_id=1, source_target_pairs={{0,16},{16,0},{1,17},{17,1},{2,18},{18,2},{3,19},{19,3},{4,20},{20... | collective-permute-start | bytes 393224 | tf_op jit(solution)/shard_map/ppermute | solution.py:353
  35.9 1.5 %collective-permute-start.18 = (bf16[64,1024]{1,0:T(8,128)(2,1)S(1)}, bf16[64,1024]{1,0:T(8,128)(2,1)S(1)}, u32[]{:S(2)}, u32[]{:S(2)}) collective-permute-start(bf16[64,1024]{1,0:T(8,128)(2,1)S(1)} %get-tuple-element.57), channel_id=1, source_target_pairs={{0,16},{16,0},{1,17},{17,1},{2,18},{18,2},{3,19},{19,3},{4,20},{20... | collective-permute-start | bytes 393224 | tf_op jit(solution)/shard_map/ppermute | solution.py:353
  36.2 1.3 %collective-permute-start.19 = (bf16[64,1024]{1,0:T(8,128)(2,1)S(1)}, bf16[64,1024]{1,0:T(8,128)(2,1)S(1)}, u32[]{:S(2)}, u32[]{:S(2)}) collective-permute-start(bf16[64,1024]{1,0:T(8,128)(2,1)S(1)} %get-tuple-element.58), channel_id=1, source_target_pairs={{0,16},{16,0},{1,17},{17,1},{2,18},{18,2},{3,19},{19,3},{4,20},{20... | collective-permute-start | bytes 393224 | tf_op jit(solution)/shard_map/ppermute | solution.py:353
  36.4 1.4 %collective-permute-start.20 = (bf16[64,1024]{1,0:T(8,128)(2,1)S(1)}, bf16[64,1024]{1,0:T(8,128)(2,1)S(1)}, u32[]{:S(2)}, u32[]{:S(2)}) collective-permute-start(bf16[64,1024]{1,0:T(8,128)(2,1)S(1)} %get-tuple-element.59), channel_id=1, source_target_pairs={{0,16},{16,0},{1,17},{17,1},{2,18},{18,2},{3,19},{19,3},{4,20},{20... | collective-permute-start | bytes 393224 | tf_op jit(solution)/shard_map/ppermute | solution.py:353
  38.1 4.5 %collective-permute-start.21 = (bf16[4,16,8192]{2,1,0:T(8,128)(2,1)S(1)}, bf16[4,16,8192]{2,1,0:T(8,128)(2,1)S(1)}, u32[]{:S(2)}, u32[]{:S(2)}) collective-permute-start(bf16[4,16,8192]{2,1,0:T(8,128)(2,1)S(1)} %shard_map.170.refs_3_), channel_id=1, source_target_pairs={{0,16},{16,0},{1,17},{17,1},{2,18},{18,2},{3,19},{19,3},{4,20},{20... | collective-permute-start | bytes 3145736 | tf_op jit(solution)/shard_map/ppermute | solution.py:353
  38.4 7.1 %collective-permute-start.25 = (bf16[64,1024]{1,0:T(8,128)(2,1)S(1)}, bf16[64,1024]{1,0:T(8,128)(2,1)S(1)}, u32[]{:S(2)}, u32[]{:S(2)}) collective-permute-start(bf16[64,1024]{1,0:T(8,128)(2,1)S(1)} %get-tuple-element.64), channel_id=1, source_target_pairs={{0,1},{1,2},{2,3},{3,0},{4,5},{5,6},{6,7},{7,4},{8,9},{9,10},{10,1... | collective-permute-start | bytes 393224 | tf_op jit(solution)/shard_map/ppermute | solution.py:50
  38.7 11.6 %collective-permute-start.26 = (bf16[64,1024]{1,0:T(8,128)(2,1)S(1)}, bf16[64,1024]{1,0:T(8,128)(2,1)S(1)}, u32[]{:S(2)}, u32[]{:S(2)}) collective-permute-start(bf16[64,1024]{1,0:T(8,128)(2,1)S(1)} %get-tuple-element.65), channel_id=1, source_target_pairs={{0,2},{1,3},{2,0},{3,1},{4,6},{5,7},{6,4},{7,5},{8,10},{9,11},{10,... | collective-permute-start | bytes 393224 | tf_op jit(solution)/shard_map/ppermute | solution.py:50
  41.0 12.1 %collective-permute-start.27 = (bf16[64,1024]{1,0:T(8,128)(2,1)S(1)}, bf16[64,1024]{1,0:T(8,128)(2,1)S(1)}, u32[]{:S(2)}, u32[]{:S(2)}) collective-permute-start(bf16[64,1024]{1,0:T(8,128)(2,1)S(1)} %get-tuple-element.66), channel_id=1, source_target_pairs={{0,3},{1,0},{2,1},{3,2},{4,7},{5,4},{6,5},{7,6},{8,11},{9,8},{10,9... | collective-permute-start | bytes 393224 | tf_op jit(solution)/shard_map/ppermute | solution.py:50
  43.5 9.6 %collective-permute-start.22 = (bf16[128,256]{1,0:T(8,128)(2,1)S(1)}, bf16[128,256]{1,0:T(8,128)(2,1)S(1)}, u32[]{:S(2)}, u32[]{:S(2)}) collective-permute-start(bf16[128,256]{1,0:T(8,128)(2,1)S(1)} %shard_map.171.refs_2_), channel_id=1, source_target_pairs={{0,4},{4,8},{8,12},{12,0},{1,5},{5,9},{9,13},{13,1},{2,6},{6,10},{... | collective-permute-start | bytes 196616 | tf_op jit(solution)/shard_map/ppermute | solution.py:50
  45.0 8.1 %collective-permute-start.23 = (bf16[128,256]{1,0:T(8,128)(2,1)S(1)}, bf16[128,256]{1,0:T(8,128)(2,1)S(1)}, u32[]{:S(2)}, u32[]{:S(2)}) collective-permute-start(bf16[128,256]{1,0:T(8,128)(2,1)S(1)} %shard_map.171.refs_2_), channel_id=1, source_target_pairs={{0,8},{4,12},{8,0},{12,4},{1,9},{5,13},{9,1},{13,5},{2,10},{6,14},... | collective-permute-start | bytes 196616 | tf_op jit(solution)/shard_map/ppermute | solution.py:50
  45.6 7.6 %collective-permute-start.24 = (bf16[128,256]{1,0:T(8,128)(2,1)S(1)}, bf16[128,256]{1,0:T(8,128)(2,1)S(1)}, u32[]{:S(2)}, u32[]{:S(2)}) collective-permute-start(bf16[128,256]{1,0:T(8,128)(2,1)S(1)} %shard_map.171.refs_2_), channel_id=1, source_target_pairs={{0,12},{4,0},{8,4},{12,8},{1,13},{5,1},{9,5},{13,9},{2,14},{6,2},{... | collective-permute-start | bytes 196616 | tf_op jit(solution)/shard_map/ppermute | solution.py:50
  53.2 6.4 %collective-permute-start.28 = (bf16[64,1024]{1,0:T(8,128)(2,1)S(1)}, bf16[64,1024]{1,0:T(8,128)(2,1)S(1)}, u32[]{:S(2)}, u32[]{:S(2)}) collective-permute-start(bf16[64,1024]{1,0:T(8,128)(2,1)S(1)} %shard_map.173.refs_2_), channel_id=1, source_target_pairs={{0,1},{1,2},{2,3},{3,0},{4,5},{5,6},{6,7},{7,4},{8,9},{9,10},{10,1... | collective-permute-start | bytes 393224 | tf_op jit(solution)/shard_map/ppermute | solution.py:50
  53.3 11.6 %collective-permute-start.29 = (bf16[64,1024]{1,0:T(8,128)(2,1)S(1)}, bf16[64,1024]{1,0:T(8,128)(2,1)S(1)}, u32[]{:S(2)}, u32[]{:S(2)}) collective-permute-start(bf16[64,1024]{1,0:T(8,128)(2,1)S(1)} %shard_map.173.refs_2_), channel_id=1, source_target_pairs={{0,2},{1,3},{2,0},{3,1},{4,6},{5,7},{6,4},{7,5},{8,10},{9,11},{10,... | collective-permute-start | bytes 393224 | tf_op jit(solution)/shard_map/ppermute | solution.py:50
  54.5 11.6 %collective-permute-start.33 = (bf16[64,1024]{1,0:T(8,128)(2,1)S(1)}, bf16[64,1024]{1,0:T(8,128)(2,1)S(1)}, u32[]{:S(2)}, u32[]{:S(2)}) collective-permute-start(bf16[64,1024]{1,0:T(8,128)(2,1)S(1)} %shard_map.173.refs_2_), channel_id=1, source_target_pairs={{0,3},{1,0},{2,1},{3,2},{4,7},{5,4},{6,5},{7,6},{8,11},{9,8},{10,9... | collective-permute-start | bytes 393224 | tf_op jit(solution)/shard_map/ppermute | solution.py:50
  55.8 10.3 %collective-permute-start.30 = (bf16[64,1024]{1,0:T(8,128)(2,1)S(1)}, bf16[64,1024]{1,0:T(8,128)(2,1)S(1)}, u32[]{:S(2)}, u32[]{:S(2)}) collective-permute-start(bf16[64,1024]{1,0:T(8,128)(2,1)S(1)} %shard_map.173.refs_2_), channel_id=1, source_target_pairs={{0,16},{16,0},{1,17},{17,1},{2,18},{18,2},{3,19},{19,3},{4,20},{20... | collective-permute-start | bytes 393224 | tf_op jit(solution)/shard_map/ppermute | solution.py:353
  59.6 6.5 %collective-permute-start.31 = (bf16[64,1024]{1,0:T(8,128)(2,1)S(1)}, bf16[64,1024]{1,0:T(8,128)(2,1)S(1)}, u32[]{:S(2)}, u32[]{:S(2)}) collective-permute-start(bf16[64,1024]{1,0:T(8,128)(2,1)S(1)} %collective-permute-done.28.refs_3_), channel_id=1, source_target_pairs={{0,16},{16,0},{1,17},{17,1},{2,18},{18,2},{3,19},{19,3},{4,20},{20... | collective-permute-start | bytes 393224 | tf_op jit(solution)/shard_map/ppermute | solution.py:353
  67.8 4.4 %collective-permute-start.35 = (bf16[64,256]{1,0:T(8,128)(2,1)S(1)}, bf16[64,256]{1,0:T(8,128)(2,1)S(1)}, u32[]{:S(2)}, u32[]{:S(2)}) collective-permute-start(bf16[64,256]{1,0:T(8,128)(2,1)S(1)} %shard_map.175.refs_2_), channel_id=1, source_target_pairs={{0,4},{4,8},{8,12},{12,0},{1,5},{5,9},{9,13},{13,1},{2,6},{6,10},{... | collective-permute-start | bytes 98312 | tf_op jit(solution)/shard_map/ppermute | solution.py:50
  69.3 4.3 %collective-permute-start.36 = (bf16[64,256]{1,0:T(8,128)(2,1)S(1)}, bf16[64,256]{1,0:T(8,128)(2,1)S(1)}, u32[]{:S(2)}, u32[]{:S(2)}) collective-permute-start(bf16[64,256]{1,0:T(8,128)(2,1)S(1)} %shard_map.175.refs_2_), channel_id=1, source_target_pairs={{0,8},{4,12},{8,0},{12,4},{1,9},{5,13},{9,1},{13,5},{2,10},{6,14},... | collective-permute-start | bytes 98312 | tf_op jit(solution)/shard_map/ppermute | solution.py:50
  69.8 4.8 %collective-permute-start.37 = (bf16[64,256]{1,0:T(8,128)(2,1)S(1)}, bf16[64,256]{1,0:T(8,128)(2,1)S(1)}, u32[]{:S(2)}, u32[]{:S(2)}) collective-permute-start(bf16[64,256]{1,0:T(8,128)(2,1)S(1)} %shard_map.175.refs_2_), channel_id=1, source_target_pairs={{0,12},{4,0},{8,4},{12,8},{1,13},{5,1},{9,5},{13,9},{2,14},{6,2},{... | collective-permute-start | bytes 98312 | tf_op jit(solution)/shard_map/ppermute | solution.py:50
  (11 other events, 53.2 us)
